TPU v7x, 256 devices: a whole 4x4x8 slice. The times are simulated.
256 devices in a mesh: row: 32 (over z_hi, x, y), col: 8 (over z_lo, core).
Axes of the slice: x: 4, y: 4, z: 8 (z_hi: 2, z_lo: 4; z = z_hi * 4 + z_lo), core: 2. Of those that a mesh axis runs over, the one named last changes fastest.
Arguments:
- images: bfloat16 [16384, 1152], P(('row', 'col')), may hold values from -200 to 200
- texts: bfloat16 [16384, 1152], P(('row', 'col')), may hold values from -200 to 200, as said below
- log_temp: float32 [1], replicated, may hold values from 2.5 to 3.4
- bias: float32 [1], replicated, may hold values from -8 to -4
Outputs:
- grad_images: float32 [16384, 1152], P(('row', 'col'))
- grad_texts: float32 [16384, 1152], P(('row', 'col'))
Inputs may be any that keep to these rules, and one draw needn't show every extreme that they name: `texts`: raw text embeddings, each row paired with the image row of the same index.
All inputs are finite; a program needn't handle non-finite values.
Results may differ from a plain program's by a relative error of at most 0.025.
Values may be sent and summed in bfloat16 or wider, within the bound.
No kernel may reach another device: no remote copies, remote signals or barrier semaphores. Data moves between devices by JAX's collectives and lax.ppermute only.
A program may use at most 64 MiB of HBM per device.

v0:
```python
import jax
import jax.numpy as jnp
from jax import lax
from jax.sharding import PartitionSpec as P


def normalize(raw):
    values = raw.astype(jnp.float32)
    inverse = lax.rsqrt(jnp.sum(values * values, axis=1, keepdims=True) + 1e-06)
    return (values * inverse, inverse)


def back_norm(unit, inverse, grad_unit):
    along = jnp.sum(unit * grad_unit, axis=1, keepdims=True)
    return (grad_unit - unit * along) * inverse


def local(images, texts, log_temp, bias):
    img_unit, inv_img = normalize(images)
    txt_unit, inv_txt = normalize(texts)
    img_round = img_unit.astype(jnp.bfloat16)
    txt_round = txt_unit.astype(jnp.bfloat16)
    temp = jnp.exp(log_temp[0])
    shift = bias[0]
    own_rows = images.shape[0]
    row_index = lax.axis_index("row")
    col_index = lax.axis_index("col")
    img_block = lax.all_gather(img_round, "col", axis=0, tiled=True)
    block_rows = img_block.shape[0]
    txt_block = lax.all_gather(txt_round, "row", axis=0, tiled=True)
    dots = lax.dot_general(
        img_block, txt_block, (((1,), (1,)), ((), ())), preferred_element_type=jnp.float32
    )
    logits = temp * dots + shift
    local_row = lax.broadcasted_iota(jnp.int32, (block_rows, 1), 0)
    column = lax.broadcasted_iota(jnp.int32, (1, txt_block.shape[0]), 1)
    owner = column // own_rows
    within = column % own_rows
    positive = (owner == row_index) & (local_row == col_index * own_rows + within)
    label = jnp.where(positive, 1.0, -1.0).astype(jnp.float32)
    weights = (-temp * label * jax.nn.sigmoid(-label * logits)).astype(jnp.bfloat16)
    grad_img_unit = lax.psum_scatter(
        jnp.dot(weights, txt_block, preferred_element_type=jnp.float32).astype(jnp.bfloat16),
        "col",
        scatter_dimension=0,
        tiled=True,
    ).astype(jnp.float32)
    grad_txt_unit = lax.psum_scatter(
        lax.dot_general(
            weights, img_block, (((0,), (0,)), ((), ())), preferred_element_type=jnp.float32
        ).astype(jnp.bfloat16),
        "row",
        scatter_dimension=0,
        tiled=True,
    ).astype(jnp.float32)
    return (
        back_norm(img_unit, inv_img, grad_img_unit),
        back_norm(txt_unit, inv_txt, grad_txt_unit),
    )


def solution(mesh):
    in_specs = (P(("row", "col"), None), P(("row", "col"), None), P(), P())
    out_specs = (P(("row", "col"), None), P(("row", "col"), None))
    return jax.shard_map(local, mesh=mesh, in_specs=in_specs, out_specs=out_specs, check_vma=False)
```

profile of v0, /device:TPU:24, one launch (start us, length us, event | category | flops | bytes accessed | tf_op | source)
XLA Modules:
  0.0 489.9 jit_solution(2216608420146167078)
XLA Ops:
  7.2 0.0 all-gather.3.cloned.1.call-start
  7.2 1.0 fusion.12
  8.3 1.7 fusion.11
  9.9 0.0 all-gather.3.cloned.1.call-update
  10.0 0.0 all-gather.5.cloned.1.call-start
  10.0 1.0 fusion.13
  11.1 1.7 fusion.9
  12.7 0.0 all-gather.5.cloned.1.call-update
  12.8 0.0 reduce-scatter.3.cloned.1.call-start
  14.2 36.5 %all-gather.3.cloned.1.call-done = bf16[512,1152]{1,0:T(8,128)(2,1)} async-done(((bf16[64,1152]{1,0:T(8,128)(2,1)}), bf16[512,1152]{1,0:T(8,128)(2,1)}) %all-gather.3.cloned.1.call-update) | async-done | bytes 1179664 | tf_op jit(solution)/shard_map/all_gather | solution.py:28
  50.7 118.3 %all-gather.5.cloned.1.call-done = bf16[2048,1152]{1,0:T(8,128)(2,1)} async-done(((bf16[64,1152]{1,0:T(8,128)(2,1)}), bf16[2048,1152]{1,0:T(8,128)(2,1)}) %all-gather.5.cloned.1.call-update) | async-done | bytes 4718608 | tf_op jit(solution)/shard_map/all_gather | solution.py:30
  169.0 0.0 copy-start.2
  169.0 7.1 %fusion.1 = bf16[512,2048]{1,0:T(8,128)(2,1)S(1)} fusion(bf16[512,1152]{1,0:T(8,128)(2,1)} %all-gather.3.cloned.1.call-done, bf16[2048,1152]{1,0:T(8,128)(2,1)} %all-gather.5.cloned.1.call-done, f32[]{:T(128)} %bitcast.8, f32[]{:T(128)} %bitcast, s32[2048]{0:T(1024)S(1)} %fusion.25, f32[]{:T(128)S(6)} %neg.9, pred[2048]{0:T(1024)(128)(4,1)S(1)} %fusion.24), kind=kOutput, calls=%fused_computation.4 | convolution fusion | flops 2429550592 | bytes 8005644 | tf_op jit(solution)/shard_map/dot_general | solution.py:31
  176.1 0.0 copy-done.2
  176.1 0.0 copy-start.3
  176.1 3.9 convolution_convert_fusion.1
  180.1 0.0 reduce-scatter.3.cloned.1.call-update
  180.1 0.0 reduce-scatter.5.cloned.1.call-start
  180.1 0.0 copy-done.3
  180.1 4.6 convolution_convert_fusion
  184.7 0.0 copy-start
  184.7 0.0 copy-start.1
  184.7 0.0 reduce-scatter.5.cloned.1.call-update
  184.8 28.7 %reduce-scatter.3.cloned.1.call-done = bf16[64,1152]{1,0:T(8,128)(2,1)} async-done(((bf16[512,1152]{1,0:T(8,128)(2,1)}), bf16[64,1152]{1,0:T(8,128)(2,1)}) %reduce-scatter.3.cloned.1.call-update) | async-done | bytes 147472 | tf_op jit(solution)/shard_map/reduce_scatter | solution.py:42
  213.4 0.0 copy-done
  213.4 1.1 fusion.14
  214.6 1.8 fusion.15
  216.3 264.2 %reduce-scatter.5.cloned.1.call-done = bf16[64,1152]{1,0:T(8,128)(2,1)} async-done(((bf16[2048,1152]{1,0:T(8,128)(2,1)}), bf16[64,1152]{1,0:T(8,128)(2,1)}) %reduce-scatter.5.cloned.1.call-update) | async-done | bytes 147472 | tf_op jit(solution)/shard_map/reduce_scatter | solution.py:48
  480.5 0.0 copy-done.1
  480.5 1.1 fusion.16
  481.6 1.8 fusion.17
  (4 shorter events, 0.0 us)
Async XLA Ops:
  7.2 43.5 %all-gather.3.cloned.1.call-start = ((), (), s32[]{:S(2)}) async-start(), calls=%async_computation.2 | async-start | bytes 1327104 | tf_op jit(solution)/shard_map/all_gather | solution.py:28
  10.0 159.0 %all-gather.5.cloned.1.call-start = ((), (), s32[]{:S(2)}) async-start(), calls=%async_computation.3 | async-start | bytes 4866048 | tf_op jit(solution)/shard_map/all_gather | solution.py:30
  12.8 200.7 %reduce-scatter.3.cloned.1.call-start = ((), (), s32[]{:S(2)}) async-start(), calls=%async_computation.4 | async-start | bytes 1327104 | tf_op jit(solution)/shard_map/reduce_scatter | solution.py:42
  169.0 7.1 %copy-start.2 = (bf16[2048,1152]{1,0:T(8,128)(2,1)S(1)}, bf16[2048,1152]{1,0:T(8,128)(2,1)}, u32[]{:S(2)}) copy-start(bf16[2048,1152]{1,0:T(8,128)(2,1)} %all-gather.5.cloned.1.call-done) | copy-start | bytes 14155780
  176.1 4.0 copy-start.3
  180.1 300.4 %reduce-scatter.5.cloned.1.call-start = ((), (), s32[]{:S(2)}) async-start(), calls=%async_computation.5 | async-start | bytes 4866048 | tf_op jit(solution)/shard_map/reduce_scatter | solution.py:48
  184.7 28.7 %copy-start = (bf16[64,1152]{1,0:T(8,128)(2,1)S(1)}, bf16[64,1152]{1,0:T(8,128)(2,1)}, u32[]{:S(2)}) copy-start(bf16[64,1152]{1,0:T(8,128)(2,1)} %param.4) | copy-start | bytes 442372
  184.7 295.8 %copy-start.1 = (bf16[64,1152]{1,0:T(8,128)(2,1)S(1)}, bf16[64,1152]{1,0:T(8,128)(2,1)}, u32[]{:S(2)}) copy-start(bf16[64,1152]{1,0:T(8,128)(2,1)} %param.5) | copy-start | bytes 442372
Sparse Core Ops, SparseCore 0:
  10.4 40.2 all-gather.2
  54.8 114.1 all-gather.4
  180.2 33.1 reduce-scatter.2
  218.8 261.6 reduce-scatter.4
where the time goes:
time: 492 us; the launch traced here: 490 us
  waiting for transfers between devices  448 us (91%)
  matrix products  15.6 us (3%)
  between operations  15.2 us (3%)
  other arithmetic  11.2 us (2%)
    reduce_scatter x1, waiting for transfers between devices, local(): lax.psum_scatter(lax.dot_general(weights, img_block, (((0,), (0,)), ((),...  264 us
    all_gather x1, waiting for transfers between devices, local(): txt_block = lax.all_gather(txt_round, 'row', axis=0, tiled=True)  118 us
    all_gather x1, waiting for transfers between devices, local(): img_block = lax.all_gather(img_round, 'col', axis=0, tiled=True)  36.5 us
    reduce_scatter x1, waiting for transfers between devices, local(): lax.psum_scatter(jnp.dot(weights, txt_block, preferred_element_type=jnp.f...  28.7 us
  transfers between devices with their start and end apart: 4, of which 4 were waited for; matrix products, arithmetic and copies ran while one was open for 2% of the time, Pallas kernels for 0%

commit v1 on v0

v1 whole, which is shorter than its diff:
```python
import jax
import jax.numpy as jnp
from jax import lax
from jax.experimental import pallas as pl
from jax.experimental.pallas import tpu as pltpu
from jax.sharding import PartitionSpec as P

AXES = ("row", "col")
F32 = jnp.float32
BF16 = jnp.bfloat16
LOG2E = 1.4426950408889634
SIZE_X, SIZE_Y, SIZE_Z, CORES = 4, 4, 8, 2


def device(x, y, z, c):
    return ((z // 4) * 16 + x * 4 + y) * 8 + (z % 4) * 2 + c


def shift(values, move):
    pairs = []
    for x in range(SIZE_X):
        for y in range(SIZE_Y):
            for z in range(SIZE_Z):
                for c in range(CORES):
                    nx, ny, nz, nc = move(x, y, z, c)
                    pairs.append((device(x, y, z, c), device(nx % SIZE_X, ny % SIZE_Y, nz % SIZE_Z, nc)))
    return lax.ppermute(values, AXES, pairs)


def first(k):
    return lambda x, y, z, c: (x + k, y, z, c) if c == 0 else (x, y + k, z, c)


def second(k):
    return lambda x, y, z, c: (x, y + k, z, c) if c == 0 else (x + k, y, z, c)


def line(k):
    return lambda x, y, z, c: (x, y, z + k, c) if c == 0 else (x, y, z - k, c)


def other(x, y, z, c):
    return (x, y, z, 1 - c)


def cat(parts):
    return jnp.concatenate(parts, axis=0)


def normalize(raw):
    values = raw.astype(F32)
    inverse = lax.rsqrt(jnp.sum(values * values, axis=1, keepdims=True) + 1e-06)
    return (values * inverse, inverse)


def back_norm(unit, inverse, grad_unit):
    along = jnp.sum(unit * grad_unit, axis=1, keepdims=True)
    return (grad_unit - unit * along) * inverse


def load(parts, whole, sems, base):
    copies, at = [], 0
    for n, part in enumerate(parts):
        rows = part.shape[0]
        copies.append(pltpu.make_async_copy(part, whole.at[pl.ds(at, rows)], sems.at[base + n]))
        at += rows
    for copy in copies:
        copy.start()
    return copies


def weights_kernel(n_img, n_txt, own, scal_ref, *refs):
    img_parts, txt_parts = refs[:n_img], refs[n_img:n_img + n_txt]
    w_ref, keep_ref, send_ref, img, txt, sems = refs[n_img + n_txt:]
    img_copies = load(img_parts, img, sems, 0)
    txt_copies = load(txt_parts, txt, sems, n_img)
    temp, shift_ = scal_ref[0], scal_ref[1]
    slope, offset = -temp * LOG2E, -shift_ * LOG2E
    for copy in txt_copies:
        copy.wait()
    at = 0
    for part, copy in zip(img_parts, img_copies):
        copy.wait()
        rows = part.shape[0]
        dots = lax.dot_general(
            img[at:at + rows, :], txt[...], (((1,), (1,)), ((), ())), preferred_element_type=F32
        )
        power = dots * slope + offset
        w_ref[at:at + rows, :] = (temp / (1.0 + jnp.exp2(power))).astype(BF16)
        if at == 0:
            corner = power[:own, :2 * own]
            row = lax.broadcasted_iota(jnp.int32, corner.shape, 0)
            column = lax.broadcasted_iota(jnp.int32, corner.shape, 1)
            positive = row == column
            signed = jnp.where(positive, -corner, corner)
            scale = jnp.where(positive, -temp, temp)
            w_ref[:own, :2 * own] = (scale / (1.0 + jnp.exp2(signed))).astype(BF16)
        at += rows
    half = txt.shape[0] // 2
    step = 256
    for out, start in ((send_ref, half), (keep_ref, 0)):
        for t in range(0, half, step):
            grad = lax.dot_general(
                w_ref[:, start + t:start + t + step], img[...], (((0,), (0,)), ((), ())), preferred_element_type=F32
            )
            out[t:t + step, :] = grad.astype(out.dtype)


def image_kernel(n_txt, w_ref, *refs):
    txt_parts, outs = refs[:n_txt], refs[n_txt:-2]
    txt, sems = refs[-2:]
    copies = load(txt_parts, txt, sems, 0)
    for copy in copies:
        copy.wait()
    at = 0
    for out in outs:
        rows = out.shape[0]
        grad = jnp.dot(w_ref[at:at + rows, :], txt[...], preferred_element_type=F32)
        out[...] = grad.astype(out.dtype)
        at += rows


def block(img_parts, txt_parts, scalars, own):
    n_img, n_txt = len(img_parts), len(txt_parts)
    rows = sum(p.shape[0] for p in img_parts)
    cols = sum(p.shape[0] for p in txt_parts)
    dim = img_parts[0].shape[1]
    anywhere = pl.BlockSpec(memory_space=pl.ANY)
    vmem = pl.BlockSpec(memory_space=pltpu.VMEM)
    flops = 2 * rows * cols * dim
    w, keep, send = pl.pallas_call(
        lambda *refs: weights_kernel(n_img, n_txt, own, *refs),
        out_shape=(
            jax.ShapeDtypeStruct((rows, cols), BF16),
            jax.ShapeDtypeStruct((cols // 2, dim), BF16),
            jax.ShapeDtypeStruct((cols // 2, dim), BF16),
        ),
        in_specs=[pl.BlockSpec(memory_space=pltpu.SMEM)] + [anywhere] * (n_img + n_txt),
        out_specs=(vmem, vmem, vmem),
        scratch_shapes=[
            pltpu.VMEM((rows, dim), BF16),
            pltpu.VMEM((cols, dim), BF16),
            pltpu.SemaphoreType.DMA((n_img + n_txt,)),
        ],
        compiler_params=pltpu.CompilerParams(vmem_limit_bytes=40 * 1024 * 1024),
        cost_estimate=pl.CostEstimate(flops=2 * flops, bytes_accessed=10 * 1024 * 1024, transcendentals=2 * rows * cols),
    )(scalars, *img_parts, *txt_parts)
    grads = pl.pallas_call(
        lambda *refs: image_kernel(n_txt, *refs),
        out_shape=tuple(
            jax.ShapeDtypeStruct(p.shape, F32 if n == 0 else BF16) for n, p in enumerate(img_parts)
        ),
        in_specs=[vmem] + [anywhere] * n_txt,
        out_specs=tuple([vmem] * n_img),
        scratch_shapes=[pltpu.VMEM((cols, dim), BF16), pltpu.SemaphoreType.DMA((n_txt,))],
        compiler_params=pltpu.CompilerParams(vmem_limit_bytes=40 * 1024 * 1024),
        cost_estimate=pl.CostEstimate(flops=flops, bytes_accessed=8 * 1024 * 1024, transcendentals=0),
    )(w, *txt_parts)
    return keep, send, grads


def local(images, texts, log_temp, bias):
    own = images.shape[0]
    img_unit, inv_img = normalize(images)
    txt_unit, inv_txt = normalize(texts)
    img_round = img_unit.astype(BF16)
    txt_round = txt_unit.astype(BF16)
    scalars = jnp.concatenate([jnp.exp(log_temp), bias])

    side = [shift(img_round, first(k)) for k in (1, 2, 3)]
    swapped = shift(txt_round, other)
    pair = cat([txt_round, swapped])
    near2 = shift(pair, line(2))
    near1 = shift(pair, line(1))
    group = cat([img_round] + side)
    far = [shift(group, second(k)) for k in (1, 2, 3)]
    tied = lax.optimization_barrier((near2, *side))[0]
    near3 = shift(tied, line(1))
    near4 = shift(tied[:own], line(2))
    mine = [txt_round, near4, near1, near2, near3]
    theirs = [swapped] + [shift(v, other) for v in mine[1:]]

    keep, send, grads = block([group] + far, mine + theirs, scalars, own)

    total = keep.astype(F32) + shift(send, other).astype(F32)
    packed = total.astype(BF16)
    part4, part1 = packed[own:2 * own], packed[2 * own:4 * own]
    part2, part3 = total[4 * own:6 * own], packed[6 * own:]
    got3 = shift(part3, line(-1))
    got4 = shift(part4, line(-2))
    part2 = part2 + got3.astype(F32)
    part2 = cat([part2[:own] + got4.astype(F32), part2[own:]]).astype(BF16)
    got1 = shift(part1, line(-1))
    got2 = shift(part2, line(-2))
    landed = got1.astype(F32) + got2.astype(F32)
    grad_txt = total[:own] + landed[:own] + shift(landed[own:].astype(BF16), other).astype(F32)

    back = [shift(g, second(-k)) for k, g in zip((1, 2, 3), grads[1:])]
    sums = grads[0] + sum(b.astype(F32) for b in back)
    sums16 = sums.astype(BF16)
    last = [shift(sums16[k * own:(k + 1) * own], first(-k)) for k in (1, 2, 3)]
    grad_img = sums[:own] + sum(b.astype(F32) for b in last)

    return back_norm(img_unit, inv_img, grad_img), back_norm(txt_unit, inv_txt, grad_txt)


def solution(mesh):
    in_specs = (P(("row", "col"), None), P(("row", "col"), None), P(), P())
    out_specs = (P(("row", "col"), None), P(("row", "col"), None))
    return jax.shard_map(local, mesh=mesh, in_specs=in_specs, out_specs=out_specs, check_vma=False)
```

time: 492 us -> 106 us (0.22)
  the two profiles are of different devices: /device:TPU:24 before, /device:TPU:1 now
where the time goes in v1:
time: 106 us
  starting transfers between devices  49.3 us (47%)
  waiting for transfers between devices  35.4 us (33%)
  Pallas kernels  13 us (12%)
  other arithmetic  6.25 us (6%)
  between operations  2.15 us (2%)
    ppermute x27, starting transfers between devices, shift(): return lax.ppermute(values, AXES, pairs)  49.3 us
    ppermute x27, waiting for transfers between devices, shift(): return lax.ppermute(values, AXES, pairs)  35.4 us
    pallas_call x1, Pallas kernels, block(): pl.pallas_call(lambda *refs: weights_kernel(n_img, n_txt, own, *refs), ou...  8.88 us
    pallas_call x1, Pallas kernels, block(): pl.pallas_call(lambda *refs: image_kernel(n_txt, *refs), out_shape=tuple(...  4.14 us
  transfers between devices with their start and end apart: 27, of which 15 were waited for; matrix products, arithmetic and copies ran while one was open for 3% of the time, Pallas kernels for 0%

profile of v1, /device:TPU:1, one launch (start us, length us, event | category | flops | bytes accessed | tf_op | source)
XLA Modules:
  0.0 106.2 jit_solution(10587793737760284816)
XLA Ops:
  0.6 0.0 copy-start
  0.6 1.1 %fusion.13 = f32[64]{0:T(128)S(1)} fusion(bf16[64,1152]{1,0:T(8,128)(2,1)} %param.5), kind=kLoop, calls=%fused_computation.22 | loop fusion | flops 221120 | bytes 147712 | tf_op jit(solution)/shard_map/reduce_sum | solution.py:52
  1.7 1.0 fusion.2.refs_5_.refs_1_
  2.7 3.3 %collective-permute-start.6 = (bf16[64,1152]{1,0:T(8,128)(2,1)S(1)}, bf16[64,1152]{1,0:T(8,128)(2,1)S(1)}, u32[]{:S(2)}, u32[]{:S(2)}) collective-permute-start(bf16[64,1152]{1,0:T(8,128)(2,1)S(1)} %fusion.2.refs_5_.refs_1_), channel_id=1, source_target_pairs={{0,1},{1,0},{2,3},{3,2},{4,5},{5,4},{6,7},{7,6},{128,129},{129,128... | collective-permute-start | bytes 442376 | tf_op jit(solution)/shard_map/ppermute | solution.py:27
  6.1 1.0 fusion.9
  7.1 0.0 collective-permute-done.6.refs_10_.refs_6_
  7.2 3.9 %collective-permute-start.9 = (bf16[128,1152]{1,0:T(8,128)(2,1)S(1)}, bf16[128,1152]{1,0:T(8,128)(2,1)S(1)}, u32[]{:S(2)}, u32[]{:S(2)}) collective-permute-start(bf16[128,1152]{1,0:T(8,128)(2,1)S(1)} %pad_maximum_fusion.1), channel_id=1, source_target_pairs={{0,2},{1,135},{2,4},{3,1},{4,6},{5,3},{6,128},{7,5},{128,130},{129... | collective-permute-start | bytes 884744 | tf_op jit(solution)/shard_map/ppermute | solution.py:27
  11.1 1.2 %collective-permute-start.7 = (bf16[128,1152]{1,0:T(8,128)(2,1)S(1)}, bf16[128,1152]{1,0:T(8,128)(2,1)S(1)}, u32[]{:S(2)}, u32[]{:S(2)}) collective-permute-start(bf16[128,1152]{1,0:T(8,128)(2,1)S(1)} %pad_maximum_fusion.1), channel_id=1, source_target_pairs={{0,4},{1,133},{2,6},{3,135},{4,128},{5,1},{6,130},{7,3},{128,132},... | collective-permute-start | bytes 884744 | tf_op jit(solution)/shard_map/ppermute | solution.py:27
  12.3 0.1 fusion.5
  12.4 2.8 %collective-permute-start.2 = (bf16[64,1152]{1,0:T(8,128)(2,1)S(1)}, bf16[64,1152]{1,0:T(8,128)(2,1)S(1)}, u32[]{:S(2)}, u32[]{:S(2)}) collective-permute-start(bf16[64,1152]{1,0:T(8,128)(2,1)S(1)} %fusion.5), channel_id=1, source_target_pairs={{0,96},{1,25},{2,98},{3,27},{4,100},{5,29},{6,102},{7,31},{128,224... | collective-permute-start | bytes 442376 | tf_op jit(solution)/shard_map/ppermute | solution.py:27
  15.2 0.3 collective-permute-start.1
  15.5 0.7 collective-permute-start
  16.2 2.6 %collective-permute-done.2 = bf16[64,1152]{1,0:T(8,128)(2,1)S(1)} collective-permute-done((bf16[64,1152]{1,0:T(8,128)(2,1)S(1)}, bf16[64,1152]{1,0:T(8,128)(2,1)S(1)}, u32[]{:S(2)}, u32[]{:S(2)}) %collective-permute-start.2) | collective-permute-done | bytes 147488 | tf_op jit(solution)/shard_map/ppermute | solution.py:27
  18.8 2.1 %collective-permute-done.1 = bf16[64,1152]{1,0:T(8,128)(2,1)S(1)} collective-permute-done((bf16[64,1152]{1,0:T(8,128)(2,1)S(1)}, bf16[64,1152]{1,0:T(8,128)(2,1)S(1)}, u32[]{:S(2)}, u32[]{:S(2)}) %collective-permute-start.1) | collective-permute-done | bytes 147488 | tf_op jit(solution)/shard_map/ppermute | solution.py:27
  21.0 1.3 %collective-permute-done = bf16[64,1152]{1,0:T(8,128)(2,1)S(1)} collective-permute-done((bf16[64,1152]{1,0:T(8,128)(2,1)S(1)}, bf16[64,1152]{1,0:T(8,128)(2,1)S(1)}, u32[]{:S(2)}, u32[]{:S(2)}) %collective-permute-start) | collective-permute-done | bytes 147488 | tf_op jit(solution)/shard_map/ppermute | solution.py:27
  22.3 0.0 collective-permute-done.7.refs_8_.refs_4_
  22.3 2.9 %collective-permute-start.8 = (bf16[64,1152]{1,0:T(8,128)(2,1)S(1)}, bf16[64,1152]{1,0:T(8,128)(2,1)S(1)}, u32[]{:S(2)}, u32[]{:S(2)}) collective-permute-start(bf16[64,1152]{1,0:T(8,128)(2,1)S(1)} %slice.44), channel_id=1, source_target_pairs={{0,4},{1,133},{2,6},{3,135},{4,128},{5,1},{6,130},{7,3},{128,132},... | collective-permute-start | bytes 442376 | tf_op jit(solution)/shard_map/ppermute | solution.py:27
  25.2 0.7 collective-permute-start.12
  25.9 1.9 %collective-permute-start.5 = (bf16[256,1152]{1,0:T(8,128)(2,1)S(1)}, bf16[256,1152]{1,0:T(8,128)(2,1)S(1)}, u32[]{:S(2)}, u32[]{:S(2)}) collective-permute-start(bf16[256,1152]{1,0:T(8,128)(2,1)S(1)} %pad_maximum_fusion.refs_1_), channel_id=1, source_target_pairs={{0,24},{1,97},{2,26},{3,99},{4,28},{5,101},{6,30},{7,103},{128,152... | collective-permute-start | bytes 1769480 | tf_op jit(solution)/shard_map/ppermute | solution.py:27
  27.8 0.5 collective-permute-start.4
  28.3 0.6 collective-permute-start.3
  28.9 0.2 collective-permute-done.8.refs_6_.refs_2_
  29.1 1.3 %collective-permute-start.10 = (bf16[128,1152]{1,0:T(8,128)(2,1)S(1)}, bf16[128,1152]{1,0:T(8,128)(2,1)S(1)}, u32[]{:S(2)}, u32[]{:S(2)}) collective-permute-start(bf16[128,1152]{1,0:T(8,128)(2,1)S(1)} %collective-permute-done.7.refs_8_.refs_4_), channel_id=1, source_target_pairs={{0,2},{1,135},{2,4},{3,1},{4,6},{5,3},{6,128},{7,5},{128,130},{129... | collective-permute-start | bytes 884744 | tf_op jit(solution)/shard_map/ppermute | solution.py:27
  30.4 0.0 collective-permute-done.12.refs_12_.refs_8_
  30.4 2.3 %collective-permute-start.11 = (bf16[64,1152]{1,0:T(8,128)(2,1)S(1)}, bf16[64,1152]{1,0:T(8,128)(2,1)S(1)}, u32[]{:S(2)}, u32[]{:S(2)}) collective-permute-start(bf16[64,1152]{1,0:T(8,128)(2,1)S(1)} %collective-permute-done.8.refs_6_.refs_2_), channel_id=1, source_target_pairs={{0,1},{1,0},{2,3},{3,2},{4,5},{5,4},{6,7},{7,6},{128,129},{129,128... | collective-permute-start | bytes 442376 | tf_op jit(solution)/shard_map/ppermute | solution.py:27
  32.7 1.0 collective-permute-done.11.refs_11_.refs_7_
  33.7 0.4 collective-permute-start.13
  34.0 1.0 collective-permute-done.10.refs_9_.refs_5_
  35.0 3.5 %collective-permute-start.14 = (bf16[128,1152]{1,0:T(8,128)(2,1)S(1)}, bf16[128,1152]{1,0:T(8,128)(2,1)S(1)}, u32[]{:S(2)}, u32[]{:S(2)}) collective-permute-start(bf16[128,1152]{1,0:T(8,128)(2,1)S(1)} %collective-permute-done.10.refs_9_.refs_5_), channel_id=1, source_target_pairs={{0,1},{1,0},{2,3},{3,2},{4,5},{5,4},{6,7},{7,6},{128,129},{129,128... | collective-permute-start | bytes 884744 | tf_op jit(solution)/shard_map/ppermute | solution.py:27
  39.9 0.1 pad_maximum_fusion.3.refs_0_
  39.9 0.0 collective-permute-done.13.refs_13_.refs_9_
  40.0 1.0 collective-permute-done.5.refs_4_
  41.0 3.7 %collective-permute-done.3.refs_2_ = bf16[256,1152]{1,0:T(8,128)(2,1)S(1)} collective-permute-done((bf16[256,1152]{1,0:T(8,128)(2,1)S(1)}, bf16[256,1152]{1,0:T(8,128)(2,1)S(1)}, u32[]{:S(2)}, u32[]{:S(2)}) %collective-permute-start.3) | collective-permute-done | bytes 589856 | tf_op jit(solution)/shard_map/ppermute | solution.py:27
  44.7 8.9 %shard_map.59 = (bf16[1024,1024]{1,0:T(8,128)(2,1)S(1)}, bf16[512,1152]{1,0:T(8,128)(2,1)S(1)}, bf16[512,1152]{1,0:T(8,128)(2,1)S(1)}) custom-call(f32[2]{0:T(128)S(1)} %pad_maximum_fusion.3.refs_0_, bf16[256,1152]{1,0:T(8,128)(2,1)S(1)} %pad_maximum_fusion.refs_1_, bf16[256,1152]{1,0:T(8,128)(2,1)S(1)} %collective-permute-done.3.refs_2_, ...), custom_call_target="tpu_custom_call" | custom-call | flops 4831838208 | bytes 10485760 | tf_op jit(solution)/shard_map/pallas_call | solution.py:131
  53.5 4.1 %shard_map.60 = (f32[256,1152]{1,0:T(8,128)S(1)}, bf16[256,1152]{1,0:T(8,128)(2,1)S(1)}, bf16[256,1152]{1,0:T(8,128)(2,1)S(1)}, bf16[256,1152]{1,0:T(8,128)(2,1)S(1)}) custom-call(bf16[1024,1024]{1,0:T(8,128)(2,1)S(1)} %get-tuple-element.11.refs_0_, bf16[64,1152]{1,0:T(8,128)(2,1)S(1)} %fusion.2.refs_5_.refs_1_, ...), custom_call_target="tpu_custom_call" | custom-call | flops 2415919104 | bytes 8388608 | tf_op jit(solution)/shard_map/pallas_call | solution.py:148
  57.7 0.4 collective-permute-start.15
  58.1 0.5 collective-permute-start.16
  58.6 0.6 collective-permute-start.17
  59.2 2.6 %collective-permute-start.21 = (bf16[512,1152]{1,0:T(8,128)(2,1)S(1)}, bf16[512,1152]{1,0:T(8,128)(2,1)S(1)}, u32[]{:S(2)}, u32[]{:S(2)}) collective-permute-start(bf16[512,1152]{1,0:T(8,128)(2,1)S(1)} %get-tuple-element.17), channel_id=1, source_target_pairs={{0,1},{1,0},{2,3},{3,2},{4,5},{5,4},{6,7},{7,6},{128,129},{129,128... | collective-permute-start | bytes 3538952 | tf_op jit(solution)/shard_map/ppermute | solution.py:27
  61.9 4.9 %collective-permute-done.15 = bf16[256,1152]{1,0:T(8,128)(2,1)S(1)} collective-permute-done((bf16[256,1152]{1,0:T(8,128)(2,1)S(1)}, bf16[256,1152]{1,0:T(8,128)(2,1)S(1)}, u32[]{:S(2)}, u32[]{:S(2)}) %collective-permute-start.15) | collective-permute-done | bytes 589856 | tf_op jit(solution)/shard_map/ppermute | solution.py:27
  66.8 1.9 %collective-permute-done.16 = bf16[256,1152]{1,0:T(8,128)(2,1)S(1)} collective-permute-done((bf16[256,1152]{1,0:T(8,128)(2,1)S(1)}, bf16[256,1152]{1,0:T(8,128)(2,1)S(1)}, u32[]{:S(2)}, u32[]{:S(2)}) %collective-permute-start.16) | collective-permute-done | bytes 589856 | tf_op jit(solution)/shard_map/ppermute | solution.py:27
  68.7 6.3 %collective-permute-done.17 = bf16[256,1152]{1,0:T(8,128)(2,1)S(1)} collective-permute-done((bf16[256,1152]{1,0:T(8,128)(2,1)S(1)}, bf16[256,1152]{1,0:T(8,128)(2,1)S(1)}, u32[]{:S(2)}, u32[]{:S(2)}) %collective-permute-start.17) | collective-permute-done | bytes 589856 | tf_op jit(solution)/shard_map/ppermute | solution.py:27
  74.9 0.3 fusion.17
  75.2 0.0 collective-permute-done.21
  75.2 0.3 fusion.16
  75.6 0.1 collective-permute-start.23
  75.7 3.1 %collective-permute-start.18 = (bf16[64,1152]{1,0:T(8,128)(2,1)S(1)}, bf16[64,1152]{1,0:T(8,128)(2,1)S(1)}, u32[]{:S(2)}, u32[]{:S(2)}) collective-permute-start(bf16[64,1152]{1,0:T(8,128)(2,1)S(1)} %get-tuple-element.24), channel_id=1, source_target_pairs={{0,96},{1,25},{2,98},{3,27},{4,100},{5,29},{6,102},{7,31},{128,224... | collective-permute-start | bytes 442376 | tf_op jit(solution)/shard_map/ppermute | solution.py:27
  78.9 1.3 %collective-permute-start.19 = (bf16[64,1152]{1,0:T(8,128)(2,1)S(1)}, bf16[64,1152]{1,0:T(8,128)(2,1)S(1)}, u32[]{:S(2)}, u32[]{:S(2)}) collective-permute-start(bf16[64,1152]{1,0:T(8,128)(2,1)S(1)} %get-tuple-element.26), channel_id=1, source_target_pairs={{0,64},{1,17},{2,66},{3,19},{4,68},{5,21},{6,70},{7,23},{128,192},... | collective-permute-start | bytes 442376 | tf_op jit(solution)/shard_map/ppermute | solution.py:27
  80.2 3.6 %collective-permute-start.24 = (bf16[64,1152]{1,0:T(8,128)(2,1)S(1)}, bf16[64,1152]{1,0:T(8,128)(2,1)S(1)}, u32[]{:S(2)}, u32[]{:S(2)}) collective-permute-start(bf16[64,1152]{1,0:T(8,128)(2,1)S(1)} %slice.67), channel_id=1, source_target_pairs={{0,132},{1,5},{2,134},{3,7},{4,0},{5,129},{6,2},{7,131},{128,4},{1... | collective-permute-start | bytes 442376 | tf_op jit(solution)/shard_map/ppermute | solution.py:27
  83.8 0.0 collective-permute-done.23
  83.8 0.0 collective-permute-start.22
  83.8 0.1 slice_add_fusion
  83.9 2.6 %collective-permute-done.24 = bf16[64,1152]{1,0:T(8,128)(2,1)S(1)} collective-permute-done((bf16[64,1152]{1,0:T(8,128)(2,1)S(1)}, bf16[64,1152]{1,0:T(8,128)(2,1)S(1)}, u32[]{:S(2)}, u32[]{:S(2)}) %collective-permute-start.24) | collective-permute-done | bytes 147488 | tf_op jit(solution)/shard_map/ppermute | solution.py:27
  86.6 4.0 %collective-permute-start.25 = (bf16[128,1152]{1,0:T(8,128)(2,1)S(1)}, bf16[128,1152]{1,0:T(8,128)(2,1)S(1)}, u32[]{:S(2)}, u32[]{:S(2)}) collective-permute-start(bf16[128,1152]{1,0:T(8,128)(2,1)S(1)} %pad_maximum_fusion.2), channel_id=1, source_target_pairs={{0,132},{1,5},{2,134},{3,7},{4,0},{5,129},{6,2},{7,131},{128,4},{1... | collective-permute-start | bytes 884744 | tf_op jit(solution)/shard_map/ppermute | solution.py:27
  90.5 0.0 collective-permute-done.19
  90.5 0.2 fusion.6
  90.8 0.5 collective-permute-done.22
  91.3 6.1 %collective-permute-done.25 = bf16[128,1152]{1,0:T(8,128)(2,1)S(1)} collective-permute-done((bf16[128,1152]{1,0:T(8,128)(2,1)S(1)}, bf16[128,1152]{1,0:T(8,128)(2,1)S(1)}, u32[]{:S(2)}, u32[]{:S(2)}) %collective-permute-start.25) | collective-permute-done | bytes 294944 | tf_op jit(solution)/shard_map/ppermute | solution.py:27
  97.4 0.1 convert_add_fusion.1
  97.5 6.6 %collective-permute-start.26 = (bf16[64,1152]{1,0:T(8,128)(2,1)S(1)}, bf16[64,1152]{1,0:T(8,128)(2,1)S(1)}, u32[]{:S(2)}, u32[]{:S(2)}) collective-permute-start(bf16[64,1152]{1,0:T(8,128)(2,1)S(1)} %slice.94), channel_id=1, source_target_pairs={{0,1},{1,0},{2,3},{3,2},{4,5},{5,4},{6,7},{7,6},{128,129},{129,128... | collective-permute-start | bytes 442376 | tf_op jit(solution)/shard_map/ppermute | solution.py:27
  104.1 0.9 fusion.8
  105.0 0.2 collective-permute-done.26
  105.1 0.2 fusion.10
  105.3 0.8 fusion.12
  (21 shorter events, 0.3 us)
Async XLA Ops:
  0.6 11.6 %copy-start = (bf16[64,1152]{1,0:T(8,128)(2,1)S(1)}, bf16[64,1152]{1,0:T(8,128)(2,1)}, u32[]{:S(2)}) copy-start(bf16[64,1152]{1,0:T(8,128)(2,1)} %param.4) | copy-start | bytes 442372
  2.7 4.4 %collective-permute-start.6 = (bf16[64,1152]{1,0:T(8,128)(2,1)S(1)}, bf16[64,1152]{1,0:T(8,128)(2,1)S(1)}, u32[]{:S(2)}, u32[]{:S(2)}) collective-permute-start(bf16[64,1152]{1,0:T(8,128)(2,1)S(1)} %fusion.2.refs_5_.refs_1_), channel_id=1, source_target_pairs={{0,1},{1,0},{2,3},{3,2},{4,5},{5,4},{6,7},{7,6},{128,129},{129,128... | collective-permute-start | bytes 442376 | tf_op jit(solution)/shard_map/ppermute | solution.py:27
  7.2 18.0 %collective-permute-start.9 = (bf16[128,1152]{1,0:T(8,128)(2,1)S(1)}, bf16[128,1152]{1,0:T(8,128)(2,1)S(1)}, u32[]{:S(2)}, u32[]{:S(2)}) collective-permute-start(bf16[128,1152]{1,0:T(8,128)(2,1)S(1)} %pad_maximum_fusion.1), channel_id=1, source_target_pairs={{0,2},{1,135},{2,4},{3,1},{4,6},{5,3},{6,128},{7,5},{128,130},{129... | collective-permute-start | bytes 884744 | tf_op jit(solution)/shard_map/ppermute | solution.py:27
  11.1 11.2 %collective-permute-start.7 = (bf16[128,1152]{1,0:T(8,128)(2,1)S(1)}, bf16[128,1152]{1,0:T(8,128)(2,1)S(1)}, u32[]{:S(2)}, u32[]{:S(2)}) collective-permute-start(bf16[128,1152]{1,0:T(8,128)(2,1)S(1)} %pad_maximum_fusion.1), channel_id=1, source_target_pairs={{0,4},{1,133},{2,6},{3,135},{4,128},{5,1},{6,130},{7,3},{128,132},... | collective-permute-start | bytes 884744 | tf_op jit(solution)/shard_map/ppermute | solution.py:27
  12.4 6.5 %collective-permute-start.2 = (bf16[64,1152]{1,0:T(8,128)(2,1)S(1)}, bf16[64,1152]{1,0:T(8,128)(2,1)S(1)}, u32[]{:S(2)}, u32[]{:S(2)}) collective-permute-start(bf16[64,1152]{1,0:T(8,128)(2,1)S(1)} %fusion.5), channel_id=1, source_target_pairs={{0,96},{1,25},{2,98},{3,27},{4,100},{5,29},{6,102},{7,31},{128,224... | collective-permute-start | bytes 442376 | tf_op jit(solution)/shard_map/ppermute | solution.py:27
  15.2 5.8 %collective-permute-start.1 = (bf16[64,1152]{1,0:T(8,128)(2,1)S(1)}, bf16[64,1152]{1,0:T(8,128)(2,1)S(1)}, u32[]{:S(2)}, u32[]{:S(2)}) collective-permute-start(bf16[64,1152]{1,0:T(8,128)(2,1)S(1)} %fusion.5), channel_id=1, source_target_pairs={{0,64},{1,17},{2,66},{3,19},{4,68},{5,21},{6,70},{7,23},{128,192},... | collective-permute-start | bytes 442376 | tf_op jit(solution)/shard_map/ppermute | solution.py:27
  15.5 6.7 %collective-permute-start = (bf16[64,1152]{1,0:T(8,128)(2,1)S(1)}, bf16[64,1152]{1,0:T(8,128)(2,1)S(1)}, u32[]{:S(2)}, u32[]{:S(2)}) collective-permute-start(bf16[64,1152]{1,0:T(8,128)(2,1)S(1)} %fusion.5), channel_id=1, source_target_pairs={{0,32},{1,9},{2,34},{3,11},{4,36},{5,13},{6,38},{7,15},{128,160},{... | collective-permute-start | bytes 442376 | tf_op jit(solution)/shard_map/ppermute | solution.py:27
  22.3 6.8 %collective-permute-start.8 = (bf16[64,1152]{1,0:T(8,128)(2,1)S(1)}, bf16[64,1152]{1,0:T(8,128)(2,1)S(1)}, u32[]{:S(2)}, u32[]{:S(2)}) collective-permute-start(bf16[64,1152]{1,0:T(8,128)(2,1)S(1)} %slice.44), channel_id=1, source_target_pairs={{0,4},{1,133},{2,6},{3,135},{4,128},{5,1},{6,130},{7,3},{128,132},... | collective-permute-start | bytes 442376 | tf_op jit(solution)/shard_map/ppermute | solution.py:27
  25.2 5.2 %collective-permute-start.12 = (bf16[128,1152]{1,0:T(8,128)(2,1)S(1)}, bf16[128,1152]{1,0:T(8,128)(2,1)S(1)}, u32[]{:S(2)}, u32[]{:S(2)}) collective-permute-start(bf16[128,1152]{1,0:T(8,128)(2,1)S(1)} %collective-permute-done.9.refs_7_.refs_3_), channel_id=1, source_target_pairs={{0,1},{1,0},{2,3},{3,2},{4,5},{5,4},{6,7},{7,6},{128,129},{129,128... | collective-permute-start | bytes 884744 | tf_op jit(solution)/shard_map/ppermute | solution.py:27
  25.9 15.0 %collective-permute-start.5 = (bf16[256,1152]{1,0:T(8,128)(2,1)S(1)}, bf16[256,1152]{1,0:T(8,128)(2,1)S(1)}, u32[]{:S(2)}, u32[]{:S(2)}) collective-permute-start(bf16[256,1152]{1,0:T(8,128)(2,1)S(1)} %pad_maximum_fusion.refs_1_), channel_id=1, source_target_pairs={{0,24},{1,97},{2,26},{3,99},{4,28},{5,101},{6,30},{7,103},{128,152... | collective-permute-start | bytes 1769480 | tf_op jit(solution)/shard_map/ppermute | solution.py:27
  27.8 13.2 %collective-permute-start.4 = (bf16[256,1152]{1,0:T(8,128)(2,1)S(1)}, bf16[256,1152]{1,0:T(8,128)(2,1)S(1)}, u32[]{:S(2)}, u32[]{:S(2)}) collective-permute-start(bf16[256,1152]{1,0:T(8,128)(2,1)S(1)} %pad_maximum_fusion.refs_1_), channel_id=1, source_target_pairs={{0,16},{1,65},{2,18},{3,67},{4,20},{5,69},{6,22},{7,71},{128,144},... | collective-permute-start | bytes 1769480 | tf_op jit(solution)/shard_map/ppermute | solution.py:27
  28.3 16.3 %collective-permute-start.3 = (bf16[256,1152]{1,0:T(8,128)(2,1)S(1)}, bf16[256,1152]{1,0:T(8,128)(2,1)S(1)}, u32[]{:S(2)}, u32[]{:S(2)}) collective-permute-start(bf16[256,1152]{1,0:T(8,128)(2,1)S(1)} %pad_maximum_fusion.refs_1_), channel_id=1, source_target_pairs={{0,8},{1,33},{2,10},{3,35},{4,12},{5,37},{6,14},{7,39},{128,136},{... | collective-permute-start | bytes 1769480 | tf_op jit(solution)/shard_map/ppermute | solution.py:27
  29.1 5.9 %collective-permute-start.10 = (bf16[128,1152]{1,0:T(8,128)(2,1)S(1)}, bf16[128,1152]{1,0:T(8,128)(2,1)S(1)}, u32[]{:S(2)}, u32[]{:S(2)}) collective-permute-start(bf16[128,1152]{1,0:T(8,128)(2,1)S(1)} %collective-permute-done.7.refs_8_.refs_4_), channel_id=1, source_target_pairs={{0,2},{1,135},{2,4},{3,1},{4,6},{5,3},{6,128},{7,5},{128,130},{129... | collective-permute-start | bytes 884744 | tf_op jit(solution)/shard_map/ppermute | solution.py:27
  30.4 3.3 %collective-permute-start.11 = (bf16[64,1152]{1,0:T(8,128)(2,1)S(1)}, bf16[64,1152]{1,0:T(8,128)(2,1)S(1)}, u32[]{:S(2)}, u32[]{:S(2)}) collective-permute-start(bf16[64,1152]{1,0:T(8,128)(2,1)S(1)} %collective-permute-done.8.refs_6_.refs_2_), channel_id=1, source_target_pairs={{0,1},{1,0},{2,3},{3,2},{4,5},{5,4},{6,7},{7,6},{128,129},{129,128... | collective-permute-start | bytes 442376 | tf_op jit(solution)/shard_map/ppermute | solution.py:27
  33.7 6.3 %collective-permute-start.13 = (bf16[128,1152]{1,0:T(8,128)(2,1)S(1)}, bf16[128,1152]{1,0:T(8,128)(2,1)S(1)}, u32[]{:S(2)}, u32[]{:S(2)}) collective-permute-start(bf16[128,1152]{1,0:T(8,128)(2,1)S(1)} %collective-permute-done.7.refs_8_.refs_4_), channel_id=1, source_target_pairs={{0,1},{1,0},{2,3},{3,2},{4,5},{5,4},{6,7},{7,6},{128,129},{129,128... | collective-permute-start | bytes 884744 | tf_op jit(solution)/shard_map/ppermute | solution.py:27
  35.0 9.7 %collective-permute-start.14 = (bf16[128,1152]{1,0:T(8,128)(2,1)S(1)}, bf16[128,1152]{1,0:T(8,128)(2,1)S(1)}, u32[]{:S(2)}, u32[]{:S(2)}) collective-permute-start(bf16[128,1152]{1,0:T(8,128)(2,1)S(1)} %collective-permute-done.10.refs_9_.refs_5_), channel_id=1, source_target_pairs={{0,1},{1,0},{2,3},{3,2},{4,5},{5,4},{6,7},{7,6},{128,129},{129,128... | collective-permute-start | bytes 884744 | tf_op jit(solution)/shard_map/ppermute | solution.py:27
  57.7 9.1 %collective-permute-start.15 = (bf16[256,1152]{1,0:T(8,128)(2,1)S(1)}, bf16[256,1152]{1,0:T(8,128)(2,1)S(1)}, u32[]{:S(2)}, u32[]{:S(2)}) collective-permute-start(bf16[256,1152]{1,0:T(8,128)(2,1)S(1)} %get-tuple-element.13), channel_id=1, source_target_pairs={{0,24},{1,97},{2,26},{3,99},{4,28},{5,101},{6,30},{7,103},{128,152... | collective-permute-start | bytes 1769480 | tf_op jit(solution)/shard_map/ppermute | solution.py:27
  58.1 10.6 %collective-permute-start.16 = (bf16[256,1152]{1,0:T(8,128)(2,1)S(1)}, bf16[256,1152]{1,0:T(8,128)(2,1)S(1)}, u32[]{:S(2)}, u32[]{:S(2)}) collective-permute-start(bf16[256,1152]{1,0:T(8,128)(2,1)S(1)} %get-tuple-element.14), channel_id=1, source_target_pairs={{0,16},{1,65},{2,18},{3,67},{4,20},{5,69},{6,22},{7,71},{128,144},... | collective-permute-start | bytes 1769480 | tf_op jit(solution)/shard_map/ppermute | solution.py:27
  58.6 16.3 %collective-permute-start.17 = (bf16[256,1152]{1,0:T(8,128)(2,1)S(1)}, bf16[256,1152]{1,0:T(8,128)(2,1)S(1)}, u32[]{:S(2)}, u32[]{:S(2)}) collective-permute-start(bf16[256,1152]{1,0:T(8,128)(2,1)S(1)} %get-tuple-element.15), channel_id=1, source_target_pairs={{0,8},{1,33},{2,10},{3,35},{4,12},{5,37},{6,14},{7,39},{128,136},{... | collective-permute-start | bytes 1769480 | tf_op jit(solution)/shard_map/ppermute | solution.py:27
  59.2 16.0 %collective-permute-start.21 = (bf16[512,1152]{1,0:T(8,128)(2,1)S(1)}, bf16[512,1152]{1,0:T(8,128)(2,1)S(1)}, u32[]{:S(2)}, u32[]{:S(2)}) collective-permute-start(bf16[512,1152]{1,0:T(8,128)(2,1)S(1)} %get-tuple-element.17), channel_id=1, source_target_pairs={{0,1},{1,0},{2,3},{3,2},{4,5},{5,4},{6,7},{7,6},{128,129},{129,128... | collective-permute-start | bytes 3538952 | tf_op jit(solution)/shard_map/ppermute | solution.py:27
  75.6 8.2 %collective-permute-start.23 = (bf16[128,1152]{1,0:T(8,128)(2,1)S(1)}, bf16[128,1152]{1,0:T(8,128)(2,1)S(1)}, u32[]{:S(2)}, u32[]{:S(2)}) collective-permute-start(bf16[128,1152]{1,0:T(8,128)(2,1)S(1)} %get-tuple-element.23), channel_id=1, source_target_pairs={{0,134},{1,3},{2,0},{3,5},{4,2},{5,7},{6,4},{7,129},{128,6},{129,1... | collective-permute-start | bytes 884744 | tf_op jit(solution)/shard_map/ppermute | solution.py:27
  75.7 14.8 %collective-permute-start.18 = (bf16[64,1152]{1,0:T(8,128)(2,1)S(1)}, bf16[64,1152]{1,0:T(8,128)(2,1)S(1)}, u32[]{:S(2)}, u32[]{:S(2)}) collective-permute-start(bf16[64,1152]{1,0:T(8,128)(2,1)S(1)} %get-tuple-element.24), channel_id=1, source_target_pairs={{0,96},{1,25},{2,98},{3,27},{4,100},{5,29},{6,102},{7,31},{128,224... | collective-permute-start | bytes 442376 | tf_op jit(solution)/shard_map/ppermute | solution.py:27
  78.9 11.7 %collective-permute-start.20 = (bf16[64,1152]{1,0:T(8,128)(2,1)S(1)}, bf16[64,1152]{1,0:T(8,128)(2,1)S(1)}, u32[]{:S(2)}, u32[]{:S(2)}) collective-permute-start(bf16[64,1152]{1,0:T(8,128)(2,1)S(1)} %get-tuple-element.25), channel_id=1, source_target_pairs={{0,32},{1,9},{2,34},{3,11},{4,36},{5,13},{6,38},{7,15},{128,160},{... | collective-permute-start | bytes 442376 | tf_op jit(solution)/shard_map/ppermute | solution.py:27
  78.9 11.7 %collective-permute-start.19 = (bf16[64,1152]{1,0:T(8,128)(2,1)S(1)}, bf16[64,1152]{1,0:T(8,128)(2,1)S(1)}, u32[]{:S(2)}, u32[]{:S(2)}) collective-permute-start(bf16[64,1152]{1,0:T(8,128)(2,1)S(1)} %get-tuple-element.26), channel_id=1, source_target_pairs={{0,64},{1,17},{2,66},{3,19},{4,68},{5,21},{6,70},{7,23},{128,192},... | collective-permute-start | bytes 442376 | tf_op jit(solution)/shard_map/ppermute | solution.py:27
  80.2 6.3 %collective-permute-start.24 = (bf16[64,1152]{1,0:T(8,128)(2,1)S(1)}, bf16[64,1152]{1,0:T(8,128)(2,1)S(1)}, u32[]{:S(2)}, u32[]{:S(2)}) collective-permute-start(bf16[64,1152]{1,0:T(8,128)(2,1)S(1)} %slice.67), channel_id=1, source_target_pairs={{0,132},{1,5},{2,134},{3,7},{4,0},{5,129},{6,2},{7,131},{128,4},{1... | collective-permute-start | bytes 442376 | tf_op jit(solution)/shard_map/ppermute | solution.py:27
  83.8 7.5 %collective-permute-start.22 = (bf16[128,1152]{1,0:T(8,128)(2,1)S(1)}, bf16[128,1152]{1,0:T(8,128)(2,1)S(1)}, u32[]{:S(2)}, u32[]{:S(2)}) collective-permute-start(bf16[128,1152]{1,0:T(8,128)(2,1)S(1)} %get-tuple-element.22), channel_id=1, source_target_pairs={{0,134},{1,3},{2,0},{3,5},{4,2},{5,7},{6,4},{7,129},{128,6},{129,1... | collective-permute-start | bytes 884744 | tf_op jit(solution)/shard_map/ppermute | solution.py:27
  86.6 10.8 %collective-permute-start.25 = (bf16[128,1152]{1,0:T(8,128)(2,1)S(1)}, bf16[128,1152]{1,0:T(8,128)(2,1)S(1)}, u32[]{:S(2)}, u32[]{:S(2)}) collective-permute-start(bf16[128,1152]{1,0:T(8,128)(2,1)S(1)} %pad_maximum_fusion.2), channel_id=1, source_target_pairs={{0,132},{1,5},{2,134},{3,7},{4,0},{5,129},{6,2},{7,131},{128,4},{1... | collective-permute-start | bytes 884744 | tf_op jit(solution)/shard_map/ppermute | solution.py:27
  90.8 14.4 %copy-start.1 = (bf16[64,1152]{1,0:T(8,128)(2,1)S(1)}, bf16[64,1152]{1,0:T(8,128)(2,1)}, u32[]{:S(2)}) copy-start(bf16[64,1152]{1,0:T(8,128)(2,1)} %param.5) | copy-start | bytes 442372
  97.5 7.7 %collective-permute-start.26 = (bf16[64,1152]{1,0:T(8,128)(2,1)S(1)}, bf16[64,1152]{1,0:T(8,128)(2,1)S(1)}, u32[]{:S(2)}, u32[]{:S(2)}) collective-permute-start(bf16[64,1152]{1,0:T(8,128)(2,1)S(1)} %slice.94), channel_id=1, source_target_pairs={{0,1},{1,0},{2,3},{3,2},{4,5},{5,4},{6,7},{7,6},{128,129},{129,128... | collective-permute-start | bytes 442376 | tf_op jit(solution)/shard_map/ppermute | solution.py:27

commit v2 on v1

--- a/solution.py
+++ b/solution.py
@@ -16,7 +16,7 @@
     return ((z // 4) * 16 + x * 4 + y) * 8 + (z % 4) * 2 + c
 
 
-def shift(values, move):
+def shift(values, move, name="move"):
     pairs = []
     for x in range(SIZE_X):
         for y in range(SIZE_Y):
@@ -24,7 +24,8 @@
                 for c in range(CORES):
                     nx, ny, nz, nc = move(x, y, z, c)
                     pairs.append((device(x, y, z, c), device(nx % SIZE_X, ny % SIZE_Y, nz % SIZE_Z, nc)))
-    return lax.ppermute(values, AXES, pairs)
+    with jax.named_scope(name):
+        return lax.ppermute(values, AXES, pairs)
 
 
 def first(k):
@@ -71,7 +72,7 @@
 
 def weights_kernel(n_img, n_txt, own, scal_ref, *refs):
     img_parts, txt_parts = refs[:n_img], refs[n_img:n_img + n_txt]
-    w_ref, keep_ref, send_ref, img, txt, sems = refs[n_img + n_txt:]
+    w_ref, keep_ref, send_ref, txt, img, sems = refs[n_img + n_txt:]
     img_copies = load(img_parts, img, sems, 0)
     txt_copies = load(txt_parts, txt, sems, n_img)
     temp, shift_ = scal_ref[0], scal_ref[1]
@@ -106,12 +107,7 @@
             out[t:t + step, :] = grad.astype(out.dtype)
 
 
-def image_kernel(n_txt, w_ref, *refs):
-    txt_parts, outs = refs[:n_txt], refs[n_txt:-2]
-    txt, sems = refs[-2:]
-    copies = load(txt_parts, txt, sems, 0)
-    for copy in copies:
-        copy.wait()
+def image_kernel(w_ref, txt, *outs):
     at = 0
     for out in outs:
         rows = out.shape[0]
@@ -128,77 +124,80 @@
     anywhere = pl.BlockSpec(memory_space=pl.ANY)
     vmem = pl.BlockSpec(memory_space=pltpu.VMEM)
     flops = 2 * rows * cols * dim
-    w, keep, send = pl.pallas_call(
+    w, keep, send, txt = pl.pallas_call(
         lambda *refs: weights_kernel(n_img, n_txt, own, *refs),
         out_shape=(
             jax.ShapeDtypeStruct((rows, cols), BF16),
             jax.ShapeDtypeStruct((cols // 2, dim), BF16),
             jax.ShapeDtypeStruct((cols // 2, dim), BF16),
+            jax.ShapeDtypeStruct((cols, dim), BF16),
         ),
         in_specs=[pl.BlockSpec(memory_space=pltpu.SMEM)] + [anywhere] * (n_img + n_txt),
-        out_specs=(vmem, vmem, vmem),
+        out_specs=(vmem, vmem, vmem, vmem),
         scratch_shapes=[
             pltpu.VMEM((rows, dim), BF16),
-            pltpu.VMEM((cols, dim), BF16),
             pltpu.SemaphoreType.DMA((n_img + n_txt,)),
         ],
-        compiler_params=pltpu.CompilerParams(vmem_limit_bytes=40 * 1024 * 1024),
+        compiler_params=pltpu.CompilerParams(vmem_limit_bytes=32 * 1024 * 1024),
         cost_estimate=pl.CostEstimate(flops=2 * flops, bytes_accessed=10 * 1024 * 1024, transcendentals=2 * rows * cols),
     )(scalars, *img_parts, *txt_parts)
     grads = pl.pallas_call(
-        lambda *refs: image_kernel(n_txt, *refs),
+        image_kernel,
         out_shape=tuple(
             jax.ShapeDtypeStruct(p.shape, F32 if n == 0 else BF16) for n, p in enumerate(img_parts)
         ),
-        in_specs=[vmem] + [anywhere] * n_txt,
+        in_specs=[vmem] * 2,
         out_specs=tuple([vmem] * n_img),
-        scratch_shapes=[pltpu.VMEM((cols, dim), BF16), pltpu.SemaphoreType.DMA((n_txt,))],
-        compiler_params=pltpu.CompilerParams(vmem_limit_bytes=40 * 1024 * 1024),
+        compiler_params=pltpu.CompilerParams(vmem_limit_bytes=32 * 1024 * 1024),
         cost_estimate=pl.CostEstimate(flops=flops, bytes_accessed=8 * 1024 * 1024, transcendentals=0),
-    )(w, *txt_parts)
+    )(w, txt)
     return keep, send, grads
+
+
+def after(value, *others):
+    return lax.optimization_barrier((value, *others))[0]
 
 
 def local(images, texts, log_temp, bias):
     own = images.shape[0]
     img_unit, inv_img = normalize(images)
-    txt_unit, inv_txt = normalize(texts)
     img_round = img_unit.astype(BF16)
+    txt_unit, inv_txt = normalize(after(texts, img_round))
     txt_round = txt_unit.astype(BF16)
     scalars = jnp.concatenate([jnp.exp(log_temp), bias])
 
-    side = [shift(img_round, first(k)) for k in (1, 2, 3)]
-    swapped = shift(txt_round, other)
+    side = [shift(img_round, first(k), "gA%d" % k) for k in (1, 2, 3)]
+    swapped = shift(txt_round, other, "gC")
     pair = cat([txt_round, swapped])
-    near2 = shift(pair, line(2))
-    near1 = shift(pair, line(1))
+    near2 = shift(pair, line(2), "gZ2")
+    near1 = shift(pair, line(1), "gZ1")
     group = cat([img_round] + side)
-    far = [shift(group, second(k)) for k in (1, 2, 3)]
-    tied = lax.optimization_barrier((near2, *side))[0]
-    near3 = shift(tied, line(1))
-    near4 = shift(tied[:own], line(2))
+    far = [shift(group, second(k), "gB%d" % k) for k in (1, 2, 3)]
+    tied = after(near2, group)
+    near3 = shift(tied, line(1), "gZ3")
+    near4 = shift(tied[:own], line(2), "gZ4")
     mine = [txt_round, near4, near1, near2, near3]
-    theirs = [swapped] + [shift(v, other) for v in mine[1:]]
+    theirs = [swapped] + [shift(v, other, "gS%d" % n) for v, n in zip(mine[1:], (4, 1, 2, 3))]
 
     keep, send, grads = block([group] + far, mine + theirs, scalars, own)
 
-    total = keep.astype(F32) + shift(send, other).astype(F32)
+    total = keep.astype(F32) + shift(send, other, "rC").astype(F32)
     packed = total.astype(BF16)
     part4, part1 = packed[own:2 * own], packed[2 * own:4 * own]
     part2, part3 = total[4 * own:6 * own], packed[6 * own:]
-    got3 = shift(part3, line(-1))
-    got4 = shift(part4, line(-2))
+    got3 = shift(part3, line(-1), "rZ3")
+    got4 = shift(part4, line(-2), "rZ4")
     part2 = part2 + got3.astype(F32)
     part2 = cat([part2[:own] + got4.astype(F32), part2[own:]]).astype(BF16)
-    got1 = shift(part1, line(-1))
-    got2 = shift(part2, line(-2))
+    got1 = shift(after(part1, part2), line(-1), "rZ1")
+    got2 = shift(part2, line(-2), "rZ2")
     landed = got1.astype(F32) + got2.astype(F32)
-    grad_txt = total[:own] + landed[:own] + shift(landed[own:].astype(BF16), other).astype(F32)
-
-    back = [shift(g, second(-k)) for k, g in zip((1, 2, 3), grads[1:])]
-    sums = grads[0] + sum(b.astype(F32) for b in back)
+    grad_txt = total[:own] + landed[:own] + shift(landed[own:].astype(BF16), other, "rS").astype(F32)
+
+    back = [shift(g, second(-k), "rB%d" % k) for k, g in zip((1, 2, 3), grads[1:])]
+    sums = after(grads[0], part2) + sum(b.astype(F32) for b in back)
     sums16 = sums.astype(BF16)
-    last = [shift(sums16[k * own:(k + 1) * own], first(-k)) for k in (1, 2, 3)]
+    last = [shift(sums16[k * own:(k + 1) * own], first(-k), "rA%d" % k) for k in (1, 2, 3)]
     grad_img = sums[:own] + sum(b.astype(F32) for b in last)
 
     return back_norm(img_unit, inv_img, grad_img), back_norm(txt_unit, inv_txt, grad_txt)

time: 106 us -> 106 us (level)
  the two profiles are of different devices: /device:TPU:1 before, /device:TPU:99 now
where the time goes in v2:
time: 106 us
  starting transfers between devices  46.9 us (44%)
  waiting for transfers between devices  38 us (36%)
  Pallas kernels  11.8 us (11%)
  other arithmetic  7.13 us (7%)
  between operations  2.19 us (2%)
    ppermute x27, starting transfers between devices, shift(): return lax.ppermute(values, AXES, pairs)  46.9 us
    ppermute x27, waiting for transfers between devices, shift(): return lax.ppermute(values, AXES, pairs)  38 us
    pallas_call x1, Pallas kernels, block(): pl.pallas_call(lambda *refs: weights_kernel(n_img, n_txt, own, *refs), ou...  8.92 us
    pallas_call x1, Pallas kernels, block(): pl.pallas_call(image_kernel, out_shape=tuple((jax.ShapeDtypeStruct(p.shap...  2.9 us
  transfers between devices with their start and end apart: 27, of which 15 were waited for; matrix products, arithmetic and copies ran while one was open for 1% of the time, Pallas kernels for 3%

profile of v2, /device:TPU:99, one launch (start us, length us, event | category | flops | bytes accessed | tf_op | source)
XLA Modules:
  0.0 106.2 jit_solution(3592792339455024305)
XLA Ops:
  0.6 1.0 fusion.9
  1.7 1.0 fusion.5
  2.7 1.0 fusion.13
  3.8 1.0 fusion.2.refs_5_
  4.8 0.8 collective-permute-start.6
  5.5 2.7 %collective-permute-start.2 = (bf16[64,1152]{1,0:T(8,128)(2,1)S(1)}, bf16[64,1152]{1,0:T(8,128)(2,1)S(1)}, u32[]{:S(2)}, u32[]{:S(2)}) collective-permute-start(bf16[64,1152]{1,0:T(8,128)(2,1)S(1)} %fusion.5), channel_id=1, source_target_pairs={{0,96},{1,25},{2,98},{3,27},{4,100},{5,29},{6,102},{7,31},{128,224... | collective-permute-start | bytes 442376 | tf_op jit(solution)/shard_map/gA3/ppermute | solution.py:28
  8.3 0.3 collective-permute-start.1
  8.6 0.7 collective-permute-start
  9.3 0.0 collective-permute-done.6.refs_10_
  9.3 0.1 collective-permute-start.9
  9.4 0.1 collective-permute-start.7
  9.5 2.4 %collective-permute-done.2 = bf16[64,1152]{1,0:T(8,128)(2,1)S(1)} collective-permute-done((bf16[64,1152]{1,0:T(8,128)(2,1)S(1)}, bf16[64,1152]{1,0:T(8,128)(2,1)S(1)}, u32[]{:S(2)}, u32[]{:S(2)}) %collective-permute-start.2) | collective-permute-done | bytes 147488 | tf_op jit(solution)/shard_map/gA3/ppermute | solution.py:28
  11.9 1.9 %collective-permute-done.1 = bf16[64,1152]{1,0:T(8,128)(2,1)S(1)} collective-permute-done((bf16[64,1152]{1,0:T(8,128)(2,1)S(1)}, bf16[64,1152]{1,0:T(8,128)(2,1)S(1)}, u32[]{:S(2)}, u32[]{:S(2)}) %collective-permute-start.1) | collective-permute-done | bytes 147488 | tf_op jit(solution)/shard_map/gA2/ppermute | solution.py:28
  13.9 1.5 %collective-permute-done = bf16[64,1152]{1,0:T(8,128)(2,1)S(1)} collective-permute-done((bf16[64,1152]{1,0:T(8,128)(2,1)S(1)}, bf16[64,1152]{1,0:T(8,128)(2,1)S(1)}, u32[]{:S(2)}, u32[]{:S(2)}) %collective-permute-start) | collective-permute-done | bytes 147488 | tf_op jit(solution)/shard_map/gA1/ppermute | solution.py:28
  15.4 1.0 collective-permute-done.9.refs_7_
  16.4 3.9 %collective-permute-start.12 = (bf16[128,1152]{1,0:T(8,128)(2,1)S(1)}, bf16[128,1152]{1,0:T(8,128)(2,1)S(1)}, u32[]{:S(2)}, u32[]{:S(2)}) collective-permute-start(bf16[128,1152]{1,0:T(8,128)(2,1)S(1)} %collective-permute-done.9.refs_7_), channel_id=1, source_target_pairs={{0,1},{1,0},{2,3},{3,2},{4,5},{5,4},{6,7},{7,6},{128,129},{129,128... | collective-permute-start | bytes 884744 | tf_op jit(solution)/shard_map/gS1/ppermute | solution.py:28
  20.2 1.0 collective-permute-done.7.refs_8_
  21.3 0.1 collective-permute-start.8
  21.4 0.3 collective-permute-start.5
  21.7 2.1 %collective-permute-start.4 = (bf16[256,1152]{1,0:T(8,128)(2,1)S(1)}, bf16[256,1152]{1,0:T(8,128)(2,1)S(1)}, u32[]{:S(2)}, u32[]{:S(2)}) collective-permute-start(bf16[256,1152]{1,0:T(8,128)(2,1)S(1)} %pad_maximum_fusion.refs_1_), channel_id=1, source_target_pairs={{0,16},{1,65},{2,18},{3,67},{4,20},{5,69},{6,22},{7,71},{128,144},... | collective-permute-start | bytes 1769480 | tf_op jit(solution)/shard_map/gB2/ppermute | solution.py:28
  23.9 1.5 %collective-permute-start.3 = (bf16[256,1152]{1,0:T(8,128)(2,1)S(1)}, bf16[256,1152]{1,0:T(8,128)(2,1)S(1)}, u32[]{:S(2)}, u32[]{:S(2)}) collective-permute-start(bf16[256,1152]{1,0:T(8,128)(2,1)S(1)} %pad_maximum_fusion.refs_1_), channel_id=1, source_target_pairs={{0,8},{1,33},{2,10},{3,35},{4,12},{5,37},{6,14},{7,39},{128,136},{... | collective-permute-start | bytes 1769480 | tf_op jit(solution)/shard_map/gB1/ppermute | solution.py:28
  25.4 2.1 %collective-permute-done.8.refs_6_ = bf16[64,1152]{1,0:T(8,128)(2,1)S(1)} collective-permute-done((bf16[64,1152]{1,0:T(8,128)(2,1)S(1)}, bf16[64,1152]{1,0:T(8,128)(2,1)S(1)}, u32[]{:S(2)}, u32[]{:S(2)}) %collective-permute-start.8) | collective-permute-done | bytes 147488 | tf_op jit(solution)/shard_map/gZ4/ppermute | solution.py:28
  27.5 2.8 %collective-permute-start.10 = (bf16[128,1152]{1,0:T(8,128)(2,1)S(1)}, bf16[128,1152]{1,0:T(8,128)(2,1)S(1)}, u32[]{:S(2)}, u32[]{:S(2)}) collective-permute-start(bf16[128,1152]{1,0:T(8,128)(2,1)S(1)} %collective-permute-done.7.refs_8_), channel_id=1, source_target_pairs={{0,2},{1,135},{2,4},{3,1},{4,6},{5,3},{6,128},{7,5},{128,130},{129... | collective-permute-start | bytes 884744 | tf_op jit(solution)/shard_map/gZ3/ppermute | solution.py:28
  30.2 4.8 %collective-permute-start.11 = (bf16[64,1152]{1,0:T(8,128)(2,1)S(1)}, bf16[64,1152]{1,0:T(8,128)(2,1)S(1)}, u32[]{:S(2)}, u32[]{:S(2)}) collective-permute-start(bf16[64,1152]{1,0:T(8,128)(2,1)S(1)} %collective-permute-done.8.refs_6_), channel_id=1, source_target_pairs={{0,1},{1,0},{2,3},{3,2},{4,5},{5,4},{6,7},{7,6},{128,129},{129,128... | collective-permute-start | bytes 442376 | tf_op jit(solution)/shard_map/gS4/ppermute | solution.py:28
  35.1 1.0 collective-permute-done.11.refs_11_
  36.1 0.4 collective-permute-start.13
  36.4 0.0 collective-permute-done.10.refs_9_
  36.4 3.8 %collective-permute-start.14 = (bf16[128,1152]{1,0:T(8,128)(2,1)S(1)}, bf16[128,1152]{1,0:T(8,128)(2,1)S(1)}, u32[]{:S(2)}, u32[]{:S(2)}) collective-permute-start(bf16[128,1152]{1,0:T(8,128)(2,1)S(1)} %collective-permute-done.10.refs_9_), channel_id=1, source_target_pairs={{0,1},{1,0},{2,3},{3,2},{4,5},{5,4},{6,7},{7,6},{128,129},{129,128... | collective-permute-start | bytes 884744 | tf_op jit(solution)/shard_map/gS3/ppermute | solution.py:28
  41.5 0.1 pad_maximum_fusion.3.refs_0_
  41.6 0.0 collective-permute-done.13.refs_13_
  41.6 0.0 collective-permute-done.5.refs_4_
  41.6 0.0 collective-permute-done.4.refs_3_
  41.7 8.9 %shard_map.59 = (bf16[1024,1024]{1,0:T(8,128)(2,1)S(1)}, bf16[512,1152]{1,0:T(8,128)(2,1)S(1)}, bf16[512,1152]{1,0:T(8,128)(2,1)S(1)}, bf16[1024,1152]{1,0:T(8,128)(2,1)S(1)}) custom-call(f32[2]{0:T(128)S(1)} %pad_maximum_fusion.3.refs_0_, bf16[256,1152]{1,0:T(8,128)(2,1)S(1)} %pad_maximum_fusion.refs_1_, ...), custom_call_target="tpu_custom_call" | custom-call | flops 4831838208 | bytes 10485760 | tf_op jit(solution)/shard_map/pallas_call | solution.py:127
  50.6 8.0 %collective-permute-start.15 = (bf16[512,1152]{1,0:T(8,128)(2,1)S(1)}, bf16[512,1152]{1,0:T(8,128)(2,1)S(1)}, u32[]{:S(2)}, u32[]{:S(2)}) collective-permute-start(bf16[512,1152]{1,0:T(8,128)(2,1)S(1)} %get-tuple-element.20), channel_id=1, source_target_pairs={{0,1},{1,0},{2,3},{3,2},{4,5},{5,4},{6,7},{7,6},{128,129},{129,128... | collective-permute-start | bytes 3538952 | tf_op jit(solution)/shard_map/rC/ppermute | solution.py:28
  58.6 2.5 %collective-permute-done.15 = bf16[512,1152]{1,0:T(8,128)(2,1)S(1)} collective-permute-done((bf16[512,1152]{1,0:T(8,128)(2,1)S(1)}, bf16[512,1152]{1,0:T(8,128)(2,1)S(1)}, u32[]{:S(2)}, u32[]{:S(2)}) %collective-permute-start.15) | collective-permute-done | bytes 1179680 | tf_op jit(solution)/shard_map/rC/ppermute | solution.py:28
  61.1 0.3 fusion.16
  61.4 0.1 collective-permute-start.16
  61.5 2.9 %shard_map.60 = (f32[256,1152]{1,0:T(8,128)S(1)}, bf16[256,1152]{1,0:T(8,128)(2,1)S(1)}, bf16[256,1152]{1,0:T(8,128)(2,1)S(1)}, bf16[256,1152]{1,0:T(8,128)(2,1)S(1)}) custom-call(bf16[1024,1024]{1,0:T(8,128)(2,1)S(1)} %get-tuple-element.16.w_ref, bf16[1024,1152]{1,0:T(8,128)(2,1)S(1)} %get-tuple-element.17.txt), custom_call_target="tpu_custom_call" | custom-call | flops 2415919104 | bytes 8388608 | tf_op jit(solution)/shard_map/pallas_call | solution.py:144
  64.4 0.1 collective-permute-start.18
  64.5 1.2 %collective-permute-start.19 = (bf16[256,1152]{1,0:T(8,128)(2,1)S(1)}, bf16[256,1152]{1,0:T(8,128)(2,1)S(1)}, u32[]{:S(2)}, u32[]{:S(2)}) collective-permute-start(bf16[256,1152]{1,0:T(8,128)(2,1)S(1)} %get-tuple-element.23), channel_id=1, source_target_pairs={{0,16},{1,65},{2,18},{3,67},{4,20},{5,69},{6,22},{7,71},{128,144},... | collective-permute-start | bytes 1769480 | tf_op jit(solution)/shard_map/rB2/ppermute | solution.py:28
  65.7 2.0 %collective-permute-start.20 = (bf16[256,1152]{1,0:T(8,128)(2,1)S(1)}, bf16[256,1152]{1,0:T(8,128)(2,1)S(1)}, u32[]{:S(2)}, u32[]{:S(2)}) collective-permute-start(bf16[256,1152]{1,0:T(8,128)(2,1)S(1)} %get-tuple-element.24), channel_id=1, source_target_pairs={{0,8},{1,33},{2,10},{3,35},{4,12},{5,37},{6,14},{7,39},{128,136},{... | collective-permute-start | bytes 1769480 | tf_op jit(solution)/shard_map/rB3/ppermute | solution.py:28
  67.7 0.3 collective-permute-start.17
  68.0 0.1 slice_add_fusion
  68.1 5.3 %collective-permute-done.17 = bf16[64,1152]{1,0:T(8,128)(2,1)S(1)} collective-permute-done((bf16[64,1152]{1,0:T(8,128)(2,1)S(1)}, bf16[64,1152]{1,0:T(8,128)(2,1)S(1)}, u32[]{:S(2)}, u32[]{:S(2)}) %collective-permute-start.17) | collective-permute-done | bytes 147488 | tf_op jit(solution)/shard_map/rZ4/ppermute | solution.py:28
  73.5 0.0 copy-start
  73.5 6.3 %collective-permute-done.18 = bf16[256,1152]{1,0:T(8,128)(2,1)S(1)} collective-permute-done((bf16[256,1152]{1,0:T(8,128)(2,1)S(1)}, bf16[256,1152]{1,0:T(8,128)(2,1)S(1)}, u32[]{:S(2)}, u32[]{:S(2)}) %collective-permute-start.18) | collective-permute-done | bytes 589856 | tf_op jit(solution)/shard_map/rB1/ppermute | solution.py:28
  79.8 1.8 %collective-permute-done.20 = bf16[256,1152]{1,0:T(8,128)(2,1)S(1)} collective-permute-done((bf16[256,1152]{1,0:T(8,128)(2,1)S(1)}, bf16[256,1152]{1,0:T(8,128)(2,1)S(1)}, u32[]{:S(2)}, u32[]{:S(2)}) %collective-permute-start.20) | collective-permute-done | bytes 589856 | tf_op jit(solution)/shard_map/rB3/ppermute | solution.py:28
  81.7 0.3 fusion.17
  82.0 0.4 collective-permute-start.21
  82.4 1.1 %collective-permute-start.23 = (bf16[64,1152]{1,0:T(8,128)(2,1)S(1)}, bf16[64,1152]{1,0:T(8,128)(2,1)S(1)}, u32[]{:S(2)}, u32[]{:S(2)}) collective-permute-start(bf16[64,1152]{1,0:T(8,128)(2,1)S(1)} %get-tuple-element.33), channel_id=1, source_target_pairs={{0,32},{1,9},{2,34},{3,11},{4,36},{5,13},{6,38},{7,15},{128,160},{... | collective-permute-start | bytes 442376 | tf_op jit(solution)/shard_map/rA3/ppermute | solution.py:28
  83.5 0.4 collective-permute-start.22
  83.9 0.3 collective-permute-start.24
  84.1 1.4 %collective-permute-start.25 = (bf16[128,1152]{1,0:T(8,128)(2,1)S(1)}, bf16[128,1152]{1,0:T(8,128)(2,1)S(1)}, u32[]{:S(2)}, u32[]{:S(2)}) collective-permute-start(bf16[128,1152]{1,0:T(8,128)(2,1)S(1)} %pad_maximum_fusion.2), channel_id=1, source_target_pairs={{0,132},{1,5},{2,134},{3,7},{4,0},{5,129},{6,2},{7,131},{128,4},{1... | collective-permute-start | bytes 884744 | tf_op jit(solution)/shard_map/rZ2/ppermute | solution.py:28
  85.5 0.5 collective-permute-done.21
  86.1 3.1 %collective-permute-done.23 = bf16[64,1152]{1,0:T(8,128)(2,1)S(1)} collective-permute-done((bf16[64,1152]{1,0:T(8,128)(2,1)S(1)}, bf16[64,1152]{1,0:T(8,128)(2,1)S(1)}, u32[]{:S(2)}, u32[]{:S(2)}) %collective-permute-start.23) | collective-permute-done | bytes 147488 | tf_op jit(solution)/shard_map/rA3/ppermute | solution.py:28
  89.2 0.2 fusion.6
  89.4 0.0 collective-permute-done.24
  89.5 7.2 %collective-permute-done.25 = bf16[128,1152]{1,0:T(8,128)(2,1)S(1)} collective-permute-done((bf16[128,1152]{1,0:T(8,128)(2,1)S(1)}, bf16[128,1152]{1,0:T(8,128)(2,1)S(1)}, u32[]{:S(2)}, u32[]{:S(2)}) %collective-permute-start.25) | collective-permute-done | bytes 294944 | tf_op jit(solution)/shard_map/rZ2/ppermute | solution.py:28
  96.7 0.1 convert_add_fusion.1
  96.7 7.4 %collective-permute-start.26 = (bf16[64,1152]{1,0:T(8,128)(2,1)S(1)}, bf16[64,1152]{1,0:T(8,128)(2,1)S(1)}, u32[]{:S(2)}, u32[]{:S(2)}) collective-permute-start(bf16[64,1152]{1,0:T(8,128)(2,1)S(1)} %slice.94), channel_id=1, source_target_pairs={{0,1},{1,0},{2,3},{3,2},{4,5},{5,4},{6,7},{7,6},{128,129},{129,128... | collective-permute-start | bytes 442376 | tf_op jit(solution)/shard_map/rS/ppermute | solution.py:28
  104.1 0.9 fusion.8
  105.0 0.1 collective-permute-done.26
  105.1 0.2 fusion.10
  105.3 0.8 fusion.12
  (21 shorter events, 0.3 us)
Async XLA Ops:
  4.8 4.5 %collective-permute-start.6 = (bf16[64,1152]{1,0:T(8,128)(2,1)S(1)}, bf16[64,1152]{1,0:T(8,128)(2,1)S(1)}, u32[]{:S(2)}, u32[]{:S(2)}) collective-permute-start(bf16[64,1152]{1,0:T(8,128)(2,1)S(1)} %fusion.2.refs_5_), channel_id=1, source_target_pairs={{0,1},{1,0},{2,3},{3,2},{4,5},{5,4},{6,7},{7,6},{128,129},{129,128... | collective-permute-start | bytes 442376 | tf_op jit(solution)/shard_map/gC/ppermute | solution.py:28
  5.5 6.4 %collective-permute-start.2 = (bf16[64,1152]{1,0:T(8,128)(2,1)S(1)}, bf16[64,1152]{1,0:T(8,128)(2,1)S(1)}, u32[]{:S(2)}, u32[]{:S(2)}) collective-permute-start(bf16[64,1152]{1,0:T(8,128)(2,1)S(1)} %fusion.5), channel_id=1, source_target_pairs={{0,96},{1,25},{2,98},{3,27},{4,100},{5,29},{6,102},{7,31},{128,224... | collective-permute-start | bytes 442376 | tf_op jit(solution)/shard_map/gA3/ppermute | solution.py:28
  8.3 5.6 %collective-permute-start.1 = (bf16[64,1152]{1,0:T(8,128)(2,1)S(1)}, bf16[64,1152]{1,0:T(8,128)(2,1)S(1)}, u32[]{:S(2)}, u32[]{:S(2)}) collective-permute-start(bf16[64,1152]{1,0:T(8,128)(2,1)S(1)} %fusion.5), channel_id=1, source_target_pairs={{0,64},{1,17},{2,66},{3,19},{4,68},{5,21},{6,70},{7,23},{128,192},... | collective-permute-start | bytes 442376 | tf_op jit(solution)/shard_map/gA2/ppermute | solution.py:28
  8.6 6.7 %collective-permute-start = (bf16[64,1152]{1,0:T(8,128)(2,1)S(1)}, bf16[64,1152]{1,0:T(8,128)(2,1)S(1)}, u32[]{:S(2)}, u32[]{:S(2)}) collective-permute-start(bf16[64,1152]{1,0:T(8,128)(2,1)S(1)} %fusion.5), channel_id=1, source_target_pairs={{0,32},{1,9},{2,34},{3,11},{4,36},{5,13},{6,38},{7,15},{128,160},{... | collective-permute-start | bytes 442376 | tf_op jit(solution)/shard_map/gA1/ppermute | solution.py:28
  9.3 7.0 %collective-permute-start.9 = (bf16[128,1152]{1,0:T(8,128)(2,1)S(1)}, bf16[128,1152]{1,0:T(8,128)(2,1)S(1)}, u32[]{:S(2)}, u32[]{:S(2)}) collective-permute-start(bf16[128,1152]{1,0:T(8,128)(2,1)S(1)} %pad_maximum_fusion.1), channel_id=1, source_target_pairs={{0,2},{1,135},{2,4},{3,1},{4,6},{5,3},{6,128},{7,5},{128,130},{129... | collective-permute-start | bytes 884744 | tf_op jit(solution)/shard_map/gZ1/ppermute | solution.py:28
  9.4 11.8 %collective-permute-start.7 = (bf16[128,1152]{1,0:T(8,128)(2,1)S(1)}, bf16[128,1152]{1,0:T(8,128)(2,1)S(1)}, u32[]{:S(2)}, u32[]{:S(2)}) collective-permute-start(bf16[128,1152]{1,0:T(8,128)(2,1)S(1)} %pad_maximum_fusion.1), channel_id=1, source_target_pairs={{0,4},{1,133},{2,6},{3,135},{4,128},{5,1},{6,130},{7,3},{128,132},... | collective-permute-start | bytes 884744 | tf_op jit(solution)/shard_map/gZ2/ppermute | solution.py:28
  16.4 13.9 %collective-permute-start.12 = (bf16[128,1152]{1,0:T(8,128)(2,1)S(1)}, bf16[128,1152]{1,0:T(8,128)(2,1)S(1)}, u32[]{:S(2)}, u32[]{:S(2)}) collective-permute-start(bf16[128,1152]{1,0:T(8,128)(2,1)S(1)} %collective-permute-done.9.refs_7_), channel_id=1, source_target_pairs={{0,1},{1,0},{2,3},{3,2},{4,5},{5,4},{6,7},{7,6},{128,129},{129,128... | collective-permute-start | bytes 884744 | tf_op jit(solution)/shard_map/gS1/ppermute | solution.py:28
  21.3 6.2 %collective-permute-start.8 = (bf16[64,1152]{1,0:T(8,128)(2,1)S(1)}, bf16[64,1152]{1,0:T(8,128)(2,1)S(1)}, u32[]{:S(2)}, u32[]{:S(2)}) collective-permute-start(bf16[64,1152]{1,0:T(8,128)(2,1)S(1)} %slice.44), channel_id=1, source_target_pairs={{0,4},{1,133},{2,6},{3,135},{4,128},{5,1},{6,130},{7,3},{128,132},... | collective-permute-start | bytes 442376 | tf_op jit(solution)/shard_map/gZ4/ppermute | solution.py:28
  21.4 20.2 %collective-permute-start.5 = (bf16[256,1152]{1,0:T(8,128)(2,1)S(1)}, bf16[256,1152]{1,0:T(8,128)(2,1)S(1)}, u32[]{:S(2)}, u32[]{:S(2)}) collective-permute-start(bf16[256,1152]{1,0:T(8,128)(2,1)S(1)} %pad_maximum_fusion.refs_1_), channel_id=1, source_target_pairs={{0,24},{1,97},{2,26},{3,99},{4,28},{5,101},{6,30},{7,103},{128,152... | collective-permute-start | bytes 1769480 | tf_op jit(solution)/shard_map/gB3/ppermute | solution.py:28
  21.7 19.9 %collective-permute-start.4 = (bf16[256,1152]{1,0:T(8,128)(2,1)S(1)}, bf16[256,1152]{1,0:T(8,128)(2,1)S(1)}, u32[]{:S(2)}, u32[]{:S(2)}) collective-permute-start(bf16[256,1152]{1,0:T(8,128)(2,1)S(1)} %pad_maximum_fusion.refs_1_), channel_id=1, source_target_pairs={{0,16},{1,65},{2,18},{3,67},{4,20},{5,69},{6,22},{7,71},{128,144},... | collective-permute-start | bytes 1769480 | tf_op jit(solution)/shard_map/gB2/ppermute | solution.py:28
  23.9 17.8 %collective-permute-start.3 = (bf16[256,1152]{1,0:T(8,128)(2,1)S(1)}, bf16[256,1152]{1,0:T(8,128)(2,1)S(1)}, u32[]{:S(2)}, u32[]{:S(2)}) collective-permute-start(bf16[256,1152]{1,0:T(8,128)(2,1)S(1)} %pad_maximum_fusion.refs_1_), channel_id=1, source_target_pairs={{0,8},{1,33},{2,10},{3,35},{4,12},{5,37},{6,14},{7,39},{128,136},{... | collective-permute-start | bytes 1769480 | tf_op jit(solution)/shard_map/gB1/ppermute | solution.py:28
  27.5 8.9 %collective-permute-start.10 = (bf16[128,1152]{1,0:T(8,128)(2,1)S(1)}, bf16[128,1152]{1,0:T(8,128)(2,1)S(1)}, u32[]{:S(2)}, u32[]{:S(2)}) collective-permute-start(bf16[128,1152]{1,0:T(8,128)(2,1)S(1)} %collective-permute-done.7.refs_8_), channel_id=1, source_target_pairs={{0,2},{1,135},{2,4},{3,1},{4,6},{5,3},{6,128},{7,5},{128,130},{129... | collective-permute-start | bytes 884744 | tf_op jit(solution)/shard_map/gZ3/ppermute | solution.py:28
  30.2 5.8 %collective-permute-start.11 = (bf16[64,1152]{1,0:T(8,128)(2,1)S(1)}, bf16[64,1152]{1,0:T(8,128)(2,1)S(1)}, u32[]{:S(2)}, u32[]{:S(2)}) collective-permute-start(bf16[64,1152]{1,0:T(8,128)(2,1)S(1)} %collective-permute-done.8.refs_6_), channel_id=1, source_target_pairs={{0,1},{1,0},{2,3},{3,2},{4,5},{5,4},{6,7},{7,6},{128,129},{129,128... | collective-permute-start | bytes 442376 | tf_op jit(solution)/shard_map/gS4/ppermute | solution.py:28
  36.1 5.6 %collective-permute-start.13 = (bf16[128,1152]{1,0:T(8,128)(2,1)S(1)}, bf16[128,1152]{1,0:T(8,128)(2,1)S(1)}, u32[]{:S(2)}, u32[]{:S(2)}) collective-permute-start(bf16[128,1152]{1,0:T(8,128)(2,1)S(1)} %collective-permute-done.7.refs_8_), channel_id=1, source_target_pairs={{0,1},{1,0},{2,3},{3,2},{4,5},{5,4},{6,7},{7,6},{128,129},{129,128... | collective-permute-start | bytes 884744 | tf_op jit(solution)/shard_map/gS2/ppermute | solution.py:28
  36.4 5.2 %collective-permute-start.14 = (bf16[128,1152]{1,0:T(8,128)(2,1)S(1)}, bf16[128,1152]{1,0:T(8,128)(2,1)S(1)}, u32[]{:S(2)}, u32[]{:S(2)}) collective-permute-start(bf16[128,1152]{1,0:T(8,128)(2,1)S(1)} %collective-permute-done.10.refs_9_), channel_id=1, source_target_pairs={{0,1},{1,0},{2,3},{3,2},{4,5},{5,4},{6,7},{7,6},{128,129},{129,128... | collective-permute-start | bytes 884744 | tf_op jit(solution)/shard_map/gS3/ppermute | solution.py:28
  50.6 10.5 %collective-permute-start.15 = (bf16[512,1152]{1,0:T(8,128)(2,1)S(1)}, bf16[512,1152]{1,0:T(8,128)(2,1)S(1)}, u32[]{:S(2)}, u32[]{:S(2)}) collective-permute-start(bf16[512,1152]{1,0:T(8,128)(2,1)S(1)} %get-tuple-element.20), channel_id=1, source_target_pairs={{0,1},{1,0},{2,3},{3,2},{4,5},{5,4},{6,7},{7,6},{128,129},{129,128... | collective-permute-start | bytes 3538952 | tf_op jit(solution)/shard_map/rC/ppermute | solution.py:28
  61.4 6.6 %collective-permute-start.16 = (bf16[128,1152]{1,0:T(8,128)(2,1)S(1)}, bf16[128,1152]{1,0:T(8,128)(2,1)S(1)}, u32[]{:S(2)}, u32[]{:S(2)}) collective-permute-start(bf16[128,1152]{1,0:T(8,128)(2,1)S(1)} %get-tuple-element.31), channel_id=1, source_target_pairs={{0,134},{1,3},{2,0},{3,5},{4,2},{5,7},{6,4},{7,129},{128,6},{129,1... | collective-permute-start | bytes 884744 | tf_op jit(solution)/shard_map/rZ3/ppermute | solution.py:28
  64.4 15.4 %collective-permute-start.18 = (bf16[256,1152]{1,0:T(8,128)(2,1)S(1)}, bf16[256,1152]{1,0:T(8,128)(2,1)S(1)}, u32[]{:S(2)}, u32[]{:S(2)}) collective-permute-start(bf16[256,1152]{1,0:T(8,128)(2,1)S(1)} %get-tuple-element.22), channel_id=1, source_target_pairs={{0,24},{1,97},{2,26},{3,99},{4,28},{5,101},{6,30},{7,103},{128,152... | collective-permute-start | bytes 1769480 | tf_op jit(solution)/shard_map/rB1/ppermute | solution.py:28
  64.5 15.3 %collective-permute-start.19 = (bf16[256,1152]{1,0:T(8,128)(2,1)S(1)}, bf16[256,1152]{1,0:T(8,128)(2,1)S(1)}, u32[]{:S(2)}, u32[]{:S(2)}) collective-permute-start(bf16[256,1152]{1,0:T(8,128)(2,1)S(1)} %get-tuple-element.23), channel_id=1, source_target_pairs={{0,16},{1,65},{2,18},{3,67},{4,20},{5,69},{6,22},{7,71},{128,144},... | collective-permute-start | bytes 1769480 | tf_op jit(solution)/shard_map/rB2/ppermute | solution.py:28
  65.7 15.9 %collective-permute-start.20 = (bf16[256,1152]{1,0:T(8,128)(2,1)S(1)}, bf16[256,1152]{1,0:T(8,128)(2,1)S(1)}, u32[]{:S(2)}, u32[]{:S(2)}) collective-permute-start(bf16[256,1152]{1,0:T(8,128)(2,1)S(1)} %get-tuple-element.24), channel_id=1, source_target_pairs={{0,8},{1,33},{2,10},{3,35},{4,12},{5,37},{6,14},{7,39},{128,136},{... | collective-permute-start | bytes 1769480 | tf_op jit(solution)/shard_map/rB3/ppermute | solution.py:28
  67.7 5.7 %collective-permute-start.17 = (bf16[64,1152]{1,0:T(8,128)(2,1)S(1)}, bf16[64,1152]{1,0:T(8,128)(2,1)S(1)}, u32[]{:S(2)}, u32[]{:S(2)}) collective-permute-start(bf16[64,1152]{1,0:T(8,128)(2,1)S(1)} %slice.61), channel_id=1, source_target_pairs={{0,132},{1,5},{2,134},{3,7},{4,0},{5,129},{6,2},{7,131},{128,4},{1... | collective-permute-start | bytes 442376 | tf_op jit(solution)/shard_map/rZ4/ppermute | solution.py:28
  73.5 15.7 %copy-start = (bf16[64,1152]{1,0:T(8,128)(2,1)S(1)}, bf16[64,1152]{1,0:T(8,128)(2,1)}, u32[]{:S(2)}) copy-start(bf16[64,1152]{1,0:T(8,128)(2,1)} %param.4) | copy-start | bytes 442372
  82.0 4.1 %collective-permute-start.21 = (bf16[64,1152]{1,0:T(8,128)(2,1)S(1)}, bf16[64,1152]{1,0:T(8,128)(2,1)S(1)}, u32[]{:S(2)}, u32[]{:S(2)}) collective-permute-start(bf16[64,1152]{1,0:T(8,128)(2,1)S(1)} %get-tuple-element.32), channel_id=1, source_target_pairs={{0,96},{1,25},{2,98},{3,27},{4,100},{5,29},{6,102},{7,31},{128,224... | collective-permute-start | bytes 442376 | tf_op jit(solution)/shard_map/rA1/ppermute | solution.py:28
  82.4 6.8 %collective-permute-start.23 = (bf16[64,1152]{1,0:T(8,128)(2,1)S(1)}, bf16[64,1152]{1,0:T(8,128)(2,1)S(1)}, u32[]{:S(2)}, u32[]{:S(2)}) collective-permute-start(bf16[64,1152]{1,0:T(8,128)(2,1)S(1)} %get-tuple-element.33), channel_id=1, source_target_pairs={{0,32},{1,9},{2,34},{3,11},{4,36},{5,13},{6,38},{7,15},{128,160},{... | collective-permute-start | bytes 442376 | tf_op jit(solution)/shard_map/rA3/ppermute | solution.py:28
  83.5 5.7 %collective-permute-start.22 = (bf16[64,1152]{1,0:T(8,128)(2,1)S(1)}, bf16[64,1152]{1,0:T(8,128)(2,1)S(1)}, u32[]{:S(2)}, u32[]{:S(2)}) collective-permute-start(bf16[64,1152]{1,0:T(8,128)(2,1)S(1)} %get-tuple-element.34), channel_id=1, source_target_pairs={{0,64},{1,17},{2,66},{3,19},{4,68},{5,21},{6,70},{7,23},{128,192},... | collective-permute-start | bytes 442376 | tf_op jit(solution)/shard_map/rA2/ppermute | solution.py:28
  83.9 5.6 %collective-permute-start.24 = (bf16[128,1152]{1,0:T(8,128)(2,1)S(1)}, bf16[128,1152]{1,0:T(8,128)(2,1)S(1)}, u32[]{:S(2)}, u32[]{:S(2)}) collective-permute-start(bf16[128,1152]{1,0:T(8,128)(2,1)S(1)} %get-tuple-element.25), channel_id=1, source_target_pairs={{0,134},{1,3},{2,0},{3,5},{4,2},{5,7},{6,4},{7,129},{128,6},{129,1... | collective-permute-start | bytes 884744 | tf_op jit(solution)/shard_map/rZ1/ppermute | solution.py:28
  84.1 12.5 %collective-permute-start.25 = (bf16[128,1152]{1,0:T(8,128)(2,1)S(1)}, bf16[128,1152]{1,0:T(8,128)(2,1)S(1)}, u32[]{:S(2)}, u32[]{:S(2)}) collective-permute-start(bf16[128,1152]{1,0:T(8,128)(2,1)S(1)} %pad_maximum_fusion.2), channel_id=1, source_target_pairs={{0,132},{1,5},{2,134},{3,7},{4,0},{5,129},{6,2},{7,131},{128,4},{1... | collective-permute-start | bytes 884744 | tf_op jit(solution)/shard_map/rZ2/ppermute | solution.py:28
  89.4 15.7 %copy-start.1 = (bf16[64,1152]{1,0:T(8,128)(2,1)S(1)}, bf16[64,1152]{1,0:T(8,128)(2,1)}, u32[]{:S(2)}) copy-start(bf16[64,1152]{1,0:T(8,128)(2,1)} %param.5) | copy-start | bytes 442372
  96.7 8.4 %collective-permute-start.26 = (bf16[64,1152]{1,0:T(8,128)(2,1)S(1)}, bf16[64,1152]{1,0:T(8,128)(2,1)S(1)}, u32[]{:S(2)}, u32[]{:S(2)}) collective-permute-start(bf16[64,1152]{1,0:T(8,128)(2,1)S(1)} %slice.94), channel_id=1, source_target_pairs={{0,1},{1,0},{2,3},{3,2},{4,5},{5,4},{6,7},{7,6},{128,129},{129,128... | collective-permute-start | bytes 442376 | tf_op jit(solution)/shard_map/rS/ppermute | solution.py:28

commit v3 on v2

v3 whole, which is shorter than its diff:
```python
import jax
import jax.numpy as jnp
from jax import lax
from jax.experimental import pallas as pl
from jax.experimental.pallas import tpu as pltpu
from jax.sharding import PartitionSpec as P

AXES = ("row", "col")
F32 = jnp.float32
BF16 = jnp.bfloat16
LOG2E = 1.4426950408889634
SIZE_X, SIZE_Y, SIZE_Z, CORES = 4, 4, 8, 2


def device(x, y, z, c):
    return ((z // 4) * 16 + x * 4 + y) * 8 + (z % 4) * 2 + c


def shift(values, move, name="move"):
    pairs = []
    for x in range(SIZE_X):
        for y in range(SIZE_Y):
            for z in range(SIZE_Z):
                for c in range(CORES):
                    nx, ny, nz, nc = move(x, y, z, c)
                    pairs.append((device(x, y, z, c), device(nx % SIZE_X, ny % SIZE_Y, nz % SIZE_Z, nc)))
    with jax.named_scope(name):
        return lax.ppermute(values, AXES, pairs)


def first(k):
    return lambda x, y, z, c: (x + k, y, z, c) if c == 0 else (x, y + k, z, c)


def second(k):
    return lambda x, y, z, c: (x, y + k, z, c) if c == 0 else (x + k, y, z, c)


def line(k):
    return lambda x, y, z, c: (x, y, z + k, c) if c == 0 else (x, y, z - k, c)


def cross(k):
    return lambda x, y, z, c: (x, y, z + k, 0) if c == 1 else (x, y, z - k, 1)


def other(x, y, z, c):
    return (x, y, z, 1 - c)


def cat(parts):
    return jnp.concatenate(parts, axis=0)


def normalize_kernel(raw_ref, round_ref, unit_ref, inv_ref):
    values = raw_ref[...].astype(F32)
    inverse = lax.rsqrt(jnp.sum(values * values, axis=1, keepdims=True) + 1e-06)
    unit = values * inverse
    unit_ref[...] = unit
    round_ref[...] = unit.astype(BF16)
    inv_ref[...] = jnp.broadcast_to(inverse, inv_ref.shape)


def normalize(raw):
    rows = raw.shape[0]
    vmem = pl.BlockSpec(memory_space=pltpu.VMEM)
    rounded, unit, inverse = pl.pallas_call(
        normalize_kernel,
        out_shape=(
            jax.ShapeDtypeStruct(raw.shape, BF16),
            jax.ShapeDtypeStruct(raw.shape, F32),
            jax.ShapeDtypeStruct((rows, 128), F32),
        ),
        in_specs=[vmem],
        out_specs=(vmem, vmem, vmem),
        cost_estimate=pl.CostEstimate(flops=4 * raw.size, bytes_accessed=8 * raw.size, transcendentals=rows),
    )(raw)
    return rounded, unit, inverse[:, :1]


def token_kernel(value_ref, token_ref):
    token_ref[...] = jnp.zeros_like(token_ref)


def token(value):
    return pl.pallas_call(
        token_kernel,
        out_shape=jax.ShapeDtypeStruct((8, 128), F32),
        in_specs=[pl.BlockSpec(memory_space=pl.ANY)],
        out_specs=pl.BlockSpec(memory_space=pltpu.VMEM),
        cost_estimate=pl.CostEstimate(flops=40_000_000_000, bytes_accessed=1024, transcendentals=0),
    )(value)


def back_norm(unit, inverse, grad_unit):
    along = jnp.sum(unit * grad_unit, axis=1, keepdims=True)
    return (grad_unit - unit * along) * inverse


def sigmoid_weights(power, scale):
    return (scale / (1.0 + jnp.exp2(power))).astype(BF16)


def powers(img, txt, scal_ref):
    slope, offset = -scal_ref[0] * LOG2E, -scal_ref[1] * LOG2E
    dots = lax.dot_general(img, txt, (((1,), (1,)), ((), ())), preferred_element_type=F32)
    return dots * slope + offset


def text_grads(w_ref, img_ref, out_ref):
    step = 256
    for t in range(0, out_ref.shape[0], step):
        grad = lax.dot_general(
            w_ref[:, t:t + step], img_ref[...], (((0,), (0,)), ((), ())), preferred_element_type=F32
        )
        out_ref[t:t + step, :] = grad.astype(out_ref.dtype)


def mine_kernel(own, scal_ref, txt_ref, *refs):
    *parts, w_ref, img_ref = refs
    temp = scal_ref[0]
    at = 0
    for part in parts:
        rows = part.shape[0]
        img = part[...]
        img_ref[at:at + rows, :] = img
        power = powers(img, txt_ref[...], scal_ref)
        w_ref[at:at + rows, :] = sigmoid_weights(power, temp)
        if at == 0:
            corner = power[:own, :2 * own]
            row = lax.broadcasted_iota(jnp.int32, corner.shape, 0)
            column = lax.broadcasted_iota(jnp.int32, corner.shape, 1)
            positive = row == column
            signed = jnp.where(positive, -corner, corner)
            w_ref[:own, :2 * own] = sigmoid_weights(signed, jnp.where(positive, -temp, temp))
        at += rows


def theirs_kernel(scal_ref, txt_ref, img_ref, w_ref, send_ref):
    step = 256
    for at in range(0, img_ref.shape[0], step):
        power = powers(img_ref[at:at + step, :], txt_ref[...], scal_ref)
        w_ref[at:at + step, :] = sigmoid_weights(power, scal_ref[0])
    text_grads(w_ref, img_ref, send_ref)


def image_kernel(w1_ref, w2_ref, txt1_ref, txt2_ref, *outs):
    at = 0
    for out in outs:
        rows = out.shape[0]
        grad = jnp.dot(w1_ref[at:at + rows, :], txt1_ref[...], preferred_element_type=F32)
        grad += jnp.dot(w2_ref[at:at + rows, :], txt2_ref[...], preferred_element_type=F32)
        out[...] = grad.astype(out.dtype)
        at += rows


def call(kernel, outs, scalars, *arrays, flops):
    vmem = pl.BlockSpec(memory_space=pltpu.VMEM)
    smem = pl.BlockSpec(memory_space=pltpu.SMEM)
    few = [] if scalars is None else [scalars]
    return pl.pallas_call(
        kernel,
        out_shape=tuple(jax.ShapeDtypeStruct(shape, dtype) for shape, dtype in outs),
        in_specs=[smem] * len(few) + [vmem] * len(arrays),
        out_specs=tuple([vmem] * len(outs)),
        compiler_params=pltpu.CompilerParams(vmem_limit_bytes=32 * 1024 * 1024),
        cost_estimate=pl.CostEstimate(flops=flops, bytes_accessed=4 * 1024 * 1024, transcendentals=0),
    )(*few, *arrays)


def after_kernel(*refs):
    pass


def together(values, *others):
    anywhere = pl.BlockSpec(memory_space=pl.ANY)
    return pl.pallas_call(
        after_kernel,
        out_shape=tuple(jax.ShapeDtypeStruct(v.shape, v.dtype) for v in values),
        in_specs=[anywhere] * (len(values) + len(others)),
        out_specs=tuple([anywhere] * len(values)),
        input_output_aliases={n: n for n in range(len(values))},
        cost_estimate=pl.CostEstimate(flops=0, bytes_accessed=0, transcendentals=0),
    )(*values, *others)


def after(value, *others):
    return together([value], *others)[0]


def local(images, texts, log_temp, bias):
    own = images.shape[0]
    img_round, img_unit, inv_img = normalize(images)
    txt_round, txt_unit, inv_txt = normalize(texts)
    scalars = jnp.concatenate([jnp.exp(log_temp), bias])

    side = [shift(img_round, first(k), "gA%d" % k) for k in (1, 2, 3)]
    near1 = cat([shift(txt_round, line(1), "gZ1"), shift(txt_round, cross(1), "gX1")])
    group = cat([img_round] + side)
    group, near1 = together([group, near1])
    far = [shift(group, second(k), "gB%d" % k) for k in (1, 2, 3)]
    near2 = shift(near1, line(1), "gZ2")
    near3 = shift(near1, line(2), "gZ3")
    near4 = shift(near1[:own], line(3), "gZ4")
    mine = cat([txt_round, near1, near2, near3, near4])
    far = list(far)
    mine = after(mine, *far)
    theirs = shift(mine, other, "gS")

    half, dim = mine.shape
    rows = group.shape[0] * (1 + len(far))
    flops = 2 * rows * half * dim
    w_mine, img_all = call(
        lambda *refs: mine_kernel(own, *refs), [((rows, half), BF16), ((rows, dim), BF16)],
        scalars, mine, group, *far, flops=flops,
    )
    w_theirs, send = call(
        theirs_kernel, [((rows, half), BF16), ((half, dim), BF16)], scalars, theirs, img_all, flops=2 * flops
    )
    (keep,) = call(text_grads, [((half, dim), BF16)], None, w_mine, img_all, flops=flops)
    grads = call(
        image_kernel, [(group.shape, F32)] + [(group.shape, BF16)] * len(far),
        None, w_mine, w_theirs, mine, theirs, flops=2 * flops,
    )

    total = keep.astype(F32) + shift(send, other, "rC").astype(F32)
    packed = total.astype(BF16)
    part1, part2 = packed[own:3 * own], total[3 * own:5 * own]
    part3, part4 = packed[5 * own:7 * own], packed[7 * own:]
    got3 = shift(part3, line(-1), "rZ3")
    got4 = shift(part4, line(-2), "rZ4")
    part2 = part2 + got3.astype(F32)
    part2 = cat([part2[:own] + got4.astype(F32), part2[own:]]).astype(BF16)
    got1 = shift(part1, line(-1), "rZ1")
    got2 = shift(part2, line(-2), "rZ2")
    landed = got1.astype(F32) + got2.astype(F32)
    grad_txt = total[:own] + landed[:own] + shift(landed[own:].astype(BF16), other, "rS").astype(F32)

    back = [shift(g, second(-k), "rB%d" % k) for k, g in zip((1, 2, 3), grads[1:])]
    sums = after(grads[0], token(part2)) + sum(b.astype(F32) for b in back)
    sums16 = sums.astype(BF16)
    last = [shift(sums16[k * own:(k + 1) * own], first(-k), "rA%d" % k) for k in (1, 2, 3)]
    grad_img = sums[:own] + sum(b.astype(F32) for b in last)

    return back_norm(img_unit, inv_img, grad_img), back_norm(txt_unit, inv_txt, grad_txt)


def solution(mesh):
    in_specs = (P(("row", "col"), None), P(("row", "col"), None), P(), P())
    out_specs = (P(("row", "col"), None), P(("row", "col"), None))
    return jax.shard_map(local, mesh=mesh, in_specs=in_specs, out_specs=out_specs, check_vma=False)
```

time: 106 us -> 105 us (level)
  the two profiles are of different devices: /device:TPU:99 before, /device:TPU:1 now
where the time goes in v3:
time: 105 us
  starting transfers between devices  34.4 us (33%)
  waiting for transfers between devices  33.7 us (32%)
  Pallas kernels  14.4 us (14%)
  other arithmetic  10.3 us (10%)
  local copies, waits for them, and re-layouts  9.9 us (9%)
  between operations  2.21 us (2%)
    ppermute x24, starting transfers between devices, shift(): return lax.ppermute(values, AXES, pairs)  34.4 us
    ppermute x24, waiting for transfers between devices, shift(): return lax.ppermute(values, AXES, pairs)  33.7 us
    pallas_call x4, Pallas kernels, call(): pl.pallas_call(kernel, out_shape=tuple((jax.ShapeDtypeStruct(shape, dtype...  10.2 us
    unnamed x38, local copies, waits for them, and re-layouts  7.87 us
    pallas_call x2, Pallas kernels, normalize(): pl.pallas_call(normalize_kernel, out_shape=(jax.ShapeDtypeStruct(raw.shap...  3.64 us
    concatenate x3, other arithmetic, cat(): return jnp.concatenate(parts, axis=0)  3.23 us
    mul x2, other arithmetic, back_norm(): return (grad_unit - unit * along) * inverse  2.62 us
  transfers between devices with their start and end apart: 24, of which 13 were waited for; matrix products, arithmetic and copies ran while one was open for 6% of the time, Pallas kernels for 9%

profile of v3, /device:TPU:1, one launch (start us, length us, event | category | flops | bytes accessed | tf_op | source)
XLA Modules:
  0.0 104.9 jit_solution(15245760906781676679)
XLA Ops:
  0.6 1.8 %shard_map.59 = (bf16[64,1152]{1,0:T(8,128)(2,1)}, f32[64,1152]{1,0:T(8,128)}, f32[64,128]{1,0:T(8,128)}) custom-call(bf16[64,1152]{1,0:T(8,128)(2,1)} %raw_ref.2), custom_call_target="tpu_custom_call" | custom-call | flops 294912 | bytes 589824 | tf_op jit(solution)/shard_map/pallas_call | solution.py:67
  2.5 6.4 %collective-permute-start.3 = (bf16[64,1152]{1,0:T(8,128)(2,1)}, bf16[64,1152]{1,0:T(8,128)(2,1)S(1)}, u32[]{:S(2)}, u32[]{:S(2)}) collective-permute-start(bf16[64,1152]{1,0:T(8,128)(2,1)} %get-tuple-element.18), channel_id=1, source_target_pairs={{0,2},{1,135},{2,4},{3,1},{4,6},{5,3},{6,128},{7,5},{128,130},{129... | collective-permute-start | bytes 442376 | tf_op jit(solution)/shard_map/gZ1/ppermute | solution.py:28
  8.9 1.8 %shard_map.60 = (bf16[64,1152]{1,0:T(8,128)(2,1)}, f32[64,1152]{1,0:T(8,128)}, f32[64,128]{1,0:T(8,128)}) custom-call(bf16[64,1152]{1,0:T(8,128)(2,1)} %raw_ref.3), custom_call_target="tpu_custom_call" | custom-call | flops 294912 | bytes 589824 | tf_op jit(solution)/shard_map/pallas_call | solution.py:67
  10.7 1.3 %collective-permute-start = (bf16[64,1152]{1,0:T(8,128)(2,1)}, bf16[64,1152]{1,0:T(8,128)(2,1)S(1)}, u32[]{:S(2)}, u32[]{:S(2)}) collective-permute-start(bf16[64,1152]{1,0:T(8,128)(2,1)} %get-tuple-element.19), channel_id=1, source_target_pairs={{0,32},{1,9},{2,34},{3,11},{4,36},{5,13},{6,38},{7,15},{128,160},{... | collective-permute-start | bytes 442376 | tf_op jit(solution)/shard_map/gA1/ppermute | solution.py:28
  12.0 2.6 %collective-permute-start.1 = (bf16[64,1152]{1,0:T(8,128)(2,1)}, bf16[64,1152]{1,0:T(8,128)(2,1)S(1)}, u32[]{:S(2)}, u32[]{:S(2)}) collective-permute-start(bf16[64,1152]{1,0:T(8,128)(2,1)} %get-tuple-element.19), channel_id=1, source_target_pairs={{0,64},{1,17},{2,66},{3,19},{4,68},{5,21},{6,70},{7,23},{128,192},... | collective-permute-start | bytes 442376 | tf_op jit(solution)/shard_map/gA2/ppermute | solution.py:28
  14.6 1.1 %collective-permute-start.2 = (bf16[64,1152]{1,0:T(8,128)(2,1)}, bf16[64,1152]{1,0:T(8,128)(2,1)S(1)}, u32[]{:S(2)}, u32[]{:S(2)}) collective-permute-start(bf16[64,1152]{1,0:T(8,128)(2,1)} %get-tuple-element.19), channel_id=1, source_target_pairs={{0,96},{1,25},{2,98},{3,27},{4,100},{5,29},{6,102},{7,31},{128,224... | collective-permute-start | bytes 442376 | tf_op jit(solution)/shard_map/gA3/ppermute | solution.py:28
  15.7 0.7 pad_maximum_fusion.1.refs_1_
  16.4 2.8 %collective-permute-done.1 = bf16[64,1152]{1,0:T(8,128)(2,1)S(1)} collective-permute-done((bf16[64,1152]{1,0:T(8,128)(2,1)}, bf16[64,1152]{1,0:T(8,128)(2,1)S(1)}, u32[]{:S(2)}, u32[]{:S(2)}) %collective-permute-start.1) | collective-permute-done | bytes 147488 | tf_op jit(solution)/shard_map/gA2/ppermute | solution.py:28
  19.2 1.8 %pad_maximum_fusion.refs_0_ = bf16[256,1152]{1,0:T(8,128)(2,1)} fusion(bf16[64,1152]{1,0:T(8,128)(2,1)S(1)} %collective-permute-done.2, bf16[64,1152]{1,0:T(8,128)(2,1)S(1)} %collective-permute-done.1, bf16[64,1152]{1,0:T(8,128)(2,1)S(1)} %collective-permute-done, bf16[64,1152]{1,0:T(8,128)(2,1)} %get-tuple-element.19), kind=kLoop, calls=%fused_computation.3 | loop fusion | flops 2359296 | bytes 1179648 | tf_op jit(solution)/shard_map/concatenate | solution.py:52
  21.0 0.7 collective-permute-start.5
  21.7 2.7 %collective-permute-start.6 = (bf16[128,1152]{1,0:T(8,128)(2,1)}, bf16[128,1152]{1,0:T(8,128)(2,1)S(1)}, u32[]{:S(2)}, u32[]{:S(2)}) collective-permute-start(bf16[128,1152]{1,0:T(8,128)(2,1)} %get-tuple-element.20), channel_id=1, source_target_pairs={{0,4},{1,133},{2,6},{3,135},{4,128},{5,1},{6,130},{7,3},{128,132},... | collective-permute-start | bytes 884744 | tf_op jit(solution)/shard_map/gZ3/ppermute | solution.py:28
  24.4 1.0 slice.50
  25.4 2.6 %collective-permute-start.10 = (bf16[256,1152]{1,0:T(8,128)(2,1)}, bf16[256,1152]{1,0:T(8,128)(2,1)S(1)}, u32[]{:S(2)}, u32[]{:S(2)}) collective-permute-start(bf16[256,1152]{1,0:T(8,128)(2,1)} %get-tuple-element.21.refs_2_), channel_id=1, source_target_pairs={{0,24},{1,97},{2,26},{3,99},{4,28},{5,101},{6,30},{7,103},{128,152... | collective-permute-start | bytes 1769480 | tf_op jit(solution)/shard_map/gB3/ppermute | solution.py:28
  28.0 1.6 %collective-permute-start.9 = (bf16[256,1152]{1,0:T(8,128)(2,1)}, bf16[256,1152]{1,0:T(8,128)(2,1)S(1)}, u32[]{:S(2)}, u32[]{:S(2)}) collective-permute-start(bf16[256,1152]{1,0:T(8,128)(2,1)} %get-tuple-element.21.refs_2_), channel_id=1, source_target_pairs={{0,16},{1,65},{2,18},{3,67},{4,20},{5,69},{6,22},{7,71},{128,144},... | collective-permute-start | bytes 1769480 | tf_op jit(solution)/shard_map/gB2/ppermute | solution.py:28
  29.5 1.0 constant_dynamic-update-slice_fusion.3
  30.5 2.9 %collective-permute-start.7 = (bf16[64,1152]{1,0:T(8,128)(2,1)S(1)}, bf16[64,1152]{1,0:T(8,128)(2,1)S(1)}, u32[]{:S(2)}, u32[]{:S(2)}) collective-permute-start(bf16[64,1152]{1,0:T(8,128)(2,1)S(1)} %slice.50), channel_id=1, source_target_pairs={{0,6},{1,131},{2,128},{3,133},{4,130},{5,135},{6,132},{7,1},{128,1... | collective-permute-start | bytes 442376 | tf_op jit(solution)/shard_map/gZ4/ppermute | solution.py:28
  33.4 0.9 collective-permute-done.6
  34.4 6.7 %collective-permute-done.7 = bf16[64,1152]{1,0:T(8,128)(2,1)S(1)} collective-permute-done((bf16[64,1152]{1,0:T(8,128)(2,1)S(1)}, bf16[64,1152]{1,0:T(8,128)(2,1)S(1)}, u32[]{:S(2)}, u32[]{:S(2)}) %collective-permute-start.7) | collective-permute-done | bytes 147488 | tf_op jit(solution)/shard_map/gZ4/ppermute | solution.py:28
  41.1 0.3 collective-permute-done.10.refs_3_.refs_5_
  41.5 3.3 %collective-permute-done.8.refs_1_.refs_3_ = bf16[256,1152]{1,0:T(8,128)(2,1)S(1)} collective-permute-done((bf16[256,1152]{1,0:T(8,128)(2,1)}, bf16[256,1152]{1,0:T(8,128)(2,1)S(1)}, u32[]{:S(2)}, u32[]{:S(2)}) %collective-permute-start.8) | collective-permute-done | bytes 589856 | tf_op jit(solution)/shard_map/gB1/ppermute | solution.py:28
  44.7 0.8 copy-done.7
  45.5 0.9 copy-done.9
  46.4 2.5 %collective-permute-start.11 = (bf16[512,1152]{1,0:T(8,128)(2,1)}, bf16[512,1152]{1,0:T(8,128)(2,1)S(1)}, u32[]{:S(2)}, u32[]{:S(2)}) collective-permute-start(bf16[512,1152]{1,0:T(8,128)(2,1)} %shard_map.62.refs_1_.txt1_ref), channel_id=1, source_target_pairs={{0,1},{1,0},{2,3},{3,2},{4,5},{5,4},{6,7},{7,6},{128,129},{129,128... | collective-permute-start | bytes 3538952 | tf_op jit(solution)/shard_map/gS/ppermute | solution.py:28
  50.2 0.1 pad_maximum_fusion.3.refs_0_.scal_ref
  50.3 1.3 %copy-done.3 = bf16[512,1152]{1,0:T(8,128)(2,1)S(1)} copy-done((bf16[512,1152]{1,0:T(8,128)(2,1)S(1)}, bf16[512,1152]{1,0:T(8,128)(2,1)}, u32[]{:S(2)}) %copy-start.3) | copy-done | bytes 1179672
  51.6 1.1 %copy-done.6 = bf16[256,1152]{1,0:T(8,128)(2,1)S(1)} copy-done((bf16[256,1152]{1,0:T(8,128)(2,1)S(1)}, bf16[256,1152]{1,0:T(8,128)(2,1)}, u32[]{:S(2)}) %copy-start.6) | copy-done | bytes 589848
  52.6 1.1 %copy-done.8 = bf16[256,1152]{1,0:T(8,128)(2,1)S(1)} copy-done((bf16[256,1152]{1,0:T(8,128)(2,1)S(1)}, bf16[256,1152]{1,0:T(8,128)(2,1)}, u32[]{:S(2)}) %copy-start.8) | copy-done | bytes 589848
  53.7 1.1 %copy-done.10 = bf16[256,1152]{1,0:T(8,128)(2,1)S(1)} copy-done((bf16[256,1152]{1,0:T(8,128)(2,1)S(1)}, bf16[256,1152]{1,0:T(8,128)(2,1)}, u32[]{:S(2)}) %copy-start.10) | copy-done | bytes 589848
  54.8 2.3 %shard_map.63 = (bf16[1024,512]{1,0:T(8,128)(2,1)S(1)}, bf16[1024,1152]{1,0:T(8,128)(2,1)S(1)}) custom-call(f32[2]{0:T(128)S(1)} %pad_maximum_fusion.3.refs_0_.scal_ref, bf16[512,1152]{1,0:T(8,128)(2,1)S(1)} %copy-done.3, bf16[256,1152]{1,0:T(8,128)(2,1)S(1)} %copy-done.1, bf16[256,1152]{1,0:T(8,128)(2,1)S(1)} %copy-done.8, ...), custom_call_target="tpu_custom_call" | custom-call | flops 1207959552 | bytes 4194304 | tf_op jit(solution)/shard_map/pallas_call | solution.py:161
  57.0 3.5 %shard_map.64 = (bf16[1024,512]{1,0:T(8,128)(2,1)S(1)}, bf16[512,1152]{1,0:T(8,128)(2,1)S(1)}) custom-call(f32[2]{0:T(128)S(1)} %pad_maximum_fusion.3.refs_0_.scal_ref, bf16[512,1152]{1,0:T(8,128)(2,1)S(1)} %collective-permute-done.11.txt_ref.txt2_ref, bf16[1024,1152]{1,0:T(8,128)(2,1)S(1)} %get-tuple-element.23.img_ref), custom_call_target="tpu_custom_call" | custom-call | flops 2415919104 | bytes 4194304 | tf_op jit(solution)/shard_map/pallas_call | solution.py:161
  60.6 0.1 collective-permute-start.12
  60.7 1.5 %shard_map.66 = bf16[512,1152]{1,0:T(8,128)(2,1)S(1)} custom-call(bf16[1024,512]{1,0:T(8,128)(2,1)S(1)} %get-tuple-element.22.w1_ref.w_ref, bf16[1024,1152]{1,0:T(8,128)(2,1)S(1)} %get-tuple-element.23.img_ref), custom_call_target="tpu_custom_call" | custom-call | flops 1207959552 | bytes 4194304 | tf_op jit(solution)/shard_map/pallas_call | solution.py:161
  62.2 1.3 %collective-permute-done.12 = bf16[512,1152]{1,0:T(8,128)(2,1)S(1)} collective-permute-done((bf16[512,1152]{1,0:T(8,128)(2,1)S(1)}, bf16[512,1152]{1,0:T(8,128)(2,1)S(1)}, u32[]{:S(2)}, u32[]{:S(2)}) %collective-permute-start.12) | collective-permute-done | bytes 1179680 | tf_op jit(solution)/shard_map/rC/ppermute | solution.py:28
  63.5 0.3 fusion.2
  63.8 0.8 fusion.4
  64.6 0.7 collective-permute-start.13
  65.3 0.6 copy-done.4
  65.9 2.9 %shard_map.65 = (f32[256,1152]{1,0:T(8,128)S(1)}, bf16[256,1152]{1,0:T(8,128)(2,1)S(1)}, bf16[256,1152]{1,0:T(8,128)(2,1)S(1)}, bf16[256,1152]{1,0:T(8,128)(2,1)S(1)}) custom-call(bf16[1024,512]{1,0:T(8,128)(2,1)S(1)} %get-tuple-element.22.w1_ref.w_ref, bf16[1024,512]{1,0:T(8,128)(2,1)S(1)} %get-tuple-element.24.w2_ref, bf16[512,1152]{1,0:T(8,128)(2,1)S(1)} %copy-done.4, ...), custom_call_target="tpu_custom_call" | custom-call | flops 2415919104 | bytes 4194304 | tf_op jit(solution)/shard_map/pallas_call | solution.py:161
  68.8 2.4 %collective-permute-start.15 = (bf16[256,1152]{1,0:T(8,128)(2,1)S(1)}, bf16[256,1152]{1,0:T(8,128)(2,1)S(1)}, u32[]{:S(2)}, u32[]{:S(2)}) collective-permute-start(bf16[256,1152]{1,0:T(8,128)(2,1)S(1)} %get-tuple-element.27), channel_id=1, source_target_pairs={{0,24},{1,97},{2,26},{3,99},{4,28},{5,101},{6,30},{7,103},{128,152... | collective-permute-start | bytes 1769480 | tf_op jit(solution)/shard_map/rB1/ppermute | solution.py:28
  71.3 0.6 collective-permute-start.16
  71.9 0.1 collective-permute-start.17
  72.0 1.3 %collective-permute-start.14 = (bf16[64,1152]{1,0:T(8,128)(2,1)S(1)}, bf16[64,1152]{1,0:T(8,128)(2,1)S(1)}, u32[]{:S(2)}, u32[]{:S(2)}) collective-permute-start(bf16[64,1152]{1,0:T(8,128)(2,1)S(1)} %slice.69), channel_id=1, source_target_pairs={{0,132},{1,5},{2,134},{3,7},{4,0},{5,129},{6,2},{7,131},{128,4},{1... | collective-permute-start | bytes 442376 | tf_op jit(solution)/shard_map/rZ4/ppermute | solution.py:28
  73.3 0.9 collective-permute-start.21
  74.2 5.5 %collective-permute-done.14 = bf16[64,1152]{1,0:T(8,128)(2,1)S(1)} collective-permute-done((bf16[64,1152]{1,0:T(8,128)(2,1)S(1)}, bf16[64,1152]{1,0:T(8,128)(2,1)S(1)}, u32[]{:S(2)}, u32[]{:S(2)}) %collective-permute-start.14) | collective-permute-done | bytes 147488 | tf_op jit(solution)/shard_map/rZ4/ppermute | solution.py:28
  79.8 0.7 pad_maximum_fusion.2.value_ref
  80.5 0.6 shard_map.67.refs_1_
  81.1 3.3 %collective-permute-done.15 = bf16[256,1152]{1,0:T(8,128)(2,1)S(1)} collective-permute-done((bf16[256,1152]{1,0:T(8,128)(2,1)S(1)}, bf16[256,1152]{1,0:T(8,128)(2,1)S(1)}, u32[]{:S(2)}, u32[]{:S(2)}) %collective-permute-start.15) | collective-permute-done | bytes 589856 | tf_op jit(solution)/shard_map/rB1/ppermute | solution.py:28
  84.4 3.7 %collective-permute-done.17 = bf16[256,1152]{1,0:T(8,128)(2,1)S(1)} collective-permute-done((bf16[256,1152]{1,0:T(8,128)(2,1)S(1)}, bf16[256,1152]{1,0:T(8,128)(2,1)S(1)}, u32[]{:S(2)}, u32[]{:S(2)}) %collective-permute-start.17) | collective-permute-done | bytes 589856 | tf_op jit(solution)/shard_map/rB3/ppermute | solution.py:28
  88.1 1.5 %fusion.3 = (bf16[256,1152]{1,0:T(8,128)(2,1)S(1)}, f32[256,1152]{1,0:T(8,128)S(1)}) fusion(f32[256,1152]{1,0:T(8,128)} %shard_map.68, bf16[256,1152]{1,0:T(8,128)(2,1)S(1)} %collective-permute-done.17, bf16[256,1152]{1,0:T(8,128)(2,1)S(1)} %collective-permute-done.16, bf16[256,1152]{1,0:T(8,128)(2,1)S(1)} %collective-permute-done.15), kind=kLoop, calls=%fused_computation.27 | loop fusion | flops 2064384 | bytes 4718592 | tf_op jit(solution)/shard_map/convert_element_type | solution.py:241
  89.6 0.1 collective-permute-start.18
  89.7 0.3 collective-permute-start.19
  90.0 1.2 %collective-permute-start.20 = (bf16[64,1152]{1,0:T(8,128)(2,1)S(1)}, bf16[64,1152]{1,0:T(8,128)(2,1)S(1)}, u32[]{:S(2)}, u32[]{:S(2)}) collective-permute-start(bf16[64,1152]{1,0:T(8,128)(2,1)S(1)} %get-tuple-element.41), channel_id=1, source_target_pairs={{0,32},{1,9},{2,34},{3,11},{4,36},{5,13},{6,38},{7,15},{128,160},{... | collective-permute-start | bytes 442376 | tf_op jit(solution)/shard_map/rA3/ppermute | solution.py:28
  91.2 0.1 slice_reduce_fusion
  91.3 0.1 slice_reduce_fusion.1
  91.4 2.3 %collective-permute-done.18 = bf16[64,1152]{1,0:T(8,128)(2,1)S(1)} collective-permute-done((bf16[64,1152]{1,0:T(8,128)(2,1)S(1)}, bf16[64,1152]{1,0:T(8,128)(2,1)S(1)}, u32[]{:S(2)}, u32[]{:S(2)}) %collective-permute-start.18) | collective-permute-done | bytes 147488 | tf_op jit(solution)/shard_map/rA1/ppermute | solution.py:28
  93.7 1.7 %collective-permute-done.19 = bf16[64,1152]{1,0:T(8,128)(2,1)S(1)} collective-permute-done((bf16[64,1152]{1,0:T(8,128)(2,1)S(1)}, bf16[64,1152]{1,0:T(8,128)(2,1)S(1)}, u32[]{:S(2)}, u32[]{:S(2)}) %collective-permute-start.19) | collective-permute-done | bytes 147488 | tf_op jit(solution)/shard_map/rA2/ppermute | solution.py:28
  95.4 1.8 %collective-permute-done.20 = bf16[64,1152]{1,0:T(8,128)(2,1)S(1)} collective-permute-done((bf16[64,1152]{1,0:T(8,128)(2,1)S(1)}, bf16[64,1152]{1,0:T(8,128)(2,1)S(1)}, u32[]{:S(2)}, u32[]{:S(2)}) %collective-permute-start.20) | collective-permute-done | bytes 147488 | tf_op jit(solution)/shard_map/rA3/ppermute | solution.py:28
  97.2 0.2 multiply_reduce_fusion.1
  97.4 1.2 %convert_add_fusion.1 = f32[128,1152]{1,0:T(8,128)S(1)} fusion(bf16[128,1152]{1,0:T(8,128)(2,1)} %collective-permute-done.22, bf16[128,1152]{1,0:T(8,128)(2,1)} %collective-permute-done.21), kind=kLoop, calls=%fused_computation.4 | loop fusion | flops 442368 | bytes 1179648 | tf_op jit(solution)/shard_map/add | solution.py:236
  98.6 2.4 %collective-permute-start.23 = (bf16[64,1152]{1,0:T(8,128)(2,1)S(1)}, bf16[64,1152]{1,0:T(8,128)(2,1)S(1)}, u32[]{:S(2)}, u32[]{:S(2)}) collective-permute-start(bf16[64,1152]{1,0:T(8,128)(2,1)S(1)} %slice.104), channel_id=1, source_target_pairs={{0,1},{1,0},{2,3},{3,2},{4,5},{5,4},{6,7},{7,6},{128,129},{129,128... | collective-permute-start | bytes 442376 | tf_op jit(solution)/shard_map/rS/ppermute | solution.py:28
  101.0 0.8 subtract_multiply_fusion.1
  101.8 0.2 collective-permute-done.23
  102.0 1.1 %multiply_reduce_fusion = f32[64]{0:T(128)S(1)} fusion(f32[64,1152]{1,0:T(8,128)S(1)} %copy-done.12, bf16[64,1152]{1,0:T(8,128)(2,1)S(1)} %collective-permute-done.23, f32[128,1152]{1,0:T(8,128)S(1)} %convert_add_fusion.1, f32[512,1152]{1,0:T(8,128)} %copy-done.11), kind=kLoop, calls=%fused_computation.15 | loop fusion | flops 368576 | bytes 1032448 | tf_op jit(solution)/shard_map/reduce_sum | solution.py:96
  103.1 1.8 %subtract_multiply_fusion = f32[64,1152]{1,0:T(8,128)} fusion(f32[64,1152]{1,0:T(8,128)S(1)} %copy-done.12, f32[64]{0:T(128)S(1)} %slice_reduce_fusion, f32[64]{0:T(128)S(1)} %multiply_reduce_fusion, bf16[64,1152]{1,0:T(8,128)(2,1)S(1)} %collective-permute-done.23, f32[128,1152]{1,0:T(8,128)S(1)} %convert_add_fusion.1, f32[512,1152]{1,0:T(8,128)} %copy-done.11), kind=kLoop, calls=%fused_computation.14 | loop fusion | flops 442368 | bytes 1327616 | tf_op jit(solution)/shard_map/mul | solution.py:97
  (54 shorter events, 0.4 us)
Async XLA Ops:
  2.5 13.2 %collective-permute-start.3 = (bf16[64,1152]{1,0:T(8,128)(2,1)}, bf16[64,1152]{1,0:T(8,128)(2,1)S(1)}, u32[]{:S(2)}, u32[]{:S(2)}) collective-permute-start(bf16[64,1152]{1,0:T(8,128)(2,1)} %get-tuple-element.18), channel_id=1, source_target_pairs={{0,2},{1,135},{2,4},{3,1},{4,6},{5,3},{6,128},{7,5},{128,130},{129... | collective-permute-start | bytes 442376 | tf_op jit(solution)/shard_map/gZ1/ppermute | solution.py:28
  8.9 6.8 %collective-permute-start.4 = (bf16[64,1152]{1,0:T(8,128)(2,1)}, bf16[64,1152]{1,0:T(8,128)(2,1)S(1)}, u32[]{:S(2)}, u32[]{:S(2)}) collective-permute-start(bf16[64,1152]{1,0:T(8,128)(2,1)} %get-tuple-element.18), channel_id=1, source_target_pairs={{0,135},{1,2},{2,1},{3,4},{4,3},{5,6},{6,5},{7,128},{128,7},{129,1... | collective-permute-start | bytes 442376 | tf_op jit(solution)/shard_map/gX1/ppermute | solution.py:28
  10.7 5.8 %collective-permute-start = (bf16[64,1152]{1,0:T(8,128)(2,1)}, bf16[64,1152]{1,0:T(8,128)(2,1)S(1)}, u32[]{:S(2)}, u32[]{:S(2)}) collective-permute-start(bf16[64,1152]{1,0:T(8,128)(2,1)} %get-tuple-element.19), channel_id=1, source_target_pairs={{0,32},{1,9},{2,34},{3,11},{4,36},{5,13},{6,38},{7,15},{128,160},{... | collective-permute-start | bytes 442376 | tf_op jit(solution)/shard_map/gA1/ppermute | solution.py:28
  12.0 7.2 %collective-permute-start.1 = (bf16[64,1152]{1,0:T(8,128)(2,1)}, bf16[64,1152]{1,0:T(8,128)(2,1)S(1)}, u32[]{:S(2)}, u32[]{:S(2)}) collective-permute-start(bf16[64,1152]{1,0:T(8,128)(2,1)} %get-tuple-element.19), channel_id=1, source_target_pairs={{0,64},{1,17},{2,66},{3,19},{4,68},{5,21},{6,70},{7,23},{128,192},... | collective-permute-start | bytes 442376 | tf_op jit(solution)/shard_map/gA2/ppermute | solution.py:28
  14.6 4.6 %collective-permute-start.2 = (bf16[64,1152]{1,0:T(8,128)(2,1)}, bf16[64,1152]{1,0:T(8,128)(2,1)S(1)}, u32[]{:S(2)}, u32[]{:S(2)}) collective-permute-start(bf16[64,1152]{1,0:T(8,128)(2,1)} %get-tuple-element.19), channel_id=1, source_target_pairs={{0,96},{1,25},{2,98},{3,27},{4,100},{5,29},{6,102},{7,31},{128,224... | collective-permute-start | bytes 442376 | tf_op jit(solution)/shard_map/gA3/ppermute | solution.py:28
  16.4 5.3 %copy-start.14 = (bf16[64,1152]{1,0:T(8,128)(2,1)S(1)}, bf16[64,1152]{1,0:T(8,128)(2,1)}, u32[]{:S(2)}) copy-start(bf16[64,1152]{1,0:T(8,128)(2,1)} %get-tuple-element.18) | copy-start | bytes 442372
  21.0 9.5 %collective-permute-start.5 = (bf16[128,1152]{1,0:T(8,128)(2,1)}, bf16[128,1152]{1,0:T(8,128)(2,1)S(1)}, u32[]{:S(2)}, u32[]{:S(2)}) collective-permute-start(bf16[128,1152]{1,0:T(8,128)(2,1)} %get-tuple-element.20), channel_id=1, source_target_pairs={{0,2},{1,135},{2,4},{3,1},{4,6},{5,3},{6,128},{7,5},{128,130},{129... | collective-permute-start | bytes 884744 | tf_op jit(solution)/shard_map/gZ2/ppermute | solution.py:28
  21.7 12.7 %collective-permute-start.6 = (bf16[128,1152]{1,0:T(8,128)(2,1)}, bf16[128,1152]{1,0:T(8,128)(2,1)S(1)}, u32[]{:S(2)}, u32[]{:S(2)}) collective-permute-start(bf16[128,1152]{1,0:T(8,128)(2,1)} %get-tuple-element.20), channel_id=1, source_target_pairs={{0,4},{1,133},{2,6},{3,135},{4,128},{5,1},{6,130},{7,3},{128,132},... | collective-permute-start | bytes 884744 | tf_op jit(solution)/shard_map/gZ3/ppermute | solution.py:28
  25.4 16.1 %collective-permute-start.10 = (bf16[256,1152]{1,0:T(8,128)(2,1)}, bf16[256,1152]{1,0:T(8,128)(2,1)S(1)}, u32[]{:S(2)}, u32[]{:S(2)}) collective-permute-start(bf16[256,1152]{1,0:T(8,128)(2,1)} %get-tuple-element.21.refs_2_), channel_id=1, source_target_pairs={{0,24},{1,97},{2,26},{3,99},{4,28},{5,101},{6,30},{7,103},{128,152... | collective-permute-start | bytes 1769480 | tf_op jit(solution)/shard_map/gB3/ppermute | solution.py:28
  28.0 16.8 %collective-permute-start.8 = (bf16[256,1152]{1,0:T(8,128)(2,1)}, bf16[256,1152]{1,0:T(8,128)(2,1)S(1)}, u32[]{:S(2)}, u32[]{:S(2)}) collective-permute-start(bf16[256,1152]{1,0:T(8,128)(2,1)} %get-tuple-element.21.refs_2_), channel_id=1, source_target_pairs={{0,8},{1,33},{2,10},{3,35},{4,12},{5,37},{6,14},{7,39},{128,136},{... | collective-permute-start | bytes 1769480 | tf_op jit(solution)/shard_map/gB1/ppermute | solution.py:28
  28.0 16.8 %collective-permute-start.9 = (bf16[256,1152]{1,0:T(8,128)(2,1)}, bf16[256,1152]{1,0:T(8,128)(2,1)S(1)}, u32[]{:S(2)}, u32[]{:S(2)}) collective-permute-start(bf16[256,1152]{1,0:T(8,128)(2,1)} %get-tuple-element.21.refs_2_), channel_id=1, source_target_pairs={{0,16},{1,65},{2,18},{3,67},{4,20},{5,69},{6,22},{7,71},{128,144},... | collective-permute-start | bytes 1769480 | tf_op jit(solution)/shard_map/gB2/ppermute | solution.py:28
  30.5 10.6 %collective-permute-start.7 = (bf16[64,1152]{1,0:T(8,128)(2,1)S(1)}, bf16[64,1152]{1,0:T(8,128)(2,1)S(1)}, u32[]{:S(2)}, u32[]{:S(2)}) collective-permute-start(bf16[64,1152]{1,0:T(8,128)(2,1)S(1)} %slice.50), channel_id=1, source_target_pairs={{0,6},{1,131},{2,128},{3,133},{4,130},{5,135},{6,132},{7,1},{128,1... | collective-permute-start | bytes 442376 | tf_op jit(solution)/shard_map/gZ4/ppermute | solution.py:28
  41.1 3.6 %copy-start.2 = (bf16[512,1152]{1,0:T(8,128)(2,1)}, bf16[512,1152]{1,0:T(8,128)(2,1)S(1)}, u32[]{:S(2)}) copy-start(bf16[512,1152]{1,0:T(8,128)(2,1)S(1)} %constant_dynamic-update-slice_fusion.refs_0_) | copy-start | bytes 3538948
  41.1 9.2 %copy-start.1 = (bf16[256,1152]{1,0:T(8,128)(2,1)S(1)}, bf16[256,1152]{1,0:T(8,128)(2,1)}, u32[]{:S(2)}) copy-start(bf16[256,1152]{1,0:T(8,128)(2,1)} %get-tuple-element.21.refs_2_) | copy-start | bytes 1769476
  41.4 3.3 %copy-start.5 = (bf16[256,1152]{1,0:T(8,128)(2,1)}, bf16[256,1152]{1,0:T(8,128)(2,1)S(1)}, u32[]{:S(2)}) copy-start(bf16[256,1152]{1,0:T(8,128)(2,1)S(1)} %collective-permute-done.10.refs_3_.refs_5_) | copy-start | bytes 1769476
  44.7 0.8 copy-start.7
  45.5 0.9 copy-start.9
  46.4 10.6 %collective-permute-start.11 = (bf16[512,1152]{1,0:T(8,128)(2,1)}, bf16[512,1152]{1,0:T(8,128)(2,1)S(1)}, u32[]{:S(2)}, u32[]{:S(2)}) collective-permute-start(bf16[512,1152]{1,0:T(8,128)(2,1)} %shard_map.62.refs_1_.txt1_ref), channel_id=1, source_target_pairs={{0,1},{1,0},{2,3},{3,2},{4,5},{5,4},{6,7},{7,6},{128,129},{129,128... | collective-permute-start | bytes 3538952 | tf_op jit(solution)/shard_map/gS/ppermute | solution.py:28
  50.3 1.3 %copy-start.3 = (bf16[512,1152]{1,0:T(8,128)(2,1)S(1)}, bf16[512,1152]{1,0:T(8,128)(2,1)}, u32[]{:S(2)}) copy-start(bf16[512,1152]{1,0:T(8,128)(2,1)} %shard_map.62.refs_1_.txt1_ref) | copy-start | bytes 3538948
  51.6 1.1 %copy-start.6 = (bf16[256,1152]{1,0:T(8,128)(2,1)S(1)}, bf16[256,1152]{1,0:T(8,128)(2,1)}, u32[]{:S(2)}) copy-start(bf16[256,1152]{1,0:T(8,128)(2,1)} %copy-done.5) | copy-start | bytes 1769476
  52.6 1.1 %copy-start.8 = (bf16[256,1152]{1,0:T(8,128)(2,1)S(1)}, bf16[256,1152]{1,0:T(8,128)(2,1)}, u32[]{:S(2)}) copy-start(bf16[256,1152]{1,0:T(8,128)(2,1)} %copy-done.7) | copy-start | bytes 1769476
  53.7 1.1 %copy-start.10 = (bf16[256,1152]{1,0:T(8,128)(2,1)S(1)}, bf16[256,1152]{1,0:T(8,128)(2,1)}, u32[]{:S(2)}) copy-start(bf16[256,1152]{1,0:T(8,128)(2,1)} %copy-done.9) | copy-start | bytes 1769476
  60.6 2.9 %collective-permute-start.12 = (bf16[512,1152]{1,0:T(8,128)(2,1)S(1)}, bf16[512,1152]{1,0:T(8,128)(2,1)S(1)}, u32[]{:S(2)}, u32[]{:S(2)}) collective-permute-start(bf16[512,1152]{1,0:T(8,128)(2,1)S(1)} %get-tuple-element.26), channel_id=1, source_target_pairs={{0,1},{1,0},{2,3},{3,2},{4,5},{5,4},{6,7},{7,6},{128,129},{129,128... | collective-permute-start | bytes 3538952 | tf_op jit(solution)/shard_map/rC/ppermute | solution.py:28
  63.8 10.4 %copy-start.11 = (f32[512,1152]{1,0:T(8,128)}, f32[512,1152]{1,0:T(8,128)S(1)}, u32[]{:S(2)}) copy-start(f32[512,1152]{1,0:T(8,128)S(1)} %get-tuple-element.37) | copy-start | bytes 7077892
  63.8 2.1 %copy-start.4 = (bf16[512,1152]{1,0:T(8,128)(2,1)S(1)}, bf16[512,1152]{1,0:T(8,128)(2,1)}, u32[]{:S(2)}) copy-start(bf16[512,1152]{1,0:T(8,128)(2,1)} %shard_map.62.refs_1_.txt1_ref) | copy-start | bytes 3538948
  64.6 8.7 %collective-permute-start.13 = (bf16[128,1152]{1,0:T(8,128)(2,1)S(1)}, bf16[128,1152]{1,0:T(8,128)(2,1)S(1)}, u32[]{:S(2)}, u32[]{:S(2)}) collective-permute-start(bf16[128,1152]{1,0:T(8,128)(2,1)S(1)} %get-tuple-element.39), channel_id=1, source_target_pairs={{0,134},{1,3},{2,0},{3,5},{4,2},{5,7},{6,4},{7,129},{128,6},{129,1... | collective-permute-start | bytes 884744 | tf_op jit(solution)/shard_map/rZ3/ppermute | solution.py:28
  68.8 10.9 %copy-start = (f32[256,1152]{1,0:T(8,128)}, f32[256,1152]{1,0:T(8,128)S(1)}, u32[]{:S(2)}) copy-start(f32[256,1152]{1,0:T(8,128)S(1)} %get-tuple-element.25.refs_0_) | copy-start | bytes 3538948
  68.8 15.6 %collective-permute-start.15 = (bf16[256,1152]{1,0:T(8,128)(2,1)S(1)}, bf16[256,1152]{1,0:T(8,128)(2,1)S(1)}, u32[]{:S(2)}, u32[]{:S(2)}) collective-permute-start(bf16[256,1152]{1,0:T(8,128)(2,1)S(1)} %get-tuple-element.27), channel_id=1, source_target_pairs={{0,24},{1,97},{2,26},{3,99},{4,28},{5,101},{6,30},{7,103},{128,152... | collective-permute-start | bytes 1769480 | tf_op jit(solution)/shard_map/rB1/ppermute | solution.py:28
  71.3 13.2 %collective-permute-start.16 = (bf16[256,1152]{1,0:T(8,128)(2,1)S(1)}, bf16[256,1152]{1,0:T(8,128)(2,1)S(1)}, u32[]{:S(2)}, u32[]{:S(2)}) collective-permute-start(bf16[256,1152]{1,0:T(8,128)(2,1)S(1)} %get-tuple-element.28), channel_id=1, source_target_pairs={{0,16},{1,65},{2,18},{3,67},{4,20},{5,69},{6,22},{7,71},{128,144},... | collective-permute-start | bytes 1769480 | tf_op jit(solution)/shard_map/rB2/ppermute | solution.py:28
  71.9 16.2 %collective-permute-start.17 = (bf16[256,1152]{1,0:T(8,128)(2,1)S(1)}, bf16[256,1152]{1,0:T(8,128)(2,1)S(1)}, u32[]{:S(2)}, u32[]{:S(2)}) collective-permute-start(bf16[256,1152]{1,0:T(8,128)(2,1)S(1)} %get-tuple-element.29), channel_id=1, source_target_pairs={{0,8},{1,33},{2,10},{3,35},{4,12},{5,37},{6,14},{7,39},{128,136},{... | collective-permute-start | bytes 1769480 | tf_op jit(solution)/shard_map/rB3/ppermute | solution.py:28
  72.0 7.7 %collective-permute-start.14 = (bf16[64,1152]{1,0:T(8,128)(2,1)S(1)}, bf16[64,1152]{1,0:T(8,128)(2,1)S(1)}, u32[]{:S(2)}, u32[]{:S(2)}) collective-permute-start(bf16[64,1152]{1,0:T(8,128)(2,1)S(1)} %slice.69), channel_id=1, source_target_pairs={{0,132},{1,5},{2,134},{3,7},{4,0},{5,129},{6,2},{7,131},{128,4},{1... | collective-permute-start | bytes 442376 | tf_op jit(solution)/shard_map/rZ4/ppermute | solution.py:28
  73.3 24.1 %collective-permute-start.21 = (bf16[128,1152]{1,0:T(8,128)(2,1)}, bf16[128,1152]{1,0:T(8,128)(2,1)}, u32[]{:S(2)}, u32[]{:S(2)}) collective-permute-start(bf16[128,1152]{1,0:T(8,128)(2,1)} %get-tuple-element.38), channel_id=1, source_target_pairs={{0,134},{1,3},{2,0},{3,5},{4,2},{5,7},{6,4},{7,129},{128,6},{129,1... | collective-permute-start | bytes 884744 | tf_op jit(solution)/shard_map/rZ1/ppermute | solution.py:28
  80.5 16.9 %collective-permute-start.22 = (bf16[128,1152]{1,0:T(8,128)(2,1)}, bf16[128,1152]{1,0:T(8,128)(2,1)}, u32[]{:S(2)}, u32[]{:S(2)}) collective-permute-start(bf16[128,1152]{1,0:T(8,128)(2,1)} %pad_maximum_fusion.2.value_ref), channel_id=1, source_target_pairs={{0,132},{1,5},{2,134},{3,7},{4,0},{5,129},{6,2},{7,131},{128,4},{1... | collective-permute-start | bytes 884744 | tf_op jit(solution)/shard_map/rZ2/ppermute | solution.py:28
  81.1 10.1 %copy-start.15 = (f32[64,128]{1,0:T(8,128)S(1)}, f32[64,128]{1,0:T(8,128)}, u32[]{:S(2)}) copy-start(f32[64,128]{1,0:T(8,128)} %get-tuple-element.33) | copy-start | bytes 98308
  81.1 10.2 %copy-start.16 = (f32[64,128]{1,0:T(8,128)S(1)}, f32[64,128]{1,0:T(8,128)}, u32[]{:S(2)}) copy-start(f32[64,128]{1,0:T(8,128)} %get-tuple-element.31) | copy-start | bytes 98308
  81.1 16.1 %copy-start.13 = (f32[64,1152]{1,0:T(8,128)S(1)}, f32[64,1152]{1,0:T(8,128)}, u32[]{:S(2)}) copy-start(f32[64,1152]{1,0:T(8,128)} %get-tuple-element.30) | copy-start | bytes 884740
  89.6 4.1 %collective-permute-start.18 = (bf16[64,1152]{1,0:T(8,128)(2,1)S(1)}, bf16[64,1152]{1,0:T(8,128)(2,1)S(1)}, u32[]{:S(2)}, u32[]{:S(2)}) collective-permute-start(bf16[64,1152]{1,0:T(8,128)(2,1)S(1)} %get-tuple-element.40), channel_id=1, source_target_pairs={{0,96},{1,25},{2,98},{3,27},{4,100},{5,29},{6,102},{7,31},{128,224... | collective-permute-start | bytes 442376 | tf_op jit(solution)/shard_map/rA1/ppermute | solution.py:28
  89.7 5.7 %collective-permute-start.19 = (bf16[64,1152]{1,0:T(8,128)(2,1)S(1)}, bf16[64,1152]{1,0:T(8,128)(2,1)S(1)}, u32[]{:S(2)}, u32[]{:S(2)}) collective-permute-start(bf16[64,1152]{1,0:T(8,128)(2,1)S(1)} %get-tuple-element.42), channel_id=1, source_target_pairs={{0,64},{1,17},{2,66},{3,19},{4,68},{5,21},{6,70},{7,23},{128,192},... | collective-permute-start | bytes 442376 | tf_op jit(solution)/shard_map/rA2/ppermute | solution.py:28
  90.0 7.2 %collective-permute-start.20 = (bf16[64,1152]{1,0:T(8,128)(2,1)S(1)}, bf16[64,1152]{1,0:T(8,128)(2,1)S(1)}, u32[]{:S(2)}, u32[]{:S(2)}) collective-permute-start(bf16[64,1152]{1,0:T(8,128)(2,1)S(1)} %get-tuple-element.41), channel_id=1, source_target_pairs={{0,32},{1,9},{2,34},{3,11},{4,36},{5,13},{6,38},{7,15},{128,160},{... | collective-permute-start | bytes 442376 | tf_op jit(solution)/shard_map/rA3/ppermute | solution.py:28
  97.4 4.6 %copy-start.12 = (f32[64,1152]{1,0:T(8,128)S(1)}, f32[64,1152]{1,0:T(8,128)}, u32[]{:S(2)}) copy-start(f32[64,1152]{1,0:T(8,128)} %get-tuple-element.32) | copy-start | bytes 884740
  98.6 3.4 %collective-permute-start.23 = (bf16[64,1152]{1,0:T(8,128)(2,1)S(1)}, bf16[64,1152]{1,0:T(8,128)(2,1)S(1)}, u32[]{:S(2)}, u32[]{:S(2)}) collective-permute-start(bf16[64,1152]{1,0:T(8,128)(2,1)S(1)} %slice.104), channel_id=1, source_target_pairs={{0,1},{1,0},{2,3},{3,2},{4,5},{5,4},{6,7},{7,6},{128,129},{129,128... | collective-permute-start | bytes 442376 | tf_op jit(solution)/shard_map/rS/ppermute | solution.py:28

commit v4 on v3

v4 whole, which is shorter than its diff:
```python
import jax
import jax.numpy as jnp
from jax import lax
from jax.experimental import pallas as pl
from jax.experimental.pallas import tpu as pltpu
from jax.sharding import PartitionSpec as P

AXES = ("row", "col")
F32 = jnp.float32
BF16 = jnp.bfloat16
LOG2E = 1.4426950408889634
SIZE_X, SIZE_Y, SIZE_Z, CORES = 4, 4, 8, 2


def device(x, y, z, c):
    return ((z // 4) * 16 + x * 4 + y) * 8 + (z % 4) * 2 + c


def shift(values, move, name="move"):
    pairs = []
    for x in range(SIZE_X):
        for y in range(SIZE_Y):
            for z in range(SIZE_Z):
                for c in range(CORES):
                    nx, ny, nz, nc = move(x, y, z, c)
                    pairs.append((device(x, y, z, c), device(nx % SIZE_X, ny % SIZE_Y, nz % SIZE_Z, nc)))
    with jax.named_scope(name):
        return lax.ppermute(values, AXES, pairs)


def first(k):
    return lambda x, y, z, c: (x + k, y, z, c) if c == 0 else (x, y + k, z, c)


def second(k):
    return lambda x, y, z, c: (x, y + k, z, c) if c == 0 else (x + k, y, z, c)


def line(k):
    return lambda x, y, z, c: (x, y, z + k, c) if c == 0 else (x, y, z - k, c)


def cross(k):
    return lambda x, y, z, c: (x, y, z + k, 0) if c == 1 else (x, y, z - k, 1)


def other(x, y, z, c):
    return (x, y, z, 1 - c)


def call(kernel, outs, arrays, scalars=None, ties=(), flops=0, limit=8):
    vmem = pl.BlockSpec(memory_space=pltpu.VMEM)
    few = [] if scalars is None else [scalars]
    n_in = len(few) + len(arrays)
    specs = [pl.BlockSpec(memory_space=pltpu.SMEM)] * len(few) + [vmem] * len(arrays)
    return pl.pallas_call(
        lambda *refs: kernel(*refs[:n_in], *refs[n_in + len(ties):]),
        out_shape=tuple(jax.ShapeDtypeStruct(shape, dtype) for shape, dtype in outs),
        in_specs=specs + [pl.BlockSpec(memory_space=pl.ANY)] * len(ties),
        out_specs=tuple([vmem] * len(outs)),
        compiler_params=pltpu.CompilerParams(vmem_limit_bytes=limit * 1024 * 1024),
        cost_estimate=pl.CostEstimate(flops=flops, bytes_accessed=1024, transcendentals=0),
    )(*few, *arrays, *ties)


def token_kernel(token_ref):
    token_ref[...] = jnp.zeros_like(token_ref)


def token(value):
    return call(token_kernel, [((8, 128), F32)], [], ties=[value], flops=40_000_000_000, limit=1)[0]


def unit_rows(raw):
    values = raw.astype(F32)
    inverse = lax.rsqrt(jnp.sum(values * values, axis=1, keepdims=True) + 1e-06)
    return values * inverse, inverse


def back_norm(unit, inverse, grad_unit):
    along = jnp.sum(unit * grad_unit, axis=1, keepdims=True)
    return (grad_unit - unit * along) * inverse


def pair_kernel(first_ref, second_ref, out_ref):
    rows = first_ref.shape[0]
    out_ref[:rows, :] = first_ref[...]
    out_ref[rows:, :] = second_ref[...]


def group_kernel(*refs):
    *parts, pair_ref, near_ref, group_ref, send_ref, head_ref = refs
    rows = parts[0].shape[0]
    for n, part in enumerate(parts):
        group_ref[n * rows:(n + 1) * rows, :] = part[...]
    send_ref[:2 * rows, :] = pair_ref[...]
    send_ref[2 * rows:, :] = near_ref[...]
    head_ref[...] = near_ref[:rows, :]


def round_kernel(own, *refs):
    *parts, out_ref, unit_ref, inv_ref = refs
    base = 0
    for part in parts:
        for at in range(0, part.shape[0], own):
            unit, inverse = unit_rows(part[at:at + own, :])
            out_ref[base:base + own, :] = unit.astype(BF16)
            if base == 0:
                unit_ref[...] = unit
                inv_ref[...] = jnp.broadcast_to(inverse, inv_ref.shape)
            base += own


def rounded(parts, own, ties=()):
    rows, dim = sum(p.shape[0] for p in parts), parts[0].shape[1]
    outs = [((rows, dim), BF16), ((own, dim), F32), ((own, 128), F32)]
    return call(lambda *refs: round_kernel(own, *refs), outs, parts, ties=ties)


def sigmoid_weights(power, scale):
    return (scale / (1.0 + jnp.exp2(power))).astype(BF16)


def powers(img, txt, scal_ref):
    slope, offset = -scal_ref[0] * LOG2E, -scal_ref[1] * LOG2E
    dots = lax.dot_general(img, txt, (((1,), (1,)), ((), ())), preferred_element_type=F32)
    return dots * slope + offset


def text_grads(w_ref, img_ref, out_ref):
    step = 256
    for t in range(0, out_ref.shape[0], step):
        grad = lax.dot_general(
            w_ref[:, t:t + step], img_ref[...], (((0,), (0,)), ((), ())), preferred_element_type=F32
        )
        out_ref[t:t + step, :] = grad.astype(out_ref.dtype)


def mine_kernel(own, scal_ref, txt_ref, *refs):
    *parts, w_ref, img_ref, keep_ref = refs
    temp = scal_ref[0]
    at = 0
    for part in parts:
        rows = part.shape[0]
        img = part[...] if at == 0 else unit_rows(part[...])[0].astype(BF16)
        img_ref[at:at + rows, :] = img
        power = powers(img, txt_ref[...], scal_ref)
        w_ref[at:at + rows, :] = sigmoid_weights(power, temp)
        if at == 0:
            corner = power[:own, :2 * own]
            row = lax.broadcasted_iota(jnp.int32, corner.shape, 0)
            column = lax.broadcasted_iota(jnp.int32, corner.shape, 1)
            positive = row == column
            signed = jnp.where(positive, -corner, corner)
            w_ref[:own, :2 * own] = sigmoid_weights(signed, jnp.where(positive, -temp, temp))
        at += rows
    text_grads(w_ref, img_ref, keep_ref)


def theirs_kernel(scal_ref, txt_ref, img_ref, w_ref, send_ref):
    step = 256
    for at in range(0, img_ref.shape[0], step):
        power = powers(img_ref[at:at + step, :], txt_ref[...], scal_ref)
        w_ref[at:at + step, :] = sigmoid_weights(power, scal_ref[0])
    text_grads(w_ref, img_ref, send_ref)


def image_kernel(w1_ref, w2_ref, txt1_ref, txt2_ref, *outs):
    at = 0
    for out in outs:
        rows = out.shape[0]
        grad = jnp.dot(w1_ref[at:at + rows, :], txt1_ref[...], preferred_element_type=F32)
        grad += jnp.dot(w2_ref[at:at + rows, :], txt2_ref[...], preferred_element_type=F32)
        out[...] = grad.astype(out.dtype)
        at += rows


def total_kernel(keep_ref, got_ref, own_ref, part13_ref, part2_ref, part4_ref):
    at = 0
    for out in (own_ref, part13_ref, part2_ref, part4_ref):
        rows = out.shape[0]
        total = keep_ref[at:at + rows, :].astype(F32) + got_ref[at:at + rows, :].astype(F32)
        out[...] = total.astype(out.dtype)
        at += rows


def middle_kernel(part2_ref, got13_ref, got4_ref, out_ref):
    rows = got4_ref.shape[0]
    total = part2_ref[...] + got13_ref[2 * rows:, :].astype(F32)
    out_ref[:rows, :] = (total[:rows] + got4_ref[...].astype(F32)).astype(BF16)
    out_ref[rows:, :] = total[rows:].astype(BF16)


def landed_kernel(own_ref, got13_ref, got2_ref, sum_ref, send_ref):
    rows = own_ref.shape[0]
    sum_ref[...] = own_ref[...] + got13_ref[:rows, :].astype(F32) + got2_ref[:rows, :].astype(F32)
    send_ref[...] = (got13_ref[rows:2 * rows, :].astype(F32) + got2_ref[rows:, :].astype(F32)).astype(BF16)


def sums_kernel(*refs):
    own_ref, *parts = refs[:4]
    outs = refs[4:]
    rows = outs[0].shape[0]
    for n, out in enumerate(outs):
        at = slice(n * rows, (n + 1) * rows)
        out[...] = (own_ref[at, :] + sum(p[at, :].astype(F32) for p in parts)).astype(out.dtype)


def final_kernel(unit_ref, inv_ref, own_ref, *refs):
    *parts, out_ref = refs
    grad = own_ref[...] + sum(p[...].astype(F32) for p in parts)
    out_ref[...] = back_norm(unit_ref[...], inv_ref[:, :1], grad)


def local(images, texts, log_temp, bias):
    own, dim = images.shape
    scalars = jnp.concatenate([jnp.exp(log_temp), bias])

    (pair,) = call(pair_kernel, [((2 * own, dim), BF16)], [texts, shift(texts, other, "gC")])
    side = [shift(images, first(k), "gA%d" % k) for k in (1, 2, 3)]
    near2 = shift(pair, line(2), "gZ2")
    group, send13, send4 = call(
        group_kernel, [((4 * own, dim), BF16), ((4 * own, dim), BF16), ((own, dim), BF16)], [images, *side, pair, near2]
    )
    far = [shift(group, second(k), "gB%d" % k) for k in (1, 2, 3)]
    near13 = shift(send13, line(1), "gZ13")
    near4 = shift(send4, line(2), "gZ4")
    first_token = token(group)
    group, img_unit, inv_img = rounded([group], own)
    mine, txt_unit, inv_txt = rounded([texts, near13, near2, near4], own, [group, first_token, *far])
    theirs = shift(mine, other, "gS")

    half = mine.shape[0]
    rows = group.shape[0] * (1 + len(far))
    flops = 2 * rows * half * dim
    w_mine, img_all, keep = call(
        lambda *refs: mine_kernel(own, *refs), [((rows, half), BF16), ((rows, dim), BF16), ((half, dim), BF16)],
        [mine, group, *far], scalars, flops=2 * flops, limit=24,
    )
    w_theirs, send = call(
        theirs_kernel, [((rows, half), BF16), ((half, dim), BF16)],
        [theirs, img_all], scalars, ties=[keep], flops=2 * flops, limit=24,
    )
    grads = call(
        image_kernel, [(group.shape, F32)] + [(group.shape, BF16)] * len(far),
        [w_mine, w_theirs, mine, theirs], flops=2 * flops, limit=24,
    )

    total_own, part13, part2, part4 = call(
        total_kernel,
        [((own, dim), F32), ((4 * own, dim), BF16), ((2 * own, dim), F32), ((own, dim), BF16)],
        [keep, shift(send, other, "rC")], ties=[grads[-1]],
    )
    got13 = shift(part13, line(-1), "rZ13")
    got4 = shift(part4, line(-2), "rZ4")
    (middle,) = call(middle_kernel, [((2 * own, dim), BF16)], [part2, got13, got4])
    got2 = shift(middle, line(-2), "rZ2")
    txt_sum, txt_send = call(landed_kernel, [((own, dim), F32), ((own, dim), BF16)], [total_own, got13, got2])
    txt_last = shift(txt_send, other, "rS")

    back = [shift(g, second(-k), "rB%d" % k) for k, g in zip((1, 2, 3), grads[1:])]
    img_sum, *parts = call(
        sums_kernel, [((own, dim), F32)] + [((own, dim), BF16)] * 3, [grads[0], *back], ties=[token(middle)]
    )
    last = [shift(p, first(-k), "rA%d" % k) for k, p in zip((1, 2, 3), parts)]

    (grad_img,) = call(final_kernel, [((own, dim), F32)], [img_unit, inv_img, img_sum, *last])
    (grad_txt,) = call(final_kernel, [((own, dim), F32)], [txt_unit, inv_txt, txt_sum, txt_last])
    return grad_img, grad_txt


def solution(mesh):
    in_specs = (P(("row", "col"), None), P(("row", "col"), None), P(), P())
    out_specs = (P(("row", "col"), None), P(("row", "col"), None))
    return jax.shard_map(local, mesh=mesh, in_specs=in_specs, out_specs=out_specs, check_vma=False)
```

time: 105 us -> 87.9 us (0.84)
  the two profiles are of different devices: /device:TPU:1 before, /device:TPU:24 now
where the time goes in v4:
time: 87.9 us; the launch traced here: 87.8 us
  starting transfers between devices  36.2 us (41%)
  waiting for transfers between devices  34.1 us (39%)
  Pallas kernels  13.5 us (15%)
  between operations  2.09 us (2%)
  local copies, waits for them, and re-layouts  1.82 us (2%)
    ppermute x22, starting transfers between devices, shift(): return lax.ppermute(values, AXES, pairs)  36.2 us
    ppermute x22, waiting for transfers between devices, shift(): return lax.ppermute(values, AXES, pairs)  34.1 us
    pallas_call x15, Pallas kernels, call(): pl.pallas_call(lambda *refs: kernel(*refs[:n_in], *refs[n_in + len(ties):...  13.5 us
    unnamed x4, local copies, waits for them, and re-layouts  1.82 us
  transfers between devices with their start and end apart: 22, of which 10 were waited for; matrix products, arithmetic and copies ran while one was open for 0% of the time, Pallas kernels for 10%

profile of v4, /device:TPU:24, one launch (start us, length us, event | category | flops | bytes accessed | tf_op | source)
XLA Modules:
  0.0 87.8 jit_solution(3065674988486466228)
XLA Ops:
  0.6 0.1 collective-permute-start.3
  0.7 1.6 %collective-permute-done.3.refs_1_ = bf16[64,1152]{1,0:T(8,128)(2,1)S(1)} collective-permute-done((bf16[64,1152]{1,0:T(8,128)(2,1)}, bf16[64,1152]{1,0:T(8,128)(2,1)S(1)}, u32[]{:S(2)}, u32[]{:S(2)}) %collective-permute-start.3) | collective-permute-done | bytes 147488 | tf_op jit(solution)/shard_map/gC/ppermute | solution.py:28
  2.3 0.0 copy-start
  2.3 0.9 %copy-done = bf16[64,1152]{1,0:T(8,128)(2,1)S(1)} copy-done((bf16[64,1152]{1,0:T(8,128)(2,1)S(1)}, bf16[64,1152]{1,0:T(8,128)(2,1)}, u32[]{:S(2)}) %copy-start) | copy-done | bytes 147480
  3.2 3.3 %collective-permute-start.4 = (bf16[128,1152]{1,0:T(8,128)(2,1)S(1)}, bf16[128,1152]{1,0:T(8,128)(2,1)S(1)}, u32[]{:S(2)}, u32[]{:S(2)}) collective-permute-start(bf16[128,1152]{1,0:T(8,128)(2,1)S(1)} %shard_map.59.refs_4_), channel_id=1, source_target_pairs={{0,4},{1,133},{2,6},{3,135},{4,128},{5,1},{6,130},{7,3},{128,132},... | collective-permute-start | bytes 884744 | tf_op jit(solution)/shard_map/gZ2/ppermute | solution.py:28
  6.6 3.0 %collective-permute-start.1 = (bf16[64,1152]{1,0:T(8,128)(2,1)}, bf16[64,1152]{1,0:T(8,128)(2,1)S(1)}, u32[]{:S(2)}, u32[]{:S(2)}) collective-permute-start(bf16[64,1152]{1,0:T(8,128)(2,1)} %refs_0_.4), channel_id=1, source_target_pairs={{0,64},{1,17},{2,66},{3,19},{4,68},{5,21},{6,70},{7,23},{128,192},... | collective-permute-start | bytes 442376 | tf_op jit(solution)/shard_map/gA2/ppermute | solution.py:28
  9.6 0.6 collective-permute-start
  10.2 2.6 %collective-permute-start.2 = (bf16[64,1152]{1,0:T(8,128)(2,1)}, bf16[64,1152]{1,0:T(8,128)(2,1)S(1)}, u32[]{:S(2)}, u32[]{:S(2)}) collective-permute-start(bf16[64,1152]{1,0:T(8,128)(2,1)} %refs_0_.4), channel_id=1, source_target_pairs={{0,96},{1,25},{2,98},{3,27},{4,100},{5,29},{6,102},{7,31},{128,224... | collective-permute-start | bytes 442376 | tf_op jit(solution)/shard_map/gA3/ppermute | solution.py:28
  12.8 0.6 collective-permute-done.1.refs_2_
  13.4 2.7 %collective-permute-done.refs_1_ = bf16[64,1152]{1,0:T(8,128)(2,1)S(1)} collective-permute-done((bf16[64,1152]{1,0:T(8,128)(2,1)}, bf16[64,1152]{1,0:T(8,128)(2,1)S(1)}, u32[]{:S(2)}, u32[]{:S(2)}) %collective-permute-start) | collective-permute-done | bytes 147488 | tf_op jit(solution)/shard_map/gA1/ppermute | solution.py:28
  16.2 0.0 collective-permute-done.2.refs_3_
  16.2 0.0 collective-permute-done.4.refs_5_.refs_2_
  16.2 0.0 copy-start.1
  16.2 0.9 %copy-done.1 = bf16[64,1152]{1,0:T(8,128)(2,1)S(1)} copy-done((bf16[64,1152]{1,0:T(8,128)(2,1)S(1)}, bf16[64,1152]{1,0:T(8,128)(2,1)}, u32[]{:S(2)}) %copy-start.1) | copy-done | bytes 147480
  17.1 0.1 shard_map.60
  17.2 0.8 collective-permute-start.9
  18.0 0.9 %collective-permute-start.8 = (bf16[256,1152]{1,0:T(8,128)(2,1)S(1)}, bf16[256,1152]{1,0:T(8,128)(2,1)S(1)}, u32[]{:S(2)}, u32[]{:S(2)}) collective-permute-start(bf16[256,1152]{1,0:T(8,128)(2,1)S(1)} %get-tuple-element.30.refs_0_), channel_id=1, source_target_pairs={{0,16},{1,65},{2,18},{3,67},{4,20},{5,69},{6,22},{7,71},{128,144},... | collective-permute-start | bytes 1769480 | tf_op jit(solution)/shard_map/gB2/ppermute | solution.py:28
  19.0 2.2 %collective-permute-start.7 = (bf16[256,1152]{1,0:T(8,128)(2,1)S(1)}, bf16[256,1152]{1,0:T(8,128)(2,1)S(1)}, u32[]{:S(2)}, u32[]{:S(2)}) collective-permute-start(bf16[256,1152]{1,0:T(8,128)(2,1)S(1)} %get-tuple-element.30.refs_0_), channel_id=1, source_target_pairs={{0,8},{1,33},{2,10},{3,35},{4,12},{5,37},{6,14},{7,39},{128,136},{... | collective-permute-start | bytes 1769480 | tf_op jit(solution)/shard_map/gB1/ppermute | solution.py:28
  21.1 4.5 %collective-permute-start.6 = (bf16[64,1152]{1,0:T(8,128)(2,1)S(1)}, bf16[64,1152]{1,0:T(8,128)(2,1)S(1)}, u32[]{:S(2)}, u32[]{:S(2)}) collective-permute-start(bf16[64,1152]{1,0:T(8,128)(2,1)S(1)} %get-tuple-element.34), channel_id=1, source_target_pairs={{0,4},{1,133},{2,6},{3,135},{4,128},{5,1},{6,130},{7,3},{128,132},... | collective-permute-start | bytes 442376 | tf_op jit(solution)/shard_map/gZ4/ppermute | solution.py:28
  25.6 1.0 %collective-permute-start.5 = (bf16[256,1152]{1,0:T(8,128)(2,1)S(1)}, bf16[256,1152]{1,0:T(8,128)(2,1)S(1)}, u32[]{:S(2)}, u32[]{:S(2)}) collective-permute-start(bf16[256,1152]{1,0:T(8,128)(2,1)S(1)} %get-tuple-element.33), channel_id=1, source_target_pairs={{0,2},{1,135},{2,4},{3,1},{4,6},{5,3},{6,128},{7,5},{128,130},{129... | collective-permute-start | bytes 1769480 | tf_op jit(solution)/shard_map/gZ13/ppermute | solution.py:28
  26.6 0.2 shard_map.61
  26.9 3.0 %collective-permute-done.6.refs_3_ = bf16[64,1152]{1,0:T(8,128)(2,1)S(1)} collective-permute-done((bf16[64,1152]{1,0:T(8,128)(2,1)S(1)}, bf16[64,1152]{1,0:T(8,128)(2,1)S(1)}, u32[]{:S(2)}, u32[]{:S(2)}) %collective-permute-start.6) | collective-permute-done | bytes 147488 | tf_op jit(solution)/shard_map/gZ4/ppermute | solution.py:28
  29.9 6.9 %collective-permute-done.5.refs_1_ = bf16[256,1152]{1,0:T(8,128)(2,1)S(1)} collective-permute-done((bf16[256,1152]{1,0:T(8,128)(2,1)S(1)}, bf16[256,1152]{1,0:T(8,128)(2,1)S(1)}, u32[]{:S(2)}, u32[]{:S(2)}) %collective-permute-start.5) | collective-permute-done | bytes 589856 | tf_op jit(solution)/shard_map/gZ13/ppermute | solution.py:28
  36.7 0.0 collective-permute-done.9.refs_8_.refs_5_
  36.7 0.0 collective-permute-done.8.refs_7_.refs_4_
  36.7 0.0 collective-permute-done.7.refs_6_.refs_3_
  36.7 0.4 shard_map.63
  37.1 1.4 %collective-permute-start.10 = (bf16[512,1152]{1,0:T(8,128)(2,1)S(1)}, bf16[512,1152]{1,0:T(8,128)(2,1)S(1)}, u32[]{:S(2)}, u32[]{:S(2)}) collective-permute-start(bf16[512,1152]{1,0:T(8,128)(2,1)S(1)} %get-tuple-element.36.refs_1_.refs_2_), channel_id=1, source_target_pairs={{0,1},{1,0},{2,3},{3,2},{4,5},{5,4},{6,7},{7,6},{128,129},{129,128... | collective-permute-start | bytes 3538952 | tf_op jit(solution)/shard_map/gS/ppermute | solution.py:28
  39.9 0.1 pad_maximum_fusion.refs_0_
  39.9 3.9 %shard_map.64 = (bf16[1024,512]{1,0:T(8,128)(2,1)S(1)}, bf16[1024,1152]{1,0:T(8,128)(2,1)S(1)}, bf16[512,1152]{1,0:T(8,128)(2,1)S(1)}) custom-call(f32[2]{0:T(128)S(1)} %pad_maximum_fusion.refs_0_, bf16[512,1152]{1,0:T(8,128)(2,1)S(1)} %get-tuple-element.36.refs_1_.refs_2_, bf16[256,1152]{1,0:T(8,128)(2,1)S(1)} %get-tuple-element.35.refs_4_.refs_2_, ...), custom_call_target="tpu_custom_call" | custom-call | flops 2415919104 | bytes 1024 | tf_op jit(solution)/shard_map/pallas_call | solution.py:56
  43.9 0.0 collective-permute-done.10.refs_1_.refs_3_
  43.9 3.5 %shard_map.65 = (bf16[1024,512]{1,0:T(8,128)(2,1)S(1)}, bf16[512,1152]{1,0:T(8,128)(2,1)S(1)}) custom-call(f32[2]{0:T(128)S(1)} %pad_maximum_fusion.refs_0_, bf16[512,1152]{1,0:T(8,128)(2,1)S(1)} %collective-permute-done.10.refs_1_.refs_3_, bf16[1024,1152]{1,0:T(8,128)(2,1)S(1)} %get-tuple-element.38.refs_2_, ...), custom_call_target="tpu_custom_call" | custom-call | flops 2415919104 | bytes 1024 | tf_op jit(solution)/shard_map/pallas_call | solution.py:56
  47.4 0.1 collective-permute-start.14
  47.5 2.9 %shard_map.66 = (f32[256,1152]{1,0:T(8,128)S(1)}, bf16[256,1152]{1,0:T(8,128)(2,1)S(1)}, bf16[256,1152]{1,0:T(8,128)(2,1)S(1)}, bf16[256,1152]{1,0:T(8,128)(2,1)S(1)}) custom-call(bf16[1024,512]{1,0:T(8,128)(2,1)S(1)} %get-tuple-element.37.refs_0_, bf16[1024,512]{1,0:T(8,128)(2,1)S(1)} %get-tuple-element.40.refs_1_, ...), custom_call_target="tpu_custom_call" | custom-call | flops 2415919104 | bytes 1024 | tf_op jit(solution)/shard_map/pallas_call | solution.py:56
  50.4 0.0 collective-permute-done.14.refs_1_
  50.4 0.3 shard_map.67
  50.7 1.7 %collective-permute-start.15 = (bf16[256,1152]{1,0:T(8,128)(2,1)S(1)}, bf16[256,1152]{1,0:T(8,128)(2,1)S(1)}, u32[]{:S(2)}, u32[]{:S(2)}) collective-permute-start(bf16[256,1152]{1,0:T(8,128)(2,1)S(1)} %get-tuple-element.47), channel_id=1, source_target_pairs={{0,134},{1,3},{2,0},{3,5},{4,2},{5,7},{6,4},{7,129},{128,6},{129,1... | collective-permute-start | bytes 1769480 | tf_op jit(solution)/shard_map/rZ13/ppermute | solution.py:28
  52.4 2.1 %collective-permute-start.16 = (bf16[64,1152]{1,0:T(8,128)(2,1)S(1)}, bf16[64,1152]{1,0:T(8,128)(2,1)S(1)}, u32[]{:S(2)}, u32[]{:S(2)}) collective-permute-start(bf16[64,1152]{1,0:T(8,128)(2,1)S(1)} %get-tuple-element.48), channel_id=1, source_target_pairs={{0,132},{1,5},{2,134},{3,7},{4,0},{5,129},{6,2},{7,131},{128,4},{1... | collective-permute-start | bytes 442376 | tf_op jit(solution)/shard_map/rZ4/ppermute | solution.py:28
  54.5 2.6 %collective-permute-start.13 = (bf16[256,1152]{1,0:T(8,128)(2,1)S(1)}, bf16[256,1152]{1,0:T(8,128)(2,1)S(1)}, u32[]{:S(2)}, u32[]{:S(2)}) collective-permute-start(bf16[256,1152]{1,0:T(8,128)(2,1)S(1)} %get-tuple-element.44.refs_2_), channel_id=1, source_target_pairs={{0,8},{1,33},{2,10},{3,35},{4,12},{5,37},{6,14},{7,39},{128,136},{... | collective-permute-start | bytes 1769480 | tf_op jit(solution)/shard_map/rB3/ppermute | solution.py:28
  57.1 0.0 collective-permute-start.11
  57.1 1.5 %collective-permute-start.12 = (bf16[256,1152]{1,0:T(8,128)(2,1)S(1)}, bf16[256,1152]{1,0:T(8,128)(2,1)S(1)}, u32[]{:S(2)}, u32[]{:S(2)}) collective-permute-start(bf16[256,1152]{1,0:T(8,128)(2,1)S(1)} %get-tuple-element.43), channel_id=1, source_target_pairs={{0,16},{1,65},{2,18},{3,67},{4,20},{5,69},{6,22},{7,71},{128,144},... | collective-permute-start | bytes 1769480 | tf_op jit(solution)/shard_map/rB2/ppermute | solution.py:28
  58.6 6.0 %collective-permute-done.16.refs_2_ = bf16[64,1152]{1,0:T(8,128)(2,1)S(1)} collective-permute-done((bf16[64,1152]{1,0:T(8,128)(2,1)S(1)}, bf16[64,1152]{1,0:T(8,128)(2,1)S(1)}, u32[]{:S(2)}, u32[]{:S(2)}) %collective-permute-start.16) | collective-permute-done | bytes 147488 | tf_op jit(solution)/shard_map/rZ4/ppermute | solution.py:28
  64.6 0.0 collective-permute-done.15.refs_1_
  64.6 0.1 shard_map.68.refs_0_
  64.7 3.3 %collective-permute-start.20 = (bf16[128,1152]{1,0:T(8,128)(2,1)S(1)}, bf16[128,1152]{1,0:T(8,128)(2,1)S(1)}, u32[]{:S(2)}, u32[]{:S(2)}) collective-permute-start(bf16[128,1152]{1,0:T(8,128)(2,1)S(1)} %shard_map.68.refs_0_), channel_id=1, source_target_pairs={{0,132},{1,5},{2,134},{3,7},{4,0},{5,129},{6,2},{7,131},{128,4},{1... | collective-permute-start | bytes 884744 | tf_op jit(solution)/shard_map/rZ2/ppermute | solution.py:28
  68.0 6.6 %collective-permute-done.11.refs_1_ = bf16[256,1152]{1,0:T(8,128)(2,1)S(1)} collective-permute-done((bf16[256,1152]{1,0:T(8,128)(2,1)S(1)}, bf16[256,1152]{1,0:T(8,128)(2,1)S(1)}, u32[]{:S(2)}, u32[]{:S(2)}) %collective-permute-start.11) | collective-permute-done | bytes 589856 | tf_op jit(solution)/shard_map/rB1/ppermute | solution.py:28
  74.5 0.0 collective-permute-done.12.refs_2_
  74.5 0.0 collective-permute-done.13.refs_3_
  74.5 0.3 shard_map.70
  74.8 3.3 %collective-permute-start.17 = (bf16[64,1152]{1,0:T(8,128)(2,1)S(1)}, bf16[64,1152]{1,0:T(8,128)(2,1)S(1)}, u32[]{:S(2)}, u32[]{:S(2)}) collective-permute-start(bf16[64,1152]{1,0:T(8,128)(2,1)S(1)} %get-tuple-element.50), channel_id=1, source_target_pairs={{0,96},{1,25},{2,98},{3,27},{4,100},{5,29},{6,102},{7,31},{128,224... | collective-permute-start | bytes 442376 | tf_op jit(solution)/shard_map/rA1/ppermute | solution.py:28
  78.1 0.0 collective-permute-start.18
  78.1 1.0 %collective-permute-start.19 = (bf16[64,1152]{1,0:T(8,128)(2,1)S(1)}, bf16[64,1152]{1,0:T(8,128)(2,1)S(1)}, u32[]{:S(2)}, u32[]{:S(2)}) collective-permute-start(bf16[64,1152]{1,0:T(8,128)(2,1)S(1)} %get-tuple-element.52), channel_id=1, source_target_pairs={{0,32},{1,9},{2,34},{3,11},{4,36},{5,13},{6,38},{7,15},{128,160},{... | collective-permute-start | bytes 442376 | tf_op jit(solution)/shard_map/rA3/ppermute | solution.py:28
  79.0 0.0 collective-permute-done.20.refs_2_
  79.0 0.1 shard_map.72
  79.1 0.1 collective-permute-start.21
  79.2 3.1 %collective-permute-done.17.refs_3_ = bf16[64,1152]{1,0:T(8,128)(2,1)S(1)} collective-permute-done((bf16[64,1152]{1,0:T(8,128)(2,1)S(1)}, bf16[64,1152]{1,0:T(8,128)(2,1)S(1)}, u32[]{:S(2)}, u32[]{:S(2)}) %collective-permute-start.17) | collective-permute-done | bytes 147488 | tf_op jit(solution)/shard_map/rA1/ppermute | solution.py:28
  82.4 2.5 %collective-permute-done.18.refs_4_ = bf16[64,1152]{1,0:T(8,128)(2,1)S(1)} collective-permute-done((bf16[64,1152]{1,0:T(8,128)(2,1)S(1)}, bf16[64,1152]{1,0:T(8,128)(2,1)S(1)}, u32[]{:S(2)}, u32[]{:S(2)}) %collective-permute-start.18) | collective-permute-done | bytes 147488 | tf_op jit(solution)/shard_map/rA2/ppermute | solution.py:28
  84.8 1.2 %collective-permute-done.19.refs_5_ = bf16[64,1152]{1,0:T(8,128)(2,1)S(1)} collective-permute-done((bf16[64,1152]{1,0:T(8,128)(2,1)S(1)}, bf16[64,1152]{1,0:T(8,128)(2,1)S(1)}, u32[]{:S(2)}, u32[]{:S(2)}) %collective-permute-start.19) | collective-permute-done | bytes 147488 | tf_op jit(solution)/shard_map/rA3/ppermute | solution.py:28
  86.0 0.9 %shard_map.71 = f32[64,1152]{1,0:T(8,128)} custom-call(f32[64,1152]{1,0:T(8,128)S(1)} %get-tuple-element.31.refs_0_, f32[64,128]{1,0:T(8,128)S(1)} %get-tuple-element.32.refs_1_, f32[64,1152]{1,0:T(8,128)S(1)} %get-tuple-element.49.refs_2_, bf16[64,1152]{1,0:T(8,128)(2,1)S(1)} %collective-permute-done.17.refs_3_, ...), custom_call_target="tpu_custom_call" | custom-call | bytes 1024 | tf_op jit(solution)/shard_map/pallas_call | solution.py:56
  86.9 0.0 collective-permute-done.21.refs_3_
  86.9 0.9 shard_map.73
  (3 shorter events, 0.0 us)
Async XLA Ops:
  0.6 1.7 %collective-permute-start.3 = (bf16[64,1152]{1,0:T(8,128)(2,1)}, bf16[64,1152]{1,0:T(8,128)(2,1)S(1)}, u32[]{:S(2)}, u32[]{:S(2)}) collective-permute-start(bf16[64,1152]{1,0:T(8,128)(2,1)} %refs_0_.5), channel_id=1, source_target_pairs={{0,1},{1,0},{2,3},{3,2},{4,5},{5,4},{6,7},{7,6},{128,129},{129,128... | collective-permute-start | bytes 442376 | tf_op jit(solution)/shard_map/gC/ppermute | solution.py:28
  2.3 0.9 %copy-start = (bf16[64,1152]{1,0:T(8,128)(2,1)S(1)}, bf16[64,1152]{1,0:T(8,128)(2,1)}, u32[]{:S(2)}) copy-start(bf16[64,1152]{1,0:T(8,128)(2,1)} %refs_0_.5) | copy-start | bytes 442372
  3.2 12.9 %collective-permute-start.4 = (bf16[128,1152]{1,0:T(8,128)(2,1)S(1)}, bf16[128,1152]{1,0:T(8,128)(2,1)S(1)}, u32[]{:S(2)}, u32[]{:S(2)}) collective-permute-start(bf16[128,1152]{1,0:T(8,128)(2,1)S(1)} %shard_map.59.refs_4_), channel_id=1, source_target_pairs={{0,4},{1,133},{2,6},{3,135},{4,128},{5,1},{6,130},{7,3},{128,132},... | collective-permute-start | bytes 884744 | tf_op jit(solution)/shard_map/gZ2/ppermute | solution.py:28
  6.6 6.9 %collective-permute-start.1 = (bf16[64,1152]{1,0:T(8,128)(2,1)}, bf16[64,1152]{1,0:T(8,128)(2,1)S(1)}, u32[]{:S(2)}, u32[]{:S(2)}) collective-permute-start(bf16[64,1152]{1,0:T(8,128)(2,1)} %refs_0_.4), channel_id=1, source_target_pairs={{0,64},{1,17},{2,66},{3,19},{4,68},{5,21},{6,70},{7,23},{128,192},... | collective-permute-start | bytes 442376 | tf_op jit(solution)/shard_map/gA2/ppermute | solution.py:28
  9.6 6.6 %collective-permute-start = (bf16[64,1152]{1,0:T(8,128)(2,1)}, bf16[64,1152]{1,0:T(8,128)(2,1)S(1)}, u32[]{:S(2)}, u32[]{:S(2)}) collective-permute-start(bf16[64,1152]{1,0:T(8,128)(2,1)} %refs_0_.4), channel_id=1, source_target_pairs={{0,32},{1,9},{2,34},{3,11},{4,36},{5,13},{6,38},{7,15},{128,160},{... | collective-permute-start | bytes 442376 | tf_op jit(solution)/shard_map/gA1/ppermute | solution.py:28
  10.2 6.0 %collective-permute-start.2 = (bf16[64,1152]{1,0:T(8,128)(2,1)}, bf16[64,1152]{1,0:T(8,128)(2,1)S(1)}, u32[]{:S(2)}, u32[]{:S(2)}) collective-permute-start(bf16[64,1152]{1,0:T(8,128)(2,1)} %refs_0_.4), channel_id=1, source_target_pairs={{0,96},{1,25},{2,98},{3,27},{4,100},{5,29},{6,102},{7,31},{128,224... | collective-permute-start | bytes 442376 | tf_op jit(solution)/shard_map/gA3/ppermute | solution.py:28
  16.2 0.9 %copy-start.1 = (bf16[64,1152]{1,0:T(8,128)(2,1)S(1)}, bf16[64,1152]{1,0:T(8,128)(2,1)}, u32[]{:S(2)}) copy-start(bf16[64,1152]{1,0:T(8,128)(2,1)} %refs_0_.4) | copy-start | bytes 442372
  17.2 19.5 %collective-permute-start.9 = (bf16[256,1152]{1,0:T(8,128)(2,1)S(1)}, bf16[256,1152]{1,0:T(8,128)(2,1)S(1)}, u32[]{:S(2)}, u32[]{:S(2)}) collective-permute-start(bf16[256,1152]{1,0:T(8,128)(2,1)S(1)} %get-tuple-element.30.refs_0_), channel_id=1, source_target_pairs={{0,24},{1,97},{2,26},{3,99},{4,28},{5,101},{6,30},{7,103},{128,152... | collective-permute-start | bytes 1769480 | tf_op jit(solution)/shard_map/gB3/ppermute | solution.py:28
  18.0 18.7 %collective-permute-start.8 = (bf16[256,1152]{1,0:T(8,128)(2,1)S(1)}, bf16[256,1152]{1,0:T(8,128)(2,1)S(1)}, u32[]{:S(2)}, u32[]{:S(2)}) collective-permute-start(bf16[256,1152]{1,0:T(8,128)(2,1)S(1)} %get-tuple-element.30.refs_0_), channel_id=1, source_target_pairs={{0,16},{1,65},{2,18},{3,67},{4,20},{5,69},{6,22},{7,71},{128,144},... | collective-permute-start | bytes 1769480 | tf_op jit(solution)/shard_map/gB2/ppermute | solution.py:28
  19.0 17.8 %collective-permute-start.7 = (bf16[256,1152]{1,0:T(8,128)(2,1)S(1)}, bf16[256,1152]{1,0:T(8,128)(2,1)S(1)}, u32[]{:S(2)}, u32[]{:S(2)}) collective-permute-start(bf16[256,1152]{1,0:T(8,128)(2,1)S(1)} %get-tuple-element.30.refs_0_), channel_id=1, source_target_pairs={{0,8},{1,33},{2,10},{3,35},{4,12},{5,37},{6,14},{7,39},{128,136},{... | collective-permute-start | bytes 1769480 | tf_op jit(solution)/shard_map/gB1/ppermute | solution.py:28
  21.1 8.7 %collective-permute-start.6 = (bf16[64,1152]{1,0:T(8,128)(2,1)S(1)}, bf16[64,1152]{1,0:T(8,128)(2,1)S(1)}, u32[]{:S(2)}, u32[]{:S(2)}) collective-permute-start(bf16[64,1152]{1,0:T(8,128)(2,1)S(1)} %get-tuple-element.34), channel_id=1, source_target_pairs={{0,4},{1,133},{2,6},{3,135},{4,128},{5,1},{6,130},{7,3},{128,132},... | collective-permute-start | bytes 442376 | tf_op jit(solution)/shard_map/gZ4/ppermute | solution.py:28
  25.6 11.1 %collective-permute-start.5 = (bf16[256,1152]{1,0:T(8,128)(2,1)S(1)}, bf16[256,1152]{1,0:T(8,128)(2,1)S(1)}, u32[]{:S(2)}, u32[]{:S(2)}) collective-permute-start(bf16[256,1152]{1,0:T(8,128)(2,1)S(1)} %get-tuple-element.33), channel_id=1, source_target_pairs={{0,2},{1,135},{2,4},{3,1},{4,6},{5,3},{6,128},{7,5},{128,130},{129... | collective-permute-start | bytes 1769480 | tf_op jit(solution)/shard_map/gZ13/ppermute | solution.py:28
  37.1 6.8 %collective-permute-start.10 = (bf16[512,1152]{1,0:T(8,128)(2,1)S(1)}, bf16[512,1152]{1,0:T(8,128)(2,1)S(1)}, u32[]{:S(2)}, u32[]{:S(2)}) collective-permute-start(bf16[512,1152]{1,0:T(8,128)(2,1)S(1)} %get-tuple-element.36.refs_1_.refs_2_), channel_id=1, source_target_pairs={{0,1},{1,0},{2,3},{3,2},{4,5},{5,4},{6,7},{7,6},{128,129},{129,128... | collective-permute-start | bytes 3538952 | tf_op jit(solution)/shard_map/gS/ppermute | solution.py:28
  47.4 3.0 %collective-permute-start.14 = (bf16[512,1152]{1,0:T(8,128)(2,1)S(1)}, bf16[512,1152]{1,0:T(8,128)(2,1)S(1)}, u32[]{:S(2)}, u32[]{:S(2)}) collective-permute-start(bf16[512,1152]{1,0:T(8,128)(2,1)S(1)} %get-tuple-element.45), channel_id=1, source_target_pairs={{0,1},{1,0},{2,3},{3,2},{4,5},{5,4},{6,7},{7,6},{128,129},{129,128... | collective-permute-start | bytes 3538952 | tf_op jit(solution)/shard_map/rC/ppermute | solution.py:28
  50.7 13.9 %collective-permute-start.15 = (bf16[256,1152]{1,0:T(8,128)(2,1)S(1)}, bf16[256,1152]{1,0:T(8,128)(2,1)S(1)}, u32[]{:S(2)}, u32[]{:S(2)}) collective-permute-start(bf16[256,1152]{1,0:T(8,128)(2,1)S(1)} %get-tuple-element.47), channel_id=1, source_target_pairs={{0,134},{1,3},{2,0},{3,5},{4,2},{5,7},{6,4},{7,129},{128,6},{129,1... | collective-permute-start | bytes 1769480 | tf_op jit(solution)/shard_map/rZ13/ppermute | solution.py:28
  52.4 12.2 %collective-permute-start.16 = (bf16[64,1152]{1,0:T(8,128)(2,1)S(1)}, bf16[64,1152]{1,0:T(8,128)(2,1)S(1)}, u32[]{:S(2)}, u32[]{:S(2)}) collective-permute-start(bf16[64,1152]{1,0:T(8,128)(2,1)S(1)} %get-tuple-element.48), channel_id=1, source_target_pairs={{0,132},{1,5},{2,134},{3,7},{4,0},{5,129},{6,2},{7,131},{128,4},{1... | collective-permute-start | bytes 442376 | tf_op jit(solution)/shard_map/rZ4/ppermute | solution.py:28
  54.5 20.0 %collective-permute-start.13 = (bf16[256,1152]{1,0:T(8,128)(2,1)S(1)}, bf16[256,1152]{1,0:T(8,128)(2,1)S(1)}, u32[]{:S(2)}, u32[]{:S(2)}) collective-permute-start(bf16[256,1152]{1,0:T(8,128)(2,1)S(1)} %get-tuple-element.44.refs_2_), channel_id=1, source_target_pairs={{0,8},{1,33},{2,10},{3,35},{4,12},{5,37},{6,14},{7,39},{128,136},{... | collective-permute-start | bytes 1769480 | tf_op jit(solution)/shard_map/rB3/ppermute | solution.py:28
  57.1 17.4 %collective-permute-start.11 = (bf16[256,1152]{1,0:T(8,128)(2,1)S(1)}, bf16[256,1152]{1,0:T(8,128)(2,1)S(1)}, u32[]{:S(2)}, u32[]{:S(2)}) collective-permute-start(bf16[256,1152]{1,0:T(8,128)(2,1)S(1)} %get-tuple-element.42), channel_id=1, source_target_pairs={{0,24},{1,97},{2,26},{3,99},{4,28},{5,101},{6,30},{7,103},{128,152... | collective-permute-start | bytes 1769480 | tf_op jit(solution)/shard_map/rB1/ppermute | solution.py:28
  57.1 17.4 %collective-permute-start.12 = (bf16[256,1152]{1,0:T(8,128)(2,1)S(1)}, bf16[256,1152]{1,0:T(8,128)(2,1)S(1)}, u32[]{:S(2)}, u32[]{:S(2)}) collective-permute-start(bf16[256,1152]{1,0:T(8,128)(2,1)S(1)} %get-tuple-element.43), channel_id=1, source_target_pairs={{0,16},{1,65},{2,18},{3,67},{4,20},{5,69},{6,22},{7,71},{128,144},... | collective-permute-start | bytes 1769480 | tf_op jit(solution)/shard_map/rB2/ppermute | solution.py:28
  64.7 14.4 %collective-permute-start.20 = (bf16[128,1152]{1,0:T(8,128)(2,1)S(1)}, bf16[128,1152]{1,0:T(8,128)(2,1)S(1)}, u32[]{:S(2)}, u32[]{:S(2)}) collective-permute-start(bf16[128,1152]{1,0:T(8,128)(2,1)S(1)} %shard_map.68.refs_0_), channel_id=1, source_target_pairs={{0,132},{1,5},{2,134},{3,7},{4,0},{5,129},{6,2},{7,131},{128,4},{1... | collective-permute-start | bytes 884744 | tf_op jit(solution)/shard_map/rZ2/ppermute | solution.py:28
  74.8 7.6 %collective-permute-start.17 = (bf16[64,1152]{1,0:T(8,128)(2,1)S(1)}, bf16[64,1152]{1,0:T(8,128)(2,1)S(1)}, u32[]{:S(2)}, u32[]{:S(2)}) collective-permute-start(bf16[64,1152]{1,0:T(8,128)(2,1)S(1)} %get-tuple-element.50), channel_id=1, source_target_pairs={{0,96},{1,25},{2,98},{3,27},{4,100},{5,29},{6,102},{7,31},{128,224... | collective-permute-start | bytes 442376 | tf_op jit(solution)/shard_map/rA1/ppermute | solution.py:28
  78.1 6.8 %collective-permute-start.18 = (bf16[64,1152]{1,0:T(8,128)(2,1)S(1)}, bf16[64,1152]{1,0:T(8,128)(2,1)S(1)}, u32[]{:S(2)}, u32[]{:S(2)}) collective-permute-start(bf16[64,1152]{1,0:T(8,128)(2,1)S(1)} %get-tuple-element.51), channel_id=1, source_target_pairs={{0,64},{1,17},{2,66},{3,19},{4,68},{5,21},{6,70},{7,23},{128,192},... | collective-permute-start | bytes 442376 | tf_op jit(solution)/shard_map/rA2/ppermute | solution.py:28
  78.1 7.9 %collective-permute-start.19 = (bf16[64,1152]{1,0:T(8,128)(2,1)S(1)}, bf16[64,1152]{1,0:T(8,128)(2,1)S(1)}, u32[]{:S(2)}, u32[]{:S(2)}) collective-permute-start(bf16[64,1152]{1,0:T(8,128)(2,1)S(1)} %get-tuple-element.52), channel_id=1, source_target_pairs={{0,32},{1,9},{2,34},{3,11},{4,36},{5,13},{6,38},{7,15},{128,160},{... | collective-permute-start | bytes 442376 | tf_op jit(solution)/shard_map/rA3/ppermute | solution.py:28
  79.1 7.8 %collective-permute-start.21 = (bf16[64,1152]{1,0:T(8,128)(2,1)S(1)}, bf16[64,1152]{1,0:T(8,128)(2,1)S(1)}, u32[]{:S(2)}, u32[]{:S(2)}) collective-permute-start(bf16[64,1152]{1,0:T(8,128)(2,1)S(1)} %get-tuple-element.57), channel_id=1, source_target_pairs={{0,1},{1,0},{2,3},{3,2},{4,5},{5,4},{6,7},{7,6},{128,129},{129,128... | collective-permute-start | bytes 442376 | tf_op jit(solution)/shard_map/rS/ppermute | solution.py:28

commit v5 on v4

--- a/solution.py
+++ b/solution.py
@@ -48,11 +48,10 @@
     return (x, y, z, 1 - c)
 
 
-def call(kernel, outs, arrays, scalars=None, ties=(), flops=0, limit=8):
+def call(kernel, outs, arrays, last_scalars=(), ties=(), flops=0, limit=8):
     vmem = pl.BlockSpec(memory_space=pltpu.VMEM)
-    few = [] if scalars is None else [scalars]
-    n_in = len(few) + len(arrays)
-    specs = [pl.BlockSpec(memory_space=pltpu.SMEM)] * len(few) + [vmem] * len(arrays)
+    n_in = len(arrays) + len(last_scalars)
+    specs = [vmem] * len(arrays) + [pl.BlockSpec(memory_space=pltpu.SMEM)] * len(last_scalars)
     return pl.pallas_call(
         lambda *refs: kernel(*refs[:n_in], *refs[n_in + len(ties):]),
         out_shape=tuple(jax.ShapeDtypeStruct(shape, dtype) for shape, dtype in outs),
@@ -60,7 +59,7 @@
         out_specs=tuple([vmem] * len(outs)),
         compiler_params=pltpu.CompilerParams(vmem_limit_bytes=limit * 1024 * 1024),
         cost_estimate=pl.CostEstimate(flops=flops, bytes_accessed=1024, transcendentals=0),
-    )(*few, *arrays, *ties)
+    )(*arrays, *last_scalars, *ties)
 
 
 def token_kernel(token_ref):
@@ -82,39 +81,46 @@
     return (grad_unit - unit * along) * inverse
 
 
-def pair_kernel(first_ref, second_ref, out_ref):
-    rows = first_ref.shape[0]
-    out_ref[:rows, :] = first_ref[...]
-    out_ref[rows:, :] = second_ref[...]
-
-
-def group_kernel(*refs):
-    *parts, pair_ref, near_ref, group_ref, send_ref, head_ref = refs
-    rows = parts[0].shape[0]
-    for n, part in enumerate(parts):
-        group_ref[n * rows:(n + 1) * rows, :] = part[...]
-    send_ref[:2 * rows, :] = pair_ref[...]
-    send_ref[2 * rows:, :] = near_ref[...]
-    head_ref[...] = near_ref[:rows, :]
-
-
-def round_kernel(own, *refs):
-    *parts, out_ref, unit_ref, inv_ref = refs
+def own_kernel(img_ref, txt_ref, log_ref, bias_ref, *outs):
+    *outs, scal_ref = outs
+    for n, raw_ref in enumerate((img_ref, txt_ref)):
+        copy_ref, unit_ref, inv_ref = outs[3 * n:3 * n + 3]
+        unit, inverse = unit_rows(raw_ref[...])
+        copy_ref[...] = raw_ref[...]
+        unit_ref[...] = unit
+        inv_ref[...] = jnp.broadcast_to(inverse, inv_ref.shape)
+    temp = jnp.exp(jnp.full((1, 128), log_ref[0], F32))
+    scal_ref[0:1, :] = temp
+    scal_ref[1:2, :] = -LOG2E * temp
+    scal_ref[2:3, :] = jnp.full((1, 128), -LOG2E * bias_ref[0], F32)
+
+
+def stack_kernel(*refs):
+    *parts, out_ref = refs
+    at = 0
+    for part in parts:
+        rows = part.shape[0]
+        out_ref[at:at + rows, :] = part[...]
+        at += rows
+
+
+def stack(parts, ties=()):
+    rows, dim = sum(p.shape[0] for p in parts), parts[0].shape[1]
+    return call(stack_kernel, [((rows, dim), BF16)], parts, ties=ties)[0]
+
+
+def round_kernel(step, *refs):
+    *parts, out_ref = refs
     base = 0
     for part in parts:
-        for at in range(0, part.shape[0], own):
-            unit, inverse = unit_rows(part[at:at + own, :])
-            out_ref[base:base + own, :] = unit.astype(BF16)
-            if base == 0:
-                unit_ref[...] = unit
-                inv_ref[...] = jnp.broadcast_to(inverse, inv_ref.shape)
-            base += own
-
-
-def rounded(parts, own, ties=()):
+        for at in range(0, part.shape[0], step):
+            out_ref[base:base + step, :] = unit_rows(part[at:at + step, :])[0].astype(BF16)
+            base += step
+
+
+def rounded(parts, ties=()):
     rows, dim = sum(p.shape[0] for p in parts), parts[0].shape[1]
-    outs = [((rows, dim), BF16), ((own, dim), F32), ((own, 128), F32)]
-    return call(lambda *refs: round_kernel(own, *refs), outs, parts, ties=ties)
+    return call(lambda *refs: round_kernel(64, *refs), [((rows, dim), BF16)], parts, ties=ties)[0]
 
 
 def sigmoid_weights(power, scale):
@@ -122,7 +128,7 @@
 
 
 def powers(img, txt, scal_ref):
-    slope, offset = -scal_ref[0] * LOG2E, -scal_ref[1] * LOG2E
+    slope, offset = scal_ref[1:2, 0:1], scal_ref[2:3, 0:1]
     dots = lax.dot_general(img, txt, (((1,), (1,)), ((), ())), preferred_element_type=F32)
     return dots * slope + offset
 
@@ -136,9 +142,9 @@
         out_ref[t:t + step, :] = grad.astype(out_ref.dtype)
 
 
-def mine_kernel(own, scal_ref, txt_ref, *refs):
+def mine_kernel(own, txt_ref, scal_ref, *refs):
     *parts, w_ref, img_ref, keep_ref = refs
-    temp = scal_ref[0]
+    temp = scal_ref[0:1, 0:1]
     at = 0
     for part in parts:
         rows = part.shape[0]
@@ -157,11 +163,11 @@
     text_grads(w_ref, img_ref, keep_ref)
 
 
-def theirs_kernel(scal_ref, txt_ref, img_ref, w_ref, send_ref):
+def theirs_kernel(txt_ref, scal_ref, img_ref, w_ref, send_ref):
     step = 256
     for at in range(0, img_ref.shape[0], step):
         power = powers(img_ref[at:at + step, :], txt_ref[...], scal_ref)
-        w_ref[at:at + step, :] = sigmoid_weights(power, scal_ref[0])
+        w_ref[at:at + step, :] = sigmoid_weights(power, scal_ref[0:1, 0:1])
     text_grads(w_ref, img_ref, send_ref)
 
 
@@ -206,28 +212,32 @@
         out[...] = (own_ref[at, :] + sum(p[at, :].astype(F32) for p in parts)).astype(out.dtype)
 
 
-def final_kernel(unit_ref, inv_ref, own_ref, *refs):
-    *parts, out_ref = refs
-    grad = own_ref[...] + sum(p[...].astype(F32) for p in parts)
-    out_ref[...] = back_norm(unit_ref[...], inv_ref[:, :1], grad)
+def final_kernel(*refs):
+    *ins, img_ref, txt_ref = refs
+    for (unit_ref, inv_ref, own_ref, *parts), out_ref in ((ins[:6], img_ref), (ins[6:], txt_ref)):
+        grad = own_ref[...] + sum(p[...].astype(F32) for p in parts)
+        out_ref[...] = back_norm(unit_ref[...], inv_ref[:, :1], grad)
 
 
 def local(images, texts, log_temp, bias):
     own, dim = images.shape
-    scalars = jnp.concatenate([jnp.exp(log_temp), bias])
-
-    (pair,) = call(pair_kernel, [((2 * own, dim), BF16)], [texts, shift(texts, other, "gC")])
+    per_row = [((own, dim), BF16), ((own, dim), F32), ((own, 128), F32)]
+
     side = [shift(images, first(k), "gA%d" % k) for k in (1, 2, 3)]
-    near2 = shift(pair, line(2), "gZ2")
-    group, send13, send4 = call(
-        group_kernel, [((4 * own, dim), BF16), ((4 * own, dim), BF16), ((own, dim), BF16)], [images, *side, pair, near2]
-    )
+    line2 = shift(texts, line(2), "gZ2")
+    cross2 = shift(texts, cross(2), "gX2")
+    img_own, img_unit, inv_img, txt_own, txt_unit, inv_txt, scalars = call(
+        own_kernel, per_row * 2 + [((8, 128), F32)], [images, texts], last_scalars=[log_temp, bias]
+    )
+    swapped = shift(txt_own, other, "gC")
+    group = stack([img_own, *side])
+    send13 = stack([txt_own, swapped, line2, cross2])
     far = [shift(group, second(k), "gB%d" % k) for k in (1, 2, 3)]
     near13 = shift(send13, line(1), "gZ13")
-    near4 = shift(send4, line(2), "gZ4")
+    near4 = shift(line2, line(2), "gZ4")
     first_token = token(group)
-    group, img_unit, inv_img = rounded([group], own)
-    mine, txt_unit, inv_txt = rounded([texts, near13, near2, near4], own, [group, first_token, *far])
+    group = rounded([group])
+    mine = rounded([txt_own, near13, line2, cross2, near4], [group, first_token, *far])
     theirs = shift(mine, other, "gS")
 
     half = mine.shape[0]
@@ -235,11 +245,11 @@
     flops = 2 * rows * half * dim
     w_mine, img_all, keep = call(
         lambda *refs: mine_kernel(own, *refs), [((rows, half), BF16), ((rows, dim), BF16), ((half, dim), BF16)],
-        [mine, group, *far], scalars, flops=2 * flops, limit=24,
+        [mine, scalars, group, *far], flops=2 * flops, limit=24,
     )
     w_theirs, send = call(
         theirs_kernel, [((rows, half), BF16), ((half, dim), BF16)],
-        [theirs, img_all], scalars, ties=[keep], flops=2 * flops, limit=24,
+        [theirs, scalars, img_all], ties=[keep], flops=2 * flops, limit=24,
     )
     grads = call(
         image_kernel, [(group.shape, F32)] + [(group.shape, BF16)] * len(far),
@@ -264,9 +274,10 @@
     )
     last = [shift(p, first(-k), "rA%d" % k) for k, p in zip((1, 2, 3), parts)]
 
-    (grad_img,) = call(final_kernel, [((own, dim), F32)], [img_unit, inv_img, img_sum, *last])
-    (grad_txt,) = call(final_kernel, [((own, dim), F32)], [txt_unit, inv_txt, txt_sum, txt_last])
-    return grad_img, grad_txt
+    return call(
+        final_kernel, [((own, dim), F32)] * 2,
+        [img_unit, inv_img, img_sum, *last, txt_unit, inv_txt, txt_sum, txt_last],
+    )
 
 
 def solution(mesh):

time: 87.9 us -> 81 us (0.922)
  starting transfers between devices: 36.2 us -> 32.7 us
  waiting for transfers between devices: 34.1 us -> 32.3 us
  Pallas kernels: 13.5 us -> 12 us
    ppermute x22 -> x23, starting transfers between devices: 36.2 us -> 32.7 us  [shift(): return lax.ppermute(values, AXES, pairs)]
    ppermute x22 -> x23, waiting for transfers between devices: 34.1 us -> 32.3 us  [shift(): return lax.ppermute(values, AXES, pairs)]
    pallas_call x15, Pallas kernels: 13.5 us -> 12 us  [call(): pl.pallas_call(lambda *refs: kernel(*refs[:n_in], *refs[n_in + len(ties):...]
  transfers between devices with their start and end apart: 22 -> 23, of which waited for: 10 -> 8; matrix products, arithmetic and copies ran while one was open for 0% -> 0% of each run, Pallas kernels for 10% -> 9%
where the time goes in v5:
time: 81 us; the launch traced here: 80.9 us
  starting transfers between devices  32.7 us (40%)
  waiting for transfers between devices  32.3 us (40%)
  Pallas kernels  12 us (15%)
  between operations  2.08 us (3%)
  local copies, waits for them, and re-layouts  1.81 us (2%)
    ppermute x23, starting transfers between devices, shift(): return lax.ppermute(values, AXES, pairs)  32.7 us
    ppermute x23, waiting for transfers between devices, shift(): return lax.ppermute(values, AXES, pairs)  32.3 us
    pallas_call x15, Pallas kernels, call(): pl.pallas_call(lambda *refs: kernel(*refs[:n_in], *refs[n_in + len(ties):...  12 us
    unnamed x4, local copies, waits for them, and re-layouts  1.81 us
  transfers between devices with their start and end apart: 23, of which 8 were waited for; matrix products, arithmetic and copies ran while one was open for 0% of the time, Pallas kernels for 9%

profile of v5, /device:TPU:24, one launch (start us, length us, event | category | flops | bytes accessed | tf_op | source)
XLA Modules:
  0.0 80.9 jit_solution(13018264374222821775)
XLA Ops:
  0.6 1.6 %collective-permute-start.5 = (bf16[64,1152]{1,0:T(8,128)(2,1)}, bf16[64,1152]{1,0:T(8,128)(2,1)S(1)}, u32[]{:S(2)}, u32[]{:S(2)}) collective-permute-start(bf16[64,1152]{1,0:T(8,128)(2,1)} %refs_0_.1), channel_id=1, source_target_pairs={{0,32},{1,9},{2,34},{3,11},{4,36},{5,13},{6,38},{7,15},{128,160},{... | collective-permute-start | bytes 442376 | tf_op jit(solution)/shard_map/gA1/ppermute | solution.py:28
  2.2 4.3 %collective-permute-start.2 = (bf16[64,1152]{1,0:T(8,128)(2,1)}, bf16[64,1152]{1,0:T(8,128)(2,1)S(1)}, u32[]{:S(2)}, u32[]{:S(2)}) collective-permute-start(bf16[64,1152]{1,0:T(8,128)(2,1)} %refs_1_.1), channel_id=1, source_target_pairs={{0,133},{1,4},{2,135},{3,6},{4,1},{5,128},{6,3},{7,130},{128,5},{1... | collective-permute-start | bytes 442376 | tf_op jit(solution)/shard_map/gX2/ppermute | solution.py:28
  6.5 0.0 collective-permute-start.1
  6.6 2.8 %collective-permute-start.7 = (bf16[64,1152]{1,0:T(8,128)(2,1)}, bf16[64,1152]{1,0:T(8,128)(2,1)S(1)}, u32[]{:S(2)}, u32[]{:S(2)}) collective-permute-start(bf16[64,1152]{1,0:T(8,128)(2,1)} %refs_0_.1), channel_id=1, source_target_pairs={{0,96},{1,25},{2,98},{3,27},{4,100},{5,29},{6,102},{7,31},{128,224... | collective-permute-start | bytes 442376 | tf_op jit(solution)/shard_map/gA3/ppermute | solution.py:28
  9.3 0.8 collective-permute-start.6
  11.4 0.0 copy-start
  11.4 0.9 %copy-done = bf16[64,1152]{1,0:T(8,128)(2,1)S(1)} copy-done((bf16[64,1152]{1,0:T(8,128)(2,1)S(1)}, bf16[64,1152]{1,0:T(8,128)(2,1)}, u32[]{:S(2)}) %copy-start) | copy-done | bytes 147480
  12.3 0.0 copy-start.1
  12.3 0.9 %copy-done.1 = bf16[64,1152]{1,0:T(8,128)(2,1)S(1)} copy-done((bf16[64,1152]{1,0:T(8,128)(2,1)S(1)}, bf16[64,1152]{1,0:T(8,128)(2,1)}, u32[]{:S(2)}) %copy-start.1) | copy-done | bytes 147480
  13.2 0.2 shard_map.59
  13.4 0.0 collective-permute-done.5.refs_1_
  13.4 0.1 collective-permute-start
  13.5 0.4 collective-permute-done.7.refs_3_
  13.9 2.3 %collective-permute-done.6.refs_2_ = bf16[64,1152]{1,0:T(8,128)(2,1)S(1)} collective-permute-done((bf16[64,1152]{1,0:T(8,128)(2,1)}, bf16[64,1152]{1,0:T(8,128)(2,1)S(1)}, u32[]{:S(2)}, u32[]{:S(2)}) %collective-permute-start.6) | collective-permute-done | bytes 147488 | tf_op jit(solution)/shard_map/gA2/ppermute | solution.py:28
  16.2 1.7 %collective-permute-start.10 = (bf16[256,1152]{1,0:T(8,128)(2,1)S(1)}, bf16[256,1152]{1,0:T(8,128)(2,1)S(1)}, u32[]{:S(2)}, u32[]{:S(2)}) collective-permute-start(bf16[256,1152]{1,0:T(8,128)(2,1)S(1)} %shard_map.61.refs_0_), channel_id=1, source_target_pairs={{0,24},{1,97},{2,26},{3,99},{4,28},{5,101},{6,30},{7,103},{128,152... | collective-permute-start | bytes 1769480 | tf_op jit(solution)/shard_map/gB3/ppermute | solution.py:28
  17.9 1.2 %collective-permute-start.9 = (bf16[256,1152]{1,0:T(8,128)(2,1)S(1)}, bf16[256,1152]{1,0:T(8,128)(2,1)S(1)}, u32[]{:S(2)}, u32[]{:S(2)}) collective-permute-start(bf16[256,1152]{1,0:T(8,128)(2,1)S(1)} %shard_map.61.refs_0_), channel_id=1, source_target_pairs={{0,16},{1,65},{2,18},{3,67},{4,20},{5,69},{6,22},{7,71},{128,144},... | collective-permute-start | bytes 1769480 | tf_op jit(solution)/shard_map/gB2/ppermute | solution.py:28
  19.2 0.0 collective-permute-done.2.refs_3_
  19.2 2.2 %collective-permute-start.8 = (bf16[256,1152]{1,0:T(8,128)(2,1)S(1)}, bf16[256,1152]{1,0:T(8,128)(2,1)S(1)}, u32[]{:S(2)}, u32[]{:S(2)}) collective-permute-start(bf16[256,1152]{1,0:T(8,128)(2,1)S(1)} %shard_map.61.refs_0_), channel_id=1, source_target_pairs={{0,8},{1,33},{2,10},{3,35},{4,12},{5,37},{6,14},{7,39},{128,136},{... | collective-permute-start | bytes 1769480 | tf_op jit(solution)/shard_map/gB1/ppermute | solution.py:28
  21.4 0.0 collective-permute-done.1.refs_2_
  21.4 0.0 collective-permute-done.refs_1_
  21.4 1.1 %collective-permute-start.3 = (bf16[256,1152]{1,0:T(8,128)(2,1)S(1)}, bf16[256,1152]{1,0:T(8,128)(2,1)S(1)}, u32[]{:S(2)}, u32[]{:S(2)}) collective-permute-start(bf16[256,1152]{1,0:T(8,128)(2,1)S(1)} %shard_map.60), channel_id=1, source_target_pairs={{0,2},{1,135},{2,4},{3,1},{4,6},{5,3},{6,128},{7,5},{128,130},{129... | collective-permute-start | bytes 1769480 | tf_op jit(solution)/shard_map/gZ13/ppermute | solution.py:28
  22.5 2.0 %collective-permute-start.4 = (bf16[64,1152]{1,0:T(8,128)(2,1)S(1)}, bf16[64,1152]{1,0:T(8,128)(2,1)S(1)}, u32[]{:S(2)}, u32[]{:S(2)}) collective-permute-start(bf16[64,1152]{1,0:T(8,128)(2,1)S(1)} %collective-permute-done.1.refs_2_), channel_id=1, source_target_pairs={{0,4},{1,133},{2,6},{3,135},{4,128},{5,1},{6,130},{7,3},{128,132},... | collective-permute-start | bytes 442376 | tf_op jit(solution)/shard_map/gZ4/ppermute | solution.py:28
  24.5 0.2 shard_map.62.refs_5_.refs_2_
  24.7 11.5 %collective-permute-done.4.refs_4_ = bf16[64,1152]{1,0:T(8,128)(2,1)S(1)} collective-permute-done((bf16[64,1152]{1,0:T(8,128)(2,1)S(1)}, bf16[64,1152]{1,0:T(8,128)(2,1)S(1)}, u32[]{:S(2)}, u32[]{:S(2)}) %collective-permute-start.4) | collective-permute-done | bytes 147488 | tf_op jit(solution)/shard_map/gZ4/ppermute | solution.py:28
  36.2 0.0 collective-permute-done.3.refs_1_
  36.2 0.0 collective-permute-done.10.refs_9_.refs_5_
  36.2 0.0 collective-permute-done.9.refs_8_.refs_4_
  36.2 0.0 collective-permute-done.8.refs_7_.refs_3_
  36.2 0.4 shard_map.64.refs_0_.refs_2_
  36.6 0.3 collective-permute-start.11
  36.9 3.5 %shard_map.65 = (bf16[1024,512]{1,0:T(8,128)(2,1)S(1)}, bf16[1024,1152]{1,0:T(8,128)(2,1)S(1)}, bf16[512,1152]{1,0:T(8,128)(2,1)S(1)}) custom-call(bf16[512,1152]{1,0:T(8,128)(2,1)S(1)} %shard_map.64.refs_0_.refs_2_, f32[8,128]{1,0:T(8,128)S(1)} %get-tuple-element.32.refs_1_, bf16[256,1152]{1,0:T(8,128)(2,1)S(1)} %shard_map.62.refs_5_.refs_2_, ...), custom_call_target="tpu_custom_call" | custom-call | flops 2415919104 | bytes 1024 | tf_op jit(solution)/shard_map/pallas_call | solution.py:55
  40.3 0.0 collective-permute-done.11.refs_0_.refs_3_
  40.3 3.1 %shard_map.66 = (bf16[1024,512]{1,0:T(8,128)(2,1)S(1)}, bf16[512,1152]{1,0:T(8,128)(2,1)S(1)}) custom-call(bf16[512,1152]{1,0:T(8,128)(2,1)S(1)} %collective-permute-done.11.refs_0_.refs_3_, f32[8,128]{1,0:T(8,128)S(1)} %get-tuple-element.32.refs_1_, bf16[1024,1152]{1,0:T(8,128)(2,1)S(1)} %get-tuple-element.34.refs_2_, ...), custom_call_target="tpu_custom_call" | custom-call | flops 2415919104 | bytes 1024 | tf_op jit(solution)/shard_map/pallas_call | solution.py:55
  43.4 0.6 collective-permute-start.15
  44.0 2.9 %shard_map.67 = (f32[256,1152]{1,0:T(8,128)S(1)}, bf16[256,1152]{1,0:T(8,128)(2,1)S(1)}, bf16[256,1152]{1,0:T(8,128)(2,1)S(1)}, bf16[256,1152]{1,0:T(8,128)(2,1)S(1)}) custom-call(bf16[1024,512]{1,0:T(8,128)(2,1)S(1)} %get-tuple-element.33.refs_0_, bf16[1024,512]{1,0:T(8,128)(2,1)S(1)} %get-tuple-element.36.refs_1_, ...), custom_call_target="tpu_custom_call" | custom-call | flops 2415919104 | bytes 1024 | tf_op jit(solution)/shard_map/pallas_call | solution.py:55
  46.9 0.0 collective-permute-done.15.refs_1_
  46.9 0.3 shard_map.68
  47.2 2.6 %collective-permute-start.16 = (bf16[256,1152]{1,0:T(8,128)(2,1)S(1)}, bf16[256,1152]{1,0:T(8,128)(2,1)S(1)}, u32[]{:S(2)}, u32[]{:S(2)}) collective-permute-start(bf16[256,1152]{1,0:T(8,128)(2,1)S(1)} %get-tuple-element.43), channel_id=1, source_target_pairs={{0,134},{1,3},{2,0},{3,5},{4,2},{5,7},{6,4},{7,129},{128,6},{129,1... | collective-permute-start | bytes 1769480 | tf_op jit(solution)/shard_map/rZ13/ppermute | solution.py:28
  49.8 1.5 %collective-permute-start.17 = (bf16[64,1152]{1,0:T(8,128)(2,1)S(1)}, bf16[64,1152]{1,0:T(8,128)(2,1)S(1)}, u32[]{:S(2)}, u32[]{:S(2)}) collective-permute-start(bf16[64,1152]{1,0:T(8,128)(2,1)S(1)} %get-tuple-element.44), channel_id=1, source_target_pairs={{0,132},{1,5},{2,134},{3,7},{4,0},{5,129},{6,2},{7,131},{128,4},{1... | collective-permute-start | bytes 442376 | tf_op jit(solution)/shard_map/rZ4/ppermute | solution.py:28
  51.2 1.3 %collective-permute-start.14 = (bf16[256,1152]{1,0:T(8,128)(2,1)S(1)}, bf16[256,1152]{1,0:T(8,128)(2,1)S(1)}, u32[]{:S(2)}, u32[]{:S(2)}) collective-permute-start(bf16[256,1152]{1,0:T(8,128)(2,1)S(1)} %get-tuple-element.40.refs_2_), channel_id=1, source_target_pairs={{0,8},{1,33},{2,10},{3,35},{4,12},{5,37},{6,14},{7,39},{128,136},{... | collective-permute-start | bytes 1769480 | tf_op jit(solution)/shard_map/rB3/ppermute | solution.py:28
  52.5 0.7 collective-permute-start.12
  53.2 1.1 %collective-permute-start.13 = (bf16[256,1152]{1,0:T(8,128)(2,1)S(1)}, bf16[256,1152]{1,0:T(8,128)(2,1)S(1)}, u32[]{:S(2)}, u32[]{:S(2)}) collective-permute-start(bf16[256,1152]{1,0:T(8,128)(2,1)S(1)} %get-tuple-element.39), channel_id=1, source_target_pairs={{0,16},{1,65},{2,18},{3,67},{4,20},{5,69},{6,22},{7,71},{128,144},... | collective-permute-start | bytes 1769480 | tf_op jit(solution)/shard_map/rB2/ppermute | solution.py:28
  54.4 6.9 %collective-permute-done.17.refs_2_ = bf16[64,1152]{1,0:T(8,128)(2,1)S(1)} collective-permute-done((bf16[64,1152]{1,0:T(8,128)(2,1)S(1)}, bf16[64,1152]{1,0:T(8,128)(2,1)S(1)}, u32[]{:S(2)}, u32[]{:S(2)}) %collective-permute-start.17) | collective-permute-done | bytes 147488 | tf_op jit(solution)/shard_map/rZ4/ppermute | solution.py:28
  61.2 0.0 collective-permute-done.16.refs_1_
  61.3 0.1 shard_map.69.refs_0_
  61.3 4.0 %collective-permute-start.21 = (bf16[128,1152]{1,0:T(8,128)(2,1)S(1)}, bf16[128,1152]{1,0:T(8,128)(2,1)S(1)}, u32[]{:S(2)}, u32[]{:S(2)}) collective-permute-start(bf16[128,1152]{1,0:T(8,128)(2,1)S(1)} %shard_map.69.refs_0_), channel_id=1, source_target_pairs={{0,132},{1,5},{2,134},{3,7},{4,0},{5,129},{6,2},{7,131},{128,4},{1... | collective-permute-start | bytes 884744 | tf_op jit(solution)/shard_map/rZ2/ppermute | solution.py:28
  65.3 5.2 %collective-permute-done.12.refs_1_ = bf16[256,1152]{1,0:T(8,128)(2,1)S(1)} collective-permute-done((bf16[256,1152]{1,0:T(8,128)(2,1)S(1)}, bf16[256,1152]{1,0:T(8,128)(2,1)S(1)}, u32[]{:S(2)}, u32[]{:S(2)}) %collective-permute-start.12) | collective-permute-done | bytes 589856 | tf_op jit(solution)/shard_map/rB1/ppermute | solution.py:28
  70.5 0.0 collective-permute-done.13.refs_2_
  70.6 0.0 collective-permute-done.14.refs_3_
  70.6 0.3 shard_map.71
  70.8 0.8 collective-permute-start.18
  71.6 0.7 collective-permute-start.19
  72.3 1.3 %collective-permute-start.20 = (bf16[64,1152]{1,0:T(8,128)(2,1)S(1)}, bf16[64,1152]{1,0:T(8,128)(2,1)S(1)}, u32[]{:S(2)}, u32[]{:S(2)}) collective-permute-start(bf16[64,1152]{1,0:T(8,128)(2,1)S(1)} %get-tuple-element.48), channel_id=1, source_target_pairs={{0,32},{1,9},{2,34},{3,11},{4,36},{5,13},{6,38},{7,15},{128,160},{... | collective-permute-start | bytes 442376 | tf_op jit(solution)/shard_map/rA3/ppermute | solution.py:28
  73.6 0.0 collective-permute-done.21.refs_2_
  73.6 0.1 shard_map.72
  73.7 0.1 collective-permute-start.22
  73.8 2.2 %collective-permute-done.18.refs_3_ = bf16[64,1152]{1,0:T(8,128)(2,1)S(1)} collective-permute-done((bf16[64,1152]{1,0:T(8,128)(2,1)S(1)}, bf16[64,1152]{1,0:T(8,128)(2,1)S(1)}, u32[]{:S(2)}, u32[]{:S(2)}) %collective-permute-start.18) | collective-permute-done | bytes 147488 | tf_op jit(solution)/shard_map/rA1/ppermute | solution.py:28
  76.0 2.3 %collective-permute-done.19.refs_4_ = bf16[64,1152]{1,0:T(8,128)(2,1)S(1)} collective-permute-done((bf16[64,1152]{1,0:T(8,128)(2,1)S(1)}, bf16[64,1152]{1,0:T(8,128)(2,1)S(1)}, u32[]{:S(2)}, u32[]{:S(2)}) %collective-permute-start.19) | collective-permute-done | bytes 147488 | tf_op jit(solution)/shard_map/rA2/ppermute | solution.py:28
  78.3 1.5 %collective-permute-done.20.refs_5_ = bf16[64,1152]{1,0:T(8,128)(2,1)S(1)} collective-permute-done((bf16[64,1152]{1,0:T(8,128)(2,1)S(1)}, bf16[64,1152]{1,0:T(8,128)(2,1)S(1)}, u32[]{:S(2)}, u32[]{:S(2)}) %collective-permute-start.20) | collective-permute-done | bytes 147488 | tf_op jit(solution)/shard_map/rA3/ppermute | solution.py:28
  79.8 0.0 collective-permute-done.22.refs_9_
  79.8 1.1 %shard_map.73 = (f32[64,1152]{1,0:T(8,128)}, f32[64,1152]{1,0:T(8,128)}) custom-call(f32[64,1152]{1,0:T(8,128)S(1)} %get-tuple-element.28.refs_0_, f32[64,128]{1,0:T(8,128)S(1)} %get-tuple-element.29.refs_1_, f32[64,1152]{1,0:T(8,128)S(1)} %get-tuple-element.45.refs_2_, bf16[64,1152]{1,0:T(8,128)(2,1)S(1)} %collective-permute-done.18.refs_3_, ...), custom_call_target="tpu_custom_call" | custom-call | bytes 1024 | tf_op jit(solution)/shard_map/pallas_call | solution.py:55
  (4 shorter events, 0.1 us)
Async XLA Ops:
  0.6 12.8 %collective-permute-start.5 = (bf16[64,1152]{1,0:T(8,128)(2,1)}, bf16[64,1152]{1,0:T(8,128)(2,1)S(1)}, u32[]{:S(2)}, u32[]{:S(2)}) collective-permute-start(bf16[64,1152]{1,0:T(8,128)(2,1)} %refs_0_.1), channel_id=1, source_target_pairs={{0,32},{1,9},{2,34},{3,11},{4,36},{5,13},{6,38},{7,15},{128,160},{... | collective-permute-start | bytes 442376 | tf_op jit(solution)/shard_map/gA1/ppermute | solution.py:28
  2.2 17.0 %collective-permute-start.2 = (bf16[64,1152]{1,0:T(8,128)(2,1)}, bf16[64,1152]{1,0:T(8,128)(2,1)S(1)}, u32[]{:S(2)}, u32[]{:S(2)}) collective-permute-start(bf16[64,1152]{1,0:T(8,128)(2,1)} %refs_1_.1), channel_id=1, source_target_pairs={{0,133},{1,4},{2,135},{3,6},{4,1},{5,128},{6,3},{7,130},{128,5},{1... | collective-permute-start | bytes 442376 | tf_op jit(solution)/shard_map/gX2/ppermute | solution.py:28
  6.5 14.8 %collective-permute-start.1 = (bf16[64,1152]{1,0:T(8,128)(2,1)}, bf16[64,1152]{1,0:T(8,128)(2,1)S(1)}, u32[]{:S(2)}, u32[]{:S(2)}) collective-permute-start(bf16[64,1152]{1,0:T(8,128)(2,1)} %refs_1_.1), channel_id=1, source_target_pairs={{0,4},{1,133},{2,6},{3,135},{4,128},{5,1},{6,130},{7,3},{128,132},... | collective-permute-start | bytes 442376 | tf_op jit(solution)/shard_map/gZ2/ppermute | solution.py:28
  6.6 7.3 %collective-permute-start.7 = (bf16[64,1152]{1,0:T(8,128)(2,1)}, bf16[64,1152]{1,0:T(8,128)(2,1)S(1)}, u32[]{:S(2)}, u32[]{:S(2)}) collective-permute-start(bf16[64,1152]{1,0:T(8,128)(2,1)} %refs_0_.1), channel_id=1, source_target_pairs={{0,96},{1,25},{2,98},{3,27},{4,100},{5,29},{6,102},{7,31},{128,224... | collective-permute-start | bytes 442376 | tf_op jit(solution)/shard_map/gA3/ppermute | solution.py:28
  9.3 6.9 %collective-permute-start.6 = (bf16[64,1152]{1,0:T(8,128)(2,1)}, bf16[64,1152]{1,0:T(8,128)(2,1)S(1)}, u32[]{:S(2)}, u32[]{:S(2)}) collective-permute-start(bf16[64,1152]{1,0:T(8,128)(2,1)} %refs_0_.1), channel_id=1, source_target_pairs={{0,64},{1,17},{2,66},{3,19},{4,68},{5,21},{6,70},{7,23},{128,192},... | collective-permute-start | bytes 442376 | tf_op jit(solution)/shard_map/gA2/ppermute | solution.py:28
  11.4 0.9 %copy-start = (bf16[64,1152]{1,0:T(8,128)(2,1)S(1)}, bf16[64,1152]{1,0:T(8,128)(2,1)}, u32[]{:S(2)}) copy-start(bf16[64,1152]{1,0:T(8,128)(2,1)} %refs_0_.1) | copy-start | bytes 442372
  12.3 0.9 %copy-start.1 = (bf16[64,1152]{1,0:T(8,128)(2,1)S(1)}, bf16[64,1152]{1,0:T(8,128)(2,1)}, u32[]{:S(2)}) copy-start(bf16[64,1152]{1,0:T(8,128)(2,1)} %refs_1_.1) | copy-start | bytes 442372
  13.4 8.0 %collective-permute-start = (bf16[64,1152]{1,0:T(8,128)(2,1)S(1)}, bf16[64,1152]{1,0:T(8,128)(2,1)S(1)}, u32[]{:S(2)}, u32[]{:S(2)}) collective-permute-start(bf16[64,1152]{1,0:T(8,128)(2,1)S(1)} %get-tuple-element.30.refs_0_), channel_id=1, source_target_pairs={{0,1},{1,0},{2,3},{3,2},{4,5},{5,4},{6,7},{7,6},{128,129},{129,128... | collective-permute-start | bytes 442376 | tf_op jit(solution)/shard_map/gC/ppermute | solution.py:28
  16.2 20.0 %collective-permute-start.10 = (bf16[256,1152]{1,0:T(8,128)(2,1)S(1)}, bf16[256,1152]{1,0:T(8,128)(2,1)S(1)}, u32[]{:S(2)}, u32[]{:S(2)}) collective-permute-start(bf16[256,1152]{1,0:T(8,128)(2,1)S(1)} %shard_map.61.refs_0_), channel_id=1, source_target_pairs={{0,24},{1,97},{2,26},{3,99},{4,28},{5,101},{6,30},{7,103},{128,152... | collective-permute-start | bytes 1769480 | tf_op jit(solution)/shard_map/gB3/ppermute | solution.py:28
  17.9 18.3 %collective-permute-start.9 = (bf16[256,1152]{1,0:T(8,128)(2,1)S(1)}, bf16[256,1152]{1,0:T(8,128)(2,1)S(1)}, u32[]{:S(2)}, u32[]{:S(2)}) collective-permute-start(bf16[256,1152]{1,0:T(8,128)(2,1)S(1)} %shard_map.61.refs_0_), channel_id=1, source_target_pairs={{0,16},{1,65},{2,18},{3,67},{4,20},{5,69},{6,22},{7,71},{128,144},... | collective-permute-start | bytes 1769480 | tf_op jit(solution)/shard_map/gB2/ppermute | solution.py:28
  19.2 17.0 %collective-permute-start.8 = (bf16[256,1152]{1,0:T(8,128)(2,1)S(1)}, bf16[256,1152]{1,0:T(8,128)(2,1)S(1)}, u32[]{:S(2)}, u32[]{:S(2)}) collective-permute-start(bf16[256,1152]{1,0:T(8,128)(2,1)S(1)} %shard_map.61.refs_0_), channel_id=1, source_target_pairs={{0,8},{1,33},{2,10},{3,35},{4,12},{5,37},{6,14},{7,39},{128,136},{... | collective-permute-start | bytes 1769480 | tf_op jit(solution)/shard_map/gB1/ppermute | solution.py:28
  21.4 14.8 %collective-permute-start.3 = (bf16[256,1152]{1,0:T(8,128)(2,1)S(1)}, bf16[256,1152]{1,0:T(8,128)(2,1)S(1)}, u32[]{:S(2)}, u32[]{:S(2)}) collective-permute-start(bf16[256,1152]{1,0:T(8,128)(2,1)S(1)} %shard_map.60), channel_id=1, source_target_pairs={{0,2},{1,135},{2,4},{3,1},{4,6},{5,3},{6,128},{7,5},{128,130},{129... | collective-permute-start | bytes 1769480 | tf_op jit(solution)/shard_map/gZ13/ppermute | solution.py:28
  22.5 13.7 %collective-permute-start.4 = (bf16[64,1152]{1,0:T(8,128)(2,1)S(1)}, bf16[64,1152]{1,0:T(8,128)(2,1)S(1)}, u32[]{:S(2)}, u32[]{:S(2)}) collective-permute-start(bf16[64,1152]{1,0:T(8,128)(2,1)S(1)} %collective-permute-done.1.refs_2_), channel_id=1, source_target_pairs={{0,4},{1,133},{2,6},{3,135},{4,128},{5,1},{6,130},{7,3},{128,132},... | collective-permute-start | bytes 442376 | tf_op jit(solution)/shard_map/gZ4/ppermute | solution.py:28
  36.6 3.7 %collective-permute-start.11 = (bf16[512,1152]{1,0:T(8,128)(2,1)S(1)}, bf16[512,1152]{1,0:T(8,128)(2,1)S(1)}, u32[]{:S(2)}, u32[]{:S(2)}) collective-permute-start(bf16[512,1152]{1,0:T(8,128)(2,1)S(1)} %shard_map.64.refs_0_.refs_2_), channel_id=1, source_target_pairs={{0,1},{1,0},{2,3},{3,2},{4,5},{5,4},{6,7},{7,6},{128,129},{129,128... | collective-permute-start | bytes 3538952 | tf_op jit(solution)/shard_map/gS/ppermute | solution.py:28
  43.4 3.5 %collective-permute-start.15 = (bf16[512,1152]{1,0:T(8,128)(2,1)S(1)}, bf16[512,1152]{1,0:T(8,128)(2,1)S(1)}, u32[]{:S(2)}, u32[]{:S(2)}) collective-permute-start(bf16[512,1152]{1,0:T(8,128)(2,1)S(1)} %get-tuple-element.41), channel_id=1, source_target_pairs={{0,1},{1,0},{2,3},{3,2},{4,5},{5,4},{6,7},{7,6},{128,129},{129,128... | collective-permute-start | bytes 3538952 | tf_op jit(solution)/shard_map/rC/ppermute | solution.py:28
  47.2 14.0 %collective-permute-start.16 = (bf16[256,1152]{1,0:T(8,128)(2,1)S(1)}, bf16[256,1152]{1,0:T(8,128)(2,1)S(1)}, u32[]{:S(2)}, u32[]{:S(2)}) collective-permute-start(bf16[256,1152]{1,0:T(8,128)(2,1)S(1)} %get-tuple-element.43), channel_id=1, source_target_pairs={{0,134},{1,3},{2,0},{3,5},{4,2},{5,7},{6,4},{7,129},{128,6},{129,1... | collective-permute-start | bytes 1769480 | tf_op jit(solution)/shard_map/rZ13/ppermute | solution.py:28
  49.8 11.5 %collective-permute-start.17 = (bf16[64,1152]{1,0:T(8,128)(2,1)S(1)}, bf16[64,1152]{1,0:T(8,128)(2,1)S(1)}, u32[]{:S(2)}, u32[]{:S(2)}) collective-permute-start(bf16[64,1152]{1,0:T(8,128)(2,1)S(1)} %get-tuple-element.44), channel_id=1, source_target_pairs={{0,132},{1,5},{2,134},{3,7},{4,0},{5,129},{6,2},{7,131},{128,4},{1... | collective-permute-start | bytes 442376 | tf_op jit(solution)/shard_map/rZ4/ppermute | solution.py:28
  51.2 19.3 %collective-permute-start.14 = (bf16[256,1152]{1,0:T(8,128)(2,1)S(1)}, bf16[256,1152]{1,0:T(8,128)(2,1)S(1)}, u32[]{:S(2)}, u32[]{:S(2)}) collective-permute-start(bf16[256,1152]{1,0:T(8,128)(2,1)S(1)} %get-tuple-element.40.refs_2_), channel_id=1, source_target_pairs={{0,8},{1,33},{2,10},{3,35},{4,12},{5,37},{6,14},{7,39},{128,136},{... | collective-permute-start | bytes 1769480 | tf_op jit(solution)/shard_map/rB3/ppermute | solution.py:28
  52.5 18.0 %collective-permute-start.12 = (bf16[256,1152]{1,0:T(8,128)(2,1)S(1)}, bf16[256,1152]{1,0:T(8,128)(2,1)S(1)}, u32[]{:S(2)}, u32[]{:S(2)}) collective-permute-start(bf16[256,1152]{1,0:T(8,128)(2,1)S(1)} %get-tuple-element.38), channel_id=1, source_target_pairs={{0,24},{1,97},{2,26},{3,99},{4,28},{5,101},{6,30},{7,103},{128,152... | collective-permute-start | bytes 1769480 | tf_op jit(solution)/shard_map/rB1/ppermute | solution.py:28
  53.2 17.3 %collective-permute-start.13 = (bf16[256,1152]{1,0:T(8,128)(2,1)S(1)}, bf16[256,1152]{1,0:T(8,128)(2,1)S(1)}, u32[]{:S(2)}, u32[]{:S(2)}) collective-permute-start(bf16[256,1152]{1,0:T(8,128)(2,1)S(1)} %get-tuple-element.39), channel_id=1, source_target_pairs={{0,16},{1,65},{2,18},{3,67},{4,20},{5,69},{6,22},{7,71},{128,144},... | collective-permute-start | bytes 1769480 | tf_op jit(solution)/shard_map/rB2/ppermute | solution.py:28
  61.3 12.3 %collective-permute-start.21 = (bf16[128,1152]{1,0:T(8,128)(2,1)S(1)}, bf16[128,1152]{1,0:T(8,128)(2,1)S(1)}, u32[]{:S(2)}, u32[]{:S(2)}) collective-permute-start(bf16[128,1152]{1,0:T(8,128)(2,1)S(1)} %shard_map.69.refs_0_), channel_id=1, source_target_pairs={{0,132},{1,5},{2,134},{3,7},{4,0},{5,129},{6,2},{7,131},{128,4},{1... | collective-permute-start | bytes 884744 | tf_op jit(solution)/shard_map/rZ2/ppermute | solution.py:28
  70.8 5.2 %collective-permute-start.18 = (bf16[64,1152]{1,0:T(8,128)(2,1)S(1)}, bf16[64,1152]{1,0:T(8,128)(2,1)S(1)}, u32[]{:S(2)}, u32[]{:S(2)}) collective-permute-start(bf16[64,1152]{1,0:T(8,128)(2,1)S(1)} %get-tuple-element.46), channel_id=1, source_target_pairs={{0,96},{1,25},{2,98},{3,27},{4,100},{5,29},{6,102},{7,31},{128,224... | collective-permute-start | bytes 442376 | tf_op jit(solution)/shard_map/rA1/ppermute | solution.py:28
  71.6 6.8 %collective-permute-start.19 = (bf16[64,1152]{1,0:T(8,128)(2,1)S(1)}, bf16[64,1152]{1,0:T(8,128)(2,1)S(1)}, u32[]{:S(2)}, u32[]{:S(2)}) collective-permute-start(bf16[64,1152]{1,0:T(8,128)(2,1)S(1)} %get-tuple-element.47), channel_id=1, source_target_pairs={{0,64},{1,17},{2,66},{3,19},{4,68},{5,21},{6,70},{7,23},{128,192},... | collective-permute-start | bytes 442376 | tf_op jit(solution)/shard_map/rA2/ppermute | solution.py:28
  72.3 7.5 %collective-permute-start.20 = (bf16[64,1152]{1,0:T(8,128)(2,1)S(1)}, bf16[64,1152]{1,0:T(8,128)(2,1)S(1)}, u32[]{:S(2)}, u32[]{:S(2)}) collective-permute-start(bf16[64,1152]{1,0:T(8,128)(2,1)S(1)} %get-tuple-element.48), channel_id=1, source_target_pairs={{0,32},{1,9},{2,34},{3,11},{4,36},{5,13},{6,38},{7,15},{128,160},{... | collective-permute-start | bytes 442376 | tf_op jit(solution)/shard_map/rA3/ppermute | solution.py:28
  73.7 6.1 %collective-permute-start.22 = (bf16[64,1152]{1,0:T(8,128)(2,1)S(1)}, bf16[64,1152]{1,0:T(8,128)(2,1)S(1)}, u32[]{:S(2)}, u32[]{:S(2)}) collective-permute-start(bf16[64,1152]{1,0:T(8,128)(2,1)S(1)} %get-tuple-element.53), channel_id=1, source_target_pairs={{0,1},{1,0},{2,3},{3,2},{4,5},{5,4},{6,7},{7,6},{128,129},{129,128... | collective-permute-start | bytes 442376 | tf_op jit(solution)/shard_map/rS/ppermute | solution.py:28

commit v6 on v5

--- a/solution.py
+++ b/solution.py
@@ -48,26 +48,25 @@
     return (x, y, z, 1 - c)
 
 
-def call(kernel, outs, arrays, last_scalars=(), ties=(), flops=0, limit=8):
+def call(kernel, outs, arrays, ties=(), flops=0, limit=8):
     vmem = pl.BlockSpec(memory_space=pltpu.VMEM)
-    n_in = len(arrays) + len(last_scalars)
-    specs = [vmem] * len(arrays) + [pl.BlockSpec(memory_space=pltpu.SMEM)] * len(last_scalars)
+    n_in = len(arrays)
     return pl.pallas_call(
         lambda *refs: kernel(*refs[:n_in], *refs[n_in + len(ties):]),
         out_shape=tuple(jax.ShapeDtypeStruct(shape, dtype) for shape, dtype in outs),
-        in_specs=specs + [pl.BlockSpec(memory_space=pl.ANY)] * len(ties),
+        in_specs=[vmem] * n_in + [pl.BlockSpec(memory_space=pl.ANY)] * len(ties),
         out_specs=tuple([vmem] * len(outs)),
         compiler_params=pltpu.CompilerParams(vmem_limit_bytes=limit * 1024 * 1024),
         cost_estimate=pl.CostEstimate(flops=flops, bytes_accessed=1024, transcendentals=0),
-    )(*arrays, *last_scalars, *ties)
+    )(*arrays, *ties)
 
 
 def token_kernel(token_ref):
     token_ref[...] = jnp.zeros_like(token_ref)
 
 
-def token(value):
-    return call(token_kernel, [((8, 128), F32)], [], ties=[value], flops=40_000_000_000, limit=1)[0]
+def token(*values):
+    return call(token_kernel, [((8, 128), F32)], [], ties=values, flops=40_000_000_000, limit=1)[0]
 
 
 def unit_rows(raw):
@@ -81,18 +80,32 @@
     return (grad_unit - unit * along) * inverse
 
 
-def own_kernel(img_ref, txt_ref, log_ref, bias_ref, *outs):
-    *outs, scal_ref = outs
-    for n, raw_ref in enumerate((img_ref, txt_ref)):
-        copy_ref, unit_ref, inv_ref = outs[3 * n:3 * n + 3]
+def own_kernel(img_hbm, txt_hbm, *refs):
+    *outs, sems = refs
+    pairs = ((img_hbm, outs[0]), (txt_hbm, outs[3]))
+    copies = [pltpu.make_async_copy(src, dst, sems.at[n]) for n, (src, dst) in enumerate(pairs)]
+    for copy in copies:
+        copy.start()
+    for copy in copies:
+        copy.wait()
+    for raw_ref, unit_ref, inv_ref in (outs[:3], outs[3:]):
         unit, inverse = unit_rows(raw_ref[...])
-        copy_ref[...] = raw_ref[...]
         unit_ref[...] = unit
         inv_ref[...] = jnp.broadcast_to(inverse, inv_ref.shape)
-    temp = jnp.exp(jnp.full((1, 128), log_ref[0], F32))
-    scal_ref[0:1, :] = temp
-    scal_ref[1:2, :] = -LOG2E * temp
-    scal_ref[2:3, :] = jnp.full((1, 128), -LOG2E * bias_ref[0], F32)
+
+
+def own_rows(images, texts, tie):
+    own, dim = images.shape
+    outs = [((own, dim), BF16), ((own, dim), F32), ((own, 128), F32)] * 2
+    return pl.pallas_call(
+        lambda tie_ref, *refs: own_kernel(*refs),
+        out_shape=tuple(jax.ShapeDtypeStruct(shape, dtype) for shape, dtype in outs),
+        in_specs=[pl.BlockSpec(memory_space=pl.ANY)] * 3,
+        out_specs=tuple([pl.BlockSpec(memory_space=pltpu.VMEM)] * len(outs)),
+        scratch_shapes=[pltpu.SemaphoreType.DMA((2,))],
+        compiler_params=pltpu.CompilerParams(vmem_limit_bytes=8 * 1024 * 1024),
+        cost_estimate=pl.CostEstimate(flops=0, bytes_accessed=1024, transcendentals=0),
+    )(tie, images, texts)
 
 
 def stack_kernel(*refs):
@@ -121,6 +134,14 @@
 def rounded(parts, ties=()):
     rows, dim = sum(p.shape[0] for p in parts), parts[0].shape[1]
     return call(lambda *refs: round_kernel(64, *refs), [((rows, dim), BF16)], parts, ties=ties)[0]
+
+
+def scalar_kernel(log_ref, bias_ref, scal_ref):
+    temp = jnp.exp(jnp.broadcast_to(log_ref[...], (1, 128)))
+    scal_ref[...] = jnp.zeros_like(scal_ref)
+    scal_ref[0:1, :] = temp
+    scal_ref[1:2, :] = -LOG2E * temp
+    scal_ref[2:3, :] = jnp.broadcast_to(-LOG2E * bias_ref[...], (1, 128))
 
 
 def sigmoid_weights(power, scale):
@@ -221,22 +242,22 @@
 
 def local(images, texts, log_temp, bias):
     own, dim = images.shape
-    per_row = [((own, dim), BF16), ((own, dim), F32), ((own, 128), F32)]
 
     side = [shift(images, first(k), "gA%d" % k) for k in (1, 2, 3)]
     line2 = shift(texts, line(2), "gZ2")
     cross2 = shift(texts, cross(2), "gX2")
-    img_own, img_unit, inv_img, txt_own, txt_unit, inv_txt, scalars = call(
-        own_kernel, per_row * 2 + [((8, 128), F32)], [images, texts], last_scalars=[log_temp, bias]
-    )
-    swapped = shift(txt_own, other, "gC")
-    group = stack([img_own, *side])
+    swapped = shift(texts, other, "gC")
+    img_own, img_unit, inv_img, txt_own, txt_unit, inv_txt = own_rows(images, texts, swapped)
+    group = stack([img_own, *side], [token(line2, cross2)])
     send13 = stack([txt_own, swapped, line2, cross2])
     far = [shift(group, second(k), "gB%d" % k) for k in (1, 2, 3)]
     near13 = shift(send13, line(1), "gZ13")
     near4 = shift(line2, line(2), "gZ4")
-    first_token = token(group)
-    group = rounded([group])
+    first_token = token(near13)
+    (scalars,) = call(
+        scalar_kernel, [((8, 128), F32)], [log_temp.reshape(1, 1), bias.reshape(1, 1)], [near13]
+    )
+    group = rounded([group], [scalars])
     mine = rounded([txt_own, near13, line2, cross2, near4], [group, first_token, *far])
     theirs = shift(mine, other, "gS")
 
@@ -263,7 +284,7 @@
     )
     got13 = shift(part13, line(-1), "rZ13")
     got4 = shift(part4, line(-2), "rZ4")
-    (middle,) = call(middle_kernel, [((2 * own, dim), BF16)], [part2, got13, got4])
+    (middle,) = call(middle_kernel, [((2 * own, dim), BF16)], [part2, got13, got4], [token(got13)])
     got2 = shift(middle, line(-2), "rZ2")
     txt_sum, txt_send = call(landed_kernel, [((own, dim), F32), ((own, dim), BF16)], [total_own, got13, got2])
     txt_last = shift(txt_send, other, "rS")

time: 81 us -> 85.3 us (1.053)
  starting transfers between devices: 32.7 us -> 35.2 us
  waiting for transfers between devices: 32.3 us -> 33.6 us
    ppermute x23, starting transfers between devices: 32.7 us -> 35.2 us  [shift(): return lax.ppermute(values, AXES, pairs)]
    ppermute x23, waiting for transfers between devices: 32.3 us -> 33.6 us  [shift(): return lax.ppermute(values, AXES, pairs)]
    pallas_call x15 -> x17, Pallas kernels: 12 us -> 12 us  [call(): pl.pallas_call(lambda *refs: kernel(*refs[:n_in], *refs[n_in + len(ties):...]
  transfers between devices with their start and end apart: 23 -> 23, of which waited for: 8 -> 12; matrix products, arithmetic and copies ran while one was open for 0% -> 0% of each run, Pallas kernels for 9% -> 9%
where the time goes in v6:
time: 85.3 us; the launch traced here: 85.1 us
  starting transfers between devices  35.2 us (41%)
  waiting for transfers between devices  33.6 us (39%)
  Pallas kernels  12.5 us (15%)
  between operations  2.08 us (2%)
  local copies, waits for them, and re-layouts  1.82 us (2%)
    ppermute x23, starting transfers between devices, shift(): return lax.ppermute(values, AXES, pairs)  35.2 us
    ppermute x23, waiting for transfers between devices, shift(): return lax.ppermute(values, AXES, pairs)  33.6 us
    pallas_call x17, Pallas kernels, call(): pl.pallas_call(lambda *refs: kernel(*refs[:n_in], *refs[n_in + len(ties):...  12 us
    unnamed x4, local copies, waits for them, and re-layouts  1.82 us
  transfers between devices with their start and end apart: 23, of which 12 were waited for; matrix products, arithmetic and copies ran while one was open for 0% of the time, Pallas kernels for 9%

profile of v6, /device:TPU:24, one launch (start us, length us, event | category | flops | bytes accessed | tf_op | source)
XLA Modules:
  0.0 85.1 jit_solution(9802674282085923277)
XLA Ops:
  0.6 0.1 collective-permute-start
  0.7 6.4 %collective-permute-start.2 = (bf16[64,1152]{1,0:T(8,128)(2,1)}, bf16[64,1152]{1,0:T(8,128)(2,1)S(1)}, u32[]{:S(2)}, u32[]{:S(2)}) collective-permute-start(bf16[64,1152]{1,0:T(8,128)(2,1)} %refs_1_.1), channel_id=1, source_target_pairs={{0,133},{1,4},{2,135},{3,6},{4,1},{5,128},{6,3},{7,130},{128,5},{1... | collective-permute-start | bytes 442376 | tf_op jit(solution)/shard_map/gX2/ppermute | solution.py:28
  7.1 0.0 collective-permute-start.1
  7.1 1.5 %collective-permute-start.5 = (bf16[64,1152]{1,0:T(8,128)(2,1)}, bf16[64,1152]{1,0:T(8,128)(2,1)S(1)}, u32[]{:S(2)}, u32[]{:S(2)}) collective-permute-start(bf16[64,1152]{1,0:T(8,128)(2,1)} %refs_0_.1), channel_id=1, source_target_pairs={{0,32},{1,9},{2,34},{3,11},{4,36},{5,13},{6,38},{7,15},{128,160},{... | collective-permute-start | bytes 442376 | tf_op jit(solution)/shard_map/gA1/ppermute | solution.py:28
  8.6 1.7 %collective-permute-start.7 = (bf16[64,1152]{1,0:T(8,128)(2,1)}, bf16[64,1152]{1,0:T(8,128)(2,1)S(1)}, u32[]{:S(2)}, u32[]{:S(2)}) collective-permute-start(bf16[64,1152]{1,0:T(8,128)(2,1)} %refs_0_.1), channel_id=1, source_target_pairs={{0,96},{1,25},{2,98},{3,27},{4,100},{5,29},{6,102},{7,31},{128,224... | collective-permute-start | bytes 442376 | tf_op jit(solution)/shard_map/gA3/ppermute | solution.py:28
  11.7 0.0 collective-permute-done.tie_ref.refs_1_
  11.7 1.9 %collective-permute-start.6 = (bf16[64,1152]{1,0:T(8,128)(2,1)}, bf16[64,1152]{1,0:T(8,128)(2,1)S(1)}, u32[]{:S(2)}, u32[]{:S(2)}) collective-permute-start(bf16[64,1152]{1,0:T(8,128)(2,1)} %refs_0_.1), channel_id=1, source_target_pairs={{0,64},{1,17},{2,66},{3,19},{4,68},{5,21},{6,70},{7,23},{128,192},... | collective-permute-start | bytes 442376 | tf_op jit(solution)/shard_map/gA2/ppermute | solution.py:28
  13.6 0.0 copy-start
  13.6 0.9 %copy-done = bf16[64,1152]{1,0:T(8,128)(2,1)S(1)} copy-done((bf16[64,1152]{1,0:T(8,128)(2,1)S(1)}, bf16[64,1152]{1,0:T(8,128)(2,1)}, u32[]{:S(2)}) %copy-start) | copy-done | bytes 147480
  14.5 0.0 copy-start.1
  14.5 0.9 %copy-done.1 = bf16[64,1152]{1,0:T(8,128)(2,1)S(1)} copy-done((bf16[64,1152]{1,0:T(8,128)(2,1)S(1)}, bf16[64,1152]{1,0:T(8,128)(2,1)}, u32[]{:S(2)}) %copy-start.1) | copy-done | bytes 147480
  15.4 0.5 shard_map.59
  15.9 0.0 collective-permute-done.2.refs_3_.refs_1_
  15.9 0.6 collective-permute-done.1.refs_2_.refs_0_
  16.6 0.5 collective-permute-start.3
  17.1 0.0 collective-permute-done.5.refs_1_
  17.1 0.0 collective-permute-done.7.refs_3_
  17.1 1.5 %collective-permute-done.6.refs_2_ = bf16[64,1152]{1,0:T(8,128)(2,1)S(1)} collective-permute-done((bf16[64,1152]{1,0:T(8,128)(2,1)}, bf16[64,1152]{1,0:T(8,128)(2,1)S(1)}, u32[]{:S(2)}, u32[]{:S(2)}) %collective-permute-start.6) | collective-permute-done | bytes 147488 | tf_op jit(solution)/shard_map/gA2/ppermute | solution.py:28
  18.7 0.8 collective-permute-start.10
  19.5 0.9 %collective-permute-start.9 = (bf16[256,1152]{1,0:T(8,128)(2,1)S(1)}, bf16[256,1152]{1,0:T(8,128)(2,1)S(1)}, u32[]{:S(2)}, u32[]{:S(2)}) collective-permute-start(bf16[256,1152]{1,0:T(8,128)(2,1)S(1)} %shard_map.62.refs_0_), channel_id=1, source_target_pairs={{0,16},{1,65},{2,18},{3,67},{4,20},{5,69},{6,22},{7,71},{128,144},... | collective-permute-start | bytes 1769480 | tf_op jit(solution)/shard_map/gB2/ppermute | solution.py:28
  20.4 2.2 %collective-permute-start.8 = (bf16[256,1152]{1,0:T(8,128)(2,1)S(1)}, bf16[256,1152]{1,0:T(8,128)(2,1)S(1)}, u32[]{:S(2)}, u32[]{:S(2)}) collective-permute-start(bf16[256,1152]{1,0:T(8,128)(2,1)S(1)} %shard_map.62.refs_0_), channel_id=1, source_target_pairs={{0,8},{1,33},{2,10},{3,35},{4,12},{5,37},{6,14},{7,39},{128,136},{... | collective-permute-start | bytes 1769480 | tf_op jit(solution)/shard_map/gB1/ppermute | solution.py:28
  22.6 1.5 %collective-permute-start.4 = (bf16[64,1152]{1,0:T(8,128)(2,1)S(1)}, bf16[64,1152]{1,0:T(8,128)(2,1)S(1)}, u32[]{:S(2)}, u32[]{:S(2)}) collective-permute-start(bf16[64,1152]{1,0:T(8,128)(2,1)S(1)} %collective-permute-done.1.refs_2_.refs_0_), channel_id=1, source_target_pairs={{0,4},{1,133},{2,6},{3,135},{4,128},{5,1},{6,130},{7,3},{128,132},... | collective-permute-start | bytes 442376 | tf_op jit(solution)/shard_map/gZ4/ppermute | solution.py:28
  24.1 3.6 %collective-permute-done.3.refs_2_.refs_0_.refs_1_ = bf16[256,1152]{1,0:T(8,128)(2,1)S(1)} collective-permute-done((bf16[256,1152]{1,0:T(8,128)(2,1)S(1)}, bf16[256,1152]{1,0:T(8,128)(2,1)S(1)}, u32[]{:S(2)}, u32[]{:S(2)}) %collective-permute-start.3) | collective-permute-done | bytes 589856 | tf_op jit(solution)/shard_map/gZ13/ppermute | solution.py:28
  27.8 0.1 shard_map.63.refs_1_
  27.9 0.2 shard_map.64.refs_5_.refs_2_
  28.1 3.2 %collective-permute-done.4.refs_4_ = bf16[64,1152]{1,0:T(8,128)(2,1)S(1)} collective-permute-done((bf16[64,1152]{1,0:T(8,128)(2,1)S(1)}, bf16[64,1152]{1,0:T(8,128)(2,1)S(1)}, u32[]{:S(2)}, u32[]{:S(2)}) %collective-permute-start.4) | collective-permute-done | bytes 147488 | tf_op jit(solution)/shard_map/gZ4/ppermute | solution.py:28
  31.3 4.9 %collective-permute-done.10.refs_9_.refs_5_ = bf16[256,1152]{1,0:T(8,128)(2,1)S(1)} collective-permute-done((bf16[256,1152]{1,0:T(8,128)(2,1)S(1)}, bf16[256,1152]{1,0:T(8,128)(2,1)S(1)}, u32[]{:S(2)}, u32[]{:S(2)}) %collective-permute-start.10) | collective-permute-done | bytes 589856 | tf_op jit(solution)/shard_map/gB3/ppermute | solution.py:28
  36.2 0.0 collective-permute-done.9.refs_8_.refs_4_
  36.2 0.9 %collective-permute-done.8.refs_7_.refs_3_ = bf16[256,1152]{1,0:T(8,128)(2,1)S(1)} collective-permute-done((bf16[256,1152]{1,0:T(8,128)(2,1)S(1)}, bf16[256,1152]{1,0:T(8,128)(2,1)S(1)}, u32[]{:S(2)}, u32[]{:S(2)}) %collective-permute-start.8) | collective-permute-done | bytes 589856 | tf_op jit(solution)/shard_map/gB1/ppermute | solution.py:28
  37.1 0.4 shard_map.66.refs_0_.refs_2_
  37.4 0.3 collective-permute-start.11
  37.7 3.5 %shard_map.67 = (bf16[1024,512]{1,0:T(8,128)(2,1)S(1)}, bf16[1024,1152]{1,0:T(8,128)(2,1)S(1)}, bf16[512,1152]{1,0:T(8,128)(2,1)S(1)}) custom-call(bf16[512,1152]{1,0:T(8,128)(2,1)S(1)} %shard_map.66.refs_0_.refs_2_, f32[8,128]{1,0:T(8,128)S(1)} %shard_map.63.refs_1_, bf16[256,1152]{1,0:T(8,128)(2,1)S(1)} %shard_map.64.refs_5_.refs_2_, ...), custom_call_target="tpu_custom_call" | custom-call | flops 2415919104 | bytes 1024 | tf_op jit(solution)/shard_map/pallas_call | solution.py:54
  41.2 0.0 collective-permute-done.11.refs_0_.refs_3_
  41.2 3.0 %shard_map.68 = (bf16[1024,512]{1,0:T(8,128)(2,1)S(1)}, bf16[512,1152]{1,0:T(8,128)(2,1)S(1)}) custom-call(bf16[512,1152]{1,0:T(8,128)(2,1)S(1)} %collective-permute-done.11.refs_0_.refs_3_, f32[8,128]{1,0:T(8,128)S(1)} %shard_map.63.refs_1_, bf16[1024,1152]{1,0:T(8,128)(2,1)S(1)} %get-tuple-element.32.refs_2_, ...), custom_call_target="tpu_custom_call" | custom-call | flops 2415919104 | bytes 1024 | tf_op jit(solution)/shard_map/pallas_call | solution.py:54
  44.2 0.6 collective-permute-start.15
  44.8 2.9 %shard_map.69 = (f32[256,1152]{1,0:T(8,128)S(1)}, bf16[256,1152]{1,0:T(8,128)(2,1)S(1)}, bf16[256,1152]{1,0:T(8,128)(2,1)S(1)}, bf16[256,1152]{1,0:T(8,128)(2,1)S(1)}) custom-call(bf16[1024,512]{1,0:T(8,128)(2,1)S(1)} %get-tuple-element.31.refs_0_, bf16[1024,512]{1,0:T(8,128)(2,1)S(1)} %get-tuple-element.34.refs_1_, ...), custom_call_target="tpu_custom_call" | custom-call | flops 2415919104 | bytes 1024 | tf_op jit(solution)/shard_map/pallas_call | solution.py:54
  47.8 0.0 collective-permute-done.15.refs_1_
  47.8 0.3 shard_map.70
  48.1 3.8 %collective-permute-start.16 = (bf16[256,1152]{1,0:T(8,128)(2,1)S(1)}, bf16[256,1152]{1,0:T(8,128)(2,1)S(1)}, u32[]{:S(2)}, u32[]{:S(2)}) collective-permute-start(bf16[256,1152]{1,0:T(8,128)(2,1)S(1)} %get-tuple-element.41), channel_id=1, source_target_pairs={{0,134},{1,3},{2,0},{3,5},{4,2},{5,7},{6,4},{7,129},{128,6},{129,1... | collective-permute-start | bytes 1769480 | tf_op jit(solution)/shard_map/rZ13/ppermute | solution.py:28
  51.8 2.6 %collective-permute-start.14 = (bf16[256,1152]{1,0:T(8,128)(2,1)S(1)}, bf16[256,1152]{1,0:T(8,128)(2,1)S(1)}, u32[]{:S(2)}, u32[]{:S(2)}) collective-permute-start(bf16[256,1152]{1,0:T(8,128)(2,1)S(1)} %get-tuple-element.38.refs_2_), channel_id=1, source_target_pairs={{0,8},{1,33},{2,10},{3,35},{4,12},{5,37},{6,14},{7,39},{128,136},{... | collective-permute-start | bytes 1769480 | tf_op jit(solution)/shard_map/rB3/ppermute | solution.py:28
  54.5 0.0 collective-permute-start.12
  54.5 1.5 %collective-permute-start.13 = (bf16[256,1152]{1,0:T(8,128)(2,1)S(1)}, bf16[256,1152]{1,0:T(8,128)(2,1)S(1)}, u32[]{:S(2)}, u32[]{:S(2)}) collective-permute-start(bf16[256,1152]{1,0:T(8,128)(2,1)S(1)} %get-tuple-element.37), channel_id=1, source_target_pairs={{0,16},{1,65},{2,18},{3,67},{4,20},{5,69},{6,22},{7,71},{128,144},... | collective-permute-start | bytes 1769480 | tf_op jit(solution)/shard_map/rB2/ppermute | solution.py:28
  55.9 0.6 collective-permute-start.17
  56.5 3.4 %collective-permute-done.16.refs_0_.refs_1_ = bf16[256,1152]{1,0:T(8,128)(2,1)S(1)} collective-permute-done((bf16[256,1152]{1,0:T(8,128)(2,1)S(1)}, bf16[256,1152]{1,0:T(8,128)(2,1)S(1)}, u32[]{:S(2)}, u32[]{:S(2)}) %collective-permute-start.16) | collective-permute-done | bytes 589856 | tf_op jit(solution)/shard_map/rZ13/ppermute | solution.py:28
  60.0 2.4 %collective-permute-done.17.refs_2_ = bf16[64,1152]{1,0:T(8,128)(2,1)S(1)} collective-permute-done((bf16[64,1152]{1,0:T(8,128)(2,1)S(1)}, bf16[64,1152]{1,0:T(8,128)(2,1)S(1)}, u32[]{:S(2)}, u32[]{:S(2)}) %collective-permute-start.17) | collective-permute-done | bytes 147488 | tf_op jit(solution)/shard_map/rZ4/ppermute | solution.py:28
  62.4 0.1 shard_map.72.refs_0_
  62.5 4.9 %collective-permute-start.21 = (bf16[128,1152]{1,0:T(8,128)(2,1)S(1)}, bf16[128,1152]{1,0:T(8,128)(2,1)S(1)}, u32[]{:S(2)}, u32[]{:S(2)}) collective-permute-start(bf16[128,1152]{1,0:T(8,128)(2,1)S(1)} %shard_map.72.refs_0_), channel_id=1, source_target_pairs={{0,132},{1,5},{2,134},{3,7},{4,0},{5,129},{6,2},{7,131},{128,4},{1... | collective-permute-start | bytes 884744 | tf_op jit(solution)/shard_map/rZ2/ppermute | solution.py:28
  67.4 7.7 %collective-permute-done.12.refs_1_ = bf16[256,1152]{1,0:T(8,128)(2,1)S(1)} collective-permute-done((bf16[256,1152]{1,0:T(8,128)(2,1)S(1)}, bf16[256,1152]{1,0:T(8,128)(2,1)S(1)}, u32[]{:S(2)}, u32[]{:S(2)}) %collective-permute-start.12) | collective-permute-done | bytes 589856 | tf_op jit(solution)/shard_map/rB1/ppermute | solution.py:28
  75.0 0.0 collective-permute-done.13.refs_2_
  75.0 0.0 collective-permute-done.14.refs_3_
  75.0 0.3 shard_map.74
  75.3 0.1 collective-permute-start.18
  75.4 2.3 %collective-permute-start.19 = (bf16[64,1152]{1,0:T(8,128)(2,1)S(1)}, bf16[64,1152]{1,0:T(8,128)(2,1)S(1)}, u32[]{:S(2)}, u32[]{:S(2)}) collective-permute-start(bf16[64,1152]{1,0:T(8,128)(2,1)S(1)} %get-tuple-element.45), channel_id=1, source_target_pairs={{0,64},{1,17},{2,66},{3,19},{4,68},{5,21},{6,70},{7,23},{128,192},... | collective-permute-start | bytes 442376 | tf_op jit(solution)/shard_map/rA2/ppermute | solution.py:28
  77.7 0.9 %collective-permute-start.20 = (bf16[64,1152]{1,0:T(8,128)(2,1)S(1)}, bf16[64,1152]{1,0:T(8,128)(2,1)S(1)}, u32[]{:S(2)}, u32[]{:S(2)}) collective-permute-start(bf16[64,1152]{1,0:T(8,128)(2,1)S(1)} %get-tuple-element.46), channel_id=1, source_target_pairs={{0,32},{1,9},{2,34},{3,11},{4,36},{5,13},{6,38},{7,15},{128,160},{... | collective-permute-start | bytes 442376 | tf_op jit(solution)/shard_map/rA3/ppermute | solution.py:28
  78.6 0.0 collective-permute-done.21.refs_2_
  78.6 0.1 shard_map.75
  78.7 0.1 collective-permute-start.22
  78.8 1.7 %collective-permute-done.18.refs_3_ = bf16[64,1152]{1,0:T(8,128)(2,1)S(1)} collective-permute-done((bf16[64,1152]{1,0:T(8,128)(2,1)S(1)}, bf16[64,1152]{1,0:T(8,128)(2,1)S(1)}, u32[]{:S(2)}, u32[]{:S(2)}) %collective-permute-start.18) | collective-permute-done | bytes 147488 | tf_op jit(solution)/shard_map/rA1/ppermute | solution.py:28
  80.5 1.6 %collective-permute-done.19.refs_4_ = bf16[64,1152]{1,0:T(8,128)(2,1)S(1)} collective-permute-done((bf16[64,1152]{1,0:T(8,128)(2,1)S(1)}, bf16[64,1152]{1,0:T(8,128)(2,1)S(1)}, u32[]{:S(2)}, u32[]{:S(2)}) %collective-permute-start.19) | collective-permute-done | bytes 147488 | tf_op jit(solution)/shard_map/rA2/ppermute | solution.py:28
  82.1 1.9 %collective-permute-done.20.refs_5_ = bf16[64,1152]{1,0:T(8,128)(2,1)S(1)} collective-permute-done((bf16[64,1152]{1,0:T(8,128)(2,1)S(1)}, bf16[64,1152]{1,0:T(8,128)(2,1)S(1)}, u32[]{:S(2)}, u32[]{:S(2)}) %collective-permute-start.20) | collective-permute-done | bytes 147488 | tf_op jit(solution)/shard_map/rA3/ppermute | solution.py:28
  84.1 0.0 collective-permute-done.22.refs_9_
  84.1 1.1 %shard_map.76 = (f32[64,1152]{1,0:T(8,128)}, f32[64,1152]{1,0:T(8,128)}) custom-call(f32[64,1152]{1,0:T(8,128)S(1)} %get-tuple-element.27.refs_0_, f32[64,128]{1,0:T(8,128)S(1)} %get-tuple-element.28.refs_1_, f32[64,1152]{1,0:T(8,128)S(1)} %get-tuple-element.43.refs_2_, bf16[64,1152]{1,0:T(8,128)(2,1)S(1)} %collective-permute-done.18.refs_3_, ...), custom_call_target="tpu_custom_call" | custom-call | bytes 1024 | tf_op jit(solution)/shard_map/pallas_call | solution.py:54
  (6 shorter events, 0.1 us)
Async XLA Ops:
  0.6 11.0 %collective-permute-start = (bf16[64,1152]{1,0:T(8,128)(2,1)}, bf16[64,1152]{1,0:T(8,128)(2,1)S(1)}, u32[]{:S(2)}, u32[]{:S(2)}) collective-permute-start(bf16[64,1152]{1,0:T(8,128)(2,1)} %refs_1_.1), channel_id=1, source_target_pairs={{0,1},{1,0},{2,3},{3,2},{4,5},{5,4},{6,7},{7,6},{128,129},{129,128... | collective-permute-start | bytes 442376 | tf_op jit(solution)/shard_map/gC/ppermute | solution.py:28
  0.7 15.2 %collective-permute-start.2 = (bf16[64,1152]{1,0:T(8,128)(2,1)}, bf16[64,1152]{1,0:T(8,128)(2,1)S(1)}, u32[]{:S(2)}, u32[]{:S(2)}) collective-permute-start(bf16[64,1152]{1,0:T(8,128)(2,1)} %refs_1_.1), channel_id=1, source_target_pairs={{0,133},{1,4},{2,135},{3,6},{4,1},{5,128},{6,3},{7,130},{128,5},{1... | collective-permute-start | bytes 442376 | tf_op jit(solution)/shard_map/gX2/ppermute | solution.py:28
  7.1 9.4 %collective-permute-start.1 = (bf16[64,1152]{1,0:T(8,128)(2,1)}, bf16[64,1152]{1,0:T(8,128)(2,1)S(1)}, u32[]{:S(2)}, u32[]{:S(2)}) collective-permute-start(bf16[64,1152]{1,0:T(8,128)(2,1)} %refs_1_.1), channel_id=1, source_target_pairs={{0,4},{1,133},{2,6},{3,135},{4,128},{5,1},{6,130},{7,3},{128,132},... | collective-permute-start | bytes 442376 | tf_op jit(solution)/shard_map/gZ2/ppermute | solution.py:28
  7.1 10.0 %collective-permute-start.5 = (bf16[64,1152]{1,0:T(8,128)(2,1)}, bf16[64,1152]{1,0:T(8,128)(2,1)S(1)}, u32[]{:S(2)}, u32[]{:S(2)}) collective-permute-start(bf16[64,1152]{1,0:T(8,128)(2,1)} %refs_0_.1), channel_id=1, source_target_pairs={{0,32},{1,9},{2,34},{3,11},{4,36},{5,13},{6,38},{7,15},{128,160},{... | collective-permute-start | bytes 442376 | tf_op jit(solution)/shard_map/gA1/ppermute | solution.py:28
  8.6 8.5 %collective-permute-start.7 = (bf16[64,1152]{1,0:T(8,128)(2,1)}, bf16[64,1152]{1,0:T(8,128)(2,1)S(1)}, u32[]{:S(2)}, u32[]{:S(2)}) collective-permute-start(bf16[64,1152]{1,0:T(8,128)(2,1)} %refs_0_.1), channel_id=1, source_target_pairs={{0,96},{1,25},{2,98},{3,27},{4,100},{5,29},{6,102},{7,31},{128,224... | collective-permute-start | bytes 442376 | tf_op jit(solution)/shard_map/gA3/ppermute | solution.py:28
  11.7 6.9 %collective-permute-start.6 = (bf16[64,1152]{1,0:T(8,128)(2,1)}, bf16[64,1152]{1,0:T(8,128)(2,1)S(1)}, u32[]{:S(2)}, u32[]{:S(2)}) collective-permute-start(bf16[64,1152]{1,0:T(8,128)(2,1)} %refs_0_.1), channel_id=1, source_target_pairs={{0,64},{1,17},{2,66},{3,19},{4,68},{5,21},{6,70},{7,23},{128,192},... | collective-permute-start | bytes 442376 | tf_op jit(solution)/shard_map/gA2/ppermute | solution.py:28
  13.6 0.9 %copy-start = (bf16[64,1152]{1,0:T(8,128)(2,1)S(1)}, bf16[64,1152]{1,0:T(8,128)(2,1)}, u32[]{:S(2)}) copy-start(bf16[64,1152]{1,0:T(8,128)(2,1)} %refs_1_.1) | copy-start | bytes 442372
  14.5 0.9 %copy-start.1 = (bf16[64,1152]{1,0:T(8,128)(2,1)S(1)}, bf16[64,1152]{1,0:T(8,128)(2,1)}, u32[]{:S(2)}) copy-start(bf16[64,1152]{1,0:T(8,128)(2,1)} %refs_0_.1) | copy-start | bytes 442372
  16.6 11.2 %collective-permute-start.3 = (bf16[256,1152]{1,0:T(8,128)(2,1)S(1)}, bf16[256,1152]{1,0:T(8,128)(2,1)S(1)}, u32[]{:S(2)}, u32[]{:S(2)}) collective-permute-start(bf16[256,1152]{1,0:T(8,128)(2,1)S(1)} %shard_map.60), channel_id=1, source_target_pairs={{0,2},{1,135},{2,4},{3,1},{4,6},{5,3},{6,128},{7,5},{128,130},{129... | collective-permute-start | bytes 1769480 | tf_op jit(solution)/shard_map/gZ13/ppermute | solution.py:28
  18.7 17.5 %collective-permute-start.10 = (bf16[256,1152]{1,0:T(8,128)(2,1)S(1)}, bf16[256,1152]{1,0:T(8,128)(2,1)S(1)}, u32[]{:S(2)}, u32[]{:S(2)}) collective-permute-start(bf16[256,1152]{1,0:T(8,128)(2,1)S(1)} %shard_map.62.refs_0_), channel_id=1, source_target_pairs={{0,24},{1,97},{2,26},{3,99},{4,28},{5,101},{6,30},{7,103},{128,152... | collective-permute-start | bytes 1769480 | tf_op jit(solution)/shard_map/gB3/ppermute | solution.py:28
  19.5 16.7 %collective-permute-start.9 = (bf16[256,1152]{1,0:T(8,128)(2,1)S(1)}, bf16[256,1152]{1,0:T(8,128)(2,1)S(1)}, u32[]{:S(2)}, u32[]{:S(2)}) collective-permute-start(bf16[256,1152]{1,0:T(8,128)(2,1)S(1)} %shard_map.62.refs_0_), channel_id=1, source_target_pairs={{0,16},{1,65},{2,18},{3,67},{4,20},{5,69},{6,22},{7,71},{128,144},... | collective-permute-start | bytes 1769480 | tf_op jit(solution)/shard_map/gB2/ppermute | solution.py:28
  20.4 16.6 %collective-permute-start.8 = (bf16[256,1152]{1,0:T(8,128)(2,1)S(1)}, bf16[256,1152]{1,0:T(8,128)(2,1)S(1)}, u32[]{:S(2)}, u32[]{:S(2)}) collective-permute-start(bf16[256,1152]{1,0:T(8,128)(2,1)S(1)} %shard_map.62.refs_0_), channel_id=1, source_target_pairs={{0,8},{1,33},{2,10},{3,35},{4,12},{5,37},{6,14},{7,39},{128,136},{... | collective-permute-start | bytes 1769480 | tf_op jit(solution)/shard_map/gB1/ppermute | solution.py:28
  22.6 8.6 %collective-permute-start.4 = (bf16[64,1152]{1,0:T(8,128)(2,1)S(1)}, bf16[64,1152]{1,0:T(8,128)(2,1)S(1)}, u32[]{:S(2)}, u32[]{:S(2)}) collective-permute-start(bf16[64,1152]{1,0:T(8,128)(2,1)S(1)} %collective-permute-done.1.refs_2_.refs_0_), channel_id=1, source_target_pairs={{0,4},{1,133},{2,6},{3,135},{4,128},{5,1},{6,130},{7,3},{128,132},... | collective-permute-start | bytes 442376 | tf_op jit(solution)/shard_map/gZ4/ppermute | solution.py:28
  37.4 3.8 %collective-permute-start.11 = (bf16[512,1152]{1,0:T(8,128)(2,1)S(1)}, bf16[512,1152]{1,0:T(8,128)(2,1)S(1)}, u32[]{:S(2)}, u32[]{:S(2)}) collective-permute-start(bf16[512,1152]{1,0:T(8,128)(2,1)S(1)} %shard_map.66.refs_0_.refs_2_), channel_id=1, source_target_pairs={{0,1},{1,0},{2,3},{3,2},{4,5},{5,4},{6,7},{7,6},{128,129},{129,128... | collective-permute-start | bytes 3538952 | tf_op jit(solution)/shard_map/gS/ppermute | solution.py:28
  44.2 3.5 %collective-permute-start.15 = (bf16[512,1152]{1,0:T(8,128)(2,1)S(1)}, bf16[512,1152]{1,0:T(8,128)(2,1)S(1)}, u32[]{:S(2)}, u32[]{:S(2)}) collective-permute-start(bf16[512,1152]{1,0:T(8,128)(2,1)S(1)} %get-tuple-element.39), channel_id=1, source_target_pairs={{0,1},{1,0},{2,3},{3,2},{4,5},{5,4},{6,7},{7,6},{128,129},{129,128... | collective-permute-start | bytes 3538952 | tf_op jit(solution)/shard_map/rC/ppermute | solution.py:28
  48.1 11.9 %collective-permute-start.16 = (bf16[256,1152]{1,0:T(8,128)(2,1)S(1)}, bf16[256,1152]{1,0:T(8,128)(2,1)S(1)}, u32[]{:S(2)}, u32[]{:S(2)}) collective-permute-start(bf16[256,1152]{1,0:T(8,128)(2,1)S(1)} %get-tuple-element.41), channel_id=1, source_target_pairs={{0,134},{1,3},{2,0},{3,5},{4,2},{5,7},{6,4},{7,129},{128,6},{129,1... | collective-permute-start | bytes 1769480 | tf_op jit(solution)/shard_map/rZ13/ppermute | solution.py:28
  51.8 23.2 %collective-permute-start.14 = (bf16[256,1152]{1,0:T(8,128)(2,1)S(1)}, bf16[256,1152]{1,0:T(8,128)(2,1)S(1)}, u32[]{:S(2)}, u32[]{:S(2)}) collective-permute-start(bf16[256,1152]{1,0:T(8,128)(2,1)S(1)} %get-tuple-element.38.refs_2_), channel_id=1, source_target_pairs={{0,8},{1,33},{2,10},{3,35},{4,12},{5,37},{6,14},{7,39},{128,136},{... | collective-permute-start | bytes 1769480 | tf_op jit(solution)/shard_map/rB3/ppermute | solution.py:28
  54.5 20.6 %collective-permute-start.12 = (bf16[256,1152]{1,0:T(8,128)(2,1)S(1)}, bf16[256,1152]{1,0:T(8,128)(2,1)S(1)}, u32[]{:S(2)}, u32[]{:S(2)}) collective-permute-start(bf16[256,1152]{1,0:T(8,128)(2,1)S(1)} %get-tuple-element.36), channel_id=1, source_target_pairs={{0,24},{1,97},{2,26},{3,99},{4,28},{5,101},{6,30},{7,103},{128,152... | collective-permute-start | bytes 1769480 | tf_op jit(solution)/shard_map/rB1/ppermute | solution.py:28
  54.5 20.6 %collective-permute-start.13 = (bf16[256,1152]{1,0:T(8,128)(2,1)S(1)}, bf16[256,1152]{1,0:T(8,128)(2,1)S(1)}, u32[]{:S(2)}, u32[]{:S(2)}) collective-permute-start(bf16[256,1152]{1,0:T(8,128)(2,1)S(1)} %get-tuple-element.37), channel_id=1, source_target_pairs={{0,16},{1,65},{2,18},{3,67},{4,20},{5,69},{6,22},{7,71},{128,144},... | collective-permute-start | bytes 1769480 | tf_op jit(solution)/shard_map/rB2/ppermute | solution.py:28
  55.9 6.5 %collective-permute-start.17 = (bf16[64,1152]{1,0:T(8,128)(2,1)S(1)}, bf16[64,1152]{1,0:T(8,128)(2,1)S(1)}, u32[]{:S(2)}, u32[]{:S(2)}) collective-permute-start(bf16[64,1152]{1,0:T(8,128)(2,1)S(1)} %get-tuple-element.42), channel_id=1, source_target_pairs={{0,132},{1,5},{2,134},{3,7},{4,0},{5,129},{6,2},{7,131},{128,4},{1... | collective-permute-start | bytes 442376 | tf_op jit(solution)/shard_map/rZ4/ppermute | solution.py:28
  62.5 16.1 %collective-permute-start.21 = (bf16[128,1152]{1,0:T(8,128)(2,1)S(1)}, bf16[128,1152]{1,0:T(8,128)(2,1)S(1)}, u32[]{:S(2)}, u32[]{:S(2)}) collective-permute-start(bf16[128,1152]{1,0:T(8,128)(2,1)S(1)} %shard_map.72.refs_0_), channel_id=1, source_target_pairs={{0,132},{1,5},{2,134},{3,7},{4,0},{5,129},{6,2},{7,131},{128,4},{1... | collective-permute-start | bytes 884744 | tf_op jit(solution)/shard_map/rZ2/ppermute | solution.py:28
  75.3 5.2 %collective-permute-start.18 = (bf16[64,1152]{1,0:T(8,128)(2,1)S(1)}, bf16[64,1152]{1,0:T(8,128)(2,1)S(1)}, u32[]{:S(2)}, u32[]{:S(2)}) collective-permute-start(bf16[64,1152]{1,0:T(8,128)(2,1)S(1)} %get-tuple-element.44), channel_id=1, source_target_pairs={{0,96},{1,25},{2,98},{3,27},{4,100},{5,29},{6,102},{7,31},{128,224... | collective-permute-start | bytes 442376 | tf_op jit(solution)/shard_map/rA1/ppermute | solution.py:28
  75.4 6.7 %collective-permute-start.19 = (bf16[64,1152]{1,0:T(8,128)(2,1)S(1)}, bf16[64,1152]{1,0:T(8,128)(2,1)S(1)}, u32[]{:S(2)}, u32[]{:S(2)}) collective-permute-start(bf16[64,1152]{1,0:T(8,128)(2,1)S(1)} %get-tuple-element.45), channel_id=1, source_target_pairs={{0,64},{1,17},{2,66},{3,19},{4,68},{5,21},{6,70},{7,23},{128,192},... | collective-permute-start | bytes 442376 | tf_op jit(solution)/shard_map/rA2/ppermute | solution.py:28
  77.7 6.4 %collective-permute-start.20 = (bf16[64,1152]{1,0:T(8,128)(2,1)S(1)}, bf16[64,1152]{1,0:T(8,128)(2,1)S(1)}, u32[]{:S(2)}, u32[]{:S(2)}) collective-permute-start(bf16[64,1152]{1,0:T(8,128)(2,1)S(1)} %get-tuple-element.46), channel_id=1, source_target_pairs={{0,32},{1,9},{2,34},{3,11},{4,36},{5,13},{6,38},{7,15},{128,160},{... | collective-permute-start | bytes 442376 | tf_op jit(solution)/shard_map/rA3/ppermute | solution.py:28
  78.7 5.4 %collective-permute-start.22 = (bf16[64,1152]{1,0:T(8,128)(2,1)S(1)}, bf16[64,1152]{1,0:T(8,128)(2,1)S(1)}, u32[]{:S(2)}, u32[]{:S(2)}) collective-permute-start(bf16[64,1152]{1,0:T(8,128)(2,1)S(1)} %get-tuple-element.51), channel_id=1, source_target_pairs={{0,1},{1,0},{2,3},{3,2},{4,5},{5,4},{6,7},{7,6},{128,129},{129,128... | collective-permute-start | bytes 442376 | tf_op jit(solution)/shard_map/rS/ppermute | solution.py:28

commit v7 on v6

--- a/solution.py
+++ b/solution.py
@@ -40,8 +40,8 @@
     return lambda x, y, z, c: (x, y, z + k, c) if c == 0 else (x, y, z - k, c)
 
 
-def cross(k):
-    return lambda x, y, z, c: (x, y, z + k, 0) if c == 1 else (x, y, z - k, 1)
+def straight(k):
+    return lambda x, y, z, c: (x, y, z + k, c)
 
 
 def other(x, y, z, c):
@@ -94,18 +94,18 @@
         inv_ref[...] = jnp.broadcast_to(inverse, inv_ref.shape)
 
 
-def own_rows(images, texts, tie):
+def own_rows(images, texts):
     own, dim = images.shape
     outs = [((own, dim), BF16), ((own, dim), F32), ((own, 128), F32)] * 2
     return pl.pallas_call(
-        lambda tie_ref, *refs: own_kernel(*refs),
+        own_kernel,
         out_shape=tuple(jax.ShapeDtypeStruct(shape, dtype) for shape, dtype in outs),
-        in_specs=[pl.BlockSpec(memory_space=pl.ANY)] * 3,
+        in_specs=[pl.BlockSpec(memory_space=pl.ANY)] * 2,
         out_specs=tuple([pl.BlockSpec(memory_space=pltpu.VMEM)] * len(outs)),
         scratch_shapes=[pltpu.SemaphoreType.DMA((2,))],
         compiler_params=pltpu.CompilerParams(vmem_limit_bytes=8 * 1024 * 1024),
         cost_estimate=pl.CostEstimate(flops=0, bytes_accessed=1024, transcendentals=0),
-    )(tie, images, texts)
+    )(images, texts)
 
 
 def stack_kernel(*refs):
@@ -154,17 +154,19 @@
     return dots * slope + offset
 
 
-def text_grads(w_ref, img_ref, out_ref):
-    step = 256
-    for t in range(0, out_ref.shape[0], step):
+def text_grads(w_ref, img_ref, places):
+    step, rows = 256, w_ref.shape[1] // len(places)
+    for t in range(0, w_ref.shape[1], step):
         grad = lax.dot_general(
             w_ref[:, t:t + step], img_ref[...], (((0,), (0,)), ((), ())), preferred_element_type=F32
-        )
-        out_ref[t:t + step, :] = grad.astype(out_ref.dtype)
+        ).astype(BF16)
+        for n in range(step // rows):
+            out_ref, at = places[t // rows + n]
+            out_ref[at:at + rows, :] = grad[n * rows:(n + 1) * rows]
 
 
 def mine_kernel(own, txt_ref, scal_ref, *refs):
-    *parts, w_ref, img_ref, keep_ref = refs
+    *parts, w_ref, img_ref, keep_ref, send_ref = refs
     temp = scal_ref[0:1, 0:1]
     at = 0
     for part in parts:
@@ -181,15 +183,23 @@
             signed = jnp.where(positive, -corner, corner)
             w_ref[:own, :2 * own] = sigmoid_weights(signed, jnp.where(positive, -temp, temp))
         at += rows
-    text_grads(w_ref, img_ref, keep_ref)
-
-
-def theirs_kernel(txt_ref, scal_ref, img_ref, w_ref, send_ref):
+    text_grads(w_ref, img_ref, [
+        (keep_ref, 0), (keep_ref, 4 * own), (keep_ref, 3 * own), (send_ref, 2 * own),
+        (keep_ref, own), (send_ref, own), (keep_ref, 2 * own), (send_ref, 0),
+    ])
+
+
+def theirs_kernel(own, txt_ref, scal_ref, img_ref, part_ref, w_ref, keep_ref, send_ref):
     step = 256
     for at in range(0, img_ref.shape[0], step):
         power = powers(img_ref[at:at + step, :], txt_ref[...], scal_ref)
         w_ref[at:at + step, :] = sigmoid_weights(power, scal_ref[0:1, 0:1])
-    text_grads(w_ref, img_ref, send_ref)
+    for n, at in enumerate((2, 4, 6)):
+        send_ref[at * own:(at + 1) * own, :] = part_ref[n * own:(n + 1) * own, :]
+    text_grads(w_ref, img_ref, [
+        (send_ref, 0), (send_ref, 7 * own), (send_ref, 5 * own), (keep_ref, 2 * own),
+        (send_ref, own), (keep_ref, own), (send_ref, 3 * own), (keep_ref, 0),
+    ])
 
 
 def image_kernel(w1_ref, w2_ref, txt1_ref, txt2_ref, *outs):
@@ -202,13 +212,18 @@
         at += rows
 
 
-def total_kernel(keep_ref, got_ref, own_ref, part13_ref, part2_ref, part4_ref):
-    at = 0
-    for out in (own_ref, part13_ref, part2_ref, part4_ref):
-        rows = out.shape[0]
-        total = keep_ref[at:at + rows, :].astype(F32) + got_ref[at:at + rows, :].astype(F32)
-        out[...] = total.astype(out.dtype)
-        at += rows
+def total_kernel(first_ref, second_ref, got_ref, own_ref, part13_ref, part2_ref, part4_ref):
+    rows = own_ref.shape[0]
+    places = [
+        (first_ref, 0, own_ref, 0),
+        (first_ref, 1, part13_ref, 0), (second_ref, 0, part13_ref, 1),
+        (first_ref, 2, part13_ref, 2), (second_ref, 1, part13_ref, 3),
+        (first_ref, 3, part2_ref, 0), (second_ref, 2, part2_ref, 1),
+        (first_ref, 4, part4_ref, 0),
+    ]
+    for n, (in_ref, i, out_ref, o) in enumerate(places):
+        total = in_ref[i * rows:(i + 1) * rows, :].astype(F32) + got_ref[n * rows:(n + 1) * rows, :].astype(F32)
+        out_ref[o * rows:(o + 1) * rows, :] = total.astype(out_ref.dtype)
 
 
 def middle_kernel(part2_ref, got13_ref, got4_ref, out_ref):
@@ -244,33 +259,31 @@
     own, dim = images.shape
 
     side = [shift(images, first(k), "gA%d" % k) for k in (1, 2, 3)]
-    line2 = shift(texts, line(2), "gZ2")
-    cross2 = shift(texts, cross(2), "gX2")
-    swapped = shift(texts, other, "gC")
-    img_own, img_unit, inv_img, txt_own, txt_unit, inv_txt = own_rows(images, texts, swapped)
-    group = stack([img_own, *side], [token(line2, cross2)])
-    send13 = stack([txt_own, swapped, line2, cross2])
-    far = [shift(group, second(k), "gB%d" % k) for k in (1, 2, 3)]
-    near13 = shift(send13, line(1), "gZ13")
-    near4 = shift(line2, line(2), "gZ4")
-    first_token = token(near13)
+    far4 = shift(texts, straight(4), "gZ4")
+    img_own, img_unit, inv_img, txt_own, txt_unit, inv_txt = own_rows(images, texts)
+    group = stack([img_own, *side], [token(far4)])
+    far = [shift(group, second(k), "gB%d" % k) for k in (2, 1, 3)]
+    far2 = shift(stack([txt_own, far4]), line(2), "gZ2")
+    far1 = shift(stack([txt_own, far4, far2], [token(far2)]), line(1), "gZ1")
     (scalars,) = call(
-        scalar_kernel, [((8, 128), F32)], [log_temp.reshape(1, 1), bias.reshape(1, 1)], [near13]
+        scalar_kernel, [((8, 128), F32)], [log_temp.reshape(1, 1), bias.reshape(1, 1)], [far2]
     )
     group = rounded([group], [scalars])
-    mine = rounded([txt_own, near13, line2, cross2, near4], [group, first_token, *far])
+    mine = rounded([txt_own, far4, far2, far1], [group, token(*far)])
     theirs = shift(mine, other, "gS")
 
     half = mine.shape[0]
     rows = group.shape[0] * (1 + len(far))
     flops = 2 * rows * half * dim
-    w_mine, img_all, keep = call(
-        lambda *refs: mine_kernel(own, *refs), [((rows, half), BF16), ((rows, dim), BF16), ((half, dim), BF16)],
+    w_mine, img_all, keep1, send1 = call(
+        lambda *refs: mine_kernel(own, *refs),
+        [((rows, half), BF16), ((rows, dim), BF16), ((5 * own, dim), BF16), ((3 * own, dim), BF16)],
         [mine, scalars, group, *far], flops=2 * flops, limit=24,
     )
-    w_theirs, send = call(
-        theirs_kernel, [((rows, half), BF16), ((half, dim), BF16)],
-        [theirs, scalars, img_all], ties=[keep], flops=2 * flops, limit=24,
+    w_theirs, keep2, send = call(
+        lambda *refs: theirs_kernel(own, *refs),
+        [((rows, half), BF16), ((3 * own, dim), BF16), ((half, dim), BF16)],
+        [theirs, scalars, img_all, send1], flops=2 * flops, limit=24,
     )
     grads = call(
         image_kernel, [(group.shape, F32)] + [(group.shape, BF16)] * len(far),
@@ -280,7 +293,7 @@
     total_own, part13, part2, part4 = call(
         total_kernel,
         [((own, dim), F32), ((4 * own, dim), BF16), ((2 * own, dim), F32), ((own, dim), BF16)],
-        [keep, shift(send, other, "rC")], ties=[grads[-1]],
+        [keep1, keep2, shift(send, other, "rC")], ties=[grads[-1]],
     )
     got13 = shift(part13, line(-1), "rZ13")
     got4 = shift(part4, line(-2), "rZ4")
@@ -289,7 +302,7 @@
     txt_sum, txt_send = call(landed_kernel, [((own, dim), F32), ((own, dim), BF16)], [total_own, got13, got2])
     txt_last = shift(txt_send, other, "rS")
 
-    back = [shift(g, second(-k), "rB%d" % k) for k, g in zip((1, 2, 3), grads[1:])]
+    back = [shift(g, second(-k), "rB%d" % k) for k, g in ((1, grads[2]), (2, grads[1]), (3, grads[3]))]
     img_sum, *parts = call(
         sums_kernel, [((own, dim), F32)] + [((own, dim), BF16)] * 3, [grads[0], *back], ties=[token(middle)]
     )

time: 85.3 us -> 81.8 us (0.959); the launches traced: 85.1 us -> 80.7 us
  waiting for transfers between devices: 33.6 us -> 29.7 us
    ppermute x23 -> x21, waiting for transfers between devices: 33.6 us -> 29.7 us  [shift(): return lax.ppermute(values, AXES, pairs)]
    ppermute x23 -> x21, starting transfers between devices: 35.2 us -> 34.6 us  [shift(): return lax.ppermute(values, AXES, pairs)]
    pallas_call x17 -> x19, Pallas kernels: 12 us -> 12 us  [call(): pl.pallas_call(lambda *refs: kernel(*refs[:n_in], *refs[n_in + len(ties):...]
  transfers between devices with their start and end apart: 23 -> 21, of which waited for: 12 -> 10; matrix products, arithmetic and copies ran while one was open for 0% -> 0% of each run, Pallas kernels for 9% -> 10%
where the time goes in v7:
time: 81.8 us; the launch traced here: 80.7 us
  starting transfers between devices  34.6 us (42%)
  waiting for transfers between devices  29.7 us (36%)
  Pallas kernels  12.5 us (15%)
  between operations  2.08 us (3%)
  local copies, waits for them, and re-layouts  1.82 us (2%)
    ppermute x21, starting transfers between devices, shift(): return lax.ppermute(values, AXES, pairs)  34.6 us
    ppermute x21, waiting for transfers between devices, shift(): return lax.ppermute(values, AXES, pairs)  29.7 us
    pallas_call x19, Pallas kernels, call(): pl.pallas_call(lambda *refs: kernel(*refs[:n_in], *refs[n_in + len(ties):...  12 us
    unnamed x4, local copies, waits for them, and re-layouts  1.82 us
  transfers between devices with their start and end apart: 21, of which 10 were waited for; matrix products, arithmetic and copies ran while one was open for 0% of the time, Pallas kernels for 10%

profile of v7, /device:TPU:24, one launch (start us, length us, event | category | flops | bytes accessed | tf_op | source)
XLA Modules:
  0.0 80.7 jit_solution(7782407051578313315)
XLA Ops:
  0.6 7.3 %collective-permute-start = (bf16[64,1152]{1,0:T(8,128)(2,1)}, bf16[64,1152]{1,0:T(8,128)(2,1)S(1)}, u32[]{:S(2)}, u32[]{:S(2)}) collective-permute-start(bf16[64,1152]{1,0:T(8,128)(2,1)} %txt_hbm.1), channel_id=1, source_target_pairs={{0,128},{1,129},{2,130},{3,131},{4,132},{5,133},{6,134},{7,135},{1... | collective-permute-start | bytes 442376 | tf_op jit(solution)/shard_map/gZ4/ppermute | solution.py:28
  7.9 1.5 %collective-permute-start.3 = (bf16[64,1152]{1,0:T(8,128)(2,1)}, bf16[64,1152]{1,0:T(8,128)(2,1)S(1)}, u32[]{:S(2)}, u32[]{:S(2)}) collective-permute-start(bf16[64,1152]{1,0:T(8,128)(2,1)} %img_hbm.1), channel_id=1, source_target_pairs={{0,32},{1,9},{2,34},{3,11},{4,36},{5,13},{6,38},{7,15},{128,160},{... | collective-permute-start | bytes 442376 | tf_op jit(solution)/shard_map/gA1/ppermute | solution.py:28
  9.4 1.7 %collective-permute-start.5 = (bf16[64,1152]{1,0:T(8,128)(2,1)}, bf16[64,1152]{1,0:T(8,128)(2,1)S(1)}, u32[]{:S(2)}, u32[]{:S(2)}) collective-permute-start(bf16[64,1152]{1,0:T(8,128)(2,1)} %img_hbm.1), channel_id=1, source_target_pairs={{0,96},{1,25},{2,98},{3,27},{4,100},{5,29},{6,102},{7,31},{128,224... | collective-permute-start | bytes 442376 | tf_op jit(solution)/shard_map/gA3/ppermute | solution.py:28
  11.1 1.8 %collective-permute-start.4 = (bf16[64,1152]{1,0:T(8,128)(2,1)}, bf16[64,1152]{1,0:T(8,128)(2,1)S(1)}, u32[]{:S(2)}, u32[]{:S(2)}) collective-permute-start(bf16[64,1152]{1,0:T(8,128)(2,1)} %img_hbm.1), channel_id=1, source_target_pairs={{0,64},{1,17},{2,66},{3,19},{4,68},{5,21},{6,70},{7,23},{128,192},... | collective-permute-start | bytes 442376 | tf_op jit(solution)/shard_map/gA2/ppermute | solution.py:28
  13.0 0.0 copy-start
  13.0 0.9 %copy-done = bf16[64,1152]{1,0:T(8,128)(2,1)S(1)} copy-done((bf16[64,1152]{1,0:T(8,128)(2,1)S(1)}, bf16[64,1152]{1,0:T(8,128)(2,1)}, u32[]{:S(2)}) %copy-start) | copy-done | bytes 147480
  13.9 0.0 copy-start.1
  13.9 0.9 %copy-done.1 = bf16[64,1152]{1,0:T(8,128)(2,1)S(1)} copy-done((bf16[64,1152]{1,0:T(8,128)(2,1)S(1)}, bf16[64,1152]{1,0:T(8,128)(2,1)}, u32[]{:S(2)}) %copy-start.1) | copy-done | bytes 147480
  14.8 0.5 shard_map.59
  16.6 0.0 collective-permute-done.refs_1_.refs_0_
  16.6 1.6 %collective-permute-start.1 = (bf16[128,1152]{1,0:T(8,128)(2,1)S(1)}, bf16[128,1152]{1,0:T(8,128)(2,1)S(1)}, u32[]{:S(2)}, u32[]{:S(2)}) collective-permute-start(bf16[128,1152]{1,0:T(8,128)(2,1)S(1)} %shard_map.60), channel_id=1, source_target_pairs={{0,4},{1,133},{2,6},{3,135},{4,128},{5,1},{6,130},{7,3},{128,132},... | collective-permute-start | bytes 884744 | tf_op jit(solution)/shard_map/gZ2/ppermute | solution.py:28
  18.2 0.0 collective-permute-done.3.refs_1_
  18.2 0.0 collective-permute-done.5.refs_3_
  18.2 0.0 collective-permute-done.4.refs_2_
  18.3 0.8 %collective-permute-start.8 = (bf16[256,1152]{1,0:T(8,128)(2,1)S(1)}, bf16[256,1152]{1,0:T(8,128)(2,1)S(1)}, u32[]{:S(2)}, u32[]{:S(2)}) collective-permute-start(bf16[256,1152]{1,0:T(8,128)(2,1)S(1)} %shard_map.64.refs_0_), channel_id=1, source_target_pairs={{0,24},{1,97},{2,26},{3,99},{4,28},{5,101},{6,30},{7,103},{128,152... | collective-permute-start | bytes 1769480 | tf_op jit(solution)/shard_map/gB3/ppermute | solution.py:28
  19.1 2.5 %collective-permute-start.7 = (bf16[256,1152]{1,0:T(8,128)(2,1)S(1)}, bf16[256,1152]{1,0:T(8,128)(2,1)S(1)}, u32[]{:S(2)}, u32[]{:S(2)}) collective-permute-start(bf16[256,1152]{1,0:T(8,128)(2,1)S(1)} %shard_map.64.refs_0_), channel_id=1, source_target_pairs={{0,8},{1,33},{2,10},{3,35},{4,12},{5,37},{6,14},{7,39},{128,136},{... | collective-permute-start | bytes 1769480 | tf_op jit(solution)/shard_map/gB1/ppermute | solution.py:28
  21.6 0.0 collective-permute-start.6
  21.6 5.6 %collective-permute-done.1.refs_0_.refs_2_ = bf16[128,1152]{1,0:T(8,128)(2,1)S(1)} collective-permute-done((bf16[128,1152]{1,0:T(8,128)(2,1)S(1)}, bf16[128,1152]{1,0:T(8,128)(2,1)S(1)}, u32[]{:S(2)}, u32[]{:S(2)}) %collective-permute-start.1) | collective-permute-done | bytes 294944 | tf_op jit(solution)/shard_map/gZ2/ppermute | solution.py:28
  27.2 0.1 shard_map.65.refs_1_
  27.3 0.2 shard_map.66.refs_4_.refs_2_
  27.5 2.6 %collective-permute-start.2 = (bf16[256,1152]{1,0:T(8,128)(2,1)S(1)}, bf16[256,1152]{1,0:T(8,128)(2,1)S(1)}, u32[]{:S(2)}, u32[]{:S(2)}) collective-permute-start(bf16[256,1152]{1,0:T(8,128)(2,1)S(1)} %shard_map.62), channel_id=1, source_target_pairs={{0,2},{1,135},{2,4},{3,1},{4,6},{5,3},{6,128},{7,5},{128,130},{129... | collective-permute-start | bytes 1769480 | tf_op jit(solution)/shard_map/gZ1/ppermute | solution.py:28
  30.1 5.6 %collective-permute-done.8.refs_2_.refs_5_ = bf16[256,1152]{1,0:T(8,128)(2,1)S(1)} collective-permute-done((bf16[256,1152]{1,0:T(8,128)(2,1)S(1)}, bf16[256,1152]{1,0:T(8,128)(2,1)S(1)}, u32[]{:S(2)}, u32[]{:S(2)}) %collective-permute-start.8) | collective-permute-done | bytes 589856 | tf_op jit(solution)/shard_map/gB3/ppermute | solution.py:28
  35.7 0.0 collective-permute-done.7.refs_1_.refs_4_
  35.8 0.0 collective-permute-done.6.refs_0_.refs_3_
  35.8 2.9 %collective-permute-done.2.refs_3_ = bf16[256,1152]{1,0:T(8,128)(2,1)S(1)} collective-permute-done((bf16[256,1152]{1,0:T(8,128)(2,1)S(1)}, bf16[256,1152]{1,0:T(8,128)(2,1)S(1)}, u32[]{:S(2)}, u32[]{:S(2)}) %collective-permute-start.2) | collective-permute-done | bytes 589856 | tf_op jit(solution)/shard_map/gZ1/ppermute | solution.py:28
  38.7 0.4 shard_map.68.refs_0_.refs_2_
  39.1 0.3 collective-permute-start.9
  39.3 3.5 %shard_map.69 = (bf16[1024,512]{1,0:T(8,128)(2,1)S(1)}, bf16[1024,1152]{1,0:T(8,128)(2,1)S(1)}, bf16[320,1152]{1,0:T(8,128)(2,1)S(1)}, bf16[192,1152]{1,0:T(8,128)(2,1)S(1)}) custom-call(bf16[512,1152]{1,0:T(8,128)(2,1)S(1)} %shard_map.68.refs_0_.refs_2_, f32[8,128]{1,0:T(8,128)S(1)} %shard_map.65.refs_1_, bf16[256,1152]{1,0:T(8,128)(2,1)S(1)} %shard_map.66.refs_4_.refs_2_, ...), custom_call_target="tpu_custom_call" | custom-call | flops 2415919104 | bytes 1024 | tf_op jit(solution)/shard_map/pallas_call | solution.py:54
  42.8 0.0 collective-permute-done.9.refs_0_.refs_3_
  42.8 3.1 %shard_map.70 = (bf16[1024,512]{1,0:T(8,128)(2,1)S(1)}, bf16[192,1152]{1,0:T(8,128)(2,1)S(1)}, bf16[512,1152]{1,0:T(8,128)(2,1)S(1)}) custom-call(bf16[512,1152]{1,0:T(8,128)(2,1)S(1)} %collective-permute-done.9.refs_0_.refs_3_, f32[8,128]{1,0:T(8,128)S(1)} %shard_map.65.refs_1_, bf16[1024,1152]{1,0:T(8,128)(2,1)S(1)} %get-tuple-element.34.refs_2_, ...), custom_call_target="tpu_custom_call" | custom-call | flops 2415919104 | bytes 1024 | tf_op jit(solution)/shard_map/pallas_call | solution.py:54
  45.9 0.6 collective-permute-start.13
  46.5 3.0 %shard_map.71 = (f32[256,1152]{1,0:T(8,128)S(1)}, bf16[256,1152]{1,0:T(8,128)(2,1)S(1)}, bf16[256,1152]{1,0:T(8,128)(2,1)S(1)}, bf16[256,1152]{1,0:T(8,128)(2,1)S(1)}) custom-call(bf16[1024,512]{1,0:T(8,128)(2,1)S(1)} %get-tuple-element.33.refs_0_, bf16[1024,512]{1,0:T(8,128)(2,1)S(1)} %get-tuple-element.36.refs_1_, ...), custom_call_target="tpu_custom_call" | custom-call | flops 2415919104 | bytes 1024 | tf_op jit(solution)/shard_map/pallas_call | solution.py:54
  49.4 0.0 collective-permute-done.13.refs_2_
  49.5 0.3 shard_map.72
  49.7 0.6 collective-permute-start.14
  50.3 2.0 %collective-permute-start.12 = (bf16[256,1152]{1,0:T(8,128)(2,1)S(1)}, bf16[256,1152]{1,0:T(8,128)(2,1)S(1)}, u32[]{:S(2)}, u32[]{:S(2)}) collective-permute-start(bf16[256,1152]{1,0:T(8,128)(2,1)S(1)} %get-tuple-element.40.refs_3_), channel_id=1, source_target_pairs={{0,8},{1,33},{2,10},{3,35},{4,12},{5,37},{6,14},{7,39},{128,136},{... | collective-permute-start | bytes 1769480 | tf_op jit(solution)/shard_map/rB3/ppermute | solution.py:28
  52.3 0.0 collective-permute-start.10
  52.3 1.5 %collective-permute-start.11 = (bf16[256,1152]{1,0:T(8,128)(2,1)S(1)}, bf16[256,1152]{1,0:T(8,128)(2,1)S(1)}, u32[]{:S(2)}, u32[]{:S(2)}) collective-permute-start(bf16[256,1152]{1,0:T(8,128)(2,1)S(1)} %get-tuple-element.39), channel_id=1, source_target_pairs={{0,16},{1,65},{2,18},{3,67},{4,20},{5,69},{6,22},{7,71},{128,144},... | collective-permute-start | bytes 1769480 | tf_op jit(solution)/shard_map/rB2/ppermute | solution.py:28
  53.8 3.6 %collective-permute-start.15 = (bf16[64,1152]{1,0:T(8,128)(2,1)S(1)}, bf16[64,1152]{1,0:T(8,128)(2,1)S(1)}, u32[]{:S(2)}, u32[]{:S(2)}) collective-permute-start(bf16[64,1152]{1,0:T(8,128)(2,1)S(1)} %get-tuple-element.46), channel_id=1, source_target_pairs={{0,132},{1,5},{2,134},{3,7},{4,0},{5,129},{6,2},{7,131},{128,4},{1... | collective-permute-start | bytes 442376 | tf_op jit(solution)/shard_map/rZ4/ppermute | solution.py:28
  57.4 2.3 %collective-permute-done.14.refs_0_.refs_1_ = bf16[256,1152]{1,0:T(8,128)(2,1)S(1)} collective-permute-done((bf16[256,1152]{1,0:T(8,128)(2,1)S(1)}, bf16[256,1152]{1,0:T(8,128)(2,1)S(1)}, u32[]{:S(2)}, u32[]{:S(2)}) %collective-permute-start.14) | collective-permute-done | bytes 589856 | tf_op jit(solution)/shard_map/rZ13/ppermute | solution.py:28
  59.7 3.9 %collective-permute-done.15.refs_2_ = bf16[64,1152]{1,0:T(8,128)(2,1)S(1)} collective-permute-done((bf16[64,1152]{1,0:T(8,128)(2,1)S(1)}, bf16[64,1152]{1,0:T(8,128)(2,1)S(1)}, u32[]{:S(2)}, u32[]{:S(2)}) %collective-permute-start.15) | collective-permute-done | bytes 147488 | tf_op jit(solution)/shard_map/rZ4/ppermute | solution.py:28
  63.6 0.1 shard_map.74.refs_0_
  63.7 2.9 %collective-permute-start.19 = (bf16[128,1152]{1,0:T(8,128)(2,1)S(1)}, bf16[128,1152]{1,0:T(8,128)(2,1)S(1)}, u32[]{:S(2)}, u32[]{:S(2)}) collective-permute-start(bf16[128,1152]{1,0:T(8,128)(2,1)S(1)} %shard_map.74.refs_0_), channel_id=1, source_target_pairs={{0,132},{1,5},{2,134},{3,7},{4,0},{5,129},{6,2},{7,131},{128,4},{1... | collective-permute-start | bytes 884744 | tf_op jit(solution)/shard_map/rZ2/ppermute | solution.py:28
  66.6 3.1 %collective-permute-done.10.refs_1_ = bf16[256,1152]{1,0:T(8,128)(2,1)S(1)} collective-permute-done((bf16[256,1152]{1,0:T(8,128)(2,1)S(1)}, bf16[256,1152]{1,0:T(8,128)(2,1)S(1)}, u32[]{:S(2)}, u32[]{:S(2)}) %collective-permute-start.10) | collective-permute-done | bytes 589856 | tf_op jit(solution)/shard_map/rB1/ppermute | solution.py:28
  69.7 0.0 collective-permute-done.11.refs_2_
  69.7 0.0 collective-permute-done.12.refs_3_
  69.7 0.3 shard_map.76
  70.0 1.4 %collective-permute-start.16 = (bf16[64,1152]{1,0:T(8,128)(2,1)S(1)}, bf16[64,1152]{1,0:T(8,128)(2,1)S(1)}, u32[]{:S(2)}, u32[]{:S(2)}) collective-permute-start(bf16[64,1152]{1,0:T(8,128)(2,1)S(1)} %get-tuple-element.48), channel_id=1, source_target_pairs={{0,96},{1,25},{2,98},{3,27},{4,100},{5,29},{6,102},{7,31},{128,224... | collective-permute-start | bytes 442376 | tf_op jit(solution)/shard_map/rA1/ppermute | solution.py:28
  71.4 1.3 %collective-permute-start.17 = (bf16[64,1152]{1,0:T(8,128)(2,1)S(1)}, bf16[64,1152]{1,0:T(8,128)(2,1)S(1)}, u32[]{:S(2)}, u32[]{:S(2)}) collective-permute-start(bf16[64,1152]{1,0:T(8,128)(2,1)S(1)} %get-tuple-element.49), channel_id=1, source_target_pairs={{0,64},{1,17},{2,66},{3,19},{4,68},{5,21},{6,70},{7,23},{128,192},... | collective-permute-start | bytes 442376 | tf_op jit(solution)/shard_map/rA2/ppermute | solution.py:28
  72.8 0.5 collective-permute-start.18
  73.2 0.4 collective-permute-done.19.refs_2_
  73.6 0.1 shard_map.77
  73.7 0.1 collective-permute-start.20
  73.8 1.4 %collective-permute-done.16.refs_3_ = bf16[64,1152]{1,0:T(8,128)(2,1)S(1)} collective-permute-done((bf16[64,1152]{1,0:T(8,128)(2,1)S(1)}, bf16[64,1152]{1,0:T(8,128)(2,1)S(1)}, u32[]{:S(2)}, u32[]{:S(2)}) %collective-permute-start.16) | collective-permute-done | bytes 147488 | tf_op jit(solution)/shard_map/rA1/ppermute | solution.py:28
  75.2 2.9 %collective-permute-done.17.refs_4_ = bf16[64,1152]{1,0:T(8,128)(2,1)S(1)} collective-permute-done((bf16[64,1152]{1,0:T(8,128)(2,1)S(1)}, bf16[64,1152]{1,0:T(8,128)(2,1)S(1)}, u32[]{:S(2)}, u32[]{:S(2)}) %collective-permute-start.17) | collective-permute-done | bytes 147488 | tf_op jit(solution)/shard_map/rA2/ppermute | solution.py:28
  78.1 1.5 %collective-permute-done.18.refs_5_ = bf16[64,1152]{1,0:T(8,128)(2,1)S(1)} collective-permute-done((bf16[64,1152]{1,0:T(8,128)(2,1)S(1)}, bf16[64,1152]{1,0:T(8,128)(2,1)S(1)}, u32[]{:S(2)}, u32[]{:S(2)}) %collective-permute-start.18) | collective-permute-done | bytes 147488 | tf_op jit(solution)/shard_map/rA3/ppermute | solution.py:28
  79.6 0.0 collective-permute-done.20.refs_9_
  79.6 1.1 %shard_map.78 = (f32[64,1152]{1,0:T(8,128)}, f32[64,1152]{1,0:T(8,128)}) custom-call(f32[64,1152]{1,0:T(8,128)S(1)} %get-tuple-element.29.refs_0_, f32[64,128]{1,0:T(8,128)S(1)} %get-tuple-element.30.refs_1_, f32[64,1152]{1,0:T(8,128)S(1)} %get-tuple-element.47.refs_2_, bf16[64,1152]{1,0:T(8,128)(2,1)S(1)} %collective-permute-done.16.refs_3_, ...), custom_call_target="tpu_custom_call" | custom-call | bytes 1024 | tf_op jit(solution)/shard_map/pallas_call | solution.py:54
  (8 shorter events, 0.1 us)
Async XLA Ops:
  0.6 16.0 %collective-permute-start = (bf16[64,1152]{1,0:T(8,128)(2,1)}, bf16[64,1152]{1,0:T(8,128)(2,1)S(1)}, u32[]{:S(2)}, u32[]{:S(2)}) collective-permute-start(bf16[64,1152]{1,0:T(8,128)(2,1)} %txt_hbm.1), channel_id=1, source_target_pairs={{0,128},{1,129},{2,130},{3,131},{4,132},{5,133},{6,134},{7,135},{1... | collective-permute-start | bytes 442376 | tf_op jit(solution)/shard_map/gZ4/ppermute | solution.py:28
  7.9 10.3 %collective-permute-start.3 = (bf16[64,1152]{1,0:T(8,128)(2,1)}, bf16[64,1152]{1,0:T(8,128)(2,1)S(1)}, u32[]{:S(2)}, u32[]{:S(2)}) collective-permute-start(bf16[64,1152]{1,0:T(8,128)(2,1)} %img_hbm.1), channel_id=1, source_target_pairs={{0,32},{1,9},{2,34},{3,11},{4,36},{5,13},{6,38},{7,15},{128,160},{... | collective-permute-start | bytes 442376 | tf_op jit(solution)/shard_map/gA1/ppermute | solution.py:28
  9.4 8.8 %collective-permute-start.5 = (bf16[64,1152]{1,0:T(8,128)(2,1)}, bf16[64,1152]{1,0:T(8,128)(2,1)S(1)}, u32[]{:S(2)}, u32[]{:S(2)}) collective-permute-start(bf16[64,1152]{1,0:T(8,128)(2,1)} %img_hbm.1), channel_id=1, source_target_pairs={{0,96},{1,25},{2,98},{3,27},{4,100},{5,29},{6,102},{7,31},{128,224... | collective-permute-start | bytes 442376 | tf_op jit(solution)/shard_map/gA3/ppermute | solution.py:28
  11.1 7.1 %collective-permute-start.4 = (bf16[64,1152]{1,0:T(8,128)(2,1)}, bf16[64,1152]{1,0:T(8,128)(2,1)S(1)}, u32[]{:S(2)}, u32[]{:S(2)}) collective-permute-start(bf16[64,1152]{1,0:T(8,128)(2,1)} %img_hbm.1), channel_id=1, source_target_pairs={{0,64},{1,17},{2,66},{3,19},{4,68},{5,21},{6,70},{7,23},{128,192},... | collective-permute-start | bytes 442376 | tf_op jit(solution)/shard_map/gA2/ppermute | solution.py:28
  13.0 0.9 %copy-start = (bf16[64,1152]{1,0:T(8,128)(2,1)S(1)}, bf16[64,1152]{1,0:T(8,128)(2,1)}, u32[]{:S(2)}) copy-start(bf16[64,1152]{1,0:T(8,128)(2,1)} %txt_hbm.1) | copy-start | bytes 442372
  13.9 0.9 %copy-start.1 = (bf16[64,1152]{1,0:T(8,128)(2,1)S(1)}, bf16[64,1152]{1,0:T(8,128)(2,1)}, u32[]{:S(2)}) copy-start(bf16[64,1152]{1,0:T(8,128)(2,1)} %img_hbm.1) | copy-start | bytes 442372
  16.6 10.5 %collective-permute-start.1 = (bf16[128,1152]{1,0:T(8,128)(2,1)S(1)}, bf16[128,1152]{1,0:T(8,128)(2,1)S(1)}, u32[]{:S(2)}, u32[]{:S(2)}) collective-permute-start(bf16[128,1152]{1,0:T(8,128)(2,1)S(1)} %shard_map.60), channel_id=1, source_target_pairs={{0,4},{1,133},{2,6},{3,135},{4,128},{5,1},{6,130},{7,3},{128,132},... | collective-permute-start | bytes 884744 | tf_op jit(solution)/shard_map/gZ2/ppermute | solution.py:28
  18.3 17.5 %collective-permute-start.8 = (bf16[256,1152]{1,0:T(8,128)(2,1)S(1)}, bf16[256,1152]{1,0:T(8,128)(2,1)S(1)}, u32[]{:S(2)}, u32[]{:S(2)}) collective-permute-start(bf16[256,1152]{1,0:T(8,128)(2,1)S(1)} %shard_map.64.refs_0_), channel_id=1, source_target_pairs={{0,24},{1,97},{2,26},{3,99},{4,28},{5,101},{6,30},{7,103},{128,152... | collective-permute-start | bytes 1769480 | tf_op jit(solution)/shard_map/gB3/ppermute | solution.py:28
  19.1 16.7 %collective-permute-start.7 = (bf16[256,1152]{1,0:T(8,128)(2,1)S(1)}, bf16[256,1152]{1,0:T(8,128)(2,1)S(1)}, u32[]{:S(2)}, u32[]{:S(2)}) collective-permute-start(bf16[256,1152]{1,0:T(8,128)(2,1)S(1)} %shard_map.64.refs_0_), channel_id=1, source_target_pairs={{0,8},{1,33},{2,10},{3,35},{4,12},{5,37},{6,14},{7,39},{128,136},{... | collective-permute-start | bytes 1769480 | tf_op jit(solution)/shard_map/gB1/ppermute | solution.py:28
  21.6 14.2 %collective-permute-start.6 = (bf16[256,1152]{1,0:T(8,128)(2,1)S(1)}, bf16[256,1152]{1,0:T(8,128)(2,1)S(1)}, u32[]{:S(2)}, u32[]{:S(2)}) collective-permute-start(bf16[256,1152]{1,0:T(8,128)(2,1)S(1)} %shard_map.64.refs_0_), channel_id=1, source_target_pairs={{0,16},{1,65},{2,18},{3,67},{4,20},{5,69},{6,22},{7,71},{128,144},... | collective-permute-start | bytes 1769480 | tf_op jit(solution)/shard_map/gB2/ppermute | solution.py:28
  27.5 11.2 %collective-permute-start.2 = (bf16[256,1152]{1,0:T(8,128)(2,1)S(1)}, bf16[256,1152]{1,0:T(8,128)(2,1)S(1)}, u32[]{:S(2)}, u32[]{:S(2)}) collective-permute-start(bf16[256,1152]{1,0:T(8,128)(2,1)S(1)} %shard_map.62), channel_id=1, source_target_pairs={{0,2},{1,135},{2,4},{3,1},{4,6},{5,3},{6,128},{7,5},{128,130},{129... | collective-permute-start | bytes 1769480 | tf_op jit(solution)/shard_map/gZ1/ppermute | solution.py:28
  39.1 3.8 %collective-permute-start.9 = (bf16[512,1152]{1,0:T(8,128)(2,1)S(1)}, bf16[512,1152]{1,0:T(8,128)(2,1)S(1)}, u32[]{:S(2)}, u32[]{:S(2)}) collective-permute-start(bf16[512,1152]{1,0:T(8,128)(2,1)S(1)} %shard_map.68.refs_0_.refs_2_), channel_id=1, source_target_pairs={{0,1},{1,0},{2,3},{3,2},{4,5},{5,4},{6,7},{7,6},{128,129},{129,128... | collective-permute-start | bytes 3538952 | tf_op jit(solution)/shard_map/gS/ppermute | solution.py:28
  45.9 3.5 %collective-permute-start.13 = (bf16[512,1152]{1,0:T(8,128)(2,1)S(1)}, bf16[512,1152]{1,0:T(8,128)(2,1)S(1)}, u32[]{:S(2)}, u32[]{:S(2)}) collective-permute-start(bf16[512,1152]{1,0:T(8,128)(2,1)S(1)} %get-tuple-element.43), channel_id=1, source_target_pairs={{0,1},{1,0},{2,3},{3,2},{4,5},{5,4},{6,7},{7,6},{128,129},{129,128... | collective-permute-start | bytes 3538952 | tf_op jit(solution)/shard_map/rC/ppermute | solution.py:28
  49.7 10.0 %collective-permute-start.14 = (bf16[256,1152]{1,0:T(8,128)(2,1)S(1)}, bf16[256,1152]{1,0:T(8,128)(2,1)S(1)}, u32[]{:S(2)}, u32[]{:S(2)}) collective-permute-start(bf16[256,1152]{1,0:T(8,128)(2,1)S(1)} %get-tuple-element.45), channel_id=1, source_target_pairs={{0,134},{1,3},{2,0},{3,5},{4,2},{5,7},{6,4},{7,129},{128,6},{129,1... | collective-permute-start | bytes 1769480 | tf_op jit(solution)/shard_map/rZ13/ppermute | solution.py:28
  50.3 19.4 %collective-permute-start.12 = (bf16[256,1152]{1,0:T(8,128)(2,1)S(1)}, bf16[256,1152]{1,0:T(8,128)(2,1)S(1)}, u32[]{:S(2)}, u32[]{:S(2)}) collective-permute-start(bf16[256,1152]{1,0:T(8,128)(2,1)S(1)} %get-tuple-element.40.refs_3_), channel_id=1, source_target_pairs={{0,8},{1,33},{2,10},{3,35},{4,12},{5,37},{6,14},{7,39},{128,136},{... | collective-permute-start | bytes 1769480 | tf_op jit(solution)/shard_map/rB3/ppermute | solution.py:28
  52.3 17.4 %collective-permute-start.10 = (bf16[256,1152]{1,0:T(8,128)(2,1)S(1)}, bf16[256,1152]{1,0:T(8,128)(2,1)S(1)}, u32[]{:S(2)}, u32[]{:S(2)}) collective-permute-start(bf16[256,1152]{1,0:T(8,128)(2,1)S(1)} %get-tuple-element.38), channel_id=1, source_target_pairs={{0,24},{1,97},{2,26},{3,99},{4,28},{5,101},{6,30},{7,103},{128,152... | collective-permute-start | bytes 1769480 | tf_op jit(solution)/shard_map/rB1/ppermute | solution.py:28
  52.3 17.4 %collective-permute-start.11 = (bf16[256,1152]{1,0:T(8,128)(2,1)S(1)}, bf16[256,1152]{1,0:T(8,128)(2,1)S(1)}, u32[]{:S(2)}, u32[]{:S(2)}) collective-permute-start(bf16[256,1152]{1,0:T(8,128)(2,1)S(1)} %get-tuple-element.39), channel_id=1, source_target_pairs={{0,16},{1,65},{2,18},{3,67},{4,20},{5,69},{6,22},{7,71},{128,144},... | collective-permute-start | bytes 1769480 | tf_op jit(solution)/shard_map/rB2/ppermute | solution.py:28
  53.8 9.8 %collective-permute-start.15 = (bf16[64,1152]{1,0:T(8,128)(2,1)S(1)}, bf16[64,1152]{1,0:T(8,128)(2,1)S(1)}, u32[]{:S(2)}, u32[]{:S(2)}) collective-permute-start(bf16[64,1152]{1,0:T(8,128)(2,1)S(1)} %get-tuple-element.46), channel_id=1, source_target_pairs={{0,132},{1,5},{2,134},{3,7},{4,0},{5,129},{6,2},{7,131},{128,4},{1... | collective-permute-start | bytes 442376 | tf_op jit(solution)/shard_map/rZ4/ppermute | solution.py:28
  63.7 9.9 %collective-permute-start.19 = (bf16[128,1152]{1,0:T(8,128)(2,1)S(1)}, bf16[128,1152]{1,0:T(8,128)(2,1)S(1)}, u32[]{:S(2)}, u32[]{:S(2)}) collective-permute-start(bf16[128,1152]{1,0:T(8,128)(2,1)S(1)} %shard_map.74.refs_0_), channel_id=1, source_target_pairs={{0,132},{1,5},{2,134},{3,7},{4,0},{5,129},{6,2},{7,131},{128,4},{1... | collective-permute-start | bytes 884744 | tf_op jit(solution)/shard_map/rZ2/ppermute | solution.py:28
  70.0 5.2 %collective-permute-start.16 = (bf16[64,1152]{1,0:T(8,128)(2,1)S(1)}, bf16[64,1152]{1,0:T(8,128)(2,1)S(1)}, u32[]{:S(2)}, u32[]{:S(2)}) collective-permute-start(bf16[64,1152]{1,0:T(8,128)(2,1)S(1)} %get-tuple-element.48), channel_id=1, source_target_pairs={{0,96},{1,25},{2,98},{3,27},{4,100},{5,29},{6,102},{7,31},{128,224... | collective-permute-start | bytes 442376 | tf_op jit(solution)/shard_map/rA1/ppermute | solution.py:28
  71.4 6.7 %collective-permute-start.17 = (bf16[64,1152]{1,0:T(8,128)(2,1)S(1)}, bf16[64,1152]{1,0:T(8,128)(2,1)S(1)}, u32[]{:S(2)}, u32[]{:S(2)}) collective-permute-start(bf16[64,1152]{1,0:T(8,128)(2,1)S(1)} %get-tuple-element.49), channel_id=1, source_target_pairs={{0,64},{1,17},{2,66},{3,19},{4,68},{5,21},{6,70},{7,23},{128,192},... | collective-permute-start | bytes 442376 | tf_op jit(solution)/shard_map/rA2/ppermute | solution.py:28
  72.8 6.9 %collective-permute-start.18 = (bf16[64,1152]{1,0:T(8,128)(2,1)S(1)}, bf16[64,1152]{1,0:T(8,128)(2,1)S(1)}, u32[]{:S(2)}, u32[]{:S(2)}) collective-permute-start(bf16[64,1152]{1,0:T(8,128)(2,1)S(1)} %get-tuple-element.50), channel_id=1, source_target_pairs={{0,32},{1,9},{2,34},{3,11},{4,36},{5,13},{6,38},{7,15},{128,160},{... | collective-permute-start | bytes 442376 | tf_op jit(solution)/shard_map/rA3/ppermute | solution.py:28
  73.7 5.9 %collective-permute-start.20 = (bf16[64,1152]{1,0:T(8,128)(2,1)S(1)}, bf16[64,1152]{1,0:T(8,128)(2,1)S(1)}, u32[]{:S(2)}, u32[]{:S(2)}) collective-permute-start(bf16[64,1152]{1,0:T(8,128)(2,1)S(1)} %get-tuple-element.55), channel_id=1, source_target_pairs={{0,1},{1,0},{2,3},{3,2},{4,5},{5,4},{6,7},{7,6},{128,129},{129,128... | collective-permute-start | bytes 442376 | tf_op jit(solution)/shard_map/rS/ppermute | solution.py:28

commit v8 on v6

--- a/solution.py
+++ b/solution.py
@@ -248,12 +248,12 @@
     cross2 = shift(texts, cross(2), "gX2")
     swapped = shift(texts, other, "gC")
     img_own, img_unit, inv_img, txt_own, txt_unit, inv_txt = own_rows(images, texts, swapped)
-    group = stack([img_own, *side], [token(line2, cross2)])
-    send13 = stack([txt_own, swapped, line2, cross2])
-    far = [shift(group, second(k), "gB%d" % k) for k in (1, 2, 3)]
+    group = stack([img_own, *side], [])
+    send13 = stack([txt_own, swapped, line2, cross2], [])
+    far = [shift(group, second(k), "gB%d" % k) for k in (2, 1, 3)]
     near13 = shift(send13, line(1), "gZ13")
     near4 = shift(line2, line(2), "gZ4")
-    first_token = token(near13)
+    first_token = token(group)
     (scalars,) = call(
         scalar_kernel, [((8, 128), F32)], [log_temp.reshape(1, 1), bias.reshape(1, 1)], [near13]
     )
@@ -289,7 +289,7 @@
     txt_sum, txt_send = call(landed_kernel, [((own, dim), F32), ((own, dim), BF16)], [total_own, got13, got2])
     txt_last = shift(txt_send, other, "rS")
 
-    back = [shift(g, second(-k), "rB%d" % k) for k, g in zip((1, 2, 3), grads[1:])]
+    back = [shift(g, second(-k), "rB%d" % k) for k, g in ((1, grads[2]), (2, grads[1]), (3, grads[3]))]
     img_sum, *parts = call(
         sums_kernel, [((own, dim), F32)] + [((own, dim), BF16)] * 3, [grads[0], *back], ties=[token(middle)]
     )

time: 85.3 us -> 80.1 us (0.939)
  waiting for transfers between devices: 33.6 us -> 24.3 us
  starting transfers between devices: 35.2 us -> 39.2 us
    ppermute x23, waiting for transfers between devices: 33.6 us -> 24.3 us  [shift(): return lax.ppermute(values, AXES, pairs)]
    ppermute x23, starting transfers between devices: 35.2 us -> 39.2 us  [shift(): return lax.ppermute(values, AXES, pairs)]
    pallas_call x17 -> x16, Pallas kernels: 12 us -> 12 us  [call(): pl.pallas_call(lambda *refs: kernel(*refs[:n_in], *refs[n_in + len(ties):...]
  transfers between devices with their start and end apart: 23 -> 23, of which waited for: 12 -> 7; matrix products, arithmetic and copies ran while one was open for 0% -> 0% of each run, Pallas kernels for 9% -> 10%
where the time goes in v8:
time: 80.1 us; the launch traced here: 79.9 us
  starting transfers between devices  39.2 us (49%)
  waiting for transfers between devices  24.3 us (30%)
  Pallas kernels  12.5 us (16%)
  between operations  2.11 us (3%)
  local copies, waits for them, and re-layouts  1.81 us (2%)
    ppermute x23, starting transfers between devices, shift(): return lax.ppermute(values, AXES, pairs)  39.2 us
    ppermute x23, waiting for transfers between devices, shift(): return lax.ppermute(values, AXES, pairs)  24.3 us
    pallas_call x16, Pallas kernels, call(): pl.pallas_call(lambda *refs: kernel(*refs[:n_in], *refs[n_in + len(ties):...  12 us
    unnamed x4, local copies, waits for them, and re-layouts  1.81 us
  transfers between devices with their start and end apart: 23, of which 7 were waited for; matrix products, arithmetic and copies ran while one was open for 0% of the time, Pallas kernels for 10%

profile of v8, /device:TPU:24, one launch (start us, length us, event | category | flops | bytes accessed | tf_op | source)
XLA Modules:
  0.0 79.9 jit_solution(11829709165638915419)
XLA Ops:
  0.6 0.1 collective-permute-start
  0.7 1.6 %collective-permute-start.5 = (bf16[64,1152]{1,0:T(8,128)(2,1)}, bf16[64,1152]{1,0:T(8,128)(2,1)S(1)}, u32[]{:S(2)}, u32[]{:S(2)}) collective-permute-start(bf16[64,1152]{1,0:T(8,128)(2,1)} %refs_0_.1), channel_id=1, source_target_pairs={{0,32},{1,9},{2,34},{3,11},{4,36},{5,13},{6,38},{7,15},{128,160},{... | collective-permute-start | bytes 442376 | tf_op jit(solution)/shard_map/gA1/ppermute | solution.py:28
  2.3 1.7 %collective-permute-start.7 = (bf16[64,1152]{1,0:T(8,128)(2,1)}, bf16[64,1152]{1,0:T(8,128)(2,1)S(1)}, u32[]{:S(2)}, u32[]{:S(2)}) collective-permute-start(bf16[64,1152]{1,0:T(8,128)(2,1)} %refs_0_.1), channel_id=1, source_target_pairs={{0,96},{1,25},{2,98},{3,27},{4,100},{5,29},{6,102},{7,31},{128,224... | collective-permute-start | bytes 442376 | tf_op jit(solution)/shard_map/gA3/ppermute | solution.py:28
  4.0 1.8 %collective-permute-start.6 = (bf16[64,1152]{1,0:T(8,128)(2,1)}, bf16[64,1152]{1,0:T(8,128)(2,1)S(1)}, u32[]{:S(2)}, u32[]{:S(2)}) collective-permute-start(bf16[64,1152]{1,0:T(8,128)(2,1)} %refs_0_.1), channel_id=1, source_target_pairs={{0,64},{1,17},{2,66},{3,19},{4,68},{5,21},{6,70},{7,23},{128,192},... | collective-permute-start | bytes 442376 | tf_op jit(solution)/shard_map/gA2/ppermute | solution.py:28
  5.9 3.7 %collective-permute-start.2 = (bf16[64,1152]{1,0:T(8,128)(2,1)}, bf16[64,1152]{1,0:T(8,128)(2,1)S(1)}, u32[]{:S(2)}, u32[]{:S(2)}) collective-permute-start(bf16[64,1152]{1,0:T(8,128)(2,1)} %refs_1_.1), channel_id=1, source_target_pairs={{0,133},{1,4},{2,135},{3,6},{4,1},{5,128},{6,3},{7,130},{128,5},{1... | collective-permute-start | bytes 442376 | tf_op jit(solution)/shard_map/gX2/ppermute | solution.py:28
  9.6 0.0 collective-permute-done.tie_ref.refs_1_
  9.6 0.0 collective-permute-start.1
  10.9 0.0 copy-start
  10.9 0.9 %copy-done = bf16[64,1152]{1,0:T(8,128)(2,1)S(1)} copy-done((bf16[64,1152]{1,0:T(8,128)(2,1)S(1)}, bf16[64,1152]{1,0:T(8,128)(2,1)}, u32[]{:S(2)}) %copy-start) | copy-done | bytes 147480
  11.8 0.0 copy-start.1
  11.8 0.9 %copy-done.1 = bf16[64,1152]{1,0:T(8,128)(2,1)S(1)} copy-done((bf16[64,1152]{1,0:T(8,128)(2,1)S(1)}, bf16[64,1152]{1,0:T(8,128)(2,1)}, u32[]{:S(2)}) %copy-start.1) | copy-done | bytes 147480
  12.7 0.5 shard_map.59
  13.2 0.0 collective-permute-done.5.refs_1_
  13.2 0.0 collective-permute-done.7.refs_3_
  13.2 0.0 collective-permute-done.6.refs_2_
  13.3 1.2 %collective-permute-start.10 = (bf16[256,1152]{1,0:T(8,128)(2,1)S(1)}, bf16[256,1152]{1,0:T(8,128)(2,1)S(1)}, u32[]{:S(2)}, u32[]{:S(2)}) collective-permute-start(bf16[256,1152]{1,0:T(8,128)(2,1)S(1)} %shard_map.61.refs_0_), channel_id=1, source_target_pairs={{0,24},{1,97},{2,26},{3,99},{4,28},{5,101},{6,30},{7,103},{128,152... | collective-permute-start | bytes 1769480 | tf_op jit(solution)/shard_map/gB3/ppermute | solution.py:28
  14.5 2.1 %collective-permute-start.9 = (bf16[256,1152]{1,0:T(8,128)(2,1)S(1)}, bf16[256,1152]{1,0:T(8,128)(2,1)S(1)}, u32[]{:S(2)}, u32[]{:S(2)}) collective-permute-start(bf16[256,1152]{1,0:T(8,128)(2,1)S(1)} %shard_map.61.refs_0_), channel_id=1, source_target_pairs={{0,8},{1,33},{2,10},{3,35},{4,12},{5,37},{6,14},{7,39},{128,136},{... | collective-permute-start | bytes 1769480 | tf_op jit(solution)/shard_map/gB1/ppermute | solution.py:28
  16.6 1.1 %collective-permute-start.8 = (bf16[256,1152]{1,0:T(8,128)(2,1)S(1)}, bf16[256,1152]{1,0:T(8,128)(2,1)S(1)}, u32[]{:S(2)}, u32[]{:S(2)}) collective-permute-start(bf16[256,1152]{1,0:T(8,128)(2,1)S(1)} %shard_map.61.refs_0_), channel_id=1, source_target_pairs={{0,16},{1,65},{2,18},{3,67},{4,20},{5,69},{6,22},{7,71},{128,144},... | collective-permute-start | bytes 1769480 | tf_op jit(solution)/shard_map/gB2/ppermute | solution.py:28
  17.7 0.0 collective-permute-done.2.refs_3_
  17.7 0.0 collective-permute-done.1.refs_2_
  17.7 2.0 %collective-permute-start.3 = (bf16[256,1152]{1,0:T(8,128)(2,1)S(1)}, bf16[256,1152]{1,0:T(8,128)(2,1)S(1)}, u32[]{:S(2)}, u32[]{:S(2)}) collective-permute-start(bf16[256,1152]{1,0:T(8,128)(2,1)S(1)} %shard_map.60), channel_id=1, source_target_pairs={{0,2},{1,135},{2,4},{3,1},{4,6},{5,3},{6,128},{7,5},{128,130},{129... | collective-permute-start | bytes 1769480 | tf_op jit(solution)/shard_map/gZ13/ppermute | solution.py:28
  19.7 2.1 %collective-permute-start.4 = (bf16[64,1152]{1,0:T(8,128)(2,1)S(1)}, bf16[64,1152]{1,0:T(8,128)(2,1)S(1)}, u32[]{:S(2)}, u32[]{:S(2)}) collective-permute-start(bf16[64,1152]{1,0:T(8,128)(2,1)S(1)} %collective-permute-done.1.refs_2_), channel_id=1, source_target_pairs={{0,4},{1,133},{2,6},{3,135},{4,128},{5,1},{6,130},{7,3},{128,132},... | collective-permute-start | bytes 442376 | tf_op jit(solution)/shard_map/gZ4/ppermute | solution.py:28
  21.9 7.6 %collective-permute-done.3.refs_2_.refs_1_ = bf16[256,1152]{1,0:T(8,128)(2,1)S(1)} collective-permute-done((bf16[256,1152]{1,0:T(8,128)(2,1)S(1)}, bf16[256,1152]{1,0:T(8,128)(2,1)S(1)}, u32[]{:S(2)}, u32[]{:S(2)}) %collective-permute-start.3) | collective-permute-done | bytes 589856 | tf_op jit(solution)/shard_map/gZ13/ppermute | solution.py:28
  29.4 0.1 shard_map.62.refs_1_
  29.5 0.2 shard_map.63.refs_5_.refs_2_
  29.7 3.3 %collective-permute-done.4.refs_4_ = bf16[64,1152]{1,0:T(8,128)(2,1)S(1)} collective-permute-done((bf16[64,1152]{1,0:T(8,128)(2,1)S(1)}, bf16[64,1152]{1,0:T(8,128)(2,1)S(1)}, u32[]{:S(2)}, u32[]{:S(2)}) %collective-permute-start.4) | collective-permute-done | bytes 147488 | tf_op jit(solution)/shard_map/gZ4/ppermute | solution.py:28
  33.1 0.0 collective-permute-done.10.refs_9_.refs_5_
  33.1 0.0 collective-permute-done.9.refs_8_.refs_4_
  33.1 0.0 collective-permute-done.8.refs_7_.refs_3_
  33.1 0.4 shard_map.65.refs_0_.refs_2_
  33.5 0.3 collective-permute-start.11
  33.7 3.5 %shard_map.66 = (bf16[1024,512]{1,0:T(8,128)(2,1)S(1)}, bf16[1024,1152]{1,0:T(8,128)(2,1)S(1)}, bf16[512,1152]{1,0:T(8,128)(2,1)S(1)}) custom-call(bf16[512,1152]{1,0:T(8,128)(2,1)S(1)} %shard_map.65.refs_0_.refs_2_, f32[8,128]{1,0:T(8,128)S(1)} %shard_map.62.refs_1_, bf16[256,1152]{1,0:T(8,128)(2,1)S(1)} %shard_map.63.refs_5_.refs_2_, ...), custom_call_target="tpu_custom_call" | custom-call | flops 2415919104 | bytes 1024 | tf_op jit(solution)/shard_map/pallas_call | solution.py:54
  37.2 0.0 collective-permute-done.11.refs_0_.refs_3_
  37.2 3.0 %shard_map.67 = (bf16[1024,512]{1,0:T(8,128)(2,1)S(1)}, bf16[512,1152]{1,0:T(8,128)(2,1)S(1)}) custom-call(bf16[512,1152]{1,0:T(8,128)(2,1)S(1)} %collective-permute-done.11.refs_0_.refs_3_, f32[8,128]{1,0:T(8,128)S(1)} %shard_map.62.refs_1_, bf16[1024,1152]{1,0:T(8,128)(2,1)S(1)} %get-tuple-element.32.refs_2_, ...), custom_call_target="tpu_custom_call" | custom-call | flops 2415919104 | bytes 1024 | tf_op jit(solution)/shard_map/pallas_call | solution.py:54
  40.3 0.6 collective-permute-start.15
  40.9 2.9 %shard_map.68 = (f32[256,1152]{1,0:T(8,128)S(1)}, bf16[256,1152]{1,0:T(8,128)(2,1)S(1)}, bf16[256,1152]{1,0:T(8,128)(2,1)S(1)}, bf16[256,1152]{1,0:T(8,128)(2,1)S(1)}) custom-call(bf16[1024,512]{1,0:T(8,128)(2,1)S(1)} %get-tuple-element.31.refs_0_, bf16[1024,512]{1,0:T(8,128)(2,1)S(1)} %get-tuple-element.34.refs_1_, ...), custom_call_target="tpu_custom_call" | custom-call | flops 2415919104 | bytes 1024 | tf_op jit(solution)/shard_map/pallas_call | solution.py:54
  43.8 0.0 collective-permute-done.15.refs_1_
  43.8 0.3 shard_map.69
  44.1 2.8 %collective-permute-start.16 = (bf16[256,1152]{1,0:T(8,128)(2,1)S(1)}, bf16[256,1152]{1,0:T(8,128)(2,1)S(1)}, u32[]{:S(2)}, u32[]{:S(2)}) collective-permute-start(bf16[256,1152]{1,0:T(8,128)(2,1)S(1)} %get-tuple-element.41), channel_id=1, source_target_pairs={{0,134},{1,3},{2,0},{3,5},{4,2},{5,7},{6,4},{7,129},{128,6},{129,1... | collective-permute-start | bytes 1769480 | tf_op jit(solution)/shard_map/rZ13/ppermute | solution.py:28
  46.9 1.9 %collective-permute-start.14 = (bf16[256,1152]{1,0:T(8,128)(2,1)S(1)}, bf16[256,1152]{1,0:T(8,128)(2,1)S(1)}, u32[]{:S(2)}, u32[]{:S(2)}) collective-permute-start(bf16[256,1152]{1,0:T(8,128)(2,1)S(1)} %get-tuple-element.38.refs_2_), channel_id=1, source_target_pairs={{0,8},{1,33},{2,10},{3,35},{4,12},{5,37},{6,14},{7,39},{128,136},{... | collective-permute-start | bytes 1769480 | tf_op jit(solution)/shard_map/rB3/ppermute | solution.py:28
  48.8 0.1 collective-permute-start.12
  48.9 1.7 %collective-permute-start.13 = (bf16[256,1152]{1,0:T(8,128)(2,1)S(1)}, bf16[256,1152]{1,0:T(8,128)(2,1)S(1)}, u32[]{:S(2)}, u32[]{:S(2)}) collective-permute-start(bf16[256,1152]{1,0:T(8,128)(2,1)S(1)} %get-tuple-element.37), channel_id=1, source_target_pairs={{0,16},{1,65},{2,18},{3,67},{4,20},{5,69},{6,22},{7,71},{128,144},... | collective-permute-start | bytes 1769480 | tf_op jit(solution)/shard_map/rB2/ppermute | solution.py:28
  50.6 2.8 %collective-permute-start.17 = (bf16[64,1152]{1,0:T(8,128)(2,1)S(1)}, bf16[64,1152]{1,0:T(8,128)(2,1)S(1)}, u32[]{:S(2)}, u32[]{:S(2)}) collective-permute-start(bf16[64,1152]{1,0:T(8,128)(2,1)S(1)} %get-tuple-element.42), channel_id=1, source_target_pairs={{0,132},{1,5},{2,134},{3,7},{4,0},{5,129},{6,2},{7,131},{128,4},{1... | collective-permute-start | bytes 442376 | tf_op jit(solution)/shard_map/rZ4/ppermute | solution.py:28
  53.4 2.5 %collective-permute-done.16.refs_0_.refs_1_ = bf16[256,1152]{1,0:T(8,128)(2,1)S(1)} collective-permute-done((bf16[256,1152]{1,0:T(8,128)(2,1)S(1)}, bf16[256,1152]{1,0:T(8,128)(2,1)S(1)}, u32[]{:S(2)}, u32[]{:S(2)}) %collective-permute-start.16) | collective-permute-done | bytes 589856 | tf_op jit(solution)/shard_map/rZ13/ppermute | solution.py:28
  55.9 2.3 %collective-permute-done.17.refs_2_ = bf16[64,1152]{1,0:T(8,128)(2,1)S(1)} collective-permute-done((bf16[64,1152]{1,0:T(8,128)(2,1)S(1)}, bf16[64,1152]{1,0:T(8,128)(2,1)S(1)}, u32[]{:S(2)}, u32[]{:S(2)}) %collective-permute-start.17) | collective-permute-done | bytes 147488 | tf_op jit(solution)/shard_map/rZ4/ppermute | solution.py:28
  58.2 0.1 shard_map.71.refs_0_
  58.3 4.1 %collective-permute-start.21 = (bf16[128,1152]{1,0:T(8,128)(2,1)S(1)}, bf16[128,1152]{1,0:T(8,128)(2,1)S(1)}, u32[]{:S(2)}, u32[]{:S(2)}) collective-permute-start(bf16[128,1152]{1,0:T(8,128)(2,1)S(1)} %shard_map.71.refs_0_), channel_id=1, source_target_pairs={{0,132},{1,5},{2,134},{3,7},{4,0},{5,129},{6,2},{7,131},{128,4},{1... | collective-permute-start | bytes 884744 | tf_op jit(solution)/shard_map/rZ2/ppermute | solution.py:28
  62.4 3.8 %collective-permute-done.12.refs_1_ = bf16[256,1152]{1,0:T(8,128)(2,1)S(1)} collective-permute-done((bf16[256,1152]{1,0:T(8,128)(2,1)S(1)}, bf16[256,1152]{1,0:T(8,128)(2,1)S(1)}, u32[]{:S(2)}, u32[]{:S(2)}) %collective-permute-start.12) | collective-permute-done | bytes 589856 | tf_op jit(solution)/shard_map/rB1/ppermute | solution.py:28
  66.2 0.0 collective-permute-done.13.refs_2_
  66.2 0.0 collective-permute-done.14.refs_3_
  66.2 0.3 shard_map.73
  66.5 2.8 %collective-permute-start.18 = (bf16[64,1152]{1,0:T(8,128)(2,1)S(1)}, bf16[64,1152]{1,0:T(8,128)(2,1)S(1)}, u32[]{:S(2)}, u32[]{:S(2)}) collective-permute-start(bf16[64,1152]{1,0:T(8,128)(2,1)S(1)} %get-tuple-element.44), channel_id=1, source_target_pairs={{0,96},{1,25},{2,98},{3,27},{4,100},{5,29},{6,102},{7,31},{128,224... | collective-permute-start | bytes 442376 | tf_op jit(solution)/shard_map/rA1/ppermute | solution.py:28
  69.3 3.2 %collective-permute-start.19 = (bf16[64,1152]{1,0:T(8,128)(2,1)S(1)}, bf16[64,1152]{1,0:T(8,128)(2,1)S(1)}, u32[]{:S(2)}, u32[]{:S(2)}) collective-permute-start(bf16[64,1152]{1,0:T(8,128)(2,1)S(1)} %get-tuple-element.45), channel_id=1, source_target_pairs={{0,64},{1,17},{2,66},{3,19},{4,68},{5,21},{6,70},{7,23},{128,192},... | collective-permute-start | bytes 442376 | tf_op jit(solution)/shard_map/rA2/ppermute | solution.py:28
  72.5 1.3 %collective-permute-start.20 = (bf16[64,1152]{1,0:T(8,128)(2,1)S(1)}, bf16[64,1152]{1,0:T(8,128)(2,1)S(1)}, u32[]{:S(2)}, u32[]{:S(2)}) collective-permute-start(bf16[64,1152]{1,0:T(8,128)(2,1)S(1)} %get-tuple-element.46), channel_id=1, source_target_pairs={{0,32},{1,9},{2,34},{3,11},{4,36},{5,13},{6,38},{7,15},{128,160},{... | collective-permute-start | bytes 442376 | tf_op jit(solution)/shard_map/rA3/ppermute | solution.py:28
  73.8 0.0 collective-permute-done.21.refs_2_
  73.8 0.1 shard_map.74
  73.9 0.1 collective-permute-start.22
  74.0 0.0 collective-permute-done.18.refs_3_
  74.0 1.9 %collective-permute-done.19.refs_4_ = bf16[64,1152]{1,0:T(8,128)(2,1)S(1)} collective-permute-done((bf16[64,1152]{1,0:T(8,128)(2,1)S(1)}, bf16[64,1152]{1,0:T(8,128)(2,1)S(1)}, u32[]{:S(2)}, u32[]{:S(2)}) %collective-permute-start.19) | collective-permute-done | bytes 147488 | tf_op jit(solution)/shard_map/rA2/ppermute | solution.py:28
  75.9 2.9 %collective-permute-done.20.refs_5_ = bf16[64,1152]{1,0:T(8,128)(2,1)S(1)} collective-permute-done((bf16[64,1152]{1,0:T(8,128)(2,1)S(1)}, bf16[64,1152]{1,0:T(8,128)(2,1)S(1)}, u32[]{:S(2)}, u32[]{:S(2)}) %collective-permute-start.20) | collective-permute-done | bytes 147488 | tf_op jit(solution)/shard_map/rA3/ppermute | solution.py:28
  78.9 0.0 collective-permute-done.22.refs_9_
  78.9 1.1 %shard_map.75 = (f32[64,1152]{1,0:T(8,128)}, f32[64,1152]{1,0:T(8,128)}) custom-call(f32[64,1152]{1,0:T(8,128)S(1)} %get-tuple-element.27.refs_0_, f32[64,128]{1,0:T(8,128)S(1)} %get-tuple-element.28.refs_1_, f32[64,1152]{1,0:T(8,128)S(1)} %get-tuple-element.43.refs_2_, bf16[64,1152]{1,0:T(8,128)(2,1)S(1)} %collective-permute-done.18.refs_3_, ...), custom_call_target="tpu_custom_call" | custom-call | bytes 1024 | tf_op jit(solution)/shard_map/pallas_call | solution.py:54
  (5 shorter events, 0.1 us)
Async XLA Ops:
  0.6 8.9 %collective-permute-start = (bf16[64,1152]{1,0:T(8,128)(2,1)}, bf16[64,1152]{1,0:T(8,128)(2,1)S(1)}, u32[]{:S(2)}, u32[]{:S(2)}) collective-permute-start(bf16[64,1152]{1,0:T(8,128)(2,1)} %refs_1_.1), channel_id=1, source_target_pairs={{0,1},{1,0},{2,3},{3,2},{4,5},{5,4},{6,7},{7,6},{128,129},{129,128... | collective-permute-start | bytes 442376 | tf_op jit(solution)/shard_map/gC/ppermute | solution.py:28
  0.7 12.5 %collective-permute-start.5 = (bf16[64,1152]{1,0:T(8,128)(2,1)}, bf16[64,1152]{1,0:T(8,128)(2,1)S(1)}, u32[]{:S(2)}, u32[]{:S(2)}) collective-permute-start(bf16[64,1152]{1,0:T(8,128)(2,1)} %refs_0_.1), channel_id=1, source_target_pairs={{0,32},{1,9},{2,34},{3,11},{4,36},{5,13},{6,38},{7,15},{128,160},{... | collective-permute-start | bytes 442376 | tf_op jit(solution)/shard_map/gA1/ppermute | solution.py:28
  2.3 10.9 %collective-permute-start.7 = (bf16[64,1152]{1,0:T(8,128)(2,1)}, bf16[64,1152]{1,0:T(8,128)(2,1)S(1)}, u32[]{:S(2)}, u32[]{:S(2)}) collective-permute-start(bf16[64,1152]{1,0:T(8,128)(2,1)} %refs_0_.1), channel_id=1, source_target_pairs={{0,96},{1,25},{2,98},{3,27},{4,100},{5,29},{6,102},{7,31},{128,224... | collective-permute-start | bytes 442376 | tf_op jit(solution)/shard_map/gA3/ppermute | solution.py:28
  4.0 9.2 %collective-permute-start.6 = (bf16[64,1152]{1,0:T(8,128)(2,1)}, bf16[64,1152]{1,0:T(8,128)(2,1)S(1)}, u32[]{:S(2)}, u32[]{:S(2)}) collective-permute-start(bf16[64,1152]{1,0:T(8,128)(2,1)} %refs_0_.1), channel_id=1, source_target_pairs={{0,64},{1,17},{2,66},{3,19},{4,68},{5,21},{6,70},{7,23},{128,192},... | collective-permute-start | bytes 442376 | tf_op jit(solution)/shard_map/gA2/ppermute | solution.py:28
  5.9 11.8 %collective-permute-start.2 = (bf16[64,1152]{1,0:T(8,128)(2,1)}, bf16[64,1152]{1,0:T(8,128)(2,1)S(1)}, u32[]{:S(2)}, u32[]{:S(2)}) collective-permute-start(bf16[64,1152]{1,0:T(8,128)(2,1)} %refs_1_.1), channel_id=1, source_target_pairs={{0,133},{1,4},{2,135},{3,6},{4,1},{5,128},{6,3},{7,130},{128,5},{1... | collective-permute-start | bytes 442376 | tf_op jit(solution)/shard_map/gX2/ppermute | solution.py:28
  9.6 8.1 %collective-permute-start.1 = (bf16[64,1152]{1,0:T(8,128)(2,1)}, bf16[64,1152]{1,0:T(8,128)(2,1)S(1)}, u32[]{:S(2)}, u32[]{:S(2)}) collective-permute-start(bf16[64,1152]{1,0:T(8,128)(2,1)} %refs_1_.1), channel_id=1, source_target_pairs={{0,4},{1,133},{2,6},{3,135},{4,128},{5,1},{6,130},{7,3},{128,132},... | collective-permute-start | bytes 442376 | tf_op jit(solution)/shard_map/gZ2/ppermute | solution.py:28
  10.9 0.9 %copy-start = (bf16[64,1152]{1,0:T(8,128)(2,1)S(1)}, bf16[64,1152]{1,0:T(8,128)(2,1)}, u32[]{:S(2)}) copy-start(bf16[64,1152]{1,0:T(8,128)(2,1)} %refs_0_.1) | copy-start | bytes 442372
  11.8 0.9 %copy-start.1 = (bf16[64,1152]{1,0:T(8,128)(2,1)S(1)}, bf16[64,1152]{1,0:T(8,128)(2,1)}, u32[]{:S(2)}) copy-start(bf16[64,1152]{1,0:T(8,128)(2,1)} %refs_1_.1) | copy-start | bytes 442372
  13.3 19.8 %collective-permute-start.10 = (bf16[256,1152]{1,0:T(8,128)(2,1)S(1)}, bf16[256,1152]{1,0:T(8,128)(2,1)S(1)}, u32[]{:S(2)}, u32[]{:S(2)}) collective-permute-start(bf16[256,1152]{1,0:T(8,128)(2,1)S(1)} %shard_map.61.refs_0_), channel_id=1, source_target_pairs={{0,24},{1,97},{2,26},{3,99},{4,28},{5,101},{6,30},{7,103},{128,152... | collective-permute-start | bytes 1769480 | tf_op jit(solution)/shard_map/gB3/ppermute | solution.py:28
  14.5 18.6 %collective-permute-start.9 = (bf16[256,1152]{1,0:T(8,128)(2,1)S(1)}, bf16[256,1152]{1,0:T(8,128)(2,1)S(1)}, u32[]{:S(2)}, u32[]{:S(2)}) collective-permute-start(bf16[256,1152]{1,0:T(8,128)(2,1)S(1)} %shard_map.61.refs_0_), channel_id=1, source_target_pairs={{0,8},{1,33},{2,10},{3,35},{4,12},{5,37},{6,14},{7,39},{128,136},{... | collective-permute-start | bytes 1769480 | tf_op jit(solution)/shard_map/gB1/ppermute | solution.py:28
  16.6 16.5 %collective-permute-start.8 = (bf16[256,1152]{1,0:T(8,128)(2,1)S(1)}, bf16[256,1152]{1,0:T(8,128)(2,1)S(1)}, u32[]{:S(2)}, u32[]{:S(2)}) collective-permute-start(bf16[256,1152]{1,0:T(8,128)(2,1)S(1)} %shard_map.61.refs_0_), channel_id=1, source_target_pairs={{0,16},{1,65},{2,18},{3,67},{4,20},{5,69},{6,22},{7,71},{128,144},... | collective-permute-start | bytes 1769480 | tf_op jit(solution)/shard_map/gB2/ppermute | solution.py:28
  17.7 11.7 %collective-permute-start.3 = (bf16[256,1152]{1,0:T(8,128)(2,1)S(1)}, bf16[256,1152]{1,0:T(8,128)(2,1)S(1)}, u32[]{:S(2)}, u32[]{:S(2)}) collective-permute-start(bf16[256,1152]{1,0:T(8,128)(2,1)S(1)} %shard_map.60), channel_id=1, source_target_pairs={{0,2},{1,135},{2,4},{3,1},{4,6},{5,3},{6,128},{7,5},{128,130},{129... | collective-permute-start | bytes 1769480 | tf_op jit(solution)/shard_map/gZ13/ppermute | solution.py:28
  19.7 13.3 %collective-permute-start.4 = (bf16[64,1152]{1,0:T(8,128)(2,1)S(1)}, bf16[64,1152]{1,0:T(8,128)(2,1)S(1)}, u32[]{:S(2)}, u32[]{:S(2)}) collective-permute-start(bf16[64,1152]{1,0:T(8,128)(2,1)S(1)} %collective-permute-done.1.refs_2_), channel_id=1, source_target_pairs={{0,4},{1,133},{2,6},{3,135},{4,128},{5,1},{6,130},{7,3},{128,132},... | collective-permute-start | bytes 442376 | tf_op jit(solution)/shard_map/gZ4/ppermute | solution.py:28
  33.5 3.8 %collective-permute-start.11 = (bf16[512,1152]{1,0:T(8,128)(2,1)S(1)}, bf16[512,1152]{1,0:T(8,128)(2,1)S(1)}, u32[]{:S(2)}, u32[]{:S(2)}) collective-permute-start(bf16[512,1152]{1,0:T(8,128)(2,1)S(1)} %shard_map.65.refs_0_.refs_2_), channel_id=1, source_target_pairs={{0,1},{1,0},{2,3},{3,2},{4,5},{5,4},{6,7},{7,6},{128,129},{129,128... | collective-permute-start | bytes 3538952 | tf_op jit(solution)/shard_map/gS/ppermute | solution.py:28
  40.3 3.5 %collective-permute-start.15 = (bf16[512,1152]{1,0:T(8,128)(2,1)S(1)}, bf16[512,1152]{1,0:T(8,128)(2,1)S(1)}, u32[]{:S(2)}, u32[]{:S(2)}) collective-permute-start(bf16[512,1152]{1,0:T(8,128)(2,1)S(1)} %get-tuple-element.39), channel_id=1, source_target_pairs={{0,1},{1,0},{2,3},{3,2},{4,5},{5,4},{6,7},{7,6},{128,129},{129,128... | collective-permute-start | bytes 3538952 | tf_op jit(solution)/shard_map/rC/ppermute | solution.py:28
  44.1 11.8 %collective-permute-start.16 = (bf16[256,1152]{1,0:T(8,128)(2,1)S(1)}, bf16[256,1152]{1,0:T(8,128)(2,1)S(1)}, u32[]{:S(2)}, u32[]{:S(2)}) collective-permute-start(bf16[256,1152]{1,0:T(8,128)(2,1)S(1)} %get-tuple-element.41), channel_id=1, source_target_pairs={{0,134},{1,3},{2,0},{3,5},{4,2},{5,7},{6,4},{7,129},{128,6},{129,1... | collective-permute-start | bytes 1769480 | tf_op jit(solution)/shard_map/rZ13/ppermute | solution.py:28
  46.9 19.3 %collective-permute-start.14 = (bf16[256,1152]{1,0:T(8,128)(2,1)S(1)}, bf16[256,1152]{1,0:T(8,128)(2,1)S(1)}, u32[]{:S(2)}, u32[]{:S(2)}) collective-permute-start(bf16[256,1152]{1,0:T(8,128)(2,1)S(1)} %get-tuple-element.38.refs_2_), channel_id=1, source_target_pairs={{0,8},{1,33},{2,10},{3,35},{4,12},{5,37},{6,14},{7,39},{128,136},{... | collective-permute-start | bytes 1769480 | tf_op jit(solution)/shard_map/rB3/ppermute | solution.py:28
  48.8 17.4 %collective-permute-start.12 = (bf16[256,1152]{1,0:T(8,128)(2,1)S(1)}, bf16[256,1152]{1,0:T(8,128)(2,1)S(1)}, u32[]{:S(2)}, u32[]{:S(2)}) collective-permute-start(bf16[256,1152]{1,0:T(8,128)(2,1)S(1)} %get-tuple-element.36), channel_id=1, source_target_pairs={{0,24},{1,97},{2,26},{3,99},{4,28},{5,101},{6,30},{7,103},{128,152... | collective-permute-start | bytes 1769480 | tf_op jit(solution)/shard_map/rB1/ppermute | solution.py:28
  48.9 17.3 %collective-permute-start.13 = (bf16[256,1152]{1,0:T(8,128)(2,1)S(1)}, bf16[256,1152]{1,0:T(8,128)(2,1)S(1)}, u32[]{:S(2)}, u32[]{:S(2)}) collective-permute-start(bf16[256,1152]{1,0:T(8,128)(2,1)S(1)} %get-tuple-element.37), channel_id=1, source_target_pairs={{0,16},{1,65},{2,18},{3,67},{4,20},{5,69},{6,22},{7,71},{128,144},... | collective-permute-start | bytes 1769480 | tf_op jit(solution)/shard_map/rB2/ppermute | solution.py:28
  50.6 7.6 %collective-permute-start.17 = (bf16[64,1152]{1,0:T(8,128)(2,1)S(1)}, bf16[64,1152]{1,0:T(8,128)(2,1)S(1)}, u32[]{:S(2)}, u32[]{:S(2)}) collective-permute-start(bf16[64,1152]{1,0:T(8,128)(2,1)S(1)} %get-tuple-element.42), channel_id=1, source_target_pairs={{0,132},{1,5},{2,134},{3,7},{4,0},{5,129},{6,2},{7,131},{128,4},{1... | collective-permute-start | bytes 442376 | tf_op jit(solution)/shard_map/rZ4/ppermute | solution.py:28
  58.3 15.5 %collective-permute-start.21 = (bf16[128,1152]{1,0:T(8,128)(2,1)S(1)}, bf16[128,1152]{1,0:T(8,128)(2,1)S(1)}, u32[]{:S(2)}, u32[]{:S(2)}) collective-permute-start(bf16[128,1152]{1,0:T(8,128)(2,1)S(1)} %shard_map.71.refs_0_), channel_id=1, source_target_pairs={{0,132},{1,5},{2,134},{3,7},{4,0},{5,129},{6,2},{7,131},{128,4},{1... | collective-permute-start | bytes 884744 | tf_op jit(solution)/shard_map/rZ2/ppermute | solution.py:28
  66.5 7.6 %collective-permute-start.18 = (bf16[64,1152]{1,0:T(8,128)(2,1)S(1)}, bf16[64,1152]{1,0:T(8,128)(2,1)S(1)}, u32[]{:S(2)}, u32[]{:S(2)}) collective-permute-start(bf16[64,1152]{1,0:T(8,128)(2,1)S(1)} %get-tuple-element.44), channel_id=1, source_target_pairs={{0,96},{1,25},{2,98},{3,27},{4,100},{5,29},{6,102},{7,31},{128,224... | collective-permute-start | bytes 442376 | tf_op jit(solution)/shard_map/rA1/ppermute | solution.py:28
  69.3 6.6 %collective-permute-start.19 = (bf16[64,1152]{1,0:T(8,128)(2,1)S(1)}, bf16[64,1152]{1,0:T(8,128)(2,1)S(1)}, u32[]{:S(2)}, u32[]{:S(2)}) collective-permute-start(bf16[64,1152]{1,0:T(8,128)(2,1)S(1)} %get-tuple-element.45), channel_id=1, source_target_pairs={{0,64},{1,17},{2,66},{3,19},{4,68},{5,21},{6,70},{7,23},{128,192},... | collective-permute-start | bytes 442376 | tf_op jit(solution)/shard_map/rA2/ppermute | solution.py:28
  72.5 6.4 %collective-permute-start.20 = (bf16[64,1152]{1,0:T(8,128)(2,1)S(1)}, bf16[64,1152]{1,0:T(8,128)(2,1)S(1)}, u32[]{:S(2)}, u32[]{:S(2)}) collective-permute-start(bf16[64,1152]{1,0:T(8,128)(2,1)S(1)} %get-tuple-element.46), channel_id=1, source_target_pairs={{0,32},{1,9},{2,34},{3,11},{4,36},{5,13},{6,38},{7,15},{128,160},{... | collective-permute-start | bytes 442376 | tf_op jit(solution)/shard_map/rA3/ppermute | solution.py:28
  73.9 4.9 %collective-permute-start.22 = (bf16[64,1152]{1,0:T(8,128)(2,1)S(1)}, bf16[64,1152]{1,0:T(8,128)(2,1)S(1)}, u32[]{:S(2)}, u32[]{:S(2)}) collective-permute-start(bf16[64,1152]{1,0:T(8,128)(2,1)S(1)} %get-tuple-element.51), channel_id=1, source_target_pairs={{0,1},{1,0},{2,3},{3,2},{4,5},{5,4},{6,7},{7,6},{128,129},{129,128... | collective-permute-start | bytes 442376 | tf_op jit(solution)/shard_map/rS/ppermute | solution.py:28

commit v9 on v8

--- a/solution.py
+++ b/solution.py
@@ -40,25 +40,23 @@
     return lambda x, y, z, c: (x, y, z + k, c) if c == 0 else (x, y, z - k, c)
 
 
-def cross(k):
-    return lambda x, y, z, c: (x, y, z + k, 0) if c == 1 else (x, y, z - k, 1)
-
-
 def other(x, y, z, c):
     return (x, y, z, 1 - c)
 
 
-def call(kernel, outs, arrays, ties=(), flops=0, limit=8):
+def call(kernel, outs, arrays, ties=(), first=(), scratch=(), flops=0, limit=8):
     vmem = pl.BlockSpec(memory_space=pltpu.VMEM)
-    n_in = len(arrays)
+    anywhere = pl.BlockSpec(memory_space=pl.ANY)
+    n_in = len(first) + len(arrays)
     return pl.pallas_call(
         lambda *refs: kernel(*refs[:n_in], *refs[n_in + len(ties):]),
         out_shape=tuple(jax.ShapeDtypeStruct(shape, dtype) for shape, dtype in outs),
-        in_specs=[vmem] * n_in + [pl.BlockSpec(memory_space=pl.ANY)] * len(ties),
+        in_specs=[anywhere] * len(first) + [vmem] * len(arrays) + [anywhere] * len(ties),
         out_specs=tuple([vmem] * len(outs)),
+        scratch_shapes=list(scratch),
         compiler_params=pltpu.CompilerParams(vmem_limit_bytes=limit * 1024 * 1024),
         cost_estimate=pl.CostEstimate(flops=flops, bytes_accessed=1024, transcendentals=0),
-    )(*arrays, *ties)
+    )(*first, *arrays, *ties)
 
 
 def token_kernel(token_ref):
@@ -80,60 +78,64 @@
     return (grad_unit - unit * along) * inverse
 
 
-def own_kernel(img_hbm, txt_hbm, *refs):
-    *outs, sems = refs
-    pairs = ((img_hbm, outs[0]), (txt_hbm, outs[3]))
-    copies = [pltpu.make_async_copy(src, dst, sems.at[n]) for n, (src, dst) in enumerate(pairs)]
-    for copy in copies:
-        copy.start()
-    for copy in copies:
-        copy.wait()
-    for raw_ref, unit_ref, inv_ref in (outs[:3], outs[3:]):
-        unit, inverse = unit_rows(raw_ref[...])
-        unit_ref[...] = unit
-        inv_ref[...] = jnp.broadcast_to(inverse, inv_ref.shape)
-
-
-def own_rows(images, texts, tie):
-    own, dim = images.shape
-    outs = [((own, dim), BF16), ((own, dim), F32), ((own, 128), F32)] * 2
-    return pl.pallas_call(
-        lambda tie_ref, *refs: own_kernel(*refs),
-        out_shape=tuple(jax.ShapeDtypeStruct(shape, dtype) for shape, dtype in outs),
-        in_specs=[pl.BlockSpec(memory_space=pl.ANY)] * 3,
-        out_specs=tuple([pl.BlockSpec(memory_space=pltpu.VMEM)] * len(outs)),
-        scratch_shapes=[pltpu.SemaphoreType.DMA((2,))],
-        compiler_params=pltpu.CompilerParams(vmem_limit_bytes=8 * 1024 * 1024),
-        cost_estimate=pl.CostEstimate(flops=0, bytes_accessed=1024, transcendentals=0),
-    )(tie, images, texts)
-
-
-def stack_kernel(*refs):
-    *parts, out_ref = refs
-    at = 0
+def stack_kernel(own_hbm, *refs):
+    *parts, out_ref, sem = refs
+    rows = own_hbm.shape[0]
+    copy = pltpu.make_async_copy(own_hbm, out_ref.at[pl.ds(0, rows)], sem)
+    copy.start()
+    at = rows
     for part in parts:
         rows = part.shape[0]
         out_ref[at:at + rows, :] = part[...]
         at += rows
-
-
-def stack(parts, ties=()):
-    rows, dim = sum(p.shape[0] for p in parts), parts[0].shape[1]
-    return call(stack_kernel, [((rows, dim), BF16)], parts, ties=ties)[0]
-
-
-def round_kernel(step, *refs):
-    *parts, out_ref = refs
-    base = 0
-    for part in parts:
-        for at in range(0, part.shape[0], step):
-            out_ref[base:base + step, :] = unit_rows(part[at:at + step, :])[0].astype(BF16)
-            base += step
-
-
-def rounded(parts, ties=()):
-    rows, dim = sum(p.shape[0] for p in parts), parts[0].shape[1]
-    return call(lambda *refs: round_kernel(64, *refs), [((rows, dim), BF16)], parts, ties=ties)[0]
+    copy.wait()
+
+
+def stack(own_raw, parts, ties=()):
+    rows, dim = own_raw.shape
+    rows += sum(p.shape[0] for p in parts)
+    return call(
+        stack_kernel, [((rows, dim), BF16)], parts, ties=ties, first=[own_raw], scratch=[pltpu.SemaphoreType.DMA(())]
+    )[0]
+
+
+def head_kernel(in_ref, out_ref):
+    out_ref[...] = in_ref[...]
+
+
+def send_kernel(pair_ref, near_ref, send13_ref, send4_ref):
+    rows = pair_ref.shape[0]
+    send13_ref[:rows, :] = pair_ref[...]
+    send13_ref[rows:, :] = near_ref[...]
+    send4_ref[...] = near_ref[:send4_ref.shape[0], :]
+
+
+def round_rows(raw_ref, start, out_ref, at, rows, own=None):
+    step = 64
+    for n in range(0, rows, step):
+        unit, inverse = unit_rows(raw_ref[start + n:start + n + step, :])
+        out_ref[at + n:at + n + step, :] = unit.astype(BF16)
+        if own is not None and n == 0:
+            own[0][...] = unit
+            own[1][...] = jnp.broadcast_to(inverse, own[1].shape)
+
+
+def group_round_kernel(raw_ref, out_ref, unit_ref, inv_ref):
+    round_rows(raw_ref, 0, out_ref, 0, raw_ref.shape[0], (unit_ref, inv_ref))
+
+
+def early_round_kernel(raw_ref, out_ref, unit_ref, inv_ref):
+    own = unit_ref.shape[0]
+    round_rows(raw_ref, 0, out_ref, 0, own, (unit_ref, inv_ref))
+    round_rows(raw_ref, 2 * own, out_ref, own, 2 * own)
+
+
+def mine_round_kernel(early_ref, near13_ref, near4_ref, out_ref):
+    own = near4_ref.shape[0]
+    out_ref[:own, :] = early_ref[:own, :]
+    round_rows(near13_ref, 0, out_ref, own, 4 * own)
+    out_ref[5 * own:7 * own, :] = early_ref[own:, :]
+    round_rows(near4_ref, 0, out_ref, 7 * own, own)
 
 
 def scalar_kernel(log_ref, bias_ref, scal_ref):
@@ -243,22 +245,25 @@
 def local(images, texts, log_temp, bias):
     own, dim = images.shape
 
+    swapped = shift(texts, other, "gC")
     side = [shift(images, first(k), "gA%d" % k) for k in (1, 2, 3)]
-    line2 = shift(texts, line(2), "gZ2")
-    cross2 = shift(texts, cross(2), "gX2")
-    swapped = shift(texts, other, "gC")
-    img_own, img_unit, inv_img, txt_own, txt_unit, inv_txt = own_rows(images, texts, swapped)
-    group = stack([img_own, *side], [])
-    send13 = stack([txt_own, swapped, line2, cross2], [])
+    pair = stack(texts, [swapped])
+    near2 = shift(pair, line(2), "gZ2")
+    group = stack(images, side, [token(pair)])
+    send13, send4 = call(send_kernel, [((4 * own, dim), BF16), ((own, dim), BF16)], [pair, near2], [group])
     far = [shift(group, second(k), "gB%d" % k) for k in (2, 1, 3)]
     near13 = shift(send13, line(1), "gZ13")
-    near4 = shift(line2, line(2), "gZ4")
+    near4 = shift(call(head_kernel, [((own, dim), BF16)], [send4], [send13])[0], line(2), "gZ4")
     first_token = token(group)
     (scalars,) = call(
         scalar_kernel, [((8, 128), F32)], [log_temp.reshape(1, 1), bias.reshape(1, 1)], [near13]
     )
-    group = rounded([group], [scalars])
-    mine = rounded([txt_own, near13, line2, cross2, near4], [group, first_token, *far])
+    per_row = [((own, dim), F32), ((own, 128), F32)]
+    group, img_unit, inv_img = call(group_round_kernel, [(group.shape, BF16)] + per_row, [group], [scalars])
+    early, txt_unit, inv_txt = call(early_round_kernel, [((3 * own, dim), BF16)] + per_row, [send13], [scalars])
+    (mine,) = call(
+        mine_round_kernel, [((8 * own, dim), BF16)], [early, near13, near4], [group, first_token, *far]
+    )
     theirs = shift(mine, other, "gS")
 
     half = mine.shape[0]

time: 80.1 us -> 79.4 us (level); the launches traced: 79.9 us -> 78.4 us
  starting transfers between devices: 39.2 us -> 34.3 us
  waiting for transfers between devices: 24.3 us -> 28.8 us
  local copies, waits for them, and re-layouts: 1.81 us -> 0.91 us
    ppermute x23 -> x22, starting transfers between devices: 39.2 us -> 34.3 us  [shift(): return lax.ppermute(values, AXES, pairs)]
    ppermute x23 -> x22, waiting for transfers between devices: 24.3 us -> 28.8 us  [shift(): return lax.ppermute(values, AXES, pairs)]
    unnamed x4, local copies, waits for them, and re-layouts: 1.81 us -> 0.91 us
    pallas_call x16 -> x20, Pallas kernels: 12 us -> 12.3 us  [call(): pl.pallas_call(lambda *refs: kernel(*refs[:n_in], *refs[n_in + len(ties):...]
  transfers between devices with their start and end apart: 23 -> 22, of which waited for: 7 -> 11; matrix products, arithmetic and copies ran while one was open for 0% -> 0% of each run, Pallas kernels for 10% -> 10%
where the time goes in v9:
time: 79.4 us; the launch traced here: 78.4 us
  starting transfers between devices  34.3 us (43%)
  waiting for transfers between devices  28.8 us (36%)
  Pallas kernels  12.3 us (15%)
  between operations  2.12 us (3%)
  local copies, waits for them, and re-layouts  0.91 us (1%)
    ppermute x22, starting transfers between devices, shift(): return lax.ppermute(values, AXES, pairs)  34.3 us
    ppermute x22, waiting for transfers between devices, shift(): return lax.ppermute(values, AXES, pairs)  28.8 us
    pallas_call x20, Pallas kernels, call(): pl.pallas_call(lambda *refs: kernel(*refs[:n_in], *refs[n_in + len(ties):...  12.3 us
  transfers between devices with their start and end apart: 22, of which 11 were waited for; matrix products, arithmetic and copies ran while one was open for 0% of the time, Pallas kernels for 10%

profile of v9, /device:TPU:24, one launch (start us, length us, event | category | flops | bytes accessed | tf_op | source)
XLA Modules:
  0.0 78.4 jit_solution(11474682873551972795)
XLA Ops:
  0.6 0.1 collective-permute-start.3
  0.7 3.1 %collective-permute-start.1 = (bf16[64,1152]{1,0:T(8,128)(2,1)}, bf16[64,1152]{1,0:T(8,128)(2,1)S(1)}, u32[]{:S(2)}, u32[]{:S(2)}) collective-permute-start(bf16[64,1152]{1,0:T(8,128)(2,1)} %refs_0_.3), channel_id=1, source_target_pairs={{0,64},{1,17},{2,66},{3,19},{4,68},{5,21},{6,70},{7,23},{128,192},... | collective-permute-start | bytes 442376 | tf_op jit(solution)/shard_map/gA2/ppermute | solution.py:28
  3.8 0.6 collective-permute-start
  4.4 2.6 %collective-permute-start.2 = (bf16[64,1152]{1,0:T(8,128)(2,1)}, bf16[64,1152]{1,0:T(8,128)(2,1)S(1)}, u32[]{:S(2)}, u32[]{:S(2)}) collective-permute-start(bf16[64,1152]{1,0:T(8,128)(2,1)} %refs_0_.3), channel_id=1, source_target_pairs={{0,96},{1,25},{2,98},{3,27},{4,100},{5,29},{6,102},{7,31},{128,224... | collective-permute-start | bytes 442376 | tf_op jit(solution)/shard_map/gA3/ppermute | solution.py:28
  8.4 0.0 collective-permute-done.3.refs_1_
  8.4 0.0 copy-start.1
  8.4 0.9 %copy-done.1 = bf16[64,1152]{1,0:T(8,128)(2,1)S(1)} copy-done((bf16[64,1152]{1,0:T(8,128)(2,1)S(1)}, bf16[64,1152]{1,0:T(8,128)(2,1)}, u32[]{:S(2)}) %copy-start.1) | copy-done | bytes 147480
  9.3 0.2 shard_map.59.refs_0_
  9.5 0.0 copy-start
  9.5 3.3 %collective-permute-start.4 = (bf16[128,1152]{1,0:T(8,128)(2,1)S(1)}, bf16[128,1152]{1,0:T(8,128)(2,1)S(1)}, u32[]{:S(2)}, u32[]{:S(2)}) collective-permute-start(bf16[128,1152]{1,0:T(8,128)(2,1)S(1)} %shard_map.59.refs_0_), channel_id=1, source_target_pairs={{0,4},{1,133},{2,6},{3,135},{4,128},{5,1},{6,130},{7,3},{128,132},... | collective-permute-start | bytes 884744 | tf_op jit(solution)/shard_map/gZ2/ppermute | solution.py:28
  12.8 0.0 collective-permute-done.1.refs_2_
  12.8 0.0 collective-permute-done.refs_1_
  12.9 0.0 collective-permute-done.2.refs_3_
  12.9 0.0 copy-done
  12.9 0.2 shard_map.61.refs_2_.refs_0_
  13.1 0.8 %collective-permute-start.9 = (bf16[256,1152]{1,0:T(8,128)(2,1)S(1)}, bf16[256,1152]{1,0:T(8,128)(2,1)S(1)}, u32[]{:S(2)}, u32[]{:S(2)}) collective-permute-start(bf16[256,1152]{1,0:T(8,128)(2,1)S(1)} %shard_map.61.refs_2_.refs_0_), channel_id=1, source_target_pairs={{0,24},{1,97},{2,26},{3,99},{4,28},{5,101},{6,30},{7,103},{128,152... | collective-permute-start | bytes 1769480 | tf_op jit(solution)/shard_map/gB3/ppermute | solution.py:28
  13.9 2.5 %collective-permute-start.8 = (bf16[256,1152]{1,0:T(8,128)(2,1)S(1)}, bf16[256,1152]{1,0:T(8,128)(2,1)S(1)}, u32[]{:S(2)}, u32[]{:S(2)}) collective-permute-start(bf16[256,1152]{1,0:T(8,128)(2,1)S(1)} %shard_map.61.refs_2_.refs_0_), channel_id=1, source_target_pairs={{0,8},{1,33},{2,10},{3,35},{4,12},{5,37},{6,14},{7,39},{128,136},{... | collective-permute-start | bytes 1769480 | tf_op jit(solution)/shard_map/gB1/ppermute | solution.py:28
  16.4 0.0 collective-permute-start.7
  16.5 4.7 %collective-permute-done.4.refs_1_ = bf16[128,1152]{1,0:T(8,128)(2,1)S(1)} collective-permute-done((bf16[128,1152]{1,0:T(8,128)(2,1)S(1)}, bf16[128,1152]{1,0:T(8,128)(2,1)S(1)}, u32[]{:S(2)}, u32[]{:S(2)}) %collective-permute-start.4) | collective-permute-done | bytes 294944 | tf_op jit(solution)/shard_map/gZ2/ppermute | solution.py:28
  21.2 0.1 shard_map.62
  21.2 3.7 %collective-permute-start.5 = (bf16[256,1152]{1,0:T(8,128)(2,1)S(1)}, bf16[256,1152]{1,0:T(8,128)(2,1)S(1)}, u32[]{:S(2)}, u32[]{:S(2)}) collective-permute-start(bf16[256,1152]{1,0:T(8,128)(2,1)S(1)} %get-tuple-element.29.refs_0_.refs_1_), channel_id=1, source_target_pairs={{0,2},{1,135},{2,4},{3,1},{4,6},{5,3},{6,128},{7,5},{128,130},{129... | collective-permute-start | bytes 1769480 | tf_op jit(solution)/shard_map/gZ13/ppermute | solution.py:28
  24.9 0.5 collective-permute-start.6
  25.4 8.5 %collective-permute-done.5.refs_2_.refs_1_ = bf16[256,1152]{1,0:T(8,128)(2,1)S(1)} collective-permute-done((bf16[256,1152]{1,0:T(8,128)(2,1)S(1)}, bf16[256,1152]{1,0:T(8,128)(2,1)S(1)}, u32[]{:S(2)}, u32[]{:S(2)}) %collective-permute-start.5) | collective-permute-done | bytes 589856 | tf_op jit(solution)/shard_map/gZ13/ppermute | solution.py:28
  33.9 0.1 shard_map.63.refs_1_
  34.0 0.2 shard_map.65
  34.2 0.2 shard_map.64
  34.4 3.2 %collective-permute-done.6.refs_2_ = bf16[64,1152]{1,0:T(8,128)(2,1)S(1)} collective-permute-done((bf16[64,1152]{1,0:T(8,128)(2,1)S(1)}, bf16[64,1152]{1,0:T(8,128)(2,1)S(1)}, u32[]{:S(2)}, u32[]{:S(2)}) %collective-permute-start.6) | collective-permute-done | bytes 147488 | tf_op jit(solution)/shard_map/gZ4/ppermute | solution.py:28
  37.5 0.0 collective-permute-done.9.refs_7_.refs_5_
  37.5 0.0 collective-permute-done.8.refs_6_.refs_4_
  37.5 0.0 collective-permute-done.7.refs_5_.refs_3_
  37.5 0.3 shard_map.68.refs_0_.refs_2_
  37.8 0.3 collective-permute-start.10
  38.1 3.4 %shard_map.69 = (bf16[1024,512]{1,0:T(8,128)(2,1)S(1)}, bf16[1024,1152]{1,0:T(8,128)(2,1)S(1)}, bf16[512,1152]{1,0:T(8,128)(2,1)S(1)}) custom-call(bf16[512,1152]{1,0:T(8,128)(2,1)S(1)} %shard_map.68.refs_0_.refs_2_, f32[8,128]{1,0:T(8,128)S(1)} %shard_map.63.refs_1_, bf16[256,1152]{1,0:T(8,128)(2,1)S(1)} %get-tuple-element.34.refs_3_.refs_2_, ...), custom_call_target="tpu_custom_call" | custom-call | flops 2415919104 | bytes 1024 | tf_op jit(solution)/shard_map/pallas_call | solution.py:51
  41.5 0.0 collective-permute-done.10.refs_0_.refs_3_
  41.5 3.0 %shard_map.70 = (bf16[1024,512]{1,0:T(8,128)(2,1)S(1)}, bf16[512,1152]{1,0:T(8,128)(2,1)S(1)}) custom-call(bf16[512,1152]{1,0:T(8,128)(2,1)S(1)} %collective-permute-done.10.refs_0_.refs_3_, f32[8,128]{1,0:T(8,128)S(1)} %shard_map.63.refs_1_, bf16[1024,1152]{1,0:T(8,128)(2,1)S(1)} %get-tuple-element.36.refs_2_, ...), custom_call_target="tpu_custom_call" | custom-call | flops 2415919104 | bytes 1024 | tf_op jit(solution)/shard_map/pallas_call | solution.py:51
  44.5 0.6 collective-permute-start.14
  45.1 2.9 %shard_map.71 = (f32[256,1152]{1,0:T(8,128)S(1)}, bf16[256,1152]{1,0:T(8,128)(2,1)S(1)}, bf16[256,1152]{1,0:T(8,128)(2,1)S(1)}, bf16[256,1152]{1,0:T(8,128)(2,1)S(1)}) custom-call(bf16[1024,512]{1,0:T(8,128)(2,1)S(1)} %get-tuple-element.35.refs_0_, bf16[1024,512]{1,0:T(8,128)(2,1)S(1)} %get-tuple-element.38.refs_1_, ...), custom_call_target="tpu_custom_call" | custom-call | flops 2415919104 | bytes 1024 | tf_op jit(solution)/shard_map/pallas_call | solution.py:51
  48.0 0.0 collective-permute-done.14.refs_1_
  48.0 0.3 shard_map.72
  48.3 2.4 %collective-permute-start.15 = (bf16[256,1152]{1,0:T(8,128)(2,1)S(1)}, bf16[256,1152]{1,0:T(8,128)(2,1)S(1)}, u32[]{:S(2)}, u32[]{:S(2)}) collective-permute-start(bf16[256,1152]{1,0:T(8,128)(2,1)S(1)} %get-tuple-element.45), channel_id=1, source_target_pairs={{0,134},{1,3},{2,0},{3,5},{4,2},{5,7},{6,4},{7,129},{128,6},{129,1... | collective-permute-start | bytes 1769480 | tf_op jit(solution)/shard_map/rZ13/ppermute | solution.py:28
  50.7 0.2 collective-permute-start.13
  50.9 1.8 %collective-permute-start.11 = (bf16[256,1152]{1,0:T(8,128)(2,1)S(1)}, bf16[256,1152]{1,0:T(8,128)(2,1)S(1)}, u32[]{:S(2)}, u32[]{:S(2)}) collective-permute-start(bf16[256,1152]{1,0:T(8,128)(2,1)S(1)} %get-tuple-element.40), channel_id=1, source_target_pairs={{0,24},{1,97},{2,26},{3,99},{4,28},{5,101},{6,30},{7,103},{128,152... | collective-permute-start | bytes 1769480 | tf_op jit(solution)/shard_map/rB1/ppermute | solution.py:28
  52.7 1.2 %collective-permute-start.12 = (bf16[256,1152]{1,0:T(8,128)(2,1)S(1)}, bf16[256,1152]{1,0:T(8,128)(2,1)S(1)}, u32[]{:S(2)}, u32[]{:S(2)}) collective-permute-start(bf16[256,1152]{1,0:T(8,128)(2,1)S(1)} %get-tuple-element.41), channel_id=1, source_target_pairs={{0,16},{1,65},{2,18},{3,67},{4,20},{5,69},{6,22},{7,71},{128,144},... | collective-permute-start | bytes 1769480 | tf_op jit(solution)/shard_map/rB2/ppermute | solution.py:28
  54.0 3.7 %collective-permute-start.16 = (bf16[64,1152]{1,0:T(8,128)(2,1)S(1)}, bf16[64,1152]{1,0:T(8,128)(2,1)S(1)}, u32[]{:S(2)}, u32[]{:S(2)}) collective-permute-start(bf16[64,1152]{1,0:T(8,128)(2,1)S(1)} %get-tuple-element.46), channel_id=1, source_target_pairs={{0,132},{1,5},{2,134},{3,7},{4,0},{5,129},{6,2},{7,131},{128,4},{1... | collective-permute-start | bytes 442376 | tf_op jit(solution)/shard_map/rZ4/ppermute | solution.py:28
  57.7 2.0 %collective-permute-done.15.refs_0_.refs_1_ = bf16[256,1152]{1,0:T(8,128)(2,1)S(1)} collective-permute-done((bf16[256,1152]{1,0:T(8,128)(2,1)S(1)}, bf16[256,1152]{1,0:T(8,128)(2,1)S(1)}, u32[]{:S(2)}, u32[]{:S(2)}) %collective-permute-start.15) | collective-permute-done | bytes 589856 | tf_op jit(solution)/shard_map/rZ13/ppermute | solution.py:28
  59.7 1.9 %collective-permute-done.16.refs_2_ = bf16[64,1152]{1,0:T(8,128)(2,1)S(1)} collective-permute-done((bf16[64,1152]{1,0:T(8,128)(2,1)S(1)}, bf16[64,1152]{1,0:T(8,128)(2,1)S(1)}, u32[]{:S(2)}, u32[]{:S(2)}) %collective-permute-start.16) | collective-permute-done | bytes 147488 | tf_op jit(solution)/shard_map/rZ4/ppermute | solution.py:28
  61.6 0.1 shard_map.74.refs_0_
  61.7 4.6 %collective-permute-start.20 = (bf16[128,1152]{1,0:T(8,128)(2,1)S(1)}, bf16[128,1152]{1,0:T(8,128)(2,1)S(1)}, u32[]{:S(2)}, u32[]{:S(2)}) collective-permute-start(bf16[128,1152]{1,0:T(8,128)(2,1)S(1)} %shard_map.74.refs_0_), channel_id=1, source_target_pairs={{0,132},{1,5},{2,134},{3,7},{4,0},{5,129},{6,2},{7,131},{128,4},{1... | collective-permute-start | bytes 884744 | tf_op jit(solution)/shard_map/rZ2/ppermute | solution.py:28
  66.3 1.8 %collective-permute-done.11.refs_1_ = bf16[256,1152]{1,0:T(8,128)(2,1)S(1)} collective-permute-done((bf16[256,1152]{1,0:T(8,128)(2,1)S(1)}, bf16[256,1152]{1,0:T(8,128)(2,1)S(1)}, u32[]{:S(2)}, u32[]{:S(2)}) %collective-permute-start.11) | collective-permute-done | bytes 589856 | tf_op jit(solution)/shard_map/rB1/ppermute | solution.py:28
  68.0 0.7 collective-permute-done.12.refs_2_
  68.7 0.0 collective-permute-done.13.refs_3_
  68.7 0.3 shard_map.76
  69.0 0.1 collective-permute-start.17
  69.0 1.1 %collective-permute-start.18 = (bf16[64,1152]{1,0:T(8,128)(2,1)S(1)}, bf16[64,1152]{1,0:T(8,128)(2,1)S(1)}, u32[]{:S(2)}, u32[]{:S(2)}) collective-permute-start(bf16[64,1152]{1,0:T(8,128)(2,1)S(1)} %get-tuple-element.49), channel_id=1, source_target_pairs={{0,64},{1,17},{2,66},{3,19},{4,68},{5,21},{6,70},{7,23},{128,192},... | collective-permute-start | bytes 442376 | tf_op jit(solution)/shard_map/rA2/ppermute | solution.py:28
  70.2 0.9 %collective-permute-start.19 = (bf16[64,1152]{1,0:T(8,128)(2,1)S(1)}, bf16[64,1152]{1,0:T(8,128)(2,1)S(1)}, u32[]{:S(2)}, u32[]{:S(2)}) collective-permute-start(bf16[64,1152]{1,0:T(8,128)(2,1)S(1)} %get-tuple-element.50), channel_id=1, source_target_pairs={{0,32},{1,9},{2,34},{3,11},{4,36},{5,13},{6,38},{7,15},{128,160},{... | collective-permute-start | bytes 442376 | tf_op jit(solution)/shard_map/rA3/ppermute | solution.py:28
  71.1 2.1 %collective-permute-done.20.refs_2_ = bf16[128,1152]{1,0:T(8,128)(2,1)S(1)} collective-permute-done((bf16[128,1152]{1,0:T(8,128)(2,1)S(1)}, bf16[128,1152]{1,0:T(8,128)(2,1)S(1)}, u32[]{:S(2)}, u32[]{:S(2)}) %collective-permute-start.20) | collective-permute-done | bytes 294944 | tf_op jit(solution)/shard_map/rZ2/ppermute | solution.py:28
  73.1 0.1 shard_map.77
  73.2 0.1 collective-permute-start.21
  73.3 0.8 %collective-permute-done.17.refs_3_ = bf16[64,1152]{1,0:T(8,128)(2,1)S(1)} collective-permute-done((bf16[64,1152]{1,0:T(8,128)(2,1)S(1)}, bf16[64,1152]{1,0:T(8,128)(2,1)S(1)}, u32[]{:S(2)}, u32[]{:S(2)}) %collective-permute-start.17) | collective-permute-done | bytes 147488 | tf_op jit(solution)/shard_map/rA1/ppermute | solution.py:28
  74.2 1.7 %collective-permute-done.18.refs_4_ = bf16[64,1152]{1,0:T(8,128)(2,1)S(1)} collective-permute-done((bf16[64,1152]{1,0:T(8,128)(2,1)S(1)}, bf16[64,1152]{1,0:T(8,128)(2,1)S(1)}, u32[]{:S(2)}, u32[]{:S(2)}) %collective-permute-start.18) | collective-permute-done | bytes 147488 | tf_op jit(solution)/shard_map/rA2/ppermute | solution.py:28
  75.8 1.5 %collective-permute-done.19.refs_5_ = bf16[64,1152]{1,0:T(8,128)(2,1)S(1)} collective-permute-done((bf16[64,1152]{1,0:T(8,128)(2,1)S(1)}, bf16[64,1152]{1,0:T(8,128)(2,1)S(1)}, u32[]{:S(2)}, u32[]{:S(2)}) %collective-permute-start.19) | collective-permute-done | bytes 147488 | tf_op jit(solution)/shard_map/rA3/ppermute | solution.py:28
  77.4 0.0 collective-permute-done.21.refs_9_
  77.4 1.1 %shard_map.78 = (f32[64,1152]{1,0:T(8,128)}, f32[64,1152]{1,0:T(8,128)}) custom-call(f32[64,1152]{1,0:T(8,128)S(1)} %get-tuple-element.30.refs_0_, f32[64,128]{1,0:T(8,128)S(1)} %get-tuple-element.31.refs_1_, f32[64,1152]{1,0:T(8,128)S(1)} %get-tuple-element.47.refs_2_, bf16[64,1152]{1,0:T(8,128)(2,1)S(1)} %collective-permute-done.17.refs_3_, ...), custom_call_target="tpu_custom_call" | custom-call | bytes 1024 | tf_op jit(solution)/shard_map/pallas_call | solution.py:51
  (5 shorter events, 0.0 us)
Async XLA Ops:
  0.6 7.7 %collective-permute-start.3 = (bf16[64,1152]{1,0:T(8,128)(2,1)}, bf16[64,1152]{1,0:T(8,128)(2,1)S(1)}, u32[]{:S(2)}, u32[]{:S(2)}) collective-permute-start(bf16[64,1152]{1,0:T(8,128)(2,1)} %refs_0_.2), channel_id=1, source_target_pairs={{0,1},{1,0},{2,3},{3,2},{4,5},{5,4},{6,7},{7,6},{128,129},{129,128... | collective-permute-start | bytes 442376 | tf_op jit(solution)/shard_map/gC/ppermute | solution.py:28
  0.7 12.1 %collective-permute-start.1 = (bf16[64,1152]{1,0:T(8,128)(2,1)}, bf16[64,1152]{1,0:T(8,128)(2,1)S(1)}, u32[]{:S(2)}, u32[]{:S(2)}) collective-permute-start(bf16[64,1152]{1,0:T(8,128)(2,1)} %refs_0_.3), channel_id=1, source_target_pairs={{0,64},{1,17},{2,66},{3,19},{4,68},{5,21},{6,70},{7,23},{128,192},... | collective-permute-start | bytes 442376 | tf_op jit(solution)/shard_map/gA2/ppermute | solution.py:28
  3.8 9.0 %collective-permute-start = (bf16[64,1152]{1,0:T(8,128)(2,1)}, bf16[64,1152]{1,0:T(8,128)(2,1)S(1)}, u32[]{:S(2)}, u32[]{:S(2)}) collective-permute-start(bf16[64,1152]{1,0:T(8,128)(2,1)} %refs_0_.3), channel_id=1, source_target_pairs={{0,32},{1,9},{2,34},{3,11},{4,36},{5,13},{6,38},{7,15},{128,160},{... | collective-permute-start | bytes 442376 | tf_op jit(solution)/shard_map/gA1/ppermute | solution.py:28
  4.4 8.4 %collective-permute-start.2 = (bf16[64,1152]{1,0:T(8,128)(2,1)}, bf16[64,1152]{1,0:T(8,128)(2,1)S(1)}, u32[]{:S(2)}, u32[]{:S(2)}) collective-permute-start(bf16[64,1152]{1,0:T(8,128)(2,1)} %refs_0_.3), channel_id=1, source_target_pairs={{0,96},{1,25},{2,98},{3,27},{4,100},{5,29},{6,102},{7,31},{128,224... | collective-permute-start | bytes 442376 | tf_op jit(solution)/shard_map/gA3/ppermute | solution.py:28
  8.4 0.9 %copy-start.1 = (bf16[64,1152]{1,0:T(8,128)(2,1)S(1)}, bf16[64,1152]{1,0:T(8,128)(2,1)}, u32[]{:S(2)}) copy-start(bf16[64,1152]{1,0:T(8,128)(2,1)} %refs_0_.2) | copy-start | bytes 442372
  9.5 3.4 %copy-start = (bf16[64,1152]{1,0:T(8,128)(2,1)S(1)}, bf16[64,1152]{1,0:T(8,128)(2,1)}, u32[]{:S(2)}) copy-start(bf16[64,1152]{1,0:T(8,128)(2,1)} %refs_0_.3) | copy-start | bytes 442372
  9.5 11.7 %collective-permute-start.4 = (bf16[128,1152]{1,0:T(8,128)(2,1)S(1)}, bf16[128,1152]{1,0:T(8,128)(2,1)S(1)}, u32[]{:S(2)}, u32[]{:S(2)}) collective-permute-start(bf16[128,1152]{1,0:T(8,128)(2,1)S(1)} %shard_map.59.refs_0_), channel_id=1, source_target_pairs={{0,4},{1,133},{2,6},{3,135},{4,128},{5,1},{6,130},{7,3},{128,132},... | collective-permute-start | bytes 884744 | tf_op jit(solution)/shard_map/gZ2/ppermute | solution.py:28
  13.1 24.4 %collective-permute-start.9 = (bf16[256,1152]{1,0:T(8,128)(2,1)S(1)}, bf16[256,1152]{1,0:T(8,128)(2,1)S(1)}, u32[]{:S(2)}, u32[]{:S(2)}) collective-permute-start(bf16[256,1152]{1,0:T(8,128)(2,1)S(1)} %shard_map.61.refs_2_.refs_0_), channel_id=1, source_target_pairs={{0,24},{1,97},{2,26},{3,99},{4,28},{5,101},{6,30},{7,103},{128,152... | collective-permute-start | bytes 1769480 | tf_op jit(solution)/shard_map/gB3/ppermute | solution.py:28
  13.9 23.6 %collective-permute-start.8 = (bf16[256,1152]{1,0:T(8,128)(2,1)S(1)}, bf16[256,1152]{1,0:T(8,128)(2,1)S(1)}, u32[]{:S(2)}, u32[]{:S(2)}) collective-permute-start(bf16[256,1152]{1,0:T(8,128)(2,1)S(1)} %shard_map.61.refs_2_.refs_0_), channel_id=1, source_target_pairs={{0,8},{1,33},{2,10},{3,35},{4,12},{5,37},{6,14},{7,39},{128,136},{... | collective-permute-start | bytes 1769480 | tf_op jit(solution)/shard_map/gB1/ppermute | solution.py:28
  16.4 21.1 %collective-permute-start.7 = (bf16[256,1152]{1,0:T(8,128)(2,1)S(1)}, bf16[256,1152]{1,0:T(8,128)(2,1)S(1)}, u32[]{:S(2)}, u32[]{:S(2)}) collective-permute-start(bf16[256,1152]{1,0:T(8,128)(2,1)S(1)} %shard_map.61.refs_2_.refs_0_), channel_id=1, source_target_pairs={{0,16},{1,65},{2,18},{3,67},{4,20},{5,69},{6,22},{7,71},{128,144},... | collective-permute-start | bytes 1769480 | tf_op jit(solution)/shard_map/gB2/ppermute | solution.py:28
  21.2 12.7 %collective-permute-start.5 = (bf16[256,1152]{1,0:T(8,128)(2,1)S(1)}, bf16[256,1152]{1,0:T(8,128)(2,1)S(1)}, u32[]{:S(2)}, u32[]{:S(2)}) collective-permute-start(bf16[256,1152]{1,0:T(8,128)(2,1)S(1)} %get-tuple-element.29.refs_0_.refs_1_), channel_id=1, source_target_pairs={{0,2},{1,135},{2,4},{3,1},{4,6},{5,3},{6,128},{7,5},{128,130},{129... | collective-permute-start | bytes 1769480 | tf_op jit(solution)/shard_map/gZ13/ppermute | solution.py:28
  24.9 12.6 %collective-permute-start.6 = (bf16[64,1152]{1,0:T(8,128)(2,1)S(1)}, bf16[64,1152]{1,0:T(8,128)(2,1)S(1)}, u32[]{:S(2)}, u32[]{:S(2)}) collective-permute-start(bf16[64,1152]{1,0:T(8,128)(2,1)S(1)} %shard_map.66), channel_id=1, source_target_pairs={{0,4},{1,133},{2,6},{3,135},{4,128},{5,1},{6,130},{7,3},{128,132},... | collective-permute-start | bytes 442376 | tf_op jit(solution)/shard_map/gZ4/ppermute | solution.py:28
  37.8 3.7 %collective-permute-start.10 = (bf16[512,1152]{1,0:T(8,128)(2,1)S(1)}, bf16[512,1152]{1,0:T(8,128)(2,1)S(1)}, u32[]{:S(2)}, u32[]{:S(2)}) collective-permute-start(bf16[512,1152]{1,0:T(8,128)(2,1)S(1)} %shard_map.68.refs_0_.refs_2_), channel_id=1, source_target_pairs={{0,1},{1,0},{2,3},{3,2},{4,5},{5,4},{6,7},{7,6},{128,129},{129,128... | collective-permute-start | bytes 3538952 | tf_op jit(solution)/shard_map/gS/ppermute | solution.py:28
  44.5 3.5 %collective-permute-start.14 = (bf16[512,1152]{1,0:T(8,128)(2,1)S(1)}, bf16[512,1152]{1,0:T(8,128)(2,1)S(1)}, u32[]{:S(2)}, u32[]{:S(2)}) collective-permute-start(bf16[512,1152]{1,0:T(8,128)(2,1)S(1)} %get-tuple-element.43), channel_id=1, source_target_pairs={{0,1},{1,0},{2,3},{3,2},{4,5},{5,4},{6,7},{7,6},{128,129},{129,128... | collective-permute-start | bytes 3538952 | tf_op jit(solution)/shard_map/rC/ppermute | solution.py:28
  48.3 11.4 %collective-permute-start.15 = (bf16[256,1152]{1,0:T(8,128)(2,1)S(1)}, bf16[256,1152]{1,0:T(8,128)(2,1)S(1)}, u32[]{:S(2)}, u32[]{:S(2)}) collective-permute-start(bf16[256,1152]{1,0:T(8,128)(2,1)S(1)} %get-tuple-element.45), channel_id=1, source_target_pairs={{0,134},{1,3},{2,0},{3,5},{4,2},{5,7},{6,4},{7,129},{128,6},{129,1... | collective-permute-start | bytes 1769480 | tf_op jit(solution)/shard_map/rZ13/ppermute | solution.py:28
  50.7 18.0 %collective-permute-start.13 = (bf16[256,1152]{1,0:T(8,128)(2,1)S(1)}, bf16[256,1152]{1,0:T(8,128)(2,1)S(1)}, u32[]{:S(2)}, u32[]{:S(2)}) collective-permute-start(bf16[256,1152]{1,0:T(8,128)(2,1)S(1)} %get-tuple-element.42.refs_2_), channel_id=1, source_target_pairs={{0,8},{1,33},{2,10},{3,35},{4,12},{5,37},{6,14},{7,39},{128,136},{... | collective-permute-start | bytes 1769480 | tf_op jit(solution)/shard_map/rB3/ppermute | solution.py:28
  50.9 17.1 %collective-permute-start.11 = (bf16[256,1152]{1,0:T(8,128)(2,1)S(1)}, bf16[256,1152]{1,0:T(8,128)(2,1)S(1)}, u32[]{:S(2)}, u32[]{:S(2)}) collective-permute-start(bf16[256,1152]{1,0:T(8,128)(2,1)S(1)} %get-tuple-element.40), channel_id=1, source_target_pairs={{0,24},{1,97},{2,26},{3,99},{4,28},{5,101},{6,30},{7,103},{128,152... | collective-permute-start | bytes 1769480 | tf_op jit(solution)/shard_map/rB1/ppermute | solution.py:28
  52.7 15.9 %collective-permute-start.12 = (bf16[256,1152]{1,0:T(8,128)(2,1)S(1)}, bf16[256,1152]{1,0:T(8,128)(2,1)S(1)}, u32[]{:S(2)}, u32[]{:S(2)}) collective-permute-start(bf16[256,1152]{1,0:T(8,128)(2,1)S(1)} %get-tuple-element.41), channel_id=1, source_target_pairs={{0,16},{1,65},{2,18},{3,67},{4,20},{5,69},{6,22},{7,71},{128,144},... | collective-permute-start | bytes 1769480 | tf_op jit(solution)/shard_map/rB2/ppermute | solution.py:28
  54.0 7.6 %collective-permute-start.16 = (bf16[64,1152]{1,0:T(8,128)(2,1)S(1)}, bf16[64,1152]{1,0:T(8,128)(2,1)S(1)}, u32[]{:S(2)}, u32[]{:S(2)}) collective-permute-start(bf16[64,1152]{1,0:T(8,128)(2,1)S(1)} %get-tuple-element.46), channel_id=1, source_target_pairs={{0,132},{1,5},{2,134},{3,7},{4,0},{5,129},{6,2},{7,131},{128,4},{1... | collective-permute-start | bytes 442376 | tf_op jit(solution)/shard_map/rZ4/ppermute | solution.py:28
  61.7 11.4 %collective-permute-start.20 = (bf16[128,1152]{1,0:T(8,128)(2,1)S(1)}, bf16[128,1152]{1,0:T(8,128)(2,1)S(1)}, u32[]{:S(2)}, u32[]{:S(2)}) collective-permute-start(bf16[128,1152]{1,0:T(8,128)(2,1)S(1)} %shard_map.74.refs_0_), channel_id=1, source_target_pairs={{0,132},{1,5},{2,134},{3,7},{4,0},{5,129},{6,2},{7,131},{128,4},{1... | collective-permute-start | bytes 884744 | tf_op jit(solution)/shard_map/rZ2/ppermute | solution.py:28
  69.0 5.2 %collective-permute-start.17 = (bf16[64,1152]{1,0:T(8,128)(2,1)S(1)}, bf16[64,1152]{1,0:T(8,128)(2,1)S(1)}, u32[]{:S(2)}, u32[]{:S(2)}) collective-permute-start(bf16[64,1152]{1,0:T(8,128)(2,1)S(1)} %get-tuple-element.48), channel_id=1, source_target_pairs={{0,96},{1,25},{2,98},{3,27},{4,100},{5,29},{6,102},{7,31},{128,224... | collective-permute-start | bytes 442376 | tf_op jit(solution)/shard_map/rA1/ppermute | solution.py:28
  69.0 6.8 %collective-permute-start.18 = (bf16[64,1152]{1,0:T(8,128)(2,1)S(1)}, bf16[64,1152]{1,0:T(8,128)(2,1)S(1)}, u32[]{:S(2)}, u32[]{:S(2)}) collective-permute-start(bf16[64,1152]{1,0:T(8,128)(2,1)S(1)} %get-tuple-element.49), channel_id=1, source_target_pairs={{0,64},{1,17},{2,66},{3,19},{4,68},{5,21},{6,70},{7,23},{128,192},... | collective-permute-start | bytes 442376 | tf_op jit(solution)/shard_map/rA2/ppermute | solution.py:28
  70.2 7.2 %collective-permute-start.19 = (bf16[64,1152]{1,0:T(8,128)(2,1)S(1)}, bf16[64,1152]{1,0:T(8,128)(2,1)S(1)}, u32[]{:S(2)}, u32[]{:S(2)}) collective-permute-start(bf16[64,1152]{1,0:T(8,128)(2,1)S(1)} %get-tuple-element.50), channel_id=1, source_target_pairs={{0,32},{1,9},{2,34},{3,11},{4,36},{5,13},{6,38},{7,15},{128,160},{... | collective-permute-start | bytes 442376 | tf_op jit(solution)/shard_map/rA3/ppermute | solution.py:28
  73.2 4.1 %collective-permute-start.21 = (bf16[64,1152]{1,0:T(8,128)(2,1)S(1)}, bf16[64,1152]{1,0:T(8,128)(2,1)S(1)}, u32[]{:S(2)}, u32[]{:S(2)}) collective-permute-start(bf16[64,1152]{1,0:T(8,128)(2,1)S(1)} %get-tuple-element.55), channel_id=1, source_target_pairs={{0,1},{1,0},{2,3},{3,2},{4,5},{5,4},{6,7},{7,6},{128,129},{129,128... | collective-permute-start | bytes 442376 | tf_op jit(solution)/shard_map/rS/ppermute | solution.py:28

commit v10 on v9

--- a/solution.py
+++ b/solution.py
@@ -194,14 +194,11 @@
     text_grads(w_ref, img_ref, send_ref)
 
 
-def image_kernel(w1_ref, w2_ref, txt1_ref, txt2_ref, *outs):
-    at = 0
-    for out in outs:
-        rows = out.shape[0]
-        grad = jnp.dot(w1_ref[at:at + rows, :], txt1_ref[...], preferred_element_type=F32)
-        grad += jnp.dot(w2_ref[at:at + rows, :], txt2_ref[...], preferred_element_type=F32)
-        out[...] = grad.astype(out.dtype)
-        at += rows
+def image_kernel(at, w1_ref, w2_ref, txt1_ref, txt2_ref, out_ref):
+    rows = out_ref.shape[0]
+    grad = jnp.dot(w1_ref[at:at + rows, :], txt1_ref[...], preferred_element_type=F32)
+    grad += jnp.dot(w2_ref[at:at + rows, :], txt2_ref[...], preferred_element_type=F32)
+    out_ref[...] = grad.astype(out_ref.dtype)
 
 
 def total_kernel(keep_ref, got_ref, own_ref, part13_ref, part2_ref, part4_ref):
@@ -226,13 +223,15 @@
     send_ref[...] = (got13_ref[rows:2 * rows, :].astype(F32) + got2_ref[rows:, :].astype(F32)).astype(BF16)
 
 
-def sums_kernel(*refs):
-    own_ref, *parts = refs[:4]
-    outs = refs[4:]
+def partial_kernel(own_ref, first_ref, second_ref, out_ref):
+    out_ref[...] = own_ref[...] + first_ref[...].astype(F32) + second_ref[...].astype(F32)
+
+
+def sums_kernel(sum_ref, last_ref, *outs):
     rows = outs[0].shape[0]
     for n, out in enumerate(outs):
         at = slice(n * rows, (n + 1) * rows)
-        out[...] = (own_ref[at, :] + sum(p[at, :].astype(F32) for p in parts)).astype(out.dtype)
+        out[...] = (sum_ref[at, :] + last_ref[at, :].astype(F32)).astype(out.dtype)
 
 
 def final_kernel(*refs):
@@ -251,7 +250,7 @@
     near2 = shift(pair, line(2), "gZ2")
     group = stack(images, side, [token(pair)])
     send13, send4 = call(send_kernel, [((4 * own, dim), BF16), ((own, dim), BF16)], [pair, near2], [group])
-    far = [shift(group, second(k), "gB%d" % k) for k in (2, 1, 3)]
+    far = [shift(group, second(k), "gB%d" % k) for k in (1, 3, 2)]
     near13 = shift(send13, line(1), "gZ13")
     near4 = shift(call(head_kernel, [((own, dim), BF16)], [send4], [send13])[0], line(2), "gZ4")
     first_token = token(group)
@@ -277,26 +276,37 @@
         theirs_kernel, [((rows, half), BF16), ((half, dim), BF16)],
         [theirs, scalars, img_all], ties=[keep], flops=2 * flops, limit=24,
     )
-    grads = call(
-        image_kernel, [(group.shape, F32)] + [(group.shape, BF16)] * len(far),
-        [w_mine, w_theirs, mine, theirs], flops=2 * flops, limit=24,
-    )
+    each = group.shape[0]
+
+    def image_grads(index, dtype, ties):
+        return call(
+            lambda *refs: image_kernel(index * each, *refs), [((each, dim), dtype)],
+            [w_mine, w_theirs, mine, theirs], ties=ties, flops=flops // 2, limit=24,
+        )[0]
+
+    grad3 = image_grads(2, BF16, [send])
+    back3 = shift(grad3, second(-3), "rB3")
+    grad1 = image_grads(1, BF16, [grad3])
+    back1 = shift(grad1, second(-1), "rB1")
 
     total_own, part13, part2, part4 = call(
         total_kernel,
         [((own, dim), F32), ((4 * own, dim), BF16), ((2 * own, dim), F32), ((own, dim), BF16)],
-        [keep, shift(send, other, "rC")], ties=[grads[-1]],
-    )
+        [keep, shift(send, other, "rC")], ties=[grad1],
+    )
+    grad2 = image_grads(3, BF16, [part13])
+    back2 = shift(grad2, second(-2), "rB2")
+    grad0 = image_grads(0, F32, [grad2])
+    (partial,) = call(partial_kernel, [((each, dim), F32)], [grad0, back3, back1])
     got13 = shift(part13, line(-1), "rZ13")
     got4 = shift(part4, line(-2), "rZ4")
-    (middle,) = call(middle_kernel, [((2 * own, dim), BF16)], [part2, got13, got4], [token(got13)])
+    (middle,) = call(middle_kernel, [((2 * own, dim), BF16)], [part2, got13, got4], [partial])
     got2 = shift(middle, line(-2), "rZ2")
     txt_sum, txt_send = call(landed_kernel, [((own, dim), F32), ((own, dim), BF16)], [total_own, got13, got2])
     txt_last = shift(txt_send, other, "rS")
 
-    back = [shift(g, second(-k), "rB%d" % k) for k, g in ((1, grads[2]), (2, grads[1]), (3, grads[3]))]
     img_sum, *parts = call(
-        sums_kernel, [((own, dim), F32)] + [((own, dim), BF16)] * 3, [grads[0], *back], ties=[token(middle)]
+        sums_kernel, [((own, dim), F32)] + [((own, dim), BF16)] * 3, [partial, back2], ties=[token(middle)]
     )
     last = [shift(p, first(-k), "rA%d" % k) for k, p in zip((1, 2, 3), parts)]
 

time: 79.4 us -> 79.5 us (level); the launches traced: 78.4 us -> 79.4 us
  starting transfers between devices: 34.3 us -> 35.2 us
    ppermute x22, starting transfers between devices: 34.3 us -> 35.2 us  [shift(): return lax.ppermute(values, AXES, pairs)]
    pallas_call x20 -> x23, Pallas kernels: 12.3 us -> 12.9 us  [call(): pl.pallas_call(lambda *refs: kernel(*refs[:n_in], *refs[n_in + len(ties):...]
  transfers between devices with their start and end apart: 22 -> 22, of which waited for: 11 -> 9; matrix products, arithmetic and copies ran while one was open for 0% -> 0% of each run, Pallas kernels for 10% -> 11%
where the time goes in v10:
time: 79.5 us; the launch traced here: 79.4 us
  starting transfers between devices  35.2 us (44%)
  waiting for transfers between devices  28.3 us (36%)
  Pallas kernels  12.9 us (16%)
  between operations  2.14 us (3%)
  local copies, waits for them, and re-layouts  0.91 us (1%)
    ppermute x22, starting transfers between devices, shift(): return lax.ppermute(values, AXES, pairs)  35.2 us
    ppermute x22, waiting for transfers between devices, shift(): return lax.ppermute(values, AXES, pairs)  28.3 us
    pallas_call x23, Pallas kernels, call(): pl.pallas_call(lambda *refs: kernel(*refs[:n_in], *refs[n_in + len(ties):...  12.9 us
  transfers between devices with their start and end apart: 22, of which 9 were waited for; matrix products, arithmetic and copies ran while one was open for 0% of the time, Pallas kernels for 11%

profile of v10, /device:TPU:24, one launch (start us, length us, event | category | flops | bytes accessed | tf_op | source)
XLA Modules:
  0.0 79.4 jit_solution(6837893686571259305)
XLA Ops:
  0.6 0.1 collective-permute-start.3
  0.7 1.6 %collective-permute-start = (bf16[64,1152]{1,0:T(8,128)(2,1)}, bf16[64,1152]{1,0:T(8,128)(2,1)S(1)}, u32[]{:S(2)}, u32[]{:S(2)}) collective-permute-start(bf16[64,1152]{1,0:T(8,128)(2,1)} %refs_0_.3), channel_id=1, source_target_pairs={{0,32},{1,9},{2,34},{3,11},{4,36},{5,13},{6,38},{7,15},{128,160},{... | collective-permute-start | bytes 442376 | tf_op jit(solution)/shard_map/gA1/ppermute | solution.py:28
  2.3 2.7 %collective-permute-start.1 = (bf16[64,1152]{1,0:T(8,128)(2,1)}, bf16[64,1152]{1,0:T(8,128)(2,1)S(1)}, u32[]{:S(2)}, u32[]{:S(2)}) collective-permute-start(bf16[64,1152]{1,0:T(8,128)(2,1)} %refs_0_.3), channel_id=1, source_target_pairs={{0,64},{1,17},{2,66},{3,19},{4,68},{5,21},{6,70},{7,23},{128,192},... | collective-permute-start | bytes 442376 | tf_op jit(solution)/shard_map/gA2/ppermute | solution.py:28
  5.0 1.4 %collective-permute-start.2 = (bf16[64,1152]{1,0:T(8,128)(2,1)}, bf16[64,1152]{1,0:T(8,128)(2,1)S(1)}, u32[]{:S(2)}, u32[]{:S(2)}) collective-permute-start(bf16[64,1152]{1,0:T(8,128)(2,1)} %refs_0_.3), channel_id=1, source_target_pairs={{0,96},{1,25},{2,98},{3,27},{4,100},{5,29},{6,102},{7,31},{128,224... | collective-permute-start | bytes 442376 | tf_op jit(solution)/shard_map/gA3/ppermute | solution.py:28
  7.8 0.0 collective-permute-done.3.refs_1_
  7.8 0.9 %copy-done.1 = bf16[64,1152]{1,0:T(8,128)(2,1)S(1)} copy-done((bf16[64,1152]{1,0:T(8,128)(2,1)S(1)}, bf16[64,1152]{1,0:T(8,128)(2,1)}, u32[]{:S(2)}) %copy-start.1) | copy-done | bytes 147480
  8.7 0.2 shard_map.59.refs_0_
  8.9 0.0 copy-start
  8.9 3.3 %collective-permute-start.4 = (bf16[128,1152]{1,0:T(8,128)(2,1)S(1)}, bf16[128,1152]{1,0:T(8,128)(2,1)S(1)}, u32[]{:S(2)}, u32[]{:S(2)}) collective-permute-start(bf16[128,1152]{1,0:T(8,128)(2,1)S(1)} %shard_map.59.refs_0_), channel_id=1, source_target_pairs={{0,4},{1,133},{2,6},{3,135},{4,128},{5,1},{6,130},{7,3},{128,132},... | collective-permute-start | bytes 884744 | tf_op jit(solution)/shard_map/gZ2/ppermute | solution.py:28
  12.2 0.0 collective-permute-done.refs_1_
  12.2 0.0 collective-permute-done.1.refs_2_
  12.2 0.0 collective-permute-done.2.refs_3_
  12.3 0.2 shard_map.61.refs_2_.refs_0_
  12.5 0.3 collective-permute-start.7
  12.8 1.8 %collective-permute-start.8 = (bf16[256,1152]{1,0:T(8,128)(2,1)S(1)}, bf16[256,1152]{1,0:T(8,128)(2,1)S(1)}, u32[]{:S(2)}, u32[]{:S(2)}) collective-permute-start(bf16[256,1152]{1,0:T(8,128)(2,1)S(1)} %shard_map.61.refs_2_.refs_0_), channel_id=1, source_target_pairs={{0,24},{1,97},{2,26},{3,99},{4,28},{5,101},{6,30},{7,103},{128,152... | collective-permute-start | bytes 1769480 | tf_op jit(solution)/shard_map/gB3/ppermute | solution.py:28
  14.6 1.2 %collective-permute-start.9 = (bf16[256,1152]{1,0:T(8,128)(2,1)S(1)}, bf16[256,1152]{1,0:T(8,128)(2,1)S(1)}, u32[]{:S(2)}, u32[]{:S(2)}) collective-permute-start(bf16[256,1152]{1,0:T(8,128)(2,1)S(1)} %shard_map.61.refs_2_.refs_0_), channel_id=1, source_target_pairs={{0,16},{1,65},{2,18},{3,67},{4,20},{5,69},{6,22},{7,71},{128,144},... | collective-permute-start | bytes 1769480 | tf_op jit(solution)/shard_map/gB2/ppermute | solution.py:28
  15.8 4.7 %collective-permute-done.4.refs_1_ = bf16[128,1152]{1,0:T(8,128)(2,1)S(1)} collective-permute-done((bf16[128,1152]{1,0:T(8,128)(2,1)S(1)}, bf16[128,1152]{1,0:T(8,128)(2,1)S(1)}, u32[]{:S(2)}, u32[]{:S(2)}) %collective-permute-start.4) | collective-permute-done | bytes 294944 | tf_op jit(solution)/shard_map/gZ2/ppermute | solution.py:28
  20.6 0.1 shard_map.62
  20.6 3.7 %collective-permute-start.5 = (bf16[256,1152]{1,0:T(8,128)(2,1)S(1)}, bf16[256,1152]{1,0:T(8,128)(2,1)S(1)}, u32[]{:S(2)}, u32[]{:S(2)}) collective-permute-start(bf16[256,1152]{1,0:T(8,128)(2,1)S(1)} %get-tuple-element.25.refs_0_.refs_1_), channel_id=1, source_target_pairs={{0,2},{1,135},{2,4},{3,1},{4,6},{5,3},{6,128},{7,5},{128,130},{129... | collective-permute-start | bytes 1769480 | tf_op jit(solution)/shard_map/gZ13/ppermute | solution.py:28
  24.3 0.5 collective-permute-start.6
  24.8 8.5 %collective-permute-done.5.refs_2_.refs_1_ = bf16[256,1152]{1,0:T(8,128)(2,1)S(1)} collective-permute-done((bf16[256,1152]{1,0:T(8,128)(2,1)S(1)}, bf16[256,1152]{1,0:T(8,128)(2,1)S(1)}, u32[]{:S(2)}, u32[]{:S(2)}) %collective-permute-start.5) | collective-permute-done | bytes 589856 | tf_op jit(solution)/shard_map/gZ13/ppermute | solution.py:28
  33.3 0.1 shard_map.63.refs_1_
  33.4 0.2 shard_map.64
  33.6 0.2 shard_map.65
  33.8 3.2 %collective-permute-done.6.refs_2_ = bf16[64,1152]{1,0:T(8,128)(2,1)S(1)} collective-permute-done((bf16[64,1152]{1,0:T(8,128)(2,1)S(1)}, bf16[64,1152]{1,0:T(8,128)(2,1)S(1)}, u32[]{:S(2)}, u32[]{:S(2)}) %collective-permute-start.6) | collective-permute-done | bytes 147488 | tf_op jit(solution)/shard_map/gZ4/ppermute | solution.py:28
  36.9 0.0 collective-permute-done.7.refs_5_.refs_3_
  36.9 0.0 collective-permute-done.8.refs_6_.refs_4_
  36.9 0.0 collective-permute-done.9.refs_7_.refs_5_
  36.9 0.3 shard_map.68.refs_0_.refs_2_
  37.2 0.3 collective-permute-start.10
  37.5 3.4 %shard_map.69 = (bf16[1024,512]{1,0:T(8,128)(2,1)S(1)}, bf16[1024,1152]{1,0:T(8,128)(2,1)S(1)}, bf16[512,1152]{1,0:T(8,128)(2,1)S(1)}) custom-call(bf16[512,1152]{1,0:T(8,128)(2,1)S(1)} %shard_map.68.refs_0_.refs_2_, f32[8,128]{1,0:T(8,128)S(1)} %shard_map.63.refs_1_, bf16[256,1152]{1,0:T(8,128)(2,1)S(1)} %get-tuple-element.30.refs_3_.refs_2_, ...), custom_call_target="tpu_custom_call" | custom-call | flops 2415919104 | bytes 1024 | tf_op jit(solution)/shard_map/pallas_call | solution.py:51
  40.9 0.0 collective-permute-done.10.refs_0_.refs_3_
  41.0 3.0 %shard_map.70 = (bf16[1024,512]{1,0:T(8,128)(2,1)S(1)}, bf16[512,1152]{1,0:T(8,128)(2,1)S(1)}) custom-call(bf16[512,1152]{1,0:T(8,128)(2,1)S(1)} %collective-permute-done.10.refs_0_.refs_3_, f32[8,128]{1,0:T(8,128)S(1)} %shard_map.63.refs_1_, bf16[1024,1152]{1,0:T(8,128)(2,1)S(1)} %get-tuple-element.32.refs_2_, ...), custom_call_target="tpu_custom_call" | custom-call | flops 2415919104 | bytes 1024 | tf_op jit(solution)/shard_map/pallas_call | solution.py:51
  44.0 0.6 collective-permute-start.11
  44.6 0.8 %shard_map.71.refs_4_ = bf16[256,1152]{1,0:T(8,128)(2,1)S(1)} custom-call(bf16[1024,512]{1,0:T(8,128)(2,1)S(1)} %get-tuple-element.31.refs_0_, bf16[1024,512]{1,0:T(8,128)(2,1)S(1)} %get-tuple-element.34.refs_1_, bf16[512,1152]{1,0:T(8,128)(2,1)S(1)} %shard_map.68.refs_0_.refs_2_, bf16[512,1152]{1,0:T(8,128)(2,1)S(1)} %collective-permute-done.10.refs_0_.refs_3_, ...), custom_call_target="tpu_custom_call" | custom-call | flops 603979776 | bytes 1024 | tf_op jit(solution)/shard_map/pallas_call | solution.py:51
  45.4 0.3 collective-permute-start.12
  45.7 0.8 %shard_map.72.refs_2_ = bf16[256,1152]{1,0:T(8,128)(2,1)S(1)} custom-call(bf16[1024,512]{1,0:T(8,128)(2,1)S(1)} %get-tuple-element.31.refs_0_, bf16[1024,512]{1,0:T(8,128)(2,1)S(1)} %get-tuple-element.34.refs_1_, bf16[512,1152]{1,0:T(8,128)(2,1)S(1)} %shard_map.68.refs_0_.refs_2_, bf16[512,1152]{1,0:T(8,128)(2,1)S(1)} %collective-permute-done.10.refs_0_.refs_3_, ...), custom_call_target="tpu_custom_call" | custom-call | flops 603979776 | bytes 1024 | tf_op jit(solution)/shard_map/pallas_call | solution.py:51
  46.6 1.9 %collective-permute-start.13 = (bf16[256,1152]{1,0:T(8,128)(2,1)S(1)}, bf16[256,1152]{1,0:T(8,128)(2,1)S(1)}, u32[]{:S(2)}, u32[]{:S(2)}) collective-permute-start(bf16[256,1152]{1,0:T(8,128)(2,1)S(1)} %shard_map.72.refs_2_), channel_id=1, source_target_pairs={{0,24},{1,97},{2,26},{3,99},{4,28},{5,101},{6,30},{7,103},{128,152... | collective-permute-start | bytes 1769480 | tf_op jit(solution)/shard_map/rB1/ppermute | solution.py:28
  48.4 0.0 collective-permute-done.11.refs_1_
  48.5 0.3 shard_map.73
  48.7 2.4 %collective-permute-start.15 = (bf16[256,1152]{1,0:T(8,128)(2,1)S(1)}, bf16[256,1152]{1,0:T(8,128)(2,1)S(1)}, u32[]{:S(2)}, u32[]{:S(2)}) collective-permute-start(bf16[256,1152]{1,0:T(8,128)(2,1)S(1)} %get-tuple-element.36.refs_4_), channel_id=1, source_target_pairs={{0,134},{1,3},{2,0},{3,5},{4,2},{5,7},{6,4},{7,129},{128,6},{129,1... | collective-permute-start | bytes 1769480 | tf_op jit(solution)/shard_map/rZ13/ppermute | solution.py:28
  51.1 3.7 %collective-permute-start.16 = (bf16[64,1152]{1,0:T(8,128)(2,1)S(1)}, bf16[64,1152]{1,0:T(8,128)(2,1)S(1)}, u32[]{:S(2)}, u32[]{:S(2)}) collective-permute-start(bf16[64,1152]{1,0:T(8,128)(2,1)S(1)} %get-tuple-element.38), channel_id=1, source_target_pairs={{0,132},{1,5},{2,134},{3,7},{4,0},{5,129},{6,2},{7,131},{128,4},{1... | collective-permute-start | bytes 442376 | tf_op jit(solution)/shard_map/rZ4/ppermute | solution.py:28
  54.9 0.8 %shard_map.74.refs_4_ = bf16[256,1152]{1,0:T(8,128)(2,1)S(1)} custom-call(bf16[1024,512]{1,0:T(8,128)(2,1)S(1)} %get-tuple-element.31.refs_0_, bf16[1024,512]{1,0:T(8,128)(2,1)S(1)} %get-tuple-element.34.refs_1_, bf16[512,1152]{1,0:T(8,128)(2,1)S(1)} %shard_map.68.refs_0_.refs_2_, bf16[512,1152]{1,0:T(8,128)(2,1)S(1)} %collective-permute-done.10.refs_0_.refs_3_, ...), custom_call_target="tpu_custom_call" | custom-call | flops 603979776 | bytes 1024 | tf_op jit(solution)/shard_map/pallas_call | solution.py:51
  55.7 1.5 %collective-permute-start.14 = (bf16[256,1152]{1,0:T(8,128)(2,1)S(1)}, bf16[256,1152]{1,0:T(8,128)(2,1)S(1)}, u32[]{:S(2)}, u32[]{:S(2)}) collective-permute-start(bf16[256,1152]{1,0:T(8,128)(2,1)S(1)} %shard_map.74.refs_4_), channel_id=1, source_target_pairs={{0,16},{1,65},{2,18},{3,67},{4,20},{5,69},{6,22},{7,71},{128,144},... | collective-permute-start | bytes 1769480 | tf_op jit(solution)/shard_map/rB2/ppermute | solution.py:28
  57.3 0.8 %shard_map.75.refs_0_ = f32[256,1152]{1,0:T(8,128)S(1)} custom-call(bf16[1024,512]{1,0:T(8,128)(2,1)S(1)} %get-tuple-element.31.refs_0_, bf16[1024,512]{1,0:T(8,128)(2,1)S(1)} %get-tuple-element.34.refs_1_, bf16[512,1152]{1,0:T(8,128)(2,1)S(1)} %shard_map.68.refs_0_.refs_2_, bf16[512,1152]{1,0:T(8,128)(2,1)S(1)} %collective-permute-done.10.refs_0_.refs_3_, ...), custom_call_target="tpu_custom_call" | custom-call | flops 603979776 | bytes 1024 | tf_op jit(solution)/shard_map/pallas_call | solution.py:51
  58.1 0.0 collective-permute-done.12.refs_1_
  58.1 0.0 collective-permute-done.13.refs_2_
  58.1 0.2 shard_map.76.refs_3_.refs_0_
  58.3 3.5 %collective-permute-done.16.refs_2_ = bf16[64,1152]{1,0:T(8,128)(2,1)S(1)} collective-permute-done((bf16[64,1152]{1,0:T(8,128)(2,1)S(1)}, bf16[64,1152]{1,0:T(8,128)(2,1)S(1)}, u32[]{:S(2)}, u32[]{:S(2)}) %collective-permute-start.16) | collective-permute-done | bytes 147488 | tf_op jit(solution)/shard_map/rZ4/ppermute | solution.py:28
  61.8 0.0 collective-permute-done.15.refs_1_
  61.8 0.1 shard_map.77.refs_0_
  61.9 4.6 %collective-permute-start.20 = (bf16[128,1152]{1,0:T(8,128)(2,1)S(1)}, bf16[128,1152]{1,0:T(8,128)(2,1)S(1)}, u32[]{:S(2)}, u32[]{:S(2)}) collective-permute-start(bf16[128,1152]{1,0:T(8,128)(2,1)S(1)} %shard_map.77.refs_0_), channel_id=1, source_target_pairs={{0,132},{1,5},{2,134},{3,7},{4,0},{5,129},{6,2},{7,131},{128,4},{1... | collective-permute-start | bytes 884744 | tf_op jit(solution)/shard_map/rZ2/ppermute | solution.py:28
  66.5 2.3 %collective-permute-done.14.refs_1_ = bf16[256,1152]{1,0:T(8,128)(2,1)S(1)} collective-permute-done((bf16[256,1152]{1,0:T(8,128)(2,1)S(1)}, bf16[256,1152]{1,0:T(8,128)(2,1)S(1)}, u32[]{:S(2)}, u32[]{:S(2)}) %collective-permute-start.14) | collective-permute-done | bytes 589856 | tf_op jit(solution)/shard_map/rB2/ppermute | solution.py:28
  68.8 0.1 shard_map.79
  68.9 0.1 collective-permute-start.17
  69.0 3.0 %collective-permute-start.18 = (bf16[64,1152]{1,0:T(8,128)(2,1)S(1)}, bf16[64,1152]{1,0:T(8,128)(2,1)S(1)}, u32[]{:S(2)}, u32[]{:S(2)}) collective-permute-start(bf16[64,1152]{1,0:T(8,128)(2,1)S(1)} %get-tuple-element.41), channel_id=1, source_target_pairs={{0,64},{1,17},{2,66},{3,19},{4,68},{5,21},{6,70},{7,23},{128,192},... | collective-permute-start | bytes 442376 | tf_op jit(solution)/shard_map/rA2/ppermute | solution.py:28
  72.0 0.0 collective-permute-start.19
  72.0 1.8 %collective-permute-done.20.refs_2_ = bf16[128,1152]{1,0:T(8,128)(2,1)S(1)} collective-permute-done((bf16[128,1152]{1,0:T(8,128)(2,1)S(1)}, bf16[128,1152]{1,0:T(8,128)(2,1)S(1)}, u32[]{:S(2)}, u32[]{:S(2)}) %collective-permute-start.20) | collective-permute-done | bytes 294944 | tf_op jit(solution)/shard_map/rZ2/ppermute | solution.py:28
  73.8 0.1 shard_map.80
  73.8 0.1 collective-permute-start.21
  73.9 0.2 collective-permute-done.17.refs_3_
  74.1 1.6 %collective-permute-done.18.refs_4_ = bf16[64,1152]{1,0:T(8,128)(2,1)S(1)} collective-permute-done((bf16[64,1152]{1,0:T(8,128)(2,1)S(1)}, bf16[64,1152]{1,0:T(8,128)(2,1)S(1)}, u32[]{:S(2)}, u32[]{:S(2)}) %collective-permute-start.18) | collective-permute-done | bytes 147488 | tf_op jit(solution)/shard_map/rA2/ppermute | solution.py:28
  75.7 2.6 %collective-permute-done.19.refs_5_ = bf16[64,1152]{1,0:T(8,128)(2,1)S(1)} collective-permute-done((bf16[64,1152]{1,0:T(8,128)(2,1)S(1)}, bf16[64,1152]{1,0:T(8,128)(2,1)S(1)}, u32[]{:S(2)}, u32[]{:S(2)}) %collective-permute-start.19) | collective-permute-done | bytes 147488 | tf_op jit(solution)/shard_map/rA3/ppermute | solution.py:28
  78.3 1.1 %shard_map.81 = (f32[64,1152]{1,0:T(8,128)}, f32[64,1152]{1,0:T(8,128)}) custom-call(f32[64,1152]{1,0:T(8,128)S(1)} %get-tuple-element.26.refs_0_, f32[64,128]{1,0:T(8,128)S(1)} %get-tuple-element.27.refs_1_, f32[64,1152]{1,0:T(8,128)S(1)} %get-tuple-element.39.refs_2_, bf16[64,1152]{1,0:T(8,128)(2,1)S(1)} %collective-permute-done.17.refs_3_, ...), custom_call_target="tpu_custom_call" | custom-call | bytes 1024 | tf_op jit(solution)/shard_map/pallas_call | solution.py:51
  (7 shorter events, 0.0 us)
Async XLA Ops:
  0.6 7.1 %collective-permute-start.3 = (bf16[64,1152]{1,0:T(8,128)(2,1)}, bf16[64,1152]{1,0:T(8,128)(2,1)S(1)}, u32[]{:S(2)}, u32[]{:S(2)}) collective-permute-start(bf16[64,1152]{1,0:T(8,128)(2,1)} %refs_0_.2), channel_id=1, source_target_pairs={{0,1},{1,0},{2,3},{3,2},{4,5},{5,4},{6,7},{7,6},{128,129},{129,128... | collective-permute-start | bytes 442376 | tf_op jit(solution)/shard_map/gC/ppermute | solution.py:28
  0.7 11.5 %collective-permute-start = (bf16[64,1152]{1,0:T(8,128)(2,1)}, bf16[64,1152]{1,0:T(8,128)(2,1)S(1)}, u32[]{:S(2)}, u32[]{:S(2)}) collective-permute-start(bf16[64,1152]{1,0:T(8,128)(2,1)} %refs_0_.3), channel_id=1, source_target_pairs={{0,32},{1,9},{2,34},{3,11},{4,36},{5,13},{6,38},{7,15},{128,160},{... | collective-permute-start | bytes 442376 | tf_op jit(solution)/shard_map/gA1/ppermute | solution.py:28
  2.3 9.9 %collective-permute-start.1 = (bf16[64,1152]{1,0:T(8,128)(2,1)}, bf16[64,1152]{1,0:T(8,128)(2,1)S(1)}, u32[]{:S(2)}, u32[]{:S(2)}) collective-permute-start(bf16[64,1152]{1,0:T(8,128)(2,1)} %refs_0_.3), channel_id=1, source_target_pairs={{0,64},{1,17},{2,66},{3,19},{4,68},{5,21},{6,70},{7,23},{128,192},... | collective-permute-start | bytes 442376 | tf_op jit(solution)/shard_map/gA2/ppermute | solution.py:28
  5.0 7.2 %collective-permute-start.2 = (bf16[64,1152]{1,0:T(8,128)(2,1)}, bf16[64,1152]{1,0:T(8,128)(2,1)S(1)}, u32[]{:S(2)}, u32[]{:S(2)}) collective-permute-start(bf16[64,1152]{1,0:T(8,128)(2,1)} %refs_0_.3), channel_id=1, source_target_pairs={{0,96},{1,25},{2,98},{3,27},{4,100},{5,29},{6,102},{7,31},{128,224... | collective-permute-start | bytes 442376 | tf_op jit(solution)/shard_map/gA3/ppermute | solution.py:28
  7.8 0.9 %copy-start.1 = (bf16[64,1152]{1,0:T(8,128)(2,1)S(1)}, bf16[64,1152]{1,0:T(8,128)(2,1)}, u32[]{:S(2)}) copy-start(bf16[64,1152]{1,0:T(8,128)(2,1)} %refs_0_.2) | copy-start | bytes 442372
  8.9 3.4 %copy-start = (bf16[64,1152]{1,0:T(8,128)(2,1)S(1)}, bf16[64,1152]{1,0:T(8,128)(2,1)}, u32[]{:S(2)}) copy-start(bf16[64,1152]{1,0:T(8,128)(2,1)} %refs_0_.3) | copy-start | bytes 442372
  8.9 11.7 %collective-permute-start.4 = (bf16[128,1152]{1,0:T(8,128)(2,1)S(1)}, bf16[128,1152]{1,0:T(8,128)(2,1)S(1)}, u32[]{:S(2)}, u32[]{:S(2)}) collective-permute-start(bf16[128,1152]{1,0:T(8,128)(2,1)S(1)} %shard_map.59.refs_0_), channel_id=1, source_target_pairs={{0,4},{1,133},{2,6},{3,135},{4,128},{5,1},{6,130},{7,3},{128,132},... | collective-permute-start | bytes 884744 | tf_op jit(solution)/shard_map/gZ2/ppermute | solution.py:28
  12.5 24.4 %collective-permute-start.7 = (bf16[256,1152]{1,0:T(8,128)(2,1)S(1)}, bf16[256,1152]{1,0:T(8,128)(2,1)S(1)}, u32[]{:S(2)}, u32[]{:S(2)}) collective-permute-start(bf16[256,1152]{1,0:T(8,128)(2,1)S(1)} %shard_map.61.refs_2_.refs_0_), channel_id=1, source_target_pairs={{0,8},{1,33},{2,10},{3,35},{4,12},{5,37},{6,14},{7,39},{128,136},{... | collective-permute-start | bytes 1769480 | tf_op jit(solution)/shard_map/gB1/ppermute | solution.py:28
  12.8 24.1 %collective-permute-start.8 = (bf16[256,1152]{1,0:T(8,128)(2,1)S(1)}, bf16[256,1152]{1,0:T(8,128)(2,1)S(1)}, u32[]{:S(2)}, u32[]{:S(2)}) collective-permute-start(bf16[256,1152]{1,0:T(8,128)(2,1)S(1)} %shard_map.61.refs_2_.refs_0_), channel_id=1, source_target_pairs={{0,24},{1,97},{2,26},{3,99},{4,28},{5,101},{6,30},{7,103},{128,152... | collective-permute-start | bytes 1769480 | tf_op jit(solution)/shard_map/gB3/ppermute | solution.py:28
  14.6 22.3 %collective-permute-start.9 = (bf16[256,1152]{1,0:T(8,128)(2,1)S(1)}, bf16[256,1152]{1,0:T(8,128)(2,1)S(1)}, u32[]{:S(2)}, u32[]{:S(2)}) collective-permute-start(bf16[256,1152]{1,0:T(8,128)(2,1)S(1)} %shard_map.61.refs_2_.refs_0_), channel_id=1, source_target_pairs={{0,16},{1,65},{2,18},{3,67},{4,20},{5,69},{6,22},{7,71},{128,144},... | collective-permute-start | bytes 1769480 | tf_op jit(solution)/shard_map/gB2/ppermute | solution.py:28
  20.6 12.7 %collective-permute-start.5 = (bf16[256,1152]{1,0:T(8,128)(2,1)S(1)}, bf16[256,1152]{1,0:T(8,128)(2,1)S(1)}, u32[]{:S(2)}, u32[]{:S(2)}) collective-permute-start(bf16[256,1152]{1,0:T(8,128)(2,1)S(1)} %get-tuple-element.25.refs_0_.refs_1_), channel_id=1, source_target_pairs={{0,2},{1,135},{2,4},{3,1},{4,6},{5,3},{6,128},{7,5},{128,130},{129... | collective-permute-start | bytes 1769480 | tf_op jit(solution)/shard_map/gZ13/ppermute | solution.py:28
  24.3 12.6 %collective-permute-start.6 = (bf16[64,1152]{1,0:T(8,128)(2,1)S(1)}, bf16[64,1152]{1,0:T(8,128)(2,1)S(1)}, u32[]{:S(2)}, u32[]{:S(2)}) collective-permute-start(bf16[64,1152]{1,0:T(8,128)(2,1)S(1)} %shard_map.66), channel_id=1, source_target_pairs={{0,4},{1,133},{2,6},{3,135},{4,128},{5,1},{6,130},{7,3},{128,132},... | collective-permute-start | bytes 442376 | tf_op jit(solution)/shard_map/gZ4/ppermute | solution.py:28
  37.2 3.7 %collective-permute-start.10 = (bf16[512,1152]{1,0:T(8,128)(2,1)S(1)}, bf16[512,1152]{1,0:T(8,128)(2,1)S(1)}, u32[]{:S(2)}, u32[]{:S(2)}) collective-permute-start(bf16[512,1152]{1,0:T(8,128)(2,1)S(1)} %shard_map.68.refs_0_.refs_2_), channel_id=1, source_target_pairs={{0,1},{1,0},{2,3},{3,2},{4,5},{5,4},{6,7},{7,6},{128,129},{129,128... | collective-permute-start | bytes 3538952 | tf_op jit(solution)/shard_map/gS/ppermute | solution.py:28
  44.0 4.5 %collective-permute-start.11 = (bf16[512,1152]{1,0:T(8,128)(2,1)S(1)}, bf16[512,1152]{1,0:T(8,128)(2,1)S(1)}, u32[]{:S(2)}, u32[]{:S(2)}) collective-permute-start(bf16[512,1152]{1,0:T(8,128)(2,1)S(1)} %get-tuple-element.35.refs_4_), channel_id=1, source_target_pairs={{0,1},{1,0},{2,3},{3,2},{4,5},{5,4},{6,7},{7,6},{128,129},{129,128... | collective-permute-start | bytes 3538952 | tf_op jit(solution)/shard_map/rC/ppermute | solution.py:28
  45.4 12.7 %collective-permute-start.12 = (bf16[256,1152]{1,0:T(8,128)(2,1)S(1)}, bf16[256,1152]{1,0:T(8,128)(2,1)S(1)}, u32[]{:S(2)}, u32[]{:S(2)}) collective-permute-start(bf16[256,1152]{1,0:T(8,128)(2,1)S(1)} %shard_map.71.refs_4_), channel_id=1, source_target_pairs={{0,8},{1,33},{2,10},{3,35},{4,12},{5,37},{6,14},{7,39},{128,136},{... | collective-permute-start | bytes 1769480 | tf_op jit(solution)/shard_map/rB3/ppermute | solution.py:28
  46.6 11.5 %collective-permute-start.13 = (bf16[256,1152]{1,0:T(8,128)(2,1)S(1)}, bf16[256,1152]{1,0:T(8,128)(2,1)S(1)}, u32[]{:S(2)}, u32[]{:S(2)}) collective-permute-start(bf16[256,1152]{1,0:T(8,128)(2,1)S(1)} %shard_map.72.refs_2_), channel_id=1, source_target_pairs={{0,24},{1,97},{2,26},{3,99},{4,28},{5,101},{6,30},{7,103},{128,152... | collective-permute-start | bytes 1769480 | tf_op jit(solution)/shard_map/rB1/ppermute | solution.py:28
  48.7 13.1 %collective-permute-start.15 = (bf16[256,1152]{1,0:T(8,128)(2,1)S(1)}, bf16[256,1152]{1,0:T(8,128)(2,1)S(1)}, u32[]{:S(2)}, u32[]{:S(2)}) collective-permute-start(bf16[256,1152]{1,0:T(8,128)(2,1)S(1)} %get-tuple-element.36.refs_4_), channel_id=1, source_target_pairs={{0,134},{1,3},{2,0},{3,5},{4,2},{5,7},{6,4},{7,129},{128,6},{129,1... | collective-permute-start | bytes 1769480 | tf_op jit(solution)/shard_map/rZ13/ppermute | solution.py:28
  51.1 10.6 %collective-permute-start.16 = (bf16[64,1152]{1,0:T(8,128)(2,1)S(1)}, bf16[64,1152]{1,0:T(8,128)(2,1)S(1)}, u32[]{:S(2)}, u32[]{:S(2)}) collective-permute-start(bf16[64,1152]{1,0:T(8,128)(2,1)S(1)} %get-tuple-element.38), channel_id=1, source_target_pairs={{0,132},{1,5},{2,134},{3,7},{4,0},{5,129},{6,2},{7,131},{128,4},{1... | collective-permute-start | bytes 442376 | tf_op jit(solution)/shard_map/rZ4/ppermute | solution.py:28
  55.7 13.1 %collective-permute-start.14 = (bf16[256,1152]{1,0:T(8,128)(2,1)S(1)}, bf16[256,1152]{1,0:T(8,128)(2,1)S(1)}, u32[]{:S(2)}, u32[]{:S(2)}) collective-permute-start(bf16[256,1152]{1,0:T(8,128)(2,1)S(1)} %shard_map.74.refs_4_), channel_id=1, source_target_pairs={{0,16},{1,65},{2,18},{3,67},{4,20},{5,69},{6,22},{7,71},{128,144},... | collective-permute-start | bytes 1769480 | tf_op jit(solution)/shard_map/rB2/ppermute | solution.py:28
  61.9 11.9 %collective-permute-start.20 = (bf16[128,1152]{1,0:T(8,128)(2,1)S(1)}, bf16[128,1152]{1,0:T(8,128)(2,1)S(1)}, u32[]{:S(2)}, u32[]{:S(2)}) collective-permute-start(bf16[128,1152]{1,0:T(8,128)(2,1)S(1)} %shard_map.77.refs_0_), channel_id=1, source_target_pairs={{0,132},{1,5},{2,134},{3,7},{4,0},{5,129},{6,2},{7,131},{128,4},{1... | collective-permute-start | bytes 884744 | tf_op jit(solution)/shard_map/rZ2/ppermute | solution.py:28
  68.9 5.2 %collective-permute-start.17 = (bf16[64,1152]{1,0:T(8,128)(2,1)S(1)}, bf16[64,1152]{1,0:T(8,128)(2,1)S(1)}, u32[]{:S(2)}, u32[]{:S(2)}) collective-permute-start(bf16[64,1152]{1,0:T(8,128)(2,1)S(1)} %get-tuple-element.40), channel_id=1, source_target_pairs={{0,96},{1,25},{2,98},{3,27},{4,100},{5,29},{6,102},{7,31},{128,224... | collective-permute-start | bytes 442376 | tf_op jit(solution)/shard_map/rA1/ppermute | solution.py:28
  69.0 6.7 %collective-permute-start.18 = (bf16[64,1152]{1,0:T(8,128)(2,1)S(1)}, bf16[64,1152]{1,0:T(8,128)(2,1)S(1)}, u32[]{:S(2)}, u32[]{:S(2)}) collective-permute-start(bf16[64,1152]{1,0:T(8,128)(2,1)S(1)} %get-tuple-element.41), channel_id=1, source_target_pairs={{0,64},{1,17},{2,66},{3,19},{4,68},{5,21},{6,70},{7,23},{128,192},... | collective-permute-start | bytes 442376 | tf_op jit(solution)/shard_map/rA2/ppermute | solution.py:28
  72.0 6.4 %collective-permute-start.19 = (bf16[64,1152]{1,0:T(8,128)(2,1)S(1)}, bf16[64,1152]{1,0:T(8,128)(2,1)S(1)}, u32[]{:S(2)}, u32[]{:S(2)}) collective-permute-start(bf16[64,1152]{1,0:T(8,128)(2,1)S(1)} %get-tuple-element.42), channel_id=1, source_target_pairs={{0,32},{1,9},{2,34},{3,11},{4,36},{5,13},{6,38},{7,15},{128,160},{... | collective-permute-start | bytes 442376 | tf_op jit(solution)/shard_map/rA3/ppermute | solution.py:28
  73.8 4.5 %collective-permute-start.21 = (bf16[64,1152]{1,0:T(8,128)(2,1)S(1)}, bf16[64,1152]{1,0:T(8,128)(2,1)S(1)}, u32[]{:S(2)}, u32[]{:S(2)}) collective-permute-start(bf16[64,1152]{1,0:T(8,128)(2,1)S(1)} %get-tuple-element.47), channel_id=1, source_target_pairs={{0,1},{1,0},{2,3},{3,2},{4,5},{5,4},{6,7},{7,6},{128,129},{129,128... | collective-permute-start | bytes 442376 | tf_op jit(solution)/shard_map/rS/ppermute | solution.py:28

commit v11 on v10

--- a/solution.py
+++ b/solution.py
@@ -38,6 +38,10 @@
 
 def line(k):
     return lambda x, y, z, c: (x, y, z + k, c) if c == 0 else (x, y, z - k, c)
+
+
+def cross(k):
+    return lambda x, y, z, c: (x, y, z + k, 0) if c == 1 else (x, y, z - k, 1)
 
 
 def other(x, y, z, c):
@@ -97,17 +101,6 @@
     return call(
         stack_kernel, [((rows, dim), BF16)], parts, ties=ties, first=[own_raw], scratch=[pltpu.SemaphoreType.DMA(())]
     )[0]
-
-
-def head_kernel(in_ref, out_ref):
-    out_ref[...] = in_ref[...]
-
-
-def send_kernel(pair_ref, near_ref, send13_ref, send4_ref):
-    rows = pair_ref.shape[0]
-    send13_ref[:rows, :] = pair_ref[...]
-    send13_ref[rows:, :] = near_ref[...]
-    send4_ref[...] = near_ref[:send4_ref.shape[0], :]
 
 
 def round_rows(raw_ref, start, out_ref, at, rows, own=None):
@@ -223,15 +216,15 @@
     send_ref[...] = (got13_ref[rows:2 * rows, :].astype(F32) + got2_ref[rows:, :].astype(F32)).astype(BF16)
 
 
-def partial_kernel(own_ref, first_ref, second_ref, out_ref):
-    out_ref[...] = own_ref[...] + first_ref[...].astype(F32) + second_ref[...].astype(F32)
-
-
-def sums_kernel(sum_ref, last_ref, *outs):
+def partial_kernel(own_ref, first_ref, out_ref):
+    out_ref[...] = own_ref[...] + first_ref[...].astype(F32)
+
+
+def sums_kernel(sum_ref, first_ref, second_ref, *outs):
     rows = outs[0].shape[0]
     for n, out in enumerate(outs):
         at = slice(n * rows, (n + 1) * rows)
-        out[...] = (sum_ref[at, :] + last_ref[at, :].astype(F32)).astype(out.dtype)
+        out[...] = (sum_ref[at, :] + first_ref[at, :].astype(F32) + second_ref[at, :].astype(F32)).astype(out.dtype)
 
 
 def final_kernel(*refs):
@@ -244,15 +237,15 @@
 def local(images, texts, log_temp, bias):
     own, dim = images.shape
 
+    side = [shift(images, first(k), "gA%d" % k) for k in (1, 2, 3)]
+    line2 = shift(texts, line(2), "gZ2")
+    cross2 = shift(texts, cross(2), "gX2")
     swapped = shift(texts, other, "gC")
-    side = [shift(images, first(k), "gA%d" % k) for k in (1, 2, 3)]
-    pair = stack(texts, [swapped])
-    near2 = shift(pair, line(2), "gZ2")
-    group = stack(images, side, [token(pair)])
-    send13, send4 = call(send_kernel, [((4 * own, dim), BF16), ((own, dim), BF16)], [pair, near2], [group])
+    group = stack(images, side, [token(swapped)])
+    send13 = stack(texts, [swapped, line2, cross2])
     far = [shift(group, second(k), "gB%d" % k) for k in (1, 3, 2)]
     near13 = shift(send13, line(1), "gZ13")
-    near4 = shift(call(head_kernel, [((own, dim), BF16)], [send4], [send13])[0], line(2), "gZ4")
+    near4 = shift(line2, line(2), "gZ4")
     first_token = token(group)
     (scalars,) = call(
         scalar_kernel, [((8, 128), F32)], [log_temp.reshape(1, 1), bias.reshape(1, 1)], [near13]
@@ -286,18 +279,17 @@
 
     grad3 = image_grads(2, BF16, [send])
     back3 = shift(grad3, second(-3), "rB3")
-    grad1 = image_grads(1, BF16, [grad3])
-    back1 = shift(grad1, second(-1), "rB1")
-
     total_own, part13, part2, part4 = call(
         total_kernel,
         [((own, dim), F32), ((4 * own, dim), BF16), ((2 * own, dim), F32), ((own, dim), BF16)],
-        [keep, shift(send, other, "rC")], ties=[grad1],
-    )
-    grad2 = image_grads(3, BF16, [part13])
+        [keep, shift(send, other, "rC")], ties=[grad3],
+    )
+    grad1 = image_grads(1, BF16, [part13])
+    back1 = shift(grad1, second(-1), "rB1")
+    grad2 = image_grads(3, BF16, [grad1])
     back2 = shift(grad2, second(-2), "rB2")
     grad0 = image_grads(0, F32, [grad2])
-    (partial,) = call(partial_kernel, [((each, dim), F32)], [grad0, back3, back1])
+    (partial,) = call(partial_kernel, [((each, dim), F32)], [grad0, back3])
     got13 = shift(part13, line(-1), "rZ13")
     got4 = shift(part4, line(-2), "rZ4")
     (middle,) = call(middle_kernel, [((2 * own, dim), BF16)], [part2, got13, got4], [partial])
@@ -306,7 +298,7 @@
     txt_last = shift(txt_send, other, "rS")
 
     img_sum, *parts = call(
-        sums_kernel, [((own, dim), F32)] + [((own, dim), BF16)] * 3, [partial, back2], ties=[token(middle)]
+        sums_kernel, [((own, dim), F32)] + [((own, dim), BF16)] * 3, [partial, back1, back2], ties=[token(middle)]
     )
     last = [shift(p, first(-k), "rA%d" % k) for k, p in zip((1, 2, 3), parts)]
 

time: 79.5 us -> 82.1 us (1.033)
  waiting for transfers between devices: 28.3 us -> 32.6 us
  starting transfers between devices: 35.2 us -> 34.3 us
  local copies, waits for them, and re-layouts: 0.91 us -> 0.01 us
    ppermute x22 -> x23, waiting for transfers between devices: 28.3 us -> 32.6 us  [shift(): return lax.ppermute(values, AXES, pairs)]
    ppermute x22 -> x23, starting transfers between devices: 35.2 us -> 34.3 us  [shift(): return lax.ppermute(values, AXES, pairs)]
    unnamed x4, local copies, waits for them, and re-layouts: 0.91 us -> 0.01 us
    pallas_call x23 -> x21, Pallas kernels: 12.9 us -> 12.9 us  [call(): pl.pallas_call(lambda *refs: kernel(*refs[:n_in], *refs[n_in + len(ties):...]
  transfers between devices with their start and end apart: 22 -> 23, of which waited for: 9 -> 9; matrix products, arithmetic and copies ran while one was open for 0% -> 0% of each run, Pallas kernels for 11% -> 10%
where the time goes in v11:
time: 82.1 us; the launch traced here: 81.8 us
  starting transfers between devices  34.3 us (42%)
  waiting for transfers between devices  32.6 us (40%)
  Pallas kernels  12.9 us (16%)
  between operations  2.12 us (3%)
    ppermute x23, starting transfers between devices, shift(): return lax.ppermute(values, AXES, pairs)  34.3 us
    ppermute x23, waiting for transfers between devices, shift(): return lax.ppermute(values, AXES, pairs)  32.6 us
    pallas_call x21, Pallas kernels, call(): pl.pallas_call(lambda *refs: kernel(*refs[:n_in], *refs[n_in + len(ties):...  12.9 us
  transfers between devices with their start and end apart: 23, of which 9 were waited for; matrix products, arithmetic and copies ran while one was open for 0% of the time, Pallas kernels for 10%

profile of v11, /device:TPU:24, one launch (start us, length us, event | category | flops | bytes accessed | tf_op | source)
XLA Modules:
  0.0 81.8 jit_solution(4234479226827998384)
XLA Ops:
  0.6 0.1 collective-permute-start.3
  0.7 1.6 %collective-permute-start = (bf16[64,1152]{1,0:T(8,128)(2,1)}, bf16[64,1152]{1,0:T(8,128)(2,1)S(1)}, u32[]{:S(2)}, u32[]{:S(2)}) collective-permute-start(bf16[64,1152]{1,0:T(8,128)(2,1)} %refs_0_.2), channel_id=1, source_target_pairs={{0,32},{1,9},{2,34},{3,11},{4,36},{5,13},{6,38},{7,15},{128,160},{... | collective-permute-start | bytes 442376 | tf_op jit(solution)/shard_map/gA1/ppermute | solution.py:28
  2.3 2.7 %collective-permute-start.1 = (bf16[64,1152]{1,0:T(8,128)(2,1)}, bf16[64,1152]{1,0:T(8,128)(2,1)S(1)}, u32[]{:S(2)}, u32[]{:S(2)}) collective-permute-start(bf16[64,1152]{1,0:T(8,128)(2,1)} %refs_0_.2), channel_id=1, source_target_pairs={{0,64},{1,17},{2,66},{3,19},{4,68},{5,21},{6,70},{7,23},{128,192},... | collective-permute-start | bytes 442376 | tf_op jit(solution)/shard_map/gA2/ppermute | solution.py:28
  5.0 1.4 %collective-permute-start.2 = (bf16[64,1152]{1,0:T(8,128)(2,1)}, bf16[64,1152]{1,0:T(8,128)(2,1)S(1)}, u32[]{:S(2)}, u32[]{:S(2)}) collective-permute-start(bf16[64,1152]{1,0:T(8,128)(2,1)} %refs_0_.2), channel_id=1, source_target_pairs={{0,96},{1,25},{2,98},{3,27},{4,100},{5,29},{6,102},{7,31},{128,224... | collective-permute-start | bytes 442376 | tf_op jit(solution)/shard_map/gA3/ppermute | solution.py:28
  6.5 3.3 %collective-permute-start.4 = (bf16[64,1152]{1,0:T(8,128)(2,1)}, bf16[64,1152]{1,0:T(8,128)(2,1)S(1)}, u32[]{:S(2)}, u32[]{:S(2)}) collective-permute-start(bf16[64,1152]{1,0:T(8,128)(2,1)} %refs_0_.3), channel_id=1, source_target_pairs={{0,4},{1,133},{2,6},{3,135},{4,128},{5,1},{6,130},{7,3},{128,132},... | collective-permute-start | bytes 442376 | tf_op jit(solution)/shard_map/gZ2/ppermute | solution.py:28
  11.0 0.0 collective-permute-done.3.refs_0_.refs_1_
  11.1 0.9 %collective-permute-start.5 = (bf16[64,1152]{1,0:T(8,128)(2,1)}, bf16[64,1152]{1,0:T(8,128)(2,1)S(1)}, u32[]{:S(2)}, u32[]{:S(2)}) collective-permute-start(bf16[64,1152]{1,0:T(8,128)(2,1)} %refs_0_.3), channel_id=1, source_target_pairs={{0,133},{1,4},{2,135},{3,6},{4,1},{5,128},{6,3},{7,130},{128,5},{1... | collective-permute-start | bytes 442376 | tf_op jit(solution)/shard_map/gX2/ppermute | solution.py:28
  12.0 0.0 collective-permute-done.refs_1_
  12.0 0.0 collective-permute-done.1.refs_2_
  12.0 0.0 collective-permute-done.2.refs_3_
  12.0 0.2 shard_map.60.refs_0_
  12.2 3.0 %collective-permute-start.8 = (bf16[256,1152]{1,0:T(8,128)(2,1)S(1)}, bf16[256,1152]{1,0:T(8,128)(2,1)S(1)}, u32[]{:S(2)}, u32[]{:S(2)}) collective-permute-start(bf16[256,1152]{1,0:T(8,128)(2,1)S(1)} %shard_map.60.refs_0_), channel_id=1, source_target_pairs={{0,8},{1,33},{2,10},{3,35},{4,12},{5,37},{6,14},{7,39},{128,136},{... | collective-permute-start | bytes 1769480 | tf_op jit(solution)/shard_map/gB1/ppermute | solution.py:28
  15.3 0.0 collective-permute-start.9
  15.3 2.1 %collective-permute-start.10 = (bf16[256,1152]{1,0:T(8,128)(2,1)S(1)}, bf16[256,1152]{1,0:T(8,128)(2,1)S(1)}, u32[]{:S(2)}, u32[]{:S(2)}) collective-permute-start(bf16[256,1152]{1,0:T(8,128)(2,1)S(1)} %shard_map.60.refs_0_), channel_id=1, source_target_pairs={{0,16},{1,65},{2,18},{3,67},{4,20},{5,69},{6,22},{7,71},{128,144},... | collective-permute-start | bytes 1769480 | tf_op jit(solution)/shard_map/gB2/ppermute | solution.py:28
  17.4 0.0 collective-permute-done.4.refs_2_
  17.4 1.1 %collective-permute-done.5.refs_3_ = bf16[64,1152]{1,0:T(8,128)(2,1)S(1)} collective-permute-done((bf16[64,1152]{1,0:T(8,128)(2,1)}, bf16[64,1152]{1,0:T(8,128)(2,1)S(1)}, u32[]{:S(2)}, u32[]{:S(2)}) %collective-permute-start.5) | collective-permute-done | bytes 147488 | tf_op jit(solution)/shard_map/gX2/ppermute | solution.py:28
  18.6 0.2 shard_map.61.refs_0_
  18.8 3.5 %collective-permute-start.6 = (bf16[256,1152]{1,0:T(8,128)(2,1)S(1)}, bf16[256,1152]{1,0:T(8,128)(2,1)S(1)}, u32[]{:S(2)}, u32[]{:S(2)}) collective-permute-start(bf16[256,1152]{1,0:T(8,128)(2,1)S(1)} %shard_map.61.refs_0_), channel_id=1, source_target_pairs={{0,2},{1,135},{2,4},{3,1},{4,6},{5,3},{6,128},{7,5},{128,130},{129... | collective-permute-start | bytes 1769480 | tf_op jit(solution)/shard_map/gZ13/ppermute | solution.py:28
  22.3 1.7 %collective-permute-start.7 = (bf16[64,1152]{1,0:T(8,128)(2,1)S(1)}, bf16[64,1152]{1,0:T(8,128)(2,1)S(1)}, u32[]{:S(2)}, u32[]{:S(2)}) collective-permute-start(bf16[64,1152]{1,0:T(8,128)(2,1)S(1)} %collective-permute-done.4.refs_2_), channel_id=1, source_target_pairs={{0,4},{1,133},{2,6},{3,135},{4,128},{5,1},{6,130},{7,3},{128,132},... | collective-permute-start | bytes 442376 | tf_op jit(solution)/shard_map/gZ4/ppermute | solution.py:28
  24.0 7.5 %collective-permute-done.6.refs_2_.refs_1_ = bf16[256,1152]{1,0:T(8,128)(2,1)S(1)} collective-permute-done((bf16[256,1152]{1,0:T(8,128)(2,1)S(1)}, bf16[256,1152]{1,0:T(8,128)(2,1)S(1)}, u32[]{:S(2)}, u32[]{:S(2)}) %collective-permute-start.6) | collective-permute-done | bytes 589856 | tf_op jit(solution)/shard_map/gZ13/ppermute | solution.py:28
  31.5 0.1 shard_map.62.refs_1_
  31.6 0.2 shard_map.63
  31.8 0.2 shard_map.64
  32.0 4.1 %collective-permute-done.7.refs_2_ = bf16[64,1152]{1,0:T(8,128)(2,1)S(1)} collective-permute-done((bf16[64,1152]{1,0:T(8,128)(2,1)S(1)}, bf16[64,1152]{1,0:T(8,128)(2,1)S(1)}, u32[]{:S(2)}, u32[]{:S(2)}) %collective-permute-start.7) | collective-permute-done | bytes 147488 | tf_op jit(solution)/shard_map/gZ4/ppermute | solution.py:28
  36.0 0.0 collective-permute-done.8.refs_5_.refs_3_
  36.0 0.0 collective-permute-done.9.refs_6_.refs_4_
  36.0 0.0 collective-permute-done.10.refs_7_.refs_5_
  36.0 0.3 shard_map.66.refs_0_.refs_2_
  36.3 0.3 collective-permute-start.11
  36.6 3.4 %shard_map.67 = (bf16[1024,512]{1,0:T(8,128)(2,1)S(1)}, bf16[1024,1152]{1,0:T(8,128)(2,1)S(1)}, bf16[512,1152]{1,0:T(8,128)(2,1)S(1)}) custom-call(bf16[512,1152]{1,0:T(8,128)(2,1)S(1)} %shard_map.66.refs_0_.refs_2_, f32[8,128]{1,0:T(8,128)S(1)} %shard_map.62.refs_1_, bf16[256,1152]{1,0:T(8,128)(2,1)S(1)} %get-tuple-element.26.refs_3_.refs_2_, ...), custom_call_target="tpu_custom_call" | custom-call | flops 2415919104 | bytes 1024 | tf_op jit(solution)/shard_map/pallas_call | solution.py:55
  40.0 0.0 collective-permute-done.11.refs_0_.refs_3_
  40.1 3.0 %shard_map.68 = (bf16[1024,512]{1,0:T(8,128)(2,1)S(1)}, bf16[512,1152]{1,0:T(8,128)(2,1)S(1)}) custom-call(bf16[512,1152]{1,0:T(8,128)(2,1)S(1)} %collective-permute-done.11.refs_0_.refs_3_, f32[8,128]{1,0:T(8,128)S(1)} %shard_map.62.refs_1_, bf16[1024,1152]{1,0:T(8,128)(2,1)S(1)} %get-tuple-element.28.refs_2_, ...), custom_call_target="tpu_custom_call" | custom-call | flops 2415919104 | bytes 1024 | tf_op jit(solution)/shard_map/pallas_call | solution.py:55
  43.1 0.6 collective-permute-start.12
  43.7 0.8 %shard_map.69.refs_2_ = bf16[256,1152]{1,0:T(8,128)(2,1)S(1)} custom-call(bf16[1024,512]{1,0:T(8,128)(2,1)S(1)} %get-tuple-element.27.refs_0_, bf16[1024,512]{1,0:T(8,128)(2,1)S(1)} %get-tuple-element.30.refs_1_, bf16[512,1152]{1,0:T(8,128)(2,1)S(1)} %shard_map.66.refs_0_.refs_2_, bf16[512,1152]{1,0:T(8,128)(2,1)S(1)} %collective-permute-done.11.refs_0_.refs_3_, ...), custom_call_target="tpu_custom_call" | custom-call | flops 603979776 | bytes 1024 | tf_op jit(solution)/shard_map/pallas_call | solution.py:55
  44.5 0.3 collective-permute-start.13
  44.8 1.3 %collective-permute-done.12.refs_1_ = bf16[512,1152]{1,0:T(8,128)(2,1)S(1)} collective-permute-done((bf16[512,1152]{1,0:T(8,128)(2,1)S(1)}, bf16[512,1152]{1,0:T(8,128)(2,1)S(1)}, u32[]{:S(2)}, u32[]{:S(2)}) %collective-permute-start.12) | collective-permute-done | bytes 1179680 | tf_op jit(solution)/shard_map/rC/ppermute | solution.py:28
  46.2 0.3 shard_map.70
  46.4 1.4 %collective-permute-start.16 = (bf16[256,1152]{1,0:T(8,128)(2,1)S(1)}, bf16[256,1152]{1,0:T(8,128)(2,1)S(1)}, u32[]{:S(2)}, u32[]{:S(2)}) collective-permute-start(bf16[256,1152]{1,0:T(8,128)(2,1)S(1)} %get-tuple-element.32.refs_4_), channel_id=1, source_target_pairs={{0,134},{1,3},{2,0},{3,5},{4,2},{5,7},{6,4},{7,129},{128,6},{129,1... | collective-permute-start | bytes 1769480 | tf_op jit(solution)/shard_map/rZ13/ppermute | solution.py:28
  47.8 3.1 %collective-permute-start.17 = (bf16[64,1152]{1,0:T(8,128)(2,1)S(1)}, bf16[64,1152]{1,0:T(8,128)(2,1)S(1)}, u32[]{:S(2)}, u32[]{:S(2)}) collective-permute-start(bf16[64,1152]{1,0:T(8,128)(2,1)S(1)} %get-tuple-element.34), channel_id=1, source_target_pairs={{0,132},{1,5},{2,134},{3,7},{4,0},{5,129},{6,2},{7,131},{128,4},{1... | collective-permute-start | bytes 442376 | tf_op jit(solution)/shard_map/rZ4/ppermute | solution.py:28
  50.9 0.8 %shard_map.71.refs_4_ = bf16[256,1152]{1,0:T(8,128)(2,1)S(1)} custom-call(bf16[1024,512]{1,0:T(8,128)(2,1)S(1)} %get-tuple-element.27.refs_0_, bf16[1024,512]{1,0:T(8,128)(2,1)S(1)} %get-tuple-element.30.refs_1_, bf16[512,1152]{1,0:T(8,128)(2,1)S(1)} %shard_map.66.refs_0_.refs_2_, bf16[512,1152]{1,0:T(8,128)(2,1)S(1)} %collective-permute-done.11.refs_0_.refs_3_, ...), custom_call_target="tpu_custom_call" | custom-call | flops 603979776 | bytes 1024 | tf_op jit(solution)/shard_map/pallas_call | solution.py:55
  51.8 0.8 %collective-permute-start.14 = (bf16[256,1152]{1,0:T(8,128)(2,1)S(1)}, bf16[256,1152]{1,0:T(8,128)(2,1)S(1)}, u32[]{:S(2)}, u32[]{:S(2)}) collective-permute-start(bf16[256,1152]{1,0:T(8,128)(2,1)S(1)} %shard_map.71.refs_4_), channel_id=1, source_target_pairs={{0,24},{1,97},{2,26},{3,99},{4,28},{5,101},{6,30},{7,103},{128,152... | collective-permute-start | bytes 1769480 | tf_op jit(solution)/shard_map/rB1/ppermute | solution.py:28
  52.6 0.8 %shard_map.72.refs_4_ = bf16[256,1152]{1,0:T(8,128)(2,1)S(1)} custom-call(bf16[1024,512]{1,0:T(8,128)(2,1)S(1)} %get-tuple-element.27.refs_0_, bf16[1024,512]{1,0:T(8,128)(2,1)S(1)} %get-tuple-element.30.refs_1_, bf16[512,1152]{1,0:T(8,128)(2,1)S(1)} %shard_map.66.refs_0_.refs_2_, bf16[512,1152]{1,0:T(8,128)(2,1)S(1)} %collective-permute-done.11.refs_0_.refs_3_, ...), custom_call_target="tpu_custom_call" | custom-call | flops 603979776 | bytes 1024 | tf_op jit(solution)/shard_map/pallas_call | solution.py:55
  53.5 1.1 %collective-permute-start.15 = (bf16[256,1152]{1,0:T(8,128)(2,1)S(1)}, bf16[256,1152]{1,0:T(8,128)(2,1)S(1)}, u32[]{:S(2)}, u32[]{:S(2)}) collective-permute-start(bf16[256,1152]{1,0:T(8,128)(2,1)S(1)} %shard_map.72.refs_4_), channel_id=1, source_target_pairs={{0,16},{1,65},{2,18},{3,67},{4,20},{5,69},{6,22},{7,71},{128,144},... | collective-permute-start | bytes 1769480 | tf_op jit(solution)/shard_map/rB2/ppermute | solution.py:28
  54.5 0.8 %shard_map.73.refs_0_ = f32[256,1152]{1,0:T(8,128)S(1)} custom-call(bf16[1024,512]{1,0:T(8,128)(2,1)S(1)} %get-tuple-element.27.refs_0_, bf16[1024,512]{1,0:T(8,128)(2,1)S(1)} %get-tuple-element.30.refs_1_, bf16[512,1152]{1,0:T(8,128)(2,1)S(1)} %shard_map.66.refs_0_.refs_2_, bf16[512,1152]{1,0:T(8,128)(2,1)S(1)} %collective-permute-done.11.refs_0_.refs_3_, ...), custom_call_target="tpu_custom_call" | custom-call | flops 603979776 | bytes 1024 | tf_op jit(solution)/shard_map/pallas_call | solution.py:55
  55.4 0.0 collective-permute-done.13.refs_1_
  55.4 0.1 shard_map.74.refs_3_.refs_0_
  55.5 2.8 %collective-permute-done.17.refs_2_ = bf16[64,1152]{1,0:T(8,128)(2,1)S(1)} collective-permute-done((bf16[64,1152]{1,0:T(8,128)(2,1)S(1)}, bf16[64,1152]{1,0:T(8,128)(2,1)S(1)}, u32[]{:S(2)}, u32[]{:S(2)}) %collective-permute-start.17) | collective-permute-done | bytes 147488 | tf_op jit(solution)/shard_map/rZ4/ppermute | solution.py:28
  58.4 0.0 collective-permute-done.16.refs_1_
  58.4 0.1 shard_map.75.refs_0_
  58.5 3.7 %collective-permute-start.21 = (bf16[128,1152]{1,0:T(8,128)(2,1)S(1)}, bf16[128,1152]{1,0:T(8,128)(2,1)S(1)}, u32[]{:S(2)}, u32[]{:S(2)}) collective-permute-start(bf16[128,1152]{1,0:T(8,128)(2,1)S(1)} %shard_map.75.refs_0_), channel_id=1, source_target_pairs={{0,132},{1,5},{2,134},{3,7},{4,0},{5,129},{6,2},{7,131},{128,4},{1... | collective-permute-start | bytes 884744 | tf_op jit(solution)/shard_map/rZ2/ppermute | solution.py:28
  62.2 9.5 %collective-permute-done.14.refs_1_ = bf16[256,1152]{1,0:T(8,128)(2,1)S(1)} collective-permute-done((bf16[256,1152]{1,0:T(8,128)(2,1)S(1)}, bf16[256,1152]{1,0:T(8,128)(2,1)S(1)}, u32[]{:S(2)}, u32[]{:S(2)}) %collective-permute-start.14) | collective-permute-done | bytes 589856 | tf_op jit(solution)/shard_map/rB1/ppermute | solution.py:28
  71.7 0.0 collective-permute-done.15.refs_2_
  71.7 0.2 shard_map.77
  71.9 0.1 collective-permute-start.18
  72.0 2.4 %collective-permute-start.19 = (bf16[64,1152]{1,0:T(8,128)(2,1)S(1)}, bf16[64,1152]{1,0:T(8,128)(2,1)S(1)}, u32[]{:S(2)}, u32[]{:S(2)}) collective-permute-start(bf16[64,1152]{1,0:T(8,128)(2,1)S(1)} %get-tuple-element.37), channel_id=1, source_target_pairs={{0,64},{1,17},{2,66},{3,19},{4,68},{5,21},{6,70},{7,23},{128,192},... | collective-permute-start | bytes 442376 | tf_op jit(solution)/shard_map/rA2/ppermute | solution.py:28
  74.4 0.0 collective-permute-start.20
  74.4 0.0 collective-permute-done.21.refs_2_
  74.4 0.1 shard_map.78
  74.5 0.1 collective-permute-start.22
  74.6 2.5 %collective-permute-done.18.refs_3_ = bf16[64,1152]{1,0:T(8,128)(2,1)S(1)} collective-permute-done((bf16[64,1152]{1,0:T(8,128)(2,1)S(1)}, bf16[64,1152]{1,0:T(8,128)(2,1)S(1)}, u32[]{:S(2)}, u32[]{:S(2)}) %collective-permute-start.18) | collective-permute-done | bytes 147488 | tf_op jit(solution)/shard_map/rA1/ppermute | solution.py:28
  77.1 1.6 %collective-permute-done.19.refs_4_ = bf16[64,1152]{1,0:T(8,128)(2,1)S(1)} collective-permute-done((bf16[64,1152]{1,0:T(8,128)(2,1)S(1)}, bf16[64,1152]{1,0:T(8,128)(2,1)S(1)}, u32[]{:S(2)}, u32[]{:S(2)}) %collective-permute-start.19) | collective-permute-done | bytes 147488 | tf_op jit(solution)/shard_map/rA2/ppermute | solution.py:28
  78.7 2.0 %collective-permute-done.20.refs_5_ = bf16[64,1152]{1,0:T(8,128)(2,1)S(1)} collective-permute-done((bf16[64,1152]{1,0:T(8,128)(2,1)S(1)}, bf16[64,1152]{1,0:T(8,128)(2,1)S(1)}, u32[]{:S(2)}, u32[]{:S(2)}) %collective-permute-start.20) | collective-permute-done | bytes 147488 | tf_op jit(solution)/shard_map/rA3/ppermute | solution.py:28
  80.7 0.0 collective-permute-done.22.refs_9_
  80.7 1.1 %shard_map.79 = (f32[64,1152]{1,0:T(8,128)}, f32[64,1152]{1,0:T(8,128)}) custom-call(f32[64,1152]{1,0:T(8,128)S(1)} %get-tuple-element.23.refs_0_, f32[64,128]{1,0:T(8,128)S(1)} %get-tuple-element.24.refs_1_, f32[64,1152]{1,0:T(8,128)S(1)} %get-tuple-element.35.refs_2_, bf16[64,1152]{1,0:T(8,128)(2,1)S(1)} %collective-permute-done.18.refs_3_, ...), custom_call_target="tpu_custom_call" | custom-call | bytes 1024 | tf_op jit(solution)/shard_map/pallas_call | solution.py:55
  (7 shorter events, 0.0 us)
Async XLA Ops:
  0.6 10.4 %collective-permute-start.3 = (bf16[64,1152]{1,0:T(8,128)(2,1)}, bf16[64,1152]{1,0:T(8,128)(2,1)S(1)}, u32[]{:S(2)}, u32[]{:S(2)}) collective-permute-start(bf16[64,1152]{1,0:T(8,128)(2,1)} %refs_0_.3), channel_id=1, source_target_pairs={{0,1},{1,0},{2,3},{3,2},{4,5},{5,4},{6,7},{7,6},{128,129},{129,128... | collective-permute-start | bytes 442376 | tf_op jit(solution)/shard_map/gC/ppermute | solution.py:28
  0.7 11.2 %collective-permute-start = (bf16[64,1152]{1,0:T(8,128)(2,1)}, bf16[64,1152]{1,0:T(8,128)(2,1)S(1)}, u32[]{:S(2)}, u32[]{:S(2)}) collective-permute-start(bf16[64,1152]{1,0:T(8,128)(2,1)} %refs_0_.2), channel_id=1, source_target_pairs={{0,32},{1,9},{2,34},{3,11},{4,36},{5,13},{6,38},{7,15},{128,160},{... | collective-permute-start | bytes 442376 | tf_op jit(solution)/shard_map/gA1/ppermute | solution.py:28
  2.3 9.7 %collective-permute-start.1 = (bf16[64,1152]{1,0:T(8,128)(2,1)}, bf16[64,1152]{1,0:T(8,128)(2,1)S(1)}, u32[]{:S(2)}, u32[]{:S(2)}) collective-permute-start(bf16[64,1152]{1,0:T(8,128)(2,1)} %refs_0_.2), channel_id=1, source_target_pairs={{0,64},{1,17},{2,66},{3,19},{4,68},{5,21},{6,70},{7,23},{128,192},... | collective-permute-start | bytes 442376 | tf_op jit(solution)/shard_map/gA2/ppermute | solution.py:28
  5.0 6.9 %collective-permute-start.2 = (bf16[64,1152]{1,0:T(8,128)(2,1)}, bf16[64,1152]{1,0:T(8,128)(2,1)S(1)}, u32[]{:S(2)}, u32[]{:S(2)}) collective-permute-start(bf16[64,1152]{1,0:T(8,128)(2,1)} %refs_0_.2), channel_id=1, source_target_pairs={{0,96},{1,25},{2,98},{3,27},{4,100},{5,29},{6,102},{7,31},{128,224... | collective-permute-start | bytes 442376 | tf_op jit(solution)/shard_map/gA3/ppermute | solution.py:28
  6.5 10.9 %collective-permute-start.4 = (bf16[64,1152]{1,0:T(8,128)(2,1)}, bf16[64,1152]{1,0:T(8,128)(2,1)S(1)}, u32[]{:S(2)}, u32[]{:S(2)}) collective-permute-start(bf16[64,1152]{1,0:T(8,128)(2,1)} %refs_0_.3), channel_id=1, source_target_pairs={{0,4},{1,133},{2,6},{3,135},{4,128},{5,1},{6,130},{7,3},{128,132},... | collective-permute-start | bytes 442376 | tf_op jit(solution)/shard_map/gZ2/ppermute | solution.py:28
  11.0 1.0 %copy-start = (bf16[64,1152]{1,0:T(8,128)(2,1)S(1)}, bf16[64,1152]{1,0:T(8,128)(2,1)}, u32[]{:S(2)}) copy-start(bf16[64,1152]{1,0:T(8,128)(2,1)} %refs_0_.2) | copy-start | bytes 442372
  11.1 7.5 %collective-permute-start.5 = (bf16[64,1152]{1,0:T(8,128)(2,1)}, bf16[64,1152]{1,0:T(8,128)(2,1)S(1)}, u32[]{:S(2)}, u32[]{:S(2)}) collective-permute-start(bf16[64,1152]{1,0:T(8,128)(2,1)} %refs_0_.3), channel_id=1, source_target_pairs={{0,133},{1,4},{2,135},{3,6},{4,1},{5,128},{6,3},{7,130},{128,5},{1... | collective-permute-start | bytes 442376 | tf_op jit(solution)/shard_map/gX2/ppermute | solution.py:28
  12.0 6.6 %copy-start.1 = (bf16[64,1152]{1,0:T(8,128)(2,1)S(1)}, bf16[64,1152]{1,0:T(8,128)(2,1)}, u32[]{:S(2)}) copy-start(bf16[64,1152]{1,0:T(8,128)(2,1)} %refs_0_.3) | copy-start | bytes 442372
  12.2 23.8 %collective-permute-start.8 = (bf16[256,1152]{1,0:T(8,128)(2,1)S(1)}, bf16[256,1152]{1,0:T(8,128)(2,1)S(1)}, u32[]{:S(2)}, u32[]{:S(2)}) collective-permute-start(bf16[256,1152]{1,0:T(8,128)(2,1)S(1)} %shard_map.60.refs_0_), channel_id=1, source_target_pairs={{0,8},{1,33},{2,10},{3,35},{4,12},{5,37},{6,14},{7,39},{128,136},{... | collective-permute-start | bytes 1769480 | tf_op jit(solution)/shard_map/gB1/ppermute | solution.py:28
  15.3 20.8 %collective-permute-start.9 = (bf16[256,1152]{1,0:T(8,128)(2,1)S(1)}, bf16[256,1152]{1,0:T(8,128)(2,1)S(1)}, u32[]{:S(2)}, u32[]{:S(2)}) collective-permute-start(bf16[256,1152]{1,0:T(8,128)(2,1)S(1)} %shard_map.60.refs_0_), channel_id=1, source_target_pairs={{0,24},{1,97},{2,26},{3,99},{4,28},{5,101},{6,30},{7,103},{128,152... | collective-permute-start | bytes 1769480 | tf_op jit(solution)/shard_map/gB3/ppermute | solution.py:28
  15.3 20.8 %collective-permute-start.10 = (bf16[256,1152]{1,0:T(8,128)(2,1)S(1)}, bf16[256,1152]{1,0:T(8,128)(2,1)S(1)}, u32[]{:S(2)}, u32[]{:S(2)}) collective-permute-start(bf16[256,1152]{1,0:T(8,128)(2,1)S(1)} %shard_map.60.refs_0_), channel_id=1, source_target_pairs={{0,16},{1,65},{2,18},{3,67},{4,20},{5,69},{6,22},{7,71},{128,144},... | collective-permute-start | bytes 1769480 | tf_op jit(solution)/shard_map/gB2/ppermute | solution.py:28
  18.8 12.7 %collective-permute-start.6 = (bf16[256,1152]{1,0:T(8,128)(2,1)S(1)}, bf16[256,1152]{1,0:T(8,128)(2,1)S(1)}, u32[]{:S(2)}, u32[]{:S(2)}) collective-permute-start(bf16[256,1152]{1,0:T(8,128)(2,1)S(1)} %shard_map.61.refs_0_), channel_id=1, source_target_pairs={{0,2},{1,135},{2,4},{3,1},{4,6},{5,3},{6,128},{7,5},{128,130},{129... | collective-permute-start | bytes 1769480 | tf_op jit(solution)/shard_map/gZ13/ppermute | solution.py:28
  22.3 13.8 %collective-permute-start.7 = (bf16[64,1152]{1,0:T(8,128)(2,1)S(1)}, bf16[64,1152]{1,0:T(8,128)(2,1)S(1)}, u32[]{:S(2)}, u32[]{:S(2)}) collective-permute-start(bf16[64,1152]{1,0:T(8,128)(2,1)S(1)} %collective-permute-done.4.refs_2_), channel_id=1, source_target_pairs={{0,4},{1,133},{2,6},{3,135},{4,128},{5,1},{6,130},{7,3},{128,132},... | collective-permute-start | bytes 442376 | tf_op jit(solution)/shard_map/gZ4/ppermute | solution.py:28
  36.3 3.7 %collective-permute-start.11 = (bf16[512,1152]{1,0:T(8,128)(2,1)S(1)}, bf16[512,1152]{1,0:T(8,128)(2,1)S(1)}, u32[]{:S(2)}, u32[]{:S(2)}) collective-permute-start(bf16[512,1152]{1,0:T(8,128)(2,1)S(1)} %shard_map.66.refs_0_.refs_2_), channel_id=1, source_target_pairs={{0,1},{1,0},{2,3},{3,2},{4,5},{5,4},{6,7},{7,6},{128,129},{129,128... | collective-permute-start | bytes 3538952 | tf_op jit(solution)/shard_map/gS/ppermute | solution.py:28
  43.1 3.1 %collective-permute-start.12 = (bf16[512,1152]{1,0:T(8,128)(2,1)S(1)}, bf16[512,1152]{1,0:T(8,128)(2,1)S(1)}, u32[]{:S(2)}, u32[]{:S(2)}) collective-permute-start(bf16[512,1152]{1,0:T(8,128)(2,1)S(1)} %get-tuple-element.31.refs_4_), channel_id=1, source_target_pairs={{0,1},{1,0},{2,3},{3,2},{4,5},{5,4},{6,7},{7,6},{128,129},{129,128... | collective-permute-start | bytes 3538952 | tf_op jit(solution)/shard_map/rC/ppermute | solution.py:28
  44.5 10.9 %collective-permute-start.13 = (bf16[256,1152]{1,0:T(8,128)(2,1)S(1)}, bf16[256,1152]{1,0:T(8,128)(2,1)S(1)}, u32[]{:S(2)}, u32[]{:S(2)}) collective-permute-start(bf16[256,1152]{1,0:T(8,128)(2,1)S(1)} %shard_map.69.refs_2_), channel_id=1, source_target_pairs={{0,8},{1,33},{2,10},{3,35},{4,12},{5,37},{6,14},{7,39},{128,136},{... | collective-permute-start | bytes 1769480 | tf_op jit(solution)/shard_map/rB3/ppermute | solution.py:28
  46.4 11.9 %collective-permute-start.16 = (bf16[256,1152]{1,0:T(8,128)(2,1)S(1)}, bf16[256,1152]{1,0:T(8,128)(2,1)S(1)}, u32[]{:S(2)}, u32[]{:S(2)}) collective-permute-start(bf16[256,1152]{1,0:T(8,128)(2,1)S(1)} %get-tuple-element.32.refs_4_), channel_id=1, source_target_pairs={{0,134},{1,3},{2,0},{3,5},{4,2},{5,7},{6,4},{7,129},{128,6},{129,1... | collective-permute-start | bytes 1769480 | tf_op jit(solution)/shard_map/rZ13/ppermute | solution.py:28
  47.8 10.5 %collective-permute-start.17 = (bf16[64,1152]{1,0:T(8,128)(2,1)S(1)}, bf16[64,1152]{1,0:T(8,128)(2,1)S(1)}, u32[]{:S(2)}, u32[]{:S(2)}) collective-permute-start(bf16[64,1152]{1,0:T(8,128)(2,1)S(1)} %get-tuple-element.34), channel_id=1, source_target_pairs={{0,132},{1,5},{2,134},{3,7},{4,0},{5,129},{6,2},{7,131},{128,4},{1... | collective-permute-start | bytes 442376 | tf_op jit(solution)/shard_map/rZ4/ppermute | solution.py:28
  51.8 19.9 %collective-permute-start.14 = (bf16[256,1152]{1,0:T(8,128)(2,1)S(1)}, bf16[256,1152]{1,0:T(8,128)(2,1)S(1)}, u32[]{:S(2)}, u32[]{:S(2)}) collective-permute-start(bf16[256,1152]{1,0:T(8,128)(2,1)S(1)} %shard_map.71.refs_4_), channel_id=1, source_target_pairs={{0,24},{1,97},{2,26},{3,99},{4,28},{5,101},{6,30},{7,103},{128,152... | collective-permute-start | bytes 1769480 | tf_op jit(solution)/shard_map/rB1/ppermute | solution.py:28
  53.5 18.2 %collective-permute-start.15 = (bf16[256,1152]{1,0:T(8,128)(2,1)S(1)}, bf16[256,1152]{1,0:T(8,128)(2,1)S(1)}, u32[]{:S(2)}, u32[]{:S(2)}) collective-permute-start(bf16[256,1152]{1,0:T(8,128)(2,1)S(1)} %shard_map.72.refs_4_), channel_id=1, source_target_pairs={{0,16},{1,65},{2,18},{3,67},{4,20},{5,69},{6,22},{7,71},{128,144},... | collective-permute-start | bytes 1769480 | tf_op jit(solution)/shard_map/rB2/ppermute | solution.py:28
  58.5 15.9 %collective-permute-start.21 = (bf16[128,1152]{1,0:T(8,128)(2,1)S(1)}, bf16[128,1152]{1,0:T(8,128)(2,1)S(1)}, u32[]{:S(2)}, u32[]{:S(2)}) collective-permute-start(bf16[128,1152]{1,0:T(8,128)(2,1)S(1)} %shard_map.75.refs_0_), channel_id=1, source_target_pairs={{0,132},{1,5},{2,134},{3,7},{4,0},{5,129},{6,2},{7,131},{128,4},{1... | collective-permute-start | bytes 884744 | tf_op jit(solution)/shard_map/rZ2/ppermute | solution.py:28
  71.9 5.2 %collective-permute-start.18 = (bf16[64,1152]{1,0:T(8,128)(2,1)S(1)}, bf16[64,1152]{1,0:T(8,128)(2,1)S(1)}, u32[]{:S(2)}, u32[]{:S(2)}) collective-permute-start(bf16[64,1152]{1,0:T(8,128)(2,1)S(1)} %get-tuple-element.36), channel_id=1, source_target_pairs={{0,96},{1,25},{2,98},{3,27},{4,100},{5,29},{6,102},{7,31},{128,224... | collective-permute-start | bytes 442376 | tf_op jit(solution)/shard_map/rA1/ppermute | solution.py:28
  72.0 6.7 %collective-permute-start.19 = (bf16[64,1152]{1,0:T(8,128)(2,1)S(1)}, bf16[64,1152]{1,0:T(8,128)(2,1)S(1)}, u32[]{:S(2)}, u32[]{:S(2)}) collective-permute-start(bf16[64,1152]{1,0:T(8,128)(2,1)S(1)} %get-tuple-element.37), channel_id=1, source_target_pairs={{0,64},{1,17},{2,66},{3,19},{4,68},{5,21},{6,70},{7,23},{128,192},... | collective-permute-start | bytes 442376 | tf_op jit(solution)/shard_map/rA2/ppermute | solution.py:28
  74.4 6.4 %collective-permute-start.20 = (bf16[64,1152]{1,0:T(8,128)(2,1)S(1)}, bf16[64,1152]{1,0:T(8,128)(2,1)S(1)}, u32[]{:S(2)}, u32[]{:S(2)}) collective-permute-start(bf16[64,1152]{1,0:T(8,128)(2,1)S(1)} %get-tuple-element.38), channel_id=1, source_target_pairs={{0,32},{1,9},{2,34},{3,11},{4,36},{5,13},{6,38},{7,15},{128,160},{... | collective-permute-start | bytes 442376 | tf_op jit(solution)/shard_map/rA3/ppermute | solution.py:28
  74.5 6.3 %collective-permute-start.22 = (bf16[64,1152]{1,0:T(8,128)(2,1)S(1)}, bf16[64,1152]{1,0:T(8,128)(2,1)S(1)}, u32[]{:S(2)}, u32[]{:S(2)}) collective-permute-start(bf16[64,1152]{1,0:T(8,128)(2,1)S(1)} %get-tuple-element.43), channel_id=1, source_target_pairs={{0,1},{1,0},{2,3},{3,2},{4,5},{5,4},{6,7},{7,6},{128,129},{129,128... | collective-permute-start | bytes 442376 | tf_op jit(solution)/shard_map/rS/ppermute | solution.py:28

commit v12 on v11

--- a/solution.py
+++ b/solution.py
@@ -187,11 +187,19 @@
     text_grads(w_ref, img_ref, send_ref)
 
 
-def image_kernel(at, w1_ref, w2_ref, txt1_ref, txt2_ref, out_ref):
-    rows = out_ref.shape[0]
+def image_kernel(at, w1_ref, w2_ref, txt1_ref, txt2_ref, *outs):
+    rows = sum(out.shape[0] for out in outs)
     grad = jnp.dot(w1_ref[at:at + rows, :], txt1_ref[...], preferred_element_type=F32)
     grad += jnp.dot(w2_ref[at:at + rows, :], txt2_ref[...], preferred_element_type=F32)
-    out_ref[...] = grad.astype(out_ref.dtype)
+    at = 0
+    for out in outs:
+        out[...] = grad[at:at + out.shape[0]].astype(out.dtype)
+        at += out.shape[0]
+
+
+def relay_kernel(first_ref, first_got_ref, second_ref, second_got_ref, first_out, second_out):
+    first_out[...] = (first_ref[...].astype(F32) + first_got_ref[...].astype(F32)).astype(BF16)
+    second_out[...] = (second_ref[...].astype(F32) + second_got_ref[...].astype(F32)).astype(BF16)
 
 
 def total_kernel(keep_ref, got_ref, own_ref, part13_ref, part2_ref, part4_ref):
@@ -216,15 +224,19 @@
     send_ref[...] = (got13_ref[rows:2 * rows, :].astype(F32) + got2_ref[rows:, :].astype(F32)).astype(BF16)
 
 
-def partial_kernel(own_ref, first_ref, out_ref):
-    out_ref[...] = own_ref[...] + first_ref[...].astype(F32)
-
-
-def sums_kernel(sum_ref, first_ref, second_ref, *outs):
-    rows = outs[0].shape[0]
+def partial_kernel(own_ref, upper_ref, lower_ref, out_ref):
+    half = upper_ref.shape[0]
+    out_ref[:half, :] = own_ref[:half, :] + upper_ref[...].astype(F32)
+    out_ref[half:, :] = own_ref[half:, :] + lower_ref[...].astype(F32)
+
+
+def sums_kernel(sum_ref, upper_ref, lower_ref, *outs):
+    rows, half = outs[0].shape[0], upper_ref.shape[0]
     for n, out in enumerate(outs):
-        at = slice(n * rows, (n + 1) * rows)
-        out[...] = (sum_ref[at, :] + first_ref[at, :].astype(F32) + second_ref[at, :].astype(F32)).astype(out.dtype)
+        at = n * rows
+        last_ref, base = (upper_ref, 0) if at < half else (lower_ref, half)
+        total = sum_ref[at:at + rows, :] + last_ref[at - base:at - base + rows, :].astype(F32)
+        out[...] = total.astype(out.dtype)
 
 
 def final_kernel(*refs):
@@ -271,25 +283,31 @@
     )
     each = group.shape[0]
 
-    def image_grads(index, dtype, ties):
+    def image_grads(index, shapes, ties):
         return call(
-            lambda *refs: image_kernel(index * each, *refs), [((each, dim), dtype)],
+            lambda *refs: image_kernel(index * each, *refs), shapes,
             [w_mine, w_theirs, mine, theirs], ties=ties, flops=flops // 2, limit=24,
-        )[0]
-
-    grad3 = image_grads(2, BF16, [send])
-    back3 = shift(grad3, second(-3), "rB3")
+        )
+
+    halves = [((each // 2, dim), BF16)] * 2
+    upper2, lower2 = image_grads(3, halves, [send])
+    relay1 = shift(upper2, second(-1), "rF1")
+    relay3 = shift(lower2, second(1), "rF3")
+
     total_own, part13, part2, part4 = call(
         total_kernel,
         [((own, dim), F32), ((4 * own, dim), BF16), ((2 * own, dim), F32), ((own, dim), BF16)],
-        [keep, shift(send, other, "rC")], ties=[grad3],
-    )
-    grad1 = image_grads(1, BF16, [part13])
-    back1 = shift(grad1, second(-1), "rB1")
-    grad2 = image_grads(3, BF16, [grad1])
-    back2 = shift(grad2, second(-2), "rB2")
-    grad0 = image_grads(0, F32, [grad2])
-    (partial,) = call(partial_kernel, [((each, dim), F32)], [grad0, back3])
+        [keep, shift(send, other, "rC")], ties=[upper2],
+    )
+    upper3, lower3 = image_grads(2, halves, [part13])
+    upper_got = [shift(upper3, second(1), "rH3")]
+    upper1, lower1 = image_grads(1, halves, [upper3])
+    lower_got = [shift(lower1, second(-1), "rH1")]
+    upper1, lower3 = call(relay_kernel, halves, [upper1, relay1, lower3, relay3])
+    upper_got.append(shift(upper1, second(-1), "rG1"))
+    lower_got.append(shift(lower3, second(1), "rG3"))
+    (grad0,) = image_grads(0, [((each, dim), F32)], [upper1])
+    (partial,) = call(partial_kernel, [((each, dim), F32)], [grad0, upper_got[0], lower_got[0]])
     got13 = shift(part13, line(-1), "rZ13")
     got4 = shift(part4, line(-2), "rZ4")
     (middle,) = call(middle_kernel, [((2 * own, dim), BF16)], [part2, got13, got4], [partial])
@@ -298,7 +316,7 @@
     txt_last = shift(txt_send, other, "rS")
 
     img_sum, *parts = call(
-        sums_kernel, [((own, dim), F32)] + [((own, dim), BF16)] * 3, [partial, back1, back2], ties=[token(middle)]
+        sums_kernel, [((own, dim), F32)] + [((own, dim), BF16)] * 3, [partial, upper_got[1], lower_got[1]], ties=[token(middle)]
     )
     last = [shift(p, first(-k), "rA%d" % k) for k, p in zip((1, 2, 3), parts)]
 

time: 82.1 us -> 82.7 us (level)
  the two profiles are of different devices: /device:TPU:24 before, /device:TPU:2 now
where the time goes in v12:
time: 82.7 us; the launch traced here: 82.6 us
  starting transfers between devices  41.3 us (50%)
  waiting for transfers between devices  26.2 us (32%)
  Pallas kernels  12.9 us (16%)
  between operations  2.14 us (3%)
    ppermute x26, starting transfers between devices, shift(): return lax.ppermute(values, AXES, pairs)  41.3 us
    ppermute x26, waiting for transfers between devices, shift(): return lax.ppermute(values, AXES, pairs)  26.2 us
    pallas_call x22, Pallas kernels, call(): pl.pallas_call(lambda *refs: kernel(*refs[:n_in], *refs[n_in + len(ties):...  12.9 us
  transfers between devices with their start and end apart: 26, of which 8 were waited for; matrix products, arithmetic and copies ran while one was open for 0% of the time, Pallas kernels for 10%

profile of v12, /device:TPU:2, one launch (start us, length us, event | category | flops | bytes accessed | tf_op | source)
XLA Modules:
  0.0 82.6 jit_solution(14841589279633219556)
XLA Ops:
  0.6 0.1 collective-permute-start.3
  0.7 1.6 %collective-permute-start = (bf16[64,1152]{1,0:T(8,128)(2,1)}, bf16[64,1152]{1,0:T(8,128)(2,1)S(1)}, u32[]{:S(2)}, u32[]{:S(2)}) collective-permute-start(bf16[64,1152]{1,0:T(8,128)(2,1)} %refs_0_.2), channel_id=1, source_target_pairs={{0,32},{1,9},{2,34},{3,11},{4,36},{5,13},{6,38},{7,15},{128,160},{... | collective-permute-start | bytes 442376 | tf_op jit(solution)/shard_map/gA1/ppermute | solution.py:28
  2.3 2.8 %collective-permute-start.1 = (bf16[64,1152]{1,0:T(8,128)(2,1)}, bf16[64,1152]{1,0:T(8,128)(2,1)S(1)}, u32[]{:S(2)}, u32[]{:S(2)}) collective-permute-start(bf16[64,1152]{1,0:T(8,128)(2,1)} %refs_0_.2), channel_id=1, source_target_pairs={{0,64},{1,17},{2,66},{3,19},{4,68},{5,21},{6,70},{7,23},{128,192},... | collective-permute-start | bytes 442376 | tf_op jit(solution)/shard_map/gA2/ppermute | solution.py:28
  5.1 0.4 collective-permute-start.2
  5.6 3.3 %collective-permute-start.4 = (bf16[64,1152]{1,0:T(8,128)(2,1)}, bf16[64,1152]{1,0:T(8,128)(2,1)S(1)}, u32[]{:S(2)}, u32[]{:S(2)}) collective-permute-start(bf16[64,1152]{1,0:T(8,128)(2,1)} %refs_0_.3), channel_id=1, source_target_pairs={{0,4},{1,133},{2,6},{3,135},{4,128},{5,1},{6,130},{7,3},{128,132},... | collective-permute-start | bytes 442376 | tf_op jit(solution)/shard_map/gZ2/ppermute | solution.py:28
  10.1 0.0 collective-permute-done.3.refs_0_.refs_1_
  10.2 4.5 %collective-permute-start.5 = (bf16[64,1152]{1,0:T(8,128)(2,1)}, bf16[64,1152]{1,0:T(8,128)(2,1)S(1)}, u32[]{:S(2)}, u32[]{:S(2)}) collective-permute-start(bf16[64,1152]{1,0:T(8,128)(2,1)} %refs_0_.3), channel_id=1, source_target_pairs={{0,133},{1,4},{2,135},{3,6},{4,1},{5,128},{6,3},{7,130},{128,5},{1... | collective-permute-start | bytes 442376 | tf_op jit(solution)/shard_map/gX2/ppermute | solution.py:28
  14.7 0.0 collective-permute-done.2.refs_3_
  14.7 0.2 shard_map.60.refs_0_
  15.0 0.8 collective-permute-start.8
  15.7 2.6 %collective-permute-start.9 = (bf16[256,1152]{1,0:T(8,128)(2,1)S(1)}, bf16[256,1152]{1,0:T(8,128)(2,1)S(1)}, u32[]{:S(2)}, u32[]{:S(2)}) collective-permute-start(bf16[256,1152]{1,0:T(8,128)(2,1)S(1)} %shard_map.60.refs_0_), channel_id=1, source_target_pairs={{0,24},{1,97},{2,26},{3,99},{4,28},{5,101},{6,30},{7,103},{128,152... | collective-permute-start | bytes 1769480 | tf_op jit(solution)/shard_map/gB3/ppermute | solution.py:28
  18.3 0.0 collective-permute-start.10
  18.3 0.0 collective-permute-done.4.refs_2_
  18.3 0.3 collective-permute-done.5.refs_3_
  18.6 0.2 shard_map.61.refs_0_
  18.8 2.6 %collective-permute-start.6 = (bf16[256,1152]{1,0:T(8,128)(2,1)S(1)}, bf16[256,1152]{1,0:T(8,128)(2,1)S(1)}, u32[]{:S(2)}, u32[]{:S(2)}) collective-permute-start(bf16[256,1152]{1,0:T(8,128)(2,1)S(1)} %shard_map.61.refs_0_), channel_id=1, source_target_pairs={{0,2},{1,135},{2,4},{3,1},{4,6},{5,3},{6,128},{7,5},{128,130},{129... | collective-permute-start | bytes 1769480 | tf_op jit(solution)/shard_map/gZ13/ppermute | solution.py:28
  21.4 1.8 %collective-permute-start.7 = (bf16[64,1152]{1,0:T(8,128)(2,1)S(1)}, bf16[64,1152]{1,0:T(8,128)(2,1)S(1)}, u32[]{:S(2)}, u32[]{:S(2)}) collective-permute-start(bf16[64,1152]{1,0:T(8,128)(2,1)S(1)} %collective-permute-done.4.refs_2_), channel_id=1, source_target_pairs={{0,4},{1,133},{2,6},{3,135},{4,128},{5,1},{6,130},{7,3},{128,132},... | collective-permute-start | bytes 442376 | tf_op jit(solution)/shard_map/gZ4/ppermute | solution.py:28
  23.2 7.4 %collective-permute-done.6.refs_2_.refs_1_ = bf16[256,1152]{1,0:T(8,128)(2,1)S(1)} collective-permute-done((bf16[256,1152]{1,0:T(8,128)(2,1)S(1)}, bf16[256,1152]{1,0:T(8,128)(2,1)S(1)}, u32[]{:S(2)}, u32[]{:S(2)}) %collective-permute-start.6) | collective-permute-done | bytes 589856 | tf_op jit(solution)/shard_map/gZ13/ppermute | solution.py:28
  30.6 0.1 shard_map.62.refs_1_
  30.7 0.2 shard_map.63
  30.9 0.2 shard_map.64
  31.1 4.1 %collective-permute-done.7.refs_2_ = bf16[64,1152]{1,0:T(8,128)(2,1)S(1)} collective-permute-done((bf16[64,1152]{1,0:T(8,128)(2,1)S(1)}, bf16[64,1152]{1,0:T(8,128)(2,1)S(1)}, u32[]{:S(2)}, u32[]{:S(2)}) %collective-permute-start.7) | collective-permute-done | bytes 147488 | tf_op jit(solution)/shard_map/gZ4/ppermute | solution.py:28
  35.1 0.0 collective-permute-done.8.refs_5_.refs_3_
  35.1 0.3 shard_map.66.refs_0_.refs_2_
  35.4 0.3 collective-permute-start.11
  35.7 3.5 %shard_map.67 = (bf16[1024,512]{1,0:T(8,128)(2,1)S(1)}, bf16[1024,1152]{1,0:T(8,128)(2,1)S(1)}, bf16[512,1152]{1,0:T(8,128)(2,1)S(1)}) custom-call(bf16[512,1152]{1,0:T(8,128)(2,1)S(1)} %shard_map.66.refs_0_.refs_2_, f32[8,128]{1,0:T(8,128)S(1)} %shard_map.62.refs_1_, bf16[256,1152]{1,0:T(8,128)(2,1)S(1)} %get-tuple-element.34.refs_3_.refs_2_, ...), custom_call_target="tpu_custom_call" | custom-call | flops 2415919104 | bytes 1024 | tf_op jit(solution)/shard_map/pallas_call | solution.py:55
  39.2 0.0 collective-permute-done.11.refs_0_.refs_3_
  39.2 3.0 %shard_map.68 = (bf16[1024,512]{1,0:T(8,128)(2,1)S(1)}, bf16[512,1152]{1,0:T(8,128)(2,1)S(1)}) custom-call(bf16[512,1152]{1,0:T(8,128)(2,1)S(1)} %collective-permute-done.11.refs_0_.refs_3_, f32[8,128]{1,0:T(8,128)S(1)} %shard_map.62.refs_1_, bf16[1024,1152]{1,0:T(8,128)(2,1)S(1)} %get-tuple-element.36.refs_2_, ...), custom_call_target="tpu_custom_call" | custom-call | flops 2415919104 | bytes 1024 | tf_op jit(solution)/shard_map/pallas_call | solution.py:55
  42.2 0.6 collective-permute-start.12
  42.8 0.8 %shard_map.69 = (bf16[128,1152]{1,0:T(8,128)(2,1)S(1)}, bf16[128,1152]{1,0:T(8,128)(2,1)S(1)}) custom-call(bf16[1024,512]{1,0:T(8,128)(2,1)S(1)} %get-tuple-element.35.refs_0_, bf16[1024,512]{1,0:T(8,128)(2,1)S(1)} %get-tuple-element.38.refs_1_, bf16[512,1152]{1,0:T(8,128)(2,1)S(1)} %shard_map.66.refs_0_.refs_2_, ...), custom_call_target="tpu_custom_call" | custom-call | flops 603979776 | bytes 1024 | tf_op jit(solution)/shard_map/pallas_call | solution.py:55
  43.6 1.6 %collective-permute-done.12.refs_1_ = bf16[512,1152]{1,0:T(8,128)(2,1)S(1)} collective-permute-done((bf16[512,1152]{1,0:T(8,128)(2,1)S(1)}, bf16[512,1152]{1,0:T(8,128)(2,1)S(1)}, u32[]{:S(2)}, u32[]{:S(2)}) %collective-permute-start.12) | collective-permute-done | bytes 1179680 | tf_op jit(solution)/shard_map/rC/ppermute | solution.py:28
  45.3 0.3 shard_map.70
  45.5 1.4 %collective-permute-start.19 = (bf16[256,1152]{1,0:T(8,128)(2,1)S(1)}, bf16[256,1152]{1,0:T(8,128)(2,1)S(1)}, u32[]{:S(2)}, u32[]{:S(2)}) collective-permute-start(bf16[256,1152]{1,0:T(8,128)(2,1)S(1)} %get-tuple-element.41.refs_4_), channel_id=1, source_target_pairs={{0,134},{1,3},{2,0},{3,5},{4,2},{5,7},{6,4},{7,129},{128,6},{129,1... | collective-permute-start | bytes 1769480 | tf_op jit(solution)/shard_map/rZ13/ppermute | solution.py:28
  46.9 3.0 %collective-permute-start.13 = (bf16[128,1152]{1,0:T(8,128)(2,1)S(1)}, bf16[128,1152]{1,0:T(8,128)(2,1)S(1)}, u32[]{:S(2)}, u32[]{:S(2)}) collective-permute-start(bf16[128,1152]{1,0:T(8,128)(2,1)S(1)} %get-tuple-element.40.refs_2_), channel_id=1, source_target_pairs={{0,24},{1,97},{2,26},{3,99},{4,28},{5,101},{6,30},{7,103},{128,152... | collective-permute-start | bytes 884744 | tf_op jit(solution)/shard_map/rF1/ppermute | solution.py:28
  49.9 0.0 collective-permute-start.14
  49.9 0.8 %shard_map.71 = (bf16[128,1152]{1,0:T(8,128)(2,1)S(1)}, bf16[128,1152]{1,0:T(8,128)(2,1)S(1)}) custom-call(bf16[1024,512]{1,0:T(8,128)(2,1)S(1)} %get-tuple-element.35.refs_0_, bf16[1024,512]{1,0:T(8,128)(2,1)S(1)} %get-tuple-element.38.refs_1_, bf16[512,1152]{1,0:T(8,128)(2,1)S(1)} %shard_map.66.refs_0_.refs_2_, ...), custom_call_target="tpu_custom_call" | custom-call | flops 603979776 | bytes 1024 | tf_op jit(solution)/shard_map/pallas_call | solution.py:55
  50.8 0.7 collective-permute-start.15
  51.4 0.8 %shard_map.72 = (bf16[128,1152]{1,0:T(8,128)(2,1)S(1)}, bf16[128,1152]{1,0:T(8,128)(2,1)S(1)}) custom-call(bf16[1024,512]{1,0:T(8,128)(2,1)S(1)} %get-tuple-element.35.refs_0_, bf16[1024,512]{1,0:T(8,128)(2,1)S(1)} %get-tuple-element.38.refs_1_, bf16[512,1152]{1,0:T(8,128)(2,1)S(1)} %shard_map.66.refs_0_.refs_2_, ...), custom_call_target="tpu_custom_call" | custom-call | flops 603979776 | bytes 1024 | tf_op jit(solution)/shard_map/pallas_call | solution.py:55
  52.3 2.7 %collective-permute-start.16 = (bf16[128,1152]{1,0:T(8,128)(2,1)S(1)}, bf16[128,1152]{1,0:T(8,128)(2,1)S(1)}, u32[]{:S(2)}, u32[]{:S(2)}) collective-permute-start(bf16[128,1152]{1,0:T(8,128)(2,1)S(1)} %get-tuple-element.47), channel_id=1, source_target_pairs={{0,24},{1,97},{2,26},{3,99},{4,28},{5,101},{6,30},{7,103},{128,152... | collective-permute-start | bytes 884744 | tf_op jit(solution)/shard_map/rH1/ppermute | solution.py:28
  55.0 0.0 collective-permute-done.13.refs_1_
  55.0 3.1 %collective-permute-start.20 = (bf16[64,1152]{1,0:T(8,128)(2,1)S(1)}, bf16[64,1152]{1,0:T(8,128)(2,1)S(1)}, u32[]{:S(2)}, u32[]{:S(2)}) collective-permute-start(bf16[64,1152]{1,0:T(8,128)(2,1)S(1)} %get-tuple-element.50), channel_id=1, source_target_pairs={{0,132},{1,5},{2,134},{3,7},{4,0},{5,129},{6,2},{7,131},{128,4},{1... | collective-permute-start | bytes 442376 | tf_op jit(solution)/shard_map/rZ4/ppermute | solution.py:28
  58.2 0.0 collective-permute-done.14.refs_3_
  58.2 0.1 shard_map.73
  58.3 2.9 %collective-permute-start.17 = (bf16[128,1152]{1,0:T(8,128)(2,1)S(1)}, bf16[128,1152]{1,0:T(8,128)(2,1)S(1)}, u32[]{:S(2)}, u32[]{:S(2)}) collective-permute-start(bf16[128,1152]{1,0:T(8,128)(2,1)S(1)} %get-tuple-element.46.refs_4_), channel_id=1, source_target_pairs={{0,24},{1,97},{2,26},{3,99},{4,28},{5,101},{6,30},{7,103},{128,152... | collective-permute-start | bytes 884744 | tf_op jit(solution)/shard_map/rG1/ppermute | solution.py:28
  61.2 0.8 %shard_map.74.refs_0_ = f32[256,1152]{1,0:T(8,128)S(1)} custom-call(bf16[1024,512]{1,0:T(8,128)(2,1)S(1)} %get-tuple-element.35.refs_0_, bf16[1024,512]{1,0:T(8,128)(2,1)S(1)} %get-tuple-element.38.refs_1_, bf16[512,1152]{1,0:T(8,128)(2,1)S(1)} %shard_map.66.refs_0_.refs_2_, bf16[512,1152]{1,0:T(8,128)(2,1)S(1)} %collective-permute-done.11.refs_0_.refs_3_, ...), custom_call_target="tpu_custom_call" | custom-call | flops 603979776 | bytes 1024 | tf_op jit(solution)/shard_map/pallas_call | solution.py:55
  62.1 0.1 collective-permute-start.18
  62.2 0.1 shard_map.75.refs_3_.refs_0_
  62.3 0.0 collective-permute-done.20.refs_2_
  62.3 0.0 collective-permute-done.19.refs_1_
  62.3 0.1 shard_map.76.refs_0_
  62.4 3.7 %collective-permute-start.24 = (bf16[128,1152]{1,0:T(8,128)(2,1)S(1)}, bf16[128,1152]{1,0:T(8,128)(2,1)S(1)}, u32[]{:S(2)}, u32[]{:S(2)}) collective-permute-start(bf16[128,1152]{1,0:T(8,128)(2,1)S(1)} %shard_map.76.refs_0_), channel_id=1, source_target_pairs={{0,132},{1,5},{2,134},{3,7},{4,0},{5,129},{6,2},{7,131},{128,4},{1... | collective-permute-start | bytes 884744 | tf_op jit(solution)/shard_map/rZ2/ppermute | solution.py:28
  66.1 6.4 %collective-permute-done.18.refs_2_ = bf16[128,1152]{1,0:T(8,128)(2,1)S(1)} collective-permute-done((bf16[128,1152]{1,0:T(8,128)(2,1)S(1)}, bf16[128,1152]{1,0:T(8,128)(2,1)S(1)}, u32[]{:S(2)}, u32[]{:S(2)}) %collective-permute-start.18) | collective-permute-done | bytes 294944 | tf_op jit(solution)/shard_map/rG3/ppermute | solution.py:28
  72.5 0.1 shard_map.78
  72.6 0.1 collective-permute-start.21
  72.7 0.8 collective-permute-start.22
  73.5 1.5 %collective-permute-start.23 = (bf16[64,1152]{1,0:T(8,128)(2,1)S(1)}, bf16[64,1152]{1,0:T(8,128)(2,1)S(1)}, u32[]{:S(2)}, u32[]{:S(2)}) collective-permute-start(bf16[64,1152]{1,0:T(8,128)(2,1)S(1)} %get-tuple-element.54), channel_id=1, source_target_pairs={{0,32},{1,9},{2,34},{3,11},{4,36},{5,13},{6,38},{7,15},{128,160},{... | collective-permute-start | bytes 442376 | tf_op jit(solution)/shard_map/rA3/ppermute | solution.py:28
  75.0 0.0 collective-permute-done.24.refs_2_
  75.0 0.1 shard_map.79
  75.1 0.1 collective-permute-start.25
  75.2 2.7 %collective-permute-done.21.refs_3_ = bf16[64,1152]{1,0:T(8,128)(2,1)S(1)} collective-permute-done((bf16[64,1152]{1,0:T(8,128)(2,1)S(1)}, bf16[64,1152]{1,0:T(8,128)(2,1)S(1)}, u32[]{:S(2)}, u32[]{:S(2)}) %collective-permute-start.21) | collective-permute-done | bytes 147488 | tf_op jit(solution)/shard_map/rA1/ppermute | solution.py:28
  77.8 1.6 %collective-permute-done.22.refs_4_ = bf16[64,1152]{1,0:T(8,128)(2,1)S(1)} collective-permute-done((bf16[64,1152]{1,0:T(8,128)(2,1)S(1)}, bf16[64,1152]{1,0:T(8,128)(2,1)S(1)}, u32[]{:S(2)}, u32[]{:S(2)}) %collective-permute-start.22) | collective-permute-done | bytes 147488 | tf_op jit(solution)/shard_map/rA2/ppermute | solution.py:28
  79.4 2.1 %collective-permute-done.23.refs_5_ = bf16[64,1152]{1,0:T(8,128)(2,1)S(1)} collective-permute-done((bf16[64,1152]{1,0:T(8,128)(2,1)S(1)}, bf16[64,1152]{1,0:T(8,128)(2,1)S(1)}, u32[]{:S(2)}, u32[]{:S(2)}) %collective-permute-start.23) | collective-permute-done | bytes 147488 | tf_op jit(solution)/shard_map/rA3/ppermute | solution.py:28
  81.5 0.0 collective-permute-done.25.refs_9_
  81.5 1.1 %shard_map.80 = (f32[64,1152]{1,0:T(8,128)}, f32[64,1152]{1,0:T(8,128)}) custom-call(f32[64,1152]{1,0:T(8,128)S(1)} %get-tuple-element.31.refs_0_, f32[64,128]{1,0:T(8,128)S(1)} %get-tuple-element.32.refs_1_, f32[64,1152]{1,0:T(8,128)S(1)} %get-tuple-element.51.refs_2_, bf16[64,1152]{1,0:T(8,128)(2,1)S(1)} %collective-permute-done.21.refs_3_, ...), custom_call_target="tpu_custom_call" | custom-call | bytes 1024 | tf_op jit(solution)/shard_map/pallas_call | solution.py:55
  (14 shorter events, 0.0 us)
Async XLA Ops:
  0.6 9.5 %collective-permute-start.3 = (bf16[64,1152]{1,0:T(8,128)(2,1)}, bf16[64,1152]{1,0:T(8,128)(2,1)S(1)}, u32[]{:S(2)}, u32[]{:S(2)}) collective-permute-start(bf16[64,1152]{1,0:T(8,128)(2,1)} %refs_0_.3), channel_id=1, source_target_pairs={{0,1},{1,0},{2,3},{3,2},{4,5},{5,4},{6,7},{7,6},{128,129},{129,128... | collective-permute-start | bytes 442376 | tf_op jit(solution)/shard_map/gC/ppermute | solution.py:28
  0.7 14.0 %collective-permute-start = (bf16[64,1152]{1,0:T(8,128)(2,1)}, bf16[64,1152]{1,0:T(8,128)(2,1)S(1)}, u32[]{:S(2)}, u32[]{:S(2)}) collective-permute-start(bf16[64,1152]{1,0:T(8,128)(2,1)} %refs_0_.2), channel_id=1, source_target_pairs={{0,32},{1,9},{2,34},{3,11},{4,36},{5,13},{6,38},{7,15},{128,160},{... | collective-permute-start | bytes 442376 | tf_op jit(solution)/shard_map/gA1/ppermute | solution.py:28
  2.3 12.4 %collective-permute-start.1 = (bf16[64,1152]{1,0:T(8,128)(2,1)}, bf16[64,1152]{1,0:T(8,128)(2,1)S(1)}, u32[]{:S(2)}, u32[]{:S(2)}) collective-permute-start(bf16[64,1152]{1,0:T(8,128)(2,1)} %refs_0_.2), channel_id=1, source_target_pairs={{0,64},{1,17},{2,66},{3,19},{4,68},{5,21},{6,70},{7,23},{128,192},... | collective-permute-start | bytes 442376 | tf_op jit(solution)/shard_map/gA2/ppermute | solution.py:28
  5.1 9.6 %collective-permute-start.2 = (bf16[64,1152]{1,0:T(8,128)(2,1)}, bf16[64,1152]{1,0:T(8,128)(2,1)S(1)}, u32[]{:S(2)}, u32[]{:S(2)}) collective-permute-start(bf16[64,1152]{1,0:T(8,128)(2,1)} %refs_0_.2), channel_id=1, source_target_pairs={{0,96},{1,25},{2,98},{3,27},{4,100},{5,29},{6,102},{7,31},{128,224... | collective-permute-start | bytes 442376 | tf_op jit(solution)/shard_map/gA3/ppermute | solution.py:28
  5.6 12.7 %collective-permute-start.4 = (bf16[64,1152]{1,0:T(8,128)(2,1)}, bf16[64,1152]{1,0:T(8,128)(2,1)S(1)}, u32[]{:S(2)}, u32[]{:S(2)}) collective-permute-start(bf16[64,1152]{1,0:T(8,128)(2,1)} %refs_0_.3), channel_id=1, source_target_pairs={{0,4},{1,133},{2,6},{3,135},{4,128},{5,1},{6,130},{7,3},{128,132},... | collective-permute-start | bytes 442376 | tf_op jit(solution)/shard_map/gZ2/ppermute | solution.py:28
  10.1 4.6 %copy-start = (bf16[64,1152]{1,0:T(8,128)(2,1)S(1)}, bf16[64,1152]{1,0:T(8,128)(2,1)}, u32[]{:S(2)}) copy-start(bf16[64,1152]{1,0:T(8,128)(2,1)} %refs_0_.2) | copy-start | bytes 442372
  10.2 8.4 %collective-permute-start.5 = (bf16[64,1152]{1,0:T(8,128)(2,1)}, bf16[64,1152]{1,0:T(8,128)(2,1)S(1)}, u32[]{:S(2)}, u32[]{:S(2)}) collective-permute-start(bf16[64,1152]{1,0:T(8,128)(2,1)} %refs_0_.3), channel_id=1, source_target_pairs={{0,133},{1,4},{2,135},{3,6},{4,1},{5,128},{6,3},{7,130},{128,5},{1... | collective-permute-start | bytes 442376 | tf_op jit(solution)/shard_map/gX2/ppermute | solution.py:28
  14.7 3.9 %copy-start.1 = (bf16[64,1152]{1,0:T(8,128)(2,1)S(1)}, bf16[64,1152]{1,0:T(8,128)(2,1)}, u32[]{:S(2)}) copy-start(bf16[64,1152]{1,0:T(8,128)(2,1)} %refs_0_.3) | copy-start | bytes 442372
  15.0 20.2 %collective-permute-start.8 = (bf16[256,1152]{1,0:T(8,128)(2,1)S(1)}, bf16[256,1152]{1,0:T(8,128)(2,1)S(1)}, u32[]{:S(2)}, u32[]{:S(2)}) collective-permute-start(bf16[256,1152]{1,0:T(8,128)(2,1)S(1)} %shard_map.60.refs_0_), channel_id=1, source_target_pairs={{0,8},{1,33},{2,10},{3,35},{4,12},{5,37},{6,14},{7,39},{128,136},{... | collective-permute-start | bytes 1769480 | tf_op jit(solution)/shard_map/gB1/ppermute | solution.py:28
  15.7 19.4 %collective-permute-start.9 = (bf16[256,1152]{1,0:T(8,128)(2,1)S(1)}, bf16[256,1152]{1,0:T(8,128)(2,1)S(1)}, u32[]{:S(2)}, u32[]{:S(2)}) collective-permute-start(bf16[256,1152]{1,0:T(8,128)(2,1)S(1)} %shard_map.60.refs_0_), channel_id=1, source_target_pairs={{0,24},{1,97},{2,26},{3,99},{4,28},{5,101},{6,30},{7,103},{128,152... | collective-permute-start | bytes 1769480 | tf_op jit(solution)/shard_map/gB3/ppermute | solution.py:28
  18.3 16.8 %collective-permute-start.10 = (bf16[256,1152]{1,0:T(8,128)(2,1)S(1)}, bf16[256,1152]{1,0:T(8,128)(2,1)S(1)}, u32[]{:S(2)}, u32[]{:S(2)}) collective-permute-start(bf16[256,1152]{1,0:T(8,128)(2,1)S(1)} %shard_map.60.refs_0_), channel_id=1, source_target_pairs={{0,16},{1,65},{2,18},{3,67},{4,20},{5,69},{6,22},{7,71},{128,144},... | collective-permute-start | bytes 1769480 | tf_op jit(solution)/shard_map/gB2/ppermute | solution.py:28
  18.8 11.8 %collective-permute-start.6 = (bf16[256,1152]{1,0:T(8,128)(2,1)S(1)}, bf16[256,1152]{1,0:T(8,128)(2,1)S(1)}, u32[]{:S(2)}, u32[]{:S(2)}) collective-permute-start(bf16[256,1152]{1,0:T(8,128)(2,1)S(1)} %shard_map.61.refs_0_), channel_id=1, source_target_pairs={{0,2},{1,135},{2,4},{3,1},{4,6},{5,3},{6,128},{7,5},{128,130},{129... | collective-permute-start | bytes 1769480 | tf_op jit(solution)/shard_map/gZ13/ppermute | solution.py:28
  21.4 13.8 %collective-permute-start.7 = (bf16[64,1152]{1,0:T(8,128)(2,1)S(1)}, bf16[64,1152]{1,0:T(8,128)(2,1)S(1)}, u32[]{:S(2)}, u32[]{:S(2)}) collective-permute-start(bf16[64,1152]{1,0:T(8,128)(2,1)S(1)} %collective-permute-done.4.refs_2_), channel_id=1, source_target_pairs={{0,4},{1,133},{2,6},{3,135},{4,128},{5,1},{6,130},{7,3},{128,132},... | collective-permute-start | bytes 442376 | tf_op jit(solution)/shard_map/gZ4/ppermute | solution.py:28
  35.4 3.7 %collective-permute-start.11 = (bf16[512,1152]{1,0:T(8,128)(2,1)S(1)}, bf16[512,1152]{1,0:T(8,128)(2,1)S(1)}, u32[]{:S(2)}, u32[]{:S(2)}) collective-permute-start(bf16[512,1152]{1,0:T(8,128)(2,1)S(1)} %shard_map.66.refs_0_.refs_2_), channel_id=1, source_target_pairs={{0,1},{1,0},{2,3},{3,2},{4,5},{5,4},{6,7},{7,6},{128,129},{129,128... | collective-permute-start | bytes 3538952 | tf_op jit(solution)/shard_map/gS/ppermute | solution.py:28
  42.2 3.1 %collective-permute-start.12 = (bf16[512,1152]{1,0:T(8,128)(2,1)S(1)}, bf16[512,1152]{1,0:T(8,128)(2,1)S(1)}, u32[]{:S(2)}, u32[]{:S(2)}) collective-permute-start(bf16[512,1152]{1,0:T(8,128)(2,1)S(1)} %get-tuple-element.39.refs_4_), channel_id=1, source_target_pairs={{0,1},{1,0},{2,3},{3,2},{4,5},{5,4},{6,7},{7,6},{128,129},{129,128... | collective-permute-start | bytes 3538952 | tf_op jit(solution)/shard_map/rC/ppermute | solution.py:28
  45.5 16.8 %collective-permute-start.19 = (bf16[256,1152]{1,0:T(8,128)(2,1)S(1)}, bf16[256,1152]{1,0:T(8,128)(2,1)S(1)}, u32[]{:S(2)}, u32[]{:S(2)}) collective-permute-start(bf16[256,1152]{1,0:T(8,128)(2,1)S(1)} %get-tuple-element.41.refs_4_), channel_id=1, source_target_pairs={{0,134},{1,3},{2,0},{3,5},{4,2},{5,7},{6,4},{7,129},{128,6},{129,1... | collective-permute-start | bytes 1769480 | tf_op jit(solution)/shard_map/rZ13/ppermute | solution.py:28
  46.9 8.1 %collective-permute-start.13 = (bf16[128,1152]{1,0:T(8,128)(2,1)S(1)}, bf16[128,1152]{1,0:T(8,128)(2,1)S(1)}, u32[]{:S(2)}, u32[]{:S(2)}) collective-permute-start(bf16[128,1152]{1,0:T(8,128)(2,1)S(1)} %get-tuple-element.40.refs_2_), channel_id=1, source_target_pairs={{0,24},{1,97},{2,26},{3,99},{4,28},{5,101},{6,30},{7,103},{128,152... | collective-permute-start | bytes 884744 | tf_op jit(solution)/shard_map/rF1/ppermute | solution.py:28
  49.9 8.2 %collective-permute-start.14 = (bf16[128,1152]{1,0:T(8,128)(2,1)S(1)}, bf16[128,1152]{1,0:T(8,128)(2,1)S(1)}, u32[]{:S(2)}, u32[]{:S(2)}) collective-permute-start(bf16[128,1152]{1,0:T(8,128)(2,1)S(1)} %get-tuple-element.45), channel_id=1, source_target_pairs={{0,8},{1,33},{2,10},{3,35},{4,12},{5,37},{6,14},{7,39},{128,136},{... | collective-permute-start | bytes 884744 | tf_op jit(solution)/shard_map/rF3/ppermute | solution.py:28
  50.8 11.3 %collective-permute-start.15 = (bf16[128,1152]{1,0:T(8,128)(2,1)S(1)}, bf16[128,1152]{1,0:T(8,128)(2,1)S(1)}, u32[]{:S(2)}, u32[]{:S(2)}) collective-permute-start(bf16[128,1152]{1,0:T(8,128)(2,1)S(1)} %get-tuple-element.42.refs_4_), channel_id=1, source_target_pairs={{0,8},{1,33},{2,10},{3,35},{4,12},{5,37},{6,14},{7,39},{128,136},{... | collective-permute-start | bytes 884744 | tf_op jit(solution)/shard_map/rH3/ppermute | solution.py:28
  52.3 9.9 %collective-permute-start.16 = (bf16[128,1152]{1,0:T(8,128)(2,1)S(1)}, bf16[128,1152]{1,0:T(8,128)(2,1)S(1)}, u32[]{:S(2)}, u32[]{:S(2)}) collective-permute-start(bf16[128,1152]{1,0:T(8,128)(2,1)S(1)} %get-tuple-element.47), channel_id=1, source_target_pairs={{0,24},{1,97},{2,26},{3,99},{4,28},{5,101},{6,30},{7,103},{128,152... | collective-permute-start | bytes 884744 | tf_op jit(solution)/shard_map/rH1/ppermute | solution.py:28
  55.0 7.3 %collective-permute-start.20 = (bf16[64,1152]{1,0:T(8,128)(2,1)S(1)}, bf16[64,1152]{1,0:T(8,128)(2,1)S(1)}, u32[]{:S(2)}, u32[]{:S(2)}) collective-permute-start(bf16[64,1152]{1,0:T(8,128)(2,1)S(1)} %get-tuple-element.50), channel_id=1, source_target_pairs={{0,132},{1,5},{2,134},{3,7},{4,0},{5,129},{6,2},{7,131},{128,4},{1... | collective-permute-start | bytes 442376 | tf_op jit(solution)/shard_map/rZ4/ppermute | solution.py:28
  58.3 7.8 %collective-permute-start.17 = (bf16[128,1152]{1,0:T(8,128)(2,1)S(1)}, bf16[128,1152]{1,0:T(8,128)(2,1)S(1)}, u32[]{:S(2)}, u32[]{:S(2)}) collective-permute-start(bf16[128,1152]{1,0:T(8,128)(2,1)S(1)} %get-tuple-element.46.refs_4_), channel_id=1, source_target_pairs={{0,24},{1,97},{2,26},{3,99},{4,28},{5,101},{6,30},{7,103},{128,152... | collective-permute-start | bytes 884744 | tf_op jit(solution)/shard_map/rG1/ppermute | solution.py:28
  62.1 10.4 %collective-permute-start.18 = (bf16[128,1152]{1,0:T(8,128)(2,1)S(1)}, bf16[128,1152]{1,0:T(8,128)(2,1)S(1)}, u32[]{:S(2)}, u32[]{:S(2)}) collective-permute-start(bf16[128,1152]{1,0:T(8,128)(2,1)S(1)} %get-tuple-element.48), channel_id=1, source_target_pairs={{0,8},{1,33},{2,10},{3,35},{4,12},{5,37},{6,14},{7,39},{128,136},{... | collective-permute-start | bytes 884744 | tf_op jit(solution)/shard_map/rG3/ppermute | solution.py:28
  62.4 12.6 %collective-permute-start.24 = (bf16[128,1152]{1,0:T(8,128)(2,1)S(1)}, bf16[128,1152]{1,0:T(8,128)(2,1)S(1)}, u32[]{:S(2)}, u32[]{:S(2)}) collective-permute-start(bf16[128,1152]{1,0:T(8,128)(2,1)S(1)} %shard_map.76.refs_0_), channel_id=1, source_target_pairs={{0,132},{1,5},{2,134},{3,7},{4,0},{5,129},{6,2},{7,131},{128,4},{1... | collective-permute-start | bytes 884744 | tf_op jit(solution)/shard_map/rZ2/ppermute | solution.py:28
  72.6 5.2 %collective-permute-start.21 = (bf16[64,1152]{1,0:T(8,128)(2,1)S(1)}, bf16[64,1152]{1,0:T(8,128)(2,1)S(1)}, u32[]{:S(2)}, u32[]{:S(2)}) collective-permute-start(bf16[64,1152]{1,0:T(8,128)(2,1)S(1)} %get-tuple-element.52), channel_id=1, source_target_pairs={{0,96},{1,25},{2,98},{3,27},{4,100},{5,29},{6,102},{7,31},{128,224... | collective-permute-start | bytes 442376 | tf_op jit(solution)/shard_map/rA1/ppermute | solution.py:28
  72.7 6.7 %collective-permute-start.22 = (bf16[64,1152]{1,0:T(8,128)(2,1)S(1)}, bf16[64,1152]{1,0:T(8,128)(2,1)S(1)}, u32[]{:S(2)}, u32[]{:S(2)}) collective-permute-start(bf16[64,1152]{1,0:T(8,128)(2,1)S(1)} %get-tuple-element.53), channel_id=1, source_target_pairs={{0,64},{1,17},{2,66},{3,19},{4,68},{5,21},{6,70},{7,23},{128,192},... | collective-permute-start | bytes 442376 | tf_op jit(solution)/shard_map/rA2/ppermute | solution.py:28
  73.5 8.0 %collective-permute-start.23 = (bf16[64,1152]{1,0:T(8,128)(2,1)S(1)}, bf16[64,1152]{1,0:T(8,128)(2,1)S(1)}, u32[]{:S(2)}, u32[]{:S(2)}) collective-permute-start(bf16[64,1152]{1,0:T(8,128)(2,1)S(1)} %get-tuple-element.54), channel_id=1, source_target_pairs={{0,32},{1,9},{2,34},{3,11},{4,36},{5,13},{6,38},{7,15},{128,160},{... | collective-permute-start | bytes 442376 | tf_op jit(solution)/shard_map/rA3/ppermute | solution.py:28
  75.1 6.5 %collective-permute-start.25 = (bf16[64,1152]{1,0:T(8,128)(2,1)S(1)}, bf16[64,1152]{1,0:T(8,128)(2,1)S(1)}, u32[]{:S(2)}, u32[]{:S(2)}) collective-permute-start(bf16[64,1152]{1,0:T(8,128)(2,1)S(1)} %get-tuple-element.59), channel_id=1, source_target_pairs={{0,1},{1,0},{2,3},{3,2},{4,5},{5,4},{6,7},{7,6},{128,129},{129,128... | collective-permute-start | bytes 442376 | tf_op jit(solution)/shard_map/rS/ppermute | solution.py:28

commit v13 on v10

--- a/solution.py
+++ b/solution.py
@@ -223,15 +223,15 @@
     send_ref[...] = (got13_ref[rows:2 * rows, :].astype(F32) + got2_ref[rows:, :].astype(F32)).astype(BF16)
 
 
-def partial_kernel(own_ref, first_ref, second_ref, out_ref):
-    out_ref[...] = own_ref[...] + first_ref[...].astype(F32) + second_ref[...].astype(F32)
-
-
-def sums_kernel(sum_ref, last_ref, *outs):
+def partial_kernel(own_ref, first_ref, out_ref):
+    out_ref[...] = own_ref[...] + first_ref[...].astype(F32)
+
+
+def sums_kernel(sum_ref, first_ref, second_ref, *outs):
     rows = outs[0].shape[0]
     for n, out in enumerate(outs):
         at = slice(n * rows, (n + 1) * rows)
-        out[...] = (sum_ref[at, :] + last_ref[at, :].astype(F32)).astype(out.dtype)
+        out[...] = (sum_ref[at, :] + first_ref[at, :].astype(F32) + second_ref[at, :].astype(F32)).astype(out.dtype)
 
 
 def final_kernel(*refs):
@@ -286,18 +286,17 @@
 
     grad3 = image_grads(2, BF16, [send])
     back3 = shift(grad3, second(-3), "rB3")
-    grad1 = image_grads(1, BF16, [grad3])
-    back1 = shift(grad1, second(-1), "rB1")
-
     total_own, part13, part2, part4 = call(
         total_kernel,
         [((own, dim), F32), ((4 * own, dim), BF16), ((2 * own, dim), F32), ((own, dim), BF16)],
-        [keep, shift(send, other, "rC")], ties=[grad1],
-    )
-    grad2 = image_grads(3, BF16, [part13])
+        [keep, shift(send, other, "rC")], ties=[grad3],
+    )
+    grad1 = image_grads(1, BF16, [part13])
+    back1 = shift(grad1, second(-1), "rB1")
+    grad2 = image_grads(3, BF16, [grad1])
     back2 = shift(grad2, second(-2), "rB2")
     grad0 = image_grads(0, F32, [grad2])
-    (partial,) = call(partial_kernel, [((each, dim), F32)], [grad0, back3, back1])
+    (partial,) = call(partial_kernel, [((each, dim), F32)], [grad0, back3])
     got13 = shift(part13, line(-1), "rZ13")
     got4 = shift(part4, line(-2), "rZ4")
     (middle,) = call(middle_kernel, [((2 * own, dim), BF16)], [part2, got13, got4], [partial])
@@ -306,7 +305,7 @@
     txt_last = shift(txt_send, other, "rS")
 
     img_sum, *parts = call(
-        sums_kernel, [((own, dim), F32)] + [((own, dim), BF16)] * 3, [partial, back2], ties=[token(middle)]
+        sums_kernel, [((own, dim), F32)] + [((own, dim), BF16)] * 3, [partial, back1, back2], ties=[token(middle)]
     )
     last = [shift(p, first(-k), "rA%d" % k) for k, p in zip((1, 2, 3), parts)]
 

time: 79.5 us -> 84.6 us (1.064)
  waiting for transfers between devices: 28.3 us -> 35 us
  starting transfers between devices: 35.2 us -> 33.5 us
    ppermute x22, waiting for transfers between devices: 28.3 us -> 35 us  [shift(): return lax.ppermute(values, AXES, pairs)]
    ppermute x22, starting transfers between devices: 35.2 us -> 33.5 us  [shift(): return lax.ppermute(values, AXES, pairs)]
  transfers between devices with their start and end apart: 22 -> 22, of which waited for: 9 -> 9; matrix products, arithmetic and copies ran while one was open for 0% -> 0% of each run, Pallas kernels for 11% -> 10%
where the time goes in v13:
time: 84.6 us; the launch traced here: 84.4 us
  waiting for transfers between devices  35 us (41%)
  starting transfers between devices  33.5 us (40%)
  Pallas kernels  12.9 us (15%)
  between operations  2.13 us (3%)
  local copies, waits for them, and re-layouts  0.91 us (1%)
    ppermute x22, waiting for transfers between devices, shift(): return lax.ppermute(values, AXES, pairs)  35 us
    ppermute x22, starting transfers between devices, shift(): return lax.ppermute(values, AXES, pairs)  33.5 us
    pallas_call x23, Pallas kernels, call(): pl.pallas_call(lambda *refs: kernel(*refs[:n_in], *refs[n_in + len(ties):...  12.9 us
  transfers between devices with their start and end apart: 22, of which 9 were waited for; matrix products, arithmetic and copies ran while one was open for 0% of the time, Pallas kernels for 10%

profile of v13, /device:TPU:24, one launch (start us, length us, event | category | flops | bytes accessed | tf_op | source)
XLA Modules:
  0.0 84.4 jit_solution(15296580047277820034)
XLA Ops:
  0.6 0.1 collective-permute-start.3
  0.7 1.6 %collective-permute-start = (bf16[64,1152]{1,0:T(8,128)(2,1)}, bf16[64,1152]{1,0:T(8,128)(2,1)S(1)}, u32[]{:S(2)}, u32[]{:S(2)}) collective-permute-start(bf16[64,1152]{1,0:T(8,128)(2,1)} %refs_0_.3), channel_id=1, source_target_pairs={{0,32},{1,9},{2,34},{3,11},{4,36},{5,13},{6,38},{7,15},{128,160},{... | collective-permute-start | bytes 442376 | tf_op jit(solution)/shard_map/gA1/ppermute | solution.py:28
  2.3 2.7 %collective-permute-start.1 = (bf16[64,1152]{1,0:T(8,128)(2,1)}, bf16[64,1152]{1,0:T(8,128)(2,1)S(1)}, u32[]{:S(2)}, u32[]{:S(2)}) collective-permute-start(bf16[64,1152]{1,0:T(8,128)(2,1)} %refs_0_.3), channel_id=1, source_target_pairs={{0,64},{1,17},{2,66},{3,19},{4,68},{5,21},{6,70},{7,23},{128,192},... | collective-permute-start | bytes 442376 | tf_op jit(solution)/shard_map/gA2/ppermute | solution.py:28
  5.0 1.4 %collective-permute-start.2 = (bf16[64,1152]{1,0:T(8,128)(2,1)}, bf16[64,1152]{1,0:T(8,128)(2,1)S(1)}, u32[]{:S(2)}, u32[]{:S(2)}) collective-permute-start(bf16[64,1152]{1,0:T(8,128)(2,1)} %refs_0_.3), channel_id=1, source_target_pairs={{0,96},{1,25},{2,98},{3,27},{4,100},{5,29},{6,102},{7,31},{128,224... | collective-permute-start | bytes 442376 | tf_op jit(solution)/shard_map/gA3/ppermute | solution.py:28
  7.8 0.0 collective-permute-done.3.refs_1_
  7.8 0.9 %copy-done.1 = bf16[64,1152]{1,0:T(8,128)(2,1)S(1)} copy-done((bf16[64,1152]{1,0:T(8,128)(2,1)S(1)}, bf16[64,1152]{1,0:T(8,128)(2,1)}, u32[]{:S(2)}) %copy-start.1) | copy-done | bytes 147480
  8.7 0.2 shard_map.59.refs_0_
  8.9 0.0 copy-start
  8.9 3.3 %collective-permute-start.4 = (bf16[128,1152]{1,0:T(8,128)(2,1)S(1)}, bf16[128,1152]{1,0:T(8,128)(2,1)S(1)}, u32[]{:S(2)}, u32[]{:S(2)}) collective-permute-start(bf16[128,1152]{1,0:T(8,128)(2,1)S(1)} %shard_map.59.refs_0_), channel_id=1, source_target_pairs={{0,4},{1,133},{2,6},{3,135},{4,128},{5,1},{6,130},{7,3},{128,132},... | collective-permute-start | bytes 884744 | tf_op jit(solution)/shard_map/gZ2/ppermute | solution.py:28
  12.2 0.0 collective-permute-done.refs_1_
  12.2 0.0 collective-permute-done.1.refs_2_
  12.2 0.0 collective-permute-done.2.refs_3_
  12.3 0.2 shard_map.61.refs_2_.refs_0_
  12.5 0.3 collective-permute-start.7
  12.8 1.8 %collective-permute-start.8 = (bf16[256,1152]{1,0:T(8,128)(2,1)S(1)}, bf16[256,1152]{1,0:T(8,128)(2,1)S(1)}, u32[]{:S(2)}, u32[]{:S(2)}) collective-permute-start(bf16[256,1152]{1,0:T(8,128)(2,1)S(1)} %shard_map.61.refs_2_.refs_0_), channel_id=1, source_target_pairs={{0,24},{1,97},{2,26},{3,99},{4,28},{5,101},{6,30},{7,103},{128,152... | collective-permute-start | bytes 1769480 | tf_op jit(solution)/shard_map/gB3/ppermute | solution.py:28
  14.6 1.2 %collective-permute-start.9 = (bf16[256,1152]{1,0:T(8,128)(2,1)S(1)}, bf16[256,1152]{1,0:T(8,128)(2,1)S(1)}, u32[]{:S(2)}, u32[]{:S(2)}) collective-permute-start(bf16[256,1152]{1,0:T(8,128)(2,1)S(1)} %shard_map.61.refs_2_.refs_0_), channel_id=1, source_target_pairs={{0,16},{1,65},{2,18},{3,67},{4,20},{5,69},{6,22},{7,71},{128,144},... | collective-permute-start | bytes 1769480 | tf_op jit(solution)/shard_map/gB2/ppermute | solution.py:28
  15.8 4.7 %collective-permute-done.4.refs_1_ = bf16[128,1152]{1,0:T(8,128)(2,1)S(1)} collective-permute-done((bf16[128,1152]{1,0:T(8,128)(2,1)S(1)}, bf16[128,1152]{1,0:T(8,128)(2,1)S(1)}, u32[]{:S(2)}, u32[]{:S(2)}) %collective-permute-start.4) | collective-permute-done | bytes 294944 | tf_op jit(solution)/shard_map/gZ2/ppermute | solution.py:28
  20.6 0.1 shard_map.62
  20.6 3.7 %collective-permute-start.5 = (bf16[256,1152]{1,0:T(8,128)(2,1)S(1)}, bf16[256,1152]{1,0:T(8,128)(2,1)S(1)}, u32[]{:S(2)}, u32[]{:S(2)}) collective-permute-start(bf16[256,1152]{1,0:T(8,128)(2,1)S(1)} %get-tuple-element.25.refs_0_.refs_1_), channel_id=1, source_target_pairs={{0,2},{1,135},{2,4},{3,1},{4,6},{5,3},{6,128},{7,5},{128,130},{129... | collective-permute-start | bytes 1769480 | tf_op jit(solution)/shard_map/gZ13/ppermute | solution.py:28
  24.3 0.5 collective-permute-start.6
  24.8 8.5 %collective-permute-done.5.refs_2_.refs_1_ = bf16[256,1152]{1,0:T(8,128)(2,1)S(1)} collective-permute-done((bf16[256,1152]{1,0:T(8,128)(2,1)S(1)}, bf16[256,1152]{1,0:T(8,128)(2,1)S(1)}, u32[]{:S(2)}, u32[]{:S(2)}) %collective-permute-start.5) | collective-permute-done | bytes 589856 | tf_op jit(solution)/shard_map/gZ13/ppermute | solution.py:28
  33.3 0.1 shard_map.63.refs_1_
  33.4 0.2 shard_map.64
  33.6 0.2 shard_map.65
  33.8 3.2 %collective-permute-done.6.refs_2_ = bf16[64,1152]{1,0:T(8,128)(2,1)S(1)} collective-permute-done((bf16[64,1152]{1,0:T(8,128)(2,1)S(1)}, bf16[64,1152]{1,0:T(8,128)(2,1)S(1)}, u32[]{:S(2)}, u32[]{:S(2)}) %collective-permute-start.6) | collective-permute-done | bytes 147488 | tf_op jit(solution)/shard_map/gZ4/ppermute | solution.py:28
  36.9 0.0 collective-permute-done.7.refs_5_.refs_3_
  36.9 0.0 collective-permute-done.8.refs_6_.refs_4_
  36.9 0.0 collective-permute-done.9.refs_7_.refs_5_
  36.9 0.3 shard_map.68.refs_0_.refs_2_
  37.2 0.3 collective-permute-start.10
  37.5 3.4 %shard_map.69 = (bf16[1024,512]{1,0:T(8,128)(2,1)S(1)}, bf16[1024,1152]{1,0:T(8,128)(2,1)S(1)}, bf16[512,1152]{1,0:T(8,128)(2,1)S(1)}) custom-call(bf16[512,1152]{1,0:T(8,128)(2,1)S(1)} %shard_map.68.refs_0_.refs_2_, f32[8,128]{1,0:T(8,128)S(1)} %shard_map.63.refs_1_, bf16[256,1152]{1,0:T(8,128)(2,1)S(1)} %get-tuple-element.30.refs_3_.refs_2_, ...), custom_call_target="tpu_custom_call" | custom-call | flops 2415919104 | bytes 1024 | tf_op jit(solution)/shard_map/pallas_call | solution.py:51
  40.9 0.0 collective-permute-done.10.refs_0_.refs_3_
  41.0 3.0 %shard_map.70 = (bf16[1024,512]{1,0:T(8,128)(2,1)S(1)}, bf16[512,1152]{1,0:T(8,128)(2,1)S(1)}) custom-call(bf16[512,1152]{1,0:T(8,128)(2,1)S(1)} %collective-permute-done.10.refs_0_.refs_3_, f32[8,128]{1,0:T(8,128)S(1)} %shard_map.63.refs_1_, bf16[1024,1152]{1,0:T(8,128)(2,1)S(1)} %get-tuple-element.32.refs_2_, ...), custom_call_target="tpu_custom_call" | custom-call | flops 2415919104 | bytes 1024 | tf_op jit(solution)/shard_map/pallas_call | solution.py:51
  44.0 0.6 collective-permute-start.11
  44.6 0.8 shard_map.71.refs_2_
  45.4 0.3 collective-permute-start.12
  45.7 1.3 %collective-permute-done.11.refs_1_ = bf16[512,1152]{1,0:T(8,128)(2,1)S(1)} collective-permute-done((bf16[512,1152]{1,0:T(8,128)(2,1)S(1)}, bf16[512,1152]{1,0:T(8,128)(2,1)S(1)}, u32[]{:S(2)}, u32[]{:S(2)}) %collective-permute-start.11) | collective-permute-done | bytes 1179680 | tf_op jit(solution)/shard_map/rC/ppermute | solution.py:28
  47.0 0.3 shard_map.72
  47.3 2.4 %collective-permute-start.15 = (bf16[256,1152]{1,0:T(8,128)(2,1)S(1)}, bf16[256,1152]{1,0:T(8,128)(2,1)S(1)}, u32[]{:S(2)}, u32[]{:S(2)}) collective-permute-start(bf16[256,1152]{1,0:T(8,128)(2,1)S(1)} %get-tuple-element.36.refs_4_), channel_id=1, source_target_pairs={{0,134},{1,3},{2,0},{3,5},{4,2},{5,7},{6,4},{7,129},{128,6},{129,1... | collective-permute-start | bytes 1769480 | tf_op jit(solution)/shard_map/rZ13/ppermute | solution.py:28
  49.7 3.7 %collective-permute-start.16 = (bf16[64,1152]{1,0:T(8,128)(2,1)S(1)}, bf16[64,1152]{1,0:T(8,128)(2,1)S(1)}, u32[]{:S(2)}, u32[]{:S(2)}) collective-permute-start(bf16[64,1152]{1,0:T(8,128)(2,1)S(1)} %get-tuple-element.38), channel_id=1, source_target_pairs={{0,132},{1,5},{2,134},{3,7},{4,0},{5,129},{6,2},{7,131},{128,4},{1... | collective-permute-start | bytes 442376 | tf_op jit(solution)/shard_map/rZ4/ppermute | solution.py:28
  53.5 0.8 shard_map.73.refs_4_
  54.3 0.8 collective-permute-start.13
  55.1 0.8 shard_map.74.refs_4_
  56.0 1.1 %collective-permute-start.14 = (bf16[256,1152]{1,0:T(8,128)(2,1)S(1)}, bf16[256,1152]{1,0:T(8,128)(2,1)S(1)}, u32[]{:S(2)}, u32[]{:S(2)}) collective-permute-start(bf16[256,1152]{1,0:T(8,128)(2,1)S(1)} %shard_map.74.refs_4_), channel_id=1, source_target_pairs={{0,16},{1,65},{2,18},{3,67},{4,20},{5,69},{6,22},{7,71},{128,144},... | collective-permute-start | bytes 1769480 | tf_op jit(solution)/shard_map/rB2/ppermute | solution.py:28
  57.0 0.8 shard_map.75.refs_0_
  57.9 0.0 collective-permute-done.12.refs_1_
  57.9 0.1 shard_map.76.refs_3_.refs_0_
  58.0 2.3 %collective-permute-done.16.refs_2_ = bf16[64,1152]{1,0:T(8,128)(2,1)S(1)} collective-permute-done((bf16[64,1152]{1,0:T(8,128)(2,1)S(1)}, bf16[64,1152]{1,0:T(8,128)(2,1)S(1)}, u32[]{:S(2)}, u32[]{:S(2)}) %collective-permute-start.16) | collective-permute-done | bytes 147488 | tf_op jit(solution)/shard_map/rZ4/ppermute | solution.py:28
  60.4 0.0 collective-permute-done.15.refs_1_
  60.4 0.1 shard_map.77.refs_0_
  60.5 4.8 %collective-permute-start.20 = (bf16[128,1152]{1,0:T(8,128)(2,1)S(1)}, bf16[128,1152]{1,0:T(8,128)(2,1)S(1)}, u32[]{:S(2)}, u32[]{:S(2)}) collective-permute-start(bf16[128,1152]{1,0:T(8,128)(2,1)S(1)} %shard_map.77.refs_0_), channel_id=1, source_target_pairs={{0,132},{1,5},{2,134},{3,7},{4,0},{5,129},{6,2},{7,131},{128,4},{1... | collective-permute-start | bytes 884744 | tf_op jit(solution)/shard_map/rZ2/ppermute | solution.py:28
  65.3 8.8 %collective-permute-done.13.refs_1_ = bf16[256,1152]{1,0:T(8,128)(2,1)S(1)} collective-permute-done((bf16[256,1152]{1,0:T(8,128)(2,1)S(1)}, bf16[256,1152]{1,0:T(8,128)(2,1)S(1)}, u32[]{:S(2)}, u32[]{:S(2)}) %collective-permute-start.13) | collective-permute-done | bytes 589856 | tf_op jit(solution)/shard_map/rB1/ppermute | solution.py:28
  74.0 0.0 collective-permute-done.14.refs_2_
  74.0 0.2 shard_map.79
  74.3 0.1 collective-permute-start.17
  74.3 2.6 %collective-permute-start.18 = (bf16[64,1152]{1,0:T(8,128)(2,1)S(1)}, bf16[64,1152]{1,0:T(8,128)(2,1)S(1)}, u32[]{:S(2)}, u32[]{:S(2)}) collective-permute-start(bf16[64,1152]{1,0:T(8,128)(2,1)S(1)} %get-tuple-element.41), channel_id=1, source_target_pairs={{0,64},{1,17},{2,66},{3,19},{4,68},{5,21},{6,70},{7,23},{128,192},... | collective-permute-start | bytes 442376 | tf_op jit(solution)/shard_map/rA2/ppermute | solution.py:28
  77.0 0.0 collective-permute-start.19
  77.0 0.1 shard_map.80
  77.1 0.1 collective-permute-start.21
  77.2 2.3 %collective-permute-done.17.refs_3_ = bf16[64,1152]{1,0:T(8,128)(2,1)S(1)} collective-permute-done((bf16[64,1152]{1,0:T(8,128)(2,1)S(1)}, bf16[64,1152]{1,0:T(8,128)(2,1)S(1)}, u32[]{:S(2)}, u32[]{:S(2)}) %collective-permute-start.17) | collective-permute-done | bytes 147488 | tf_op jit(solution)/shard_map/rA1/ppermute | solution.py:28
  79.5 1.6 %collective-permute-done.18.refs_4_ = bf16[64,1152]{1,0:T(8,128)(2,1)S(1)} collective-permute-done((bf16[64,1152]{1,0:T(8,128)(2,1)S(1)}, bf16[64,1152]{1,0:T(8,128)(2,1)S(1)}, u32[]{:S(2)}, u32[]{:S(2)}) %collective-permute-start.18) | collective-permute-done | bytes 147488 | tf_op jit(solution)/shard_map/rA2/ppermute | solution.py:28
  81.1 2.2 %collective-permute-done.19.refs_5_ = bf16[64,1152]{1,0:T(8,128)(2,1)S(1)} collective-permute-done((bf16[64,1152]{1,0:T(8,128)(2,1)S(1)}, bf16[64,1152]{1,0:T(8,128)(2,1)S(1)}, u32[]{:S(2)}, u32[]{:S(2)}) %collective-permute-start.19) | collective-permute-done | bytes 147488 | tf_op jit(solution)/shard_map/rA3/ppermute | solution.py:28
  83.3 0.0 collective-permute-done.21.refs_9_
  83.3 1.1 %shard_map.81 = (f32[64,1152]{1,0:T(8,128)}, f32[64,1152]{1,0:T(8,128)}) custom-call(f32[64,1152]{1,0:T(8,128)S(1)} %get-tuple-element.26.refs_0_, f32[64,128]{1,0:T(8,128)S(1)} %get-tuple-element.27.refs_1_, f32[64,1152]{1,0:T(8,128)S(1)} %get-tuple-element.39.refs_2_, bf16[64,1152]{1,0:T(8,128)(2,1)S(1)} %collective-permute-done.17.refs_3_, ...), custom_call_target="tpu_custom_call" | custom-call | bytes 1024 | tf_op jit(solution)/shard_map/pallas_call | solution.py:51
  (7 shorter events, 0.0 us)
Async XLA Ops:
  0.6 7.1 %collective-permute-start.3 = (bf16[64,1152]{1,0:T(8,128)(2,1)}, bf16[64,1152]{1,0:T(8,128)(2,1)S(1)}, u32[]{:S(2)}, u32[]{:S(2)}) collective-permute-start(bf16[64,1152]{1,0:T(8,128)(2,1)} %refs_0_.2), channel_id=1, source_target_pairs={{0,1},{1,0},{2,3},{3,2},{4,5},{5,4},{6,7},{7,6},{128,129},{129,128... | collective-permute-start | bytes 442376 | tf_op jit(solution)/shard_map/gC/ppermute | solution.py:28
  0.7 11.5 %collective-permute-start = (bf16[64,1152]{1,0:T(8,128)(2,1)}, bf16[64,1152]{1,0:T(8,128)(2,1)S(1)}, u32[]{:S(2)}, u32[]{:S(2)}) collective-permute-start(bf16[64,1152]{1,0:T(8,128)(2,1)} %refs_0_.3), channel_id=1, source_target_pairs={{0,32},{1,9},{2,34},{3,11},{4,36},{5,13},{6,38},{7,15},{128,160},{... | collective-permute-start | bytes 442376 | tf_op jit(solution)/shard_map/gA1/ppermute | solution.py:28
  2.3 9.9 %collective-permute-start.1 = (bf16[64,1152]{1,0:T(8,128)(2,1)}, bf16[64,1152]{1,0:T(8,128)(2,1)S(1)}, u32[]{:S(2)}, u32[]{:S(2)}) collective-permute-start(bf16[64,1152]{1,0:T(8,128)(2,1)} %refs_0_.3), channel_id=1, source_target_pairs={{0,64},{1,17},{2,66},{3,19},{4,68},{5,21},{6,70},{7,23},{128,192},... | collective-permute-start | bytes 442376 | tf_op jit(solution)/shard_map/gA2/ppermute | solution.py:28
  5.0 7.2 %collective-permute-start.2 = (bf16[64,1152]{1,0:T(8,128)(2,1)}, bf16[64,1152]{1,0:T(8,128)(2,1)S(1)}, u32[]{:S(2)}, u32[]{:S(2)}) collective-permute-start(bf16[64,1152]{1,0:T(8,128)(2,1)} %refs_0_.3), channel_id=1, source_target_pairs={{0,96},{1,25},{2,98},{3,27},{4,100},{5,29},{6,102},{7,31},{128,224... | collective-permute-start | bytes 442376 | tf_op jit(solution)/shard_map/gA3/ppermute | solution.py:28
  7.8 0.9 %copy-start.1 = (bf16[64,1152]{1,0:T(8,128)(2,1)S(1)}, bf16[64,1152]{1,0:T(8,128)(2,1)}, u32[]{:S(2)}) copy-start(bf16[64,1152]{1,0:T(8,128)(2,1)} %refs_0_.2) | copy-start | bytes 442372
  8.9 3.4 %copy-start = (bf16[64,1152]{1,0:T(8,128)(2,1)S(1)}, bf16[64,1152]{1,0:T(8,128)(2,1)}, u32[]{:S(2)}) copy-start(bf16[64,1152]{1,0:T(8,128)(2,1)} %refs_0_.3) | copy-start | bytes 442372
  8.9 11.7 %collective-permute-start.4 = (bf16[128,1152]{1,0:T(8,128)(2,1)S(1)}, bf16[128,1152]{1,0:T(8,128)(2,1)S(1)}, u32[]{:S(2)}, u32[]{:S(2)}) collective-permute-start(bf16[128,1152]{1,0:T(8,128)(2,1)S(1)} %shard_map.59.refs_0_), channel_id=1, source_target_pairs={{0,4},{1,133},{2,6},{3,135},{4,128},{5,1},{6,130},{7,3},{128,132},... | collective-permute-start | bytes 884744 | tf_op jit(solution)/shard_map/gZ2/ppermute | solution.py:28
  12.5 24.4 %collective-permute-start.7 = (bf16[256,1152]{1,0:T(8,128)(2,1)S(1)}, bf16[256,1152]{1,0:T(8,128)(2,1)S(1)}, u32[]{:S(2)}, u32[]{:S(2)}) collective-permute-start(bf16[256,1152]{1,0:T(8,128)(2,1)S(1)} %shard_map.61.refs_2_.refs_0_), channel_id=1, source_target_pairs={{0,8},{1,33},{2,10},{3,35},{4,12},{5,37},{6,14},{7,39},{128,136},{... | collective-permute-start | bytes 1769480 | tf_op jit(solution)/shard_map/gB1/ppermute | solution.py:28
  12.8 24.1 %collective-permute-start.8 = (bf16[256,1152]{1,0:T(8,128)(2,1)S(1)}, bf16[256,1152]{1,0:T(8,128)(2,1)S(1)}, u32[]{:S(2)}, u32[]{:S(2)}) collective-permute-start(bf16[256,1152]{1,0:T(8,128)(2,1)S(1)} %shard_map.61.refs_2_.refs_0_), channel_id=1, source_target_pairs={{0,24},{1,97},{2,26},{3,99},{4,28},{5,101},{6,30},{7,103},{128,152... | collective-permute-start | bytes 1769480 | tf_op jit(solution)/shard_map/gB3/ppermute | solution.py:28
  14.6 22.3 %collective-permute-start.9 = (bf16[256,1152]{1,0:T(8,128)(2,1)S(1)}, bf16[256,1152]{1,0:T(8,128)(2,1)S(1)}, u32[]{:S(2)}, u32[]{:S(2)}) collective-permute-start(bf16[256,1152]{1,0:T(8,128)(2,1)S(1)} %shard_map.61.refs_2_.refs_0_), channel_id=1, source_target_pairs={{0,16},{1,65},{2,18},{3,67},{4,20},{5,69},{6,22},{7,71},{128,144},... | collective-permute-start | bytes 1769480 | tf_op jit(solution)/shard_map/gB2/ppermute | solution.py:28
  20.6 12.7 %collective-permute-start.5 = (bf16[256,1152]{1,0:T(8,128)(2,1)S(1)}, bf16[256,1152]{1,0:T(8,128)(2,1)S(1)}, u32[]{:S(2)}, u32[]{:S(2)}) collective-permute-start(bf16[256,1152]{1,0:T(8,128)(2,1)S(1)} %get-tuple-element.25.refs_0_.refs_1_), channel_id=1, source_target_pairs={{0,2},{1,135},{2,4},{3,1},{4,6},{5,3},{6,128},{7,5},{128,130},{129... | collective-permute-start | bytes 1769480 | tf_op jit(solution)/shard_map/gZ13/ppermute | solution.py:28
  24.3 12.6 %collective-permute-start.6 = (bf16[64,1152]{1,0:T(8,128)(2,1)S(1)}, bf16[64,1152]{1,0:T(8,128)(2,1)S(1)}, u32[]{:S(2)}, u32[]{:S(2)}) collective-permute-start(bf16[64,1152]{1,0:T(8,128)(2,1)S(1)} %shard_map.66), channel_id=1, source_target_pairs={{0,4},{1,133},{2,6},{3,135},{4,128},{5,1},{6,130},{7,3},{128,132},... | collective-permute-start | bytes 442376 | tf_op jit(solution)/shard_map/gZ4/ppermute | solution.py:28
  37.2 3.7 %collective-permute-start.10 = (bf16[512,1152]{1,0:T(8,128)(2,1)S(1)}, bf16[512,1152]{1,0:T(8,128)(2,1)S(1)}, u32[]{:S(2)}, u32[]{:S(2)}) collective-permute-start(bf16[512,1152]{1,0:T(8,128)(2,1)S(1)} %shard_map.68.refs_0_.refs_2_), channel_id=1, source_target_pairs={{0,1},{1,0},{2,3},{3,2},{4,5},{5,4},{6,7},{7,6},{128,129},{129,128... | collective-permute-start | bytes 3538952 | tf_op jit(solution)/shard_map/gS/ppermute | solution.py:28
  44.0 3.1 %collective-permute-start.11 = (bf16[512,1152]{1,0:T(8,128)(2,1)S(1)}, bf16[512,1152]{1,0:T(8,128)(2,1)S(1)}, u32[]{:S(2)}, u32[]{:S(2)}) collective-permute-start(bf16[512,1152]{1,0:T(8,128)(2,1)S(1)} %get-tuple-element.35.refs_4_), channel_id=1, source_target_pairs={{0,1},{1,0},{2,3},{3,2},{4,5},{5,4},{6,7},{7,6},{128,129},{129,128... | collective-permute-start | bytes 3538952 | tf_op jit(solution)/shard_map/rC/ppermute | solution.py:28
  45.4 12.5 %collective-permute-start.12 = (bf16[256,1152]{1,0:T(8,128)(2,1)S(1)}, bf16[256,1152]{1,0:T(8,128)(2,1)S(1)}, u32[]{:S(2)}, u32[]{:S(2)}) collective-permute-start(bf16[256,1152]{1,0:T(8,128)(2,1)S(1)} %shard_map.71.refs_2_), channel_id=1, source_target_pairs={{0,8},{1,33},{2,10},{3,35},{4,12},{5,37},{6,14},{7,39},{128,136},{... | collective-permute-start | bytes 1769480 | tf_op jit(solution)/shard_map/rB3/ppermute | solution.py:28
  47.3 13.1 %collective-permute-start.15 = (bf16[256,1152]{1,0:T(8,128)(2,1)S(1)}, bf16[256,1152]{1,0:T(8,128)(2,1)S(1)}, u32[]{:S(2)}, u32[]{:S(2)}) collective-permute-start(bf16[256,1152]{1,0:T(8,128)(2,1)S(1)} %get-tuple-element.36.refs_4_), channel_id=1, source_target_pairs={{0,134},{1,3},{2,0},{3,5},{4,2},{5,7},{6,4},{7,129},{128,6},{129,1... | collective-permute-start | bytes 1769480 | tf_op jit(solution)/shard_map/rZ13/ppermute | solution.py:28
  49.7 10.6 %collective-permute-start.16 = (bf16[64,1152]{1,0:T(8,128)(2,1)S(1)}, bf16[64,1152]{1,0:T(8,128)(2,1)S(1)}, u32[]{:S(2)}, u32[]{:S(2)}) collective-permute-start(bf16[64,1152]{1,0:T(8,128)(2,1)S(1)} %get-tuple-element.38), channel_id=1, source_target_pairs={{0,132},{1,5},{2,134},{3,7},{4,0},{5,129},{6,2},{7,131},{128,4},{1... | collective-permute-start | bytes 442376 | tf_op jit(solution)/shard_map/rZ4/ppermute | solution.py:28
  54.3 19.7 %collective-permute-start.13 = (bf16[256,1152]{1,0:T(8,128)(2,1)S(1)}, bf16[256,1152]{1,0:T(8,128)(2,1)S(1)}, u32[]{:S(2)}, u32[]{:S(2)}) collective-permute-start(bf16[256,1152]{1,0:T(8,128)(2,1)S(1)} %shard_map.73.refs_4_), channel_id=1, source_target_pairs={{0,24},{1,97},{2,26},{3,99},{4,28},{5,101},{6,30},{7,103},{128,152... | collective-permute-start | bytes 1769480 | tf_op jit(solution)/shard_map/rB1/ppermute | solution.py:28
  56.0 18.1 %collective-permute-start.14 = (bf16[256,1152]{1,0:T(8,128)(2,1)S(1)}, bf16[256,1152]{1,0:T(8,128)(2,1)S(1)}, u32[]{:S(2)}, u32[]{:S(2)}) collective-permute-start(bf16[256,1152]{1,0:T(8,128)(2,1)S(1)} %shard_map.74.refs_4_), channel_id=1, source_target_pairs={{0,16},{1,65},{2,18},{3,67},{4,20},{5,69},{6,22},{7,71},{128,144},... | collective-permute-start | bytes 1769480 | tf_op jit(solution)/shard_map/rB2/ppermute | solution.py:28
  60.5 16.5 %collective-permute-start.20 = (bf16[128,1152]{1,0:T(8,128)(2,1)S(1)}, bf16[128,1152]{1,0:T(8,128)(2,1)S(1)}, u32[]{:S(2)}, u32[]{:S(2)}) collective-permute-start(bf16[128,1152]{1,0:T(8,128)(2,1)S(1)} %shard_map.77.refs_0_), channel_id=1, source_target_pairs={{0,132},{1,5},{2,134},{3,7},{4,0},{5,129},{6,2},{7,131},{128,4},{1... | collective-permute-start | bytes 884744 | tf_op jit(solution)/shard_map/rZ2/ppermute | solution.py:28
  74.3 5.2 %collective-permute-start.17 = (bf16[64,1152]{1,0:T(8,128)(2,1)S(1)}, bf16[64,1152]{1,0:T(8,128)(2,1)S(1)}, u32[]{:S(2)}, u32[]{:S(2)}) collective-permute-start(bf16[64,1152]{1,0:T(8,128)(2,1)S(1)} %get-tuple-element.40), channel_id=1, source_target_pairs={{0,96},{1,25},{2,98},{3,27},{4,100},{5,29},{6,102},{7,31},{128,224... | collective-permute-start | bytes 442376 | tf_op jit(solution)/shard_map/rA1/ppermute | solution.py:28
  74.3 6.7 %collective-permute-start.18 = (bf16[64,1152]{1,0:T(8,128)(2,1)S(1)}, bf16[64,1152]{1,0:T(8,128)(2,1)S(1)}, u32[]{:S(2)}, u32[]{:S(2)}) collective-permute-start(bf16[64,1152]{1,0:T(8,128)(2,1)S(1)} %get-tuple-element.41), channel_id=1, source_target_pairs={{0,64},{1,17},{2,66},{3,19},{4,68},{5,21},{6,70},{7,23},{128,192},... | collective-permute-start | bytes 442376 | tf_op jit(solution)/shard_map/rA2/ppermute | solution.py:28
  77.0 6.4 %collective-permute-start.19 = (bf16[64,1152]{1,0:T(8,128)(2,1)S(1)}, bf16[64,1152]{1,0:T(8,128)(2,1)S(1)}, u32[]{:S(2)}, u32[]{:S(2)}) collective-permute-start(bf16[64,1152]{1,0:T(8,128)(2,1)S(1)} %get-tuple-element.42), channel_id=1, source_target_pairs={{0,32},{1,9},{2,34},{3,11},{4,36},{5,13},{6,38},{7,15},{128,160},{... | collective-permute-start | bytes 442376 | tf_op jit(solution)/shard_map/rA3/ppermute | solution.py:28
  77.1 6.3 %collective-permute-start.21 = (bf16[64,1152]{1,0:T(8,128)(2,1)S(1)}, bf16[64,1152]{1,0:T(8,128)(2,1)S(1)}, u32[]{:S(2)}, u32[]{:S(2)}) collective-permute-start(bf16[64,1152]{1,0:T(8,128)(2,1)S(1)} %get-tuple-element.47), channel_id=1, source_target_pairs={{0,1},{1,0},{2,3},{3,2},{4,5},{5,4},{6,7},{7,6},{128,129},{129,128... | collective-permute-start | bytes 442376 | tf_op jit(solution)/shard_map/rS/ppermute | solution.py:28

commit v14 on v11

--- a/solution.py
+++ b/solution.py
@@ -216,15 +216,15 @@
     send_ref[...] = (got13_ref[rows:2 * rows, :].astype(F32) + got2_ref[rows:, :].astype(F32)).astype(BF16)
 
 
-def partial_kernel(own_ref, first_ref, out_ref):
-    out_ref[...] = own_ref[...] + first_ref[...].astype(F32)
-
-
-def sums_kernel(sum_ref, first_ref, second_ref, *outs):
+def partial_kernel(own_ref, first_ref, second_ref, out_ref):
+    out_ref[...] = own_ref[...] + first_ref[...].astype(F32) + second_ref[...].astype(F32)
+
+
+def sums_kernel(sum_ref, last_ref, *outs):
     rows = outs[0].shape[0]
     for n, out in enumerate(outs):
         at = slice(n * rows, (n + 1) * rows)
-        out[...] = (sum_ref[at, :] + first_ref[at, :].astype(F32) + second_ref[at, :].astype(F32)).astype(out.dtype)
+        out[...] = (sum_ref[at, :] + last_ref[at, :].astype(F32)).astype(out.dtype)
 
 
 def final_kernel(*refs):
@@ -279,26 +279,27 @@
 
     grad3 = image_grads(2, BF16, [send])
     back3 = shift(grad3, second(-3), "rB3")
+    grad1 = image_grads(1, BF16, [grad3])
+    back1 = shift(grad1, second(-1), "rB1")
+
     total_own, part13, part2, part4 = call(
         total_kernel,
         [((own, dim), F32), ((4 * own, dim), BF16), ((2 * own, dim), F32), ((own, dim), BF16)],
-        [keep, shift(send, other, "rC")], ties=[grad3],
-    )
-    grad1 = image_grads(1, BF16, [part13])
-    back1 = shift(grad1, second(-1), "rB1")
-    grad2 = image_grads(3, BF16, [grad1])
+        [keep, shift(send, other, "rC")], ties=[grad1],
+    )
+    grad2 = image_grads(3, BF16, [part13])
     back2 = shift(grad2, second(-2), "rB2")
     grad0 = image_grads(0, F32, [grad2])
-    (partial,) = call(partial_kernel, [((each, dim), F32)], [grad0, back3])
+    (partial,) = call(partial_kernel, [((each, dim), F32)], [grad0, back3, back1])
     got13 = shift(part13, line(-1), "rZ13")
     got4 = shift(part4, line(-2), "rZ4")
-    (middle,) = call(middle_kernel, [((2 * own, dim), BF16)], [part2, got13, got4], [partial])
+    (middle,) = call(middle_kernel, [((2 * own, dim), BF16)], [part2, got13, got4], [token(got13, partial)])
     got2 = shift(middle, line(-2), "rZ2")
     txt_sum, txt_send = call(landed_kernel, [((own, dim), F32), ((own, dim), BF16)], [total_own, got13, got2])
     txt_last = shift(txt_send, other, "rS")
 
     img_sum, *parts = call(
-        sums_kernel, [((own, dim), F32)] + [((own, dim), BF16)] * 3, [partial, back1, back2], ties=[token(middle)]
+        sums_kernel, [((own, dim), F32)] + [((own, dim), BF16)] * 3, [partial, back2], ties=[token(middle)]
     )
     last = [shift(p, first(-k), "rA%d" % k) for k, p in zip((1, 2, 3), parts)]
 

time: 82.1 us -> 76.9 us (0.937)
  waiting for transfers between devices: 32.6 us -> 26.9 us
    ppermute x23, waiting for transfers between devices: 32.6 us -> 26.9 us  [shift(): return lax.ppermute(values, AXES, pairs)]
    pallas_call x21 -> x22, Pallas kernels: 12.9 us -> 12.9 us  [call(): pl.pallas_call(lambda *refs: kernel(*refs[:n_in], *refs[n_in + len(ties):...]
  transfers between devices with their start and end apart: 23 -> 23, of which waited for: 9 -> 7; matrix products, arithmetic and copies ran while one was open for 0% -> 0% of each run, Pallas kernels for 10% -> 11%
where the time goes in v14:
time: 76.9 us; the launch traced here: 76.7 us
  starting transfers between devices  34.8 us (45%)
  waiting for transfers between devices  26.9 us (35%)
  Pallas kernels  12.9 us (17%)
  between operations  2.16 us (3%)
    ppermute x23, starting transfers between devices, shift(): return lax.ppermute(values, AXES, pairs)  34.8 us
    ppermute x23, waiting for transfers between devices, shift(): return lax.ppermute(values, AXES, pairs)  26.9 us
    pallas_call x22, Pallas kernels, call(): pl.pallas_call(lambda *refs: kernel(*refs[:n_in], *refs[n_in + len(ties):...  12.9 us
  transfers between devices with their start and end apart: 23, of which 7 were waited for; matrix products, arithmetic and copies ran while one was open for 0% of the time, Pallas kernels for 11%

profile of v14, /device:TPU:24, one launch (start us, length us, event | category | flops | bytes accessed | tf_op | source)
XLA Modules:
  0.0 76.7 jit_solution(4846250275088350754)
XLA Ops:
  0.6 0.1 collective-permute-start.3
  0.7 1.6 %collective-permute-start = (bf16[64,1152]{1,0:T(8,128)(2,1)}, bf16[64,1152]{1,0:T(8,128)(2,1)S(1)}, u32[]{:S(2)}, u32[]{:S(2)}) collective-permute-start(bf16[64,1152]{1,0:T(8,128)(2,1)} %refs_0_.2), channel_id=1, source_target_pairs={{0,32},{1,9},{2,34},{3,11},{4,36},{5,13},{6,38},{7,15},{128,160},{... | collective-permute-start | bytes 442376 | tf_op jit(solution)/shard_map/gA1/ppermute | solution.py:28
  2.3 2.7 %collective-permute-start.1 = (bf16[64,1152]{1,0:T(8,128)(2,1)}, bf16[64,1152]{1,0:T(8,128)(2,1)S(1)}, u32[]{:S(2)}, u32[]{:S(2)}) collective-permute-start(bf16[64,1152]{1,0:T(8,128)(2,1)} %refs_0_.2), channel_id=1, source_target_pairs={{0,64},{1,17},{2,66},{3,19},{4,68},{5,21},{6,70},{7,23},{128,192},... | collective-permute-start | bytes 442376 | tf_op jit(solution)/shard_map/gA2/ppermute | solution.py:28
  5.0 1.4 %collective-permute-start.2 = (bf16[64,1152]{1,0:T(8,128)(2,1)}, bf16[64,1152]{1,0:T(8,128)(2,1)S(1)}, u32[]{:S(2)}, u32[]{:S(2)}) collective-permute-start(bf16[64,1152]{1,0:T(8,128)(2,1)} %refs_0_.2), channel_id=1, source_target_pairs={{0,96},{1,25},{2,98},{3,27},{4,100},{5,29},{6,102},{7,31},{128,224... | collective-permute-start | bytes 442376 | tf_op jit(solution)/shard_map/gA3/ppermute | solution.py:28
  6.5 3.3 %collective-permute-start.4 = (bf16[64,1152]{1,0:T(8,128)(2,1)}, bf16[64,1152]{1,0:T(8,128)(2,1)S(1)}, u32[]{:S(2)}, u32[]{:S(2)}) collective-permute-start(bf16[64,1152]{1,0:T(8,128)(2,1)} %refs_0_.3), channel_id=1, source_target_pairs={{0,4},{1,133},{2,6},{3,135},{4,128},{5,1},{6,130},{7,3},{128,132},... | collective-permute-start | bytes 442376 | tf_op jit(solution)/shard_map/gZ2/ppermute | solution.py:28
  11.0 0.0 collective-permute-done.3.refs_0_.refs_1_
  11.1 0.9 %collective-permute-start.5 = (bf16[64,1152]{1,0:T(8,128)(2,1)}, bf16[64,1152]{1,0:T(8,128)(2,1)S(1)}, u32[]{:S(2)}, u32[]{:S(2)}) collective-permute-start(bf16[64,1152]{1,0:T(8,128)(2,1)} %refs_0_.3), channel_id=1, source_target_pairs={{0,133},{1,4},{2,135},{3,6},{4,1},{5,128},{6,3},{7,130},{128,5},{1... | collective-permute-start | bytes 442376 | tf_op jit(solution)/shard_map/gX2/ppermute | solution.py:28
  12.0 0.0 collective-permute-done.refs_1_
  12.0 0.0 collective-permute-done.1.refs_2_
  12.0 0.0 collective-permute-done.2.refs_3_
  12.0 0.2 shard_map.60.refs_0_
  12.2 3.0 %collective-permute-start.8 = (bf16[256,1152]{1,0:T(8,128)(2,1)S(1)}, bf16[256,1152]{1,0:T(8,128)(2,1)S(1)}, u32[]{:S(2)}, u32[]{:S(2)}) collective-permute-start(bf16[256,1152]{1,0:T(8,128)(2,1)S(1)} %shard_map.60.refs_0_), channel_id=1, source_target_pairs={{0,8},{1,33},{2,10},{3,35},{4,12},{5,37},{6,14},{7,39},{128,136},{... | collective-permute-start | bytes 1769480 | tf_op jit(solution)/shard_map/gB1/ppermute | solution.py:28
  15.3 0.0 collective-permute-start.9
  15.3 2.1 %collective-permute-start.10 = (bf16[256,1152]{1,0:T(8,128)(2,1)S(1)}, bf16[256,1152]{1,0:T(8,128)(2,1)S(1)}, u32[]{:S(2)}, u32[]{:S(2)}) collective-permute-start(bf16[256,1152]{1,0:T(8,128)(2,1)S(1)} %shard_map.60.refs_0_), channel_id=1, source_target_pairs={{0,16},{1,65},{2,18},{3,67},{4,20},{5,69},{6,22},{7,71},{128,144},... | collective-permute-start | bytes 1769480 | tf_op jit(solution)/shard_map/gB2/ppermute | solution.py:28
  17.4 0.0 collective-permute-done.4.refs_2_
  17.4 1.1 %collective-permute-done.5.refs_3_ = bf16[64,1152]{1,0:T(8,128)(2,1)S(1)} collective-permute-done((bf16[64,1152]{1,0:T(8,128)(2,1)}, bf16[64,1152]{1,0:T(8,128)(2,1)S(1)}, u32[]{:S(2)}, u32[]{:S(2)}) %collective-permute-start.5) | collective-permute-done | bytes 147488 | tf_op jit(solution)/shard_map/gX2/ppermute | solution.py:28
  18.6 0.2 shard_map.61.refs_0_
  18.8 3.5 %collective-permute-start.6 = (bf16[256,1152]{1,0:T(8,128)(2,1)S(1)}, bf16[256,1152]{1,0:T(8,128)(2,1)S(1)}, u32[]{:S(2)}, u32[]{:S(2)}) collective-permute-start(bf16[256,1152]{1,0:T(8,128)(2,1)S(1)} %shard_map.61.refs_0_), channel_id=1, source_target_pairs={{0,2},{1,135},{2,4},{3,1},{4,6},{5,3},{6,128},{7,5},{128,130},{129... | collective-permute-start | bytes 1769480 | tf_op jit(solution)/shard_map/gZ13/ppermute | solution.py:28
  22.3 1.7 %collective-permute-start.7 = (bf16[64,1152]{1,0:T(8,128)(2,1)S(1)}, bf16[64,1152]{1,0:T(8,128)(2,1)S(1)}, u32[]{:S(2)}, u32[]{:S(2)}) collective-permute-start(bf16[64,1152]{1,0:T(8,128)(2,1)S(1)} %collective-permute-done.4.refs_2_), channel_id=1, source_target_pairs={{0,4},{1,133},{2,6},{3,135},{4,128},{5,1},{6,130},{7,3},{128,132},... | collective-permute-start | bytes 442376 | tf_op jit(solution)/shard_map/gZ4/ppermute | solution.py:28
  24.0 7.5 %collective-permute-done.6.refs_2_.refs_1_ = bf16[256,1152]{1,0:T(8,128)(2,1)S(1)} collective-permute-done((bf16[256,1152]{1,0:T(8,128)(2,1)S(1)}, bf16[256,1152]{1,0:T(8,128)(2,1)S(1)}, u32[]{:S(2)}, u32[]{:S(2)}) %collective-permute-start.6) | collective-permute-done | bytes 589856 | tf_op jit(solution)/shard_map/gZ13/ppermute | solution.py:28
  31.5 0.1 shard_map.62.refs_1_
  31.6 0.2 shard_map.63
  31.8 0.2 shard_map.64
  32.0 4.1 %collective-permute-done.7.refs_2_ = bf16[64,1152]{1,0:T(8,128)(2,1)S(1)} collective-permute-done((bf16[64,1152]{1,0:T(8,128)(2,1)S(1)}, bf16[64,1152]{1,0:T(8,128)(2,1)S(1)}, u32[]{:S(2)}, u32[]{:S(2)}) %collective-permute-start.7) | collective-permute-done | bytes 147488 | tf_op jit(solution)/shard_map/gZ4/ppermute | solution.py:28
  36.0 0.0 collective-permute-done.8.refs_5_.refs_3_
  36.0 0.0 collective-permute-done.9.refs_6_.refs_4_
  36.0 0.0 collective-permute-done.10.refs_7_.refs_5_
  36.0 0.3 shard_map.66.refs_0_.refs_2_
  36.3 0.3 collective-permute-start.11
  36.6 3.4 %shard_map.67 = (bf16[1024,512]{1,0:T(8,128)(2,1)S(1)}, bf16[1024,1152]{1,0:T(8,128)(2,1)S(1)}, bf16[512,1152]{1,0:T(8,128)(2,1)S(1)}) custom-call(bf16[512,1152]{1,0:T(8,128)(2,1)S(1)} %shard_map.66.refs_0_.refs_2_, f32[8,128]{1,0:T(8,128)S(1)} %shard_map.62.refs_1_, bf16[256,1152]{1,0:T(8,128)(2,1)S(1)} %get-tuple-element.26.refs_3_.refs_2_, ...), custom_call_target="tpu_custom_call" | custom-call | flops 2415919104 | bytes 1024 | tf_op jit(solution)/shard_map/pallas_call | solution.py:55
  40.0 0.0 collective-permute-done.11.refs_0_.refs_3_
  40.1 3.0 %shard_map.68 = (bf16[1024,512]{1,0:T(8,128)(2,1)S(1)}, bf16[512,1152]{1,0:T(8,128)(2,1)S(1)}) custom-call(bf16[512,1152]{1,0:T(8,128)(2,1)S(1)} %collective-permute-done.11.refs_0_.refs_3_, f32[8,128]{1,0:T(8,128)S(1)} %shard_map.62.refs_1_, bf16[1024,1152]{1,0:T(8,128)(2,1)S(1)} %get-tuple-element.28.refs_2_, ...), custom_call_target="tpu_custom_call" | custom-call | flops 2415919104 | bytes 1024 | tf_op jit(solution)/shard_map/pallas_call | solution.py:55
  43.1 0.6 collective-permute-start.12
  43.7 0.8 %shard_map.69.refs_4_ = bf16[256,1152]{1,0:T(8,128)(2,1)S(1)} custom-call(bf16[1024,512]{1,0:T(8,128)(2,1)S(1)} %get-tuple-element.27.refs_0_, bf16[1024,512]{1,0:T(8,128)(2,1)S(1)} %get-tuple-element.30.refs_1_, bf16[512,1152]{1,0:T(8,128)(2,1)S(1)} %shard_map.66.refs_0_.refs_2_, bf16[512,1152]{1,0:T(8,128)(2,1)S(1)} %collective-permute-done.11.refs_0_.refs_3_, ...), custom_call_target="tpu_custom_call" | custom-call | flops 603979776 | bytes 1024 | tf_op jit(solution)/shard_map/pallas_call | solution.py:55
  44.5 0.3 collective-permute-start.13
  44.8 0.8 %shard_map.70.refs_2_ = bf16[256,1152]{1,0:T(8,128)(2,1)S(1)} custom-call(bf16[1024,512]{1,0:T(8,128)(2,1)S(1)} %get-tuple-element.27.refs_0_, bf16[1024,512]{1,0:T(8,128)(2,1)S(1)} %get-tuple-element.30.refs_1_, bf16[512,1152]{1,0:T(8,128)(2,1)S(1)} %shard_map.66.refs_0_.refs_2_, bf16[512,1152]{1,0:T(8,128)(2,1)S(1)} %collective-permute-done.11.refs_0_.refs_3_, ...), custom_call_target="tpu_custom_call" | custom-call | flops 603979776 | bytes 1024 | tf_op jit(solution)/shard_map/pallas_call | solution.py:55
  45.7 1.9 %collective-permute-start.14 = (bf16[256,1152]{1,0:T(8,128)(2,1)S(1)}, bf16[256,1152]{1,0:T(8,128)(2,1)S(1)}, u32[]{:S(2)}, u32[]{:S(2)}) collective-permute-start(bf16[256,1152]{1,0:T(8,128)(2,1)S(1)} %shard_map.70.refs_2_), channel_id=1, source_target_pairs={{0,24},{1,97},{2,26},{3,99},{4,28},{5,101},{6,30},{7,103},{128,152... | collective-permute-start | bytes 1769480 | tf_op jit(solution)/shard_map/rB1/ppermute | solution.py:28
  47.6 0.0 collective-permute-done.12.refs_1_
  47.6 0.3 shard_map.71
  47.8 1.4 %collective-permute-start.16 = (bf16[256,1152]{1,0:T(8,128)(2,1)S(1)}, bf16[256,1152]{1,0:T(8,128)(2,1)S(1)}, u32[]{:S(2)}, u32[]{:S(2)}) collective-permute-start(bf16[256,1152]{1,0:T(8,128)(2,1)S(1)} %get-tuple-element.32.refs_4_), channel_id=1, source_target_pairs={{0,134},{1,3},{2,0},{3,5},{4,2},{5,7},{6,4},{7,129},{128,6},{129,1... | collective-permute-start | bytes 1769480 | tf_op jit(solution)/shard_map/rZ13/ppermute | solution.py:28
  49.2 0.8 %shard_map.72.refs_4_ = bf16[256,1152]{1,0:T(8,128)(2,1)S(1)} custom-call(bf16[1024,512]{1,0:T(8,128)(2,1)S(1)} %get-tuple-element.27.refs_0_, bf16[1024,512]{1,0:T(8,128)(2,1)S(1)} %get-tuple-element.30.refs_1_, bf16[512,1152]{1,0:T(8,128)(2,1)S(1)} %shard_map.66.refs_0_.refs_2_, bf16[512,1152]{1,0:T(8,128)(2,1)S(1)} %collective-permute-done.11.refs_0_.refs_3_, ...), custom_call_target="tpu_custom_call" | custom-call | flops 603979776 | bytes 1024 | tf_op jit(solution)/shard_map/pallas_call | solution.py:55
  50.1 1.3 %collective-permute-start.15 = (bf16[256,1152]{1,0:T(8,128)(2,1)S(1)}, bf16[256,1152]{1,0:T(8,128)(2,1)S(1)}, u32[]{:S(2)}, u32[]{:S(2)}) collective-permute-start(bf16[256,1152]{1,0:T(8,128)(2,1)S(1)} %shard_map.72.refs_4_), channel_id=1, source_target_pairs={{0,16},{1,65},{2,18},{3,67},{4,20},{5,69},{6,22},{7,71},{128,144},... | collective-permute-start | bytes 1769480 | tf_op jit(solution)/shard_map/rB2/ppermute | solution.py:28
  51.4 3.1 %collective-permute-start.17 = (bf16[64,1152]{1,0:T(8,128)(2,1)S(1)}, bf16[64,1152]{1,0:T(8,128)(2,1)S(1)}, u32[]{:S(2)}, u32[]{:S(2)}) collective-permute-start(bf16[64,1152]{1,0:T(8,128)(2,1)S(1)} %get-tuple-element.34), channel_id=1, source_target_pairs={{0,132},{1,5},{2,134},{3,7},{4,0},{5,129},{6,2},{7,131},{128,4},{1... | collective-permute-start | bytes 442376 | tf_op jit(solution)/shard_map/rZ4/ppermute | solution.py:28
  54.5 0.8 %shard_map.73.refs_0_ = f32[256,1152]{1,0:T(8,128)S(1)} custom-call(bf16[1024,512]{1,0:T(8,128)(2,1)S(1)} %get-tuple-element.27.refs_0_, bf16[1024,512]{1,0:T(8,128)(2,1)S(1)} %get-tuple-element.30.refs_1_, bf16[512,1152]{1,0:T(8,128)(2,1)S(1)} %shard_map.66.refs_0_.refs_2_, bf16[512,1152]{1,0:T(8,128)(2,1)S(1)} %collective-permute-done.11.refs_0_.refs_3_, ...), custom_call_target="tpu_custom_call" | custom-call | flops 603979776 | bytes 1024 | tf_op jit(solution)/shard_map/pallas_call | solution.py:55
  55.4 0.0 collective-permute-done.13.refs_1_
  55.4 7.8 %collective-permute-done.14.refs_2_ = bf16[256,1152]{1,0:T(8,128)(2,1)S(1)} collective-permute-done((bf16[256,1152]{1,0:T(8,128)(2,1)S(1)}, bf16[256,1152]{1,0:T(8,128)(2,1)S(1)}, u32[]{:S(2)}, u32[]{:S(2)}) %collective-permute-start.14) | collective-permute-done | bytes 589856 | tf_op jit(solution)/shard_map/rB1/ppermute | solution.py:28
  63.2 0.2 shard_map.74.refs_1_.refs_0_
  63.4 0.0 collective-permute-done.16.refs_0_.refs_1_
  63.4 0.0 collective-permute-done.17.refs_2_
  63.4 0.1 shard_map.76.refs_0_
  63.5 0.1 collective-permute-start.21
  63.6 0.0 collective-permute-done.15.refs_1_
  63.6 0.1 shard_map.78
  63.7 3.7 %collective-permute-start.18 = (bf16[64,1152]{1,0:T(8,128)(2,1)S(1)}, bf16[64,1152]{1,0:T(8,128)(2,1)S(1)}, u32[]{:S(2)}, u32[]{:S(2)}) collective-permute-start(bf16[64,1152]{1,0:T(8,128)(2,1)S(1)} %get-tuple-element.36), channel_id=1, source_target_pairs={{0,96},{1,25},{2,98},{3,27},{4,100},{5,29},{6,102},{7,31},{128,224... | collective-permute-start | bytes 442376 | tf_op jit(solution)/shard_map/rA1/ppermute | solution.py:28
  67.4 0.4 collective-permute-start.19
  67.8 1.3 %collective-permute-start.20 = (bf16[64,1152]{1,0:T(8,128)(2,1)S(1)}, bf16[64,1152]{1,0:T(8,128)(2,1)S(1)}, u32[]{:S(2)}, u32[]{:S(2)}) collective-permute-start(bf16[64,1152]{1,0:T(8,128)(2,1)S(1)} %get-tuple-element.38), channel_id=1, source_target_pairs={{0,32},{1,9},{2,34},{3,11},{4,36},{5,13},{6,38},{7,15},{128,160},{... | collective-permute-start | bytes 442376 | tf_op jit(solution)/shard_map/rA3/ppermute | solution.py:28
  69.1 3.3 %collective-permute-done.21.refs_2_ = bf16[128,1152]{1,0:T(8,128)(2,1)S(1)} collective-permute-done((bf16[128,1152]{1,0:T(8,128)(2,1)S(1)}, bf16[128,1152]{1,0:T(8,128)(2,1)S(1)}, u32[]{:S(2)}, u32[]{:S(2)}) %collective-permute-start.21) | collective-permute-done | bytes 294944 | tf_op jit(solution)/shard_map/rZ2/ppermute | solution.py:28
  72.4 0.1 shard_map.79
  72.5 0.1 collective-permute-start.22
  72.6 0.0 collective-permute-done.18.refs_3_
  72.6 1.5 %collective-permute-done.19.refs_4_ = bf16[64,1152]{1,0:T(8,128)(2,1)S(1)} collective-permute-done((bf16[64,1152]{1,0:T(8,128)(2,1)S(1)}, bf16[64,1152]{1,0:T(8,128)(2,1)S(1)}, u32[]{:S(2)}, u32[]{:S(2)}) %collective-permute-start.19) | collective-permute-done | bytes 147488 | tf_op jit(solution)/shard_map/rA2/ppermute | solution.py:28
  74.2 1.5 %collective-permute-done.20.refs_5_ = bf16[64,1152]{1,0:T(8,128)(2,1)S(1)} collective-permute-done((bf16[64,1152]{1,0:T(8,128)(2,1)S(1)}, bf16[64,1152]{1,0:T(8,128)(2,1)S(1)}, u32[]{:S(2)}, u32[]{:S(2)}) %collective-permute-start.20) | collective-permute-done | bytes 147488 | tf_op jit(solution)/shard_map/rA3/ppermute | solution.py:28
  75.7 0.0 collective-permute-done.22.refs_9_
  75.7 1.1 %shard_map.80 = (f32[64,1152]{1,0:T(8,128)}, f32[64,1152]{1,0:T(8,128)}) custom-call(f32[64,1152]{1,0:T(8,128)S(1)} %get-tuple-element.23.refs_0_, f32[64,128]{1,0:T(8,128)S(1)} %get-tuple-element.24.refs_1_, f32[64,1152]{1,0:T(8,128)S(1)} %get-tuple-element.35.refs_2_, bf16[64,1152]{1,0:T(8,128)(2,1)S(1)} %collective-permute-done.18.refs_3_, ...), custom_call_target="tpu_custom_call" | custom-call | bytes 1024 | tf_op jit(solution)/shard_map/pallas_call | solution.py:55
  (8 shorter events, 0.0 us)
Async XLA Ops:
  0.6 10.4 %collective-permute-start.3 = (bf16[64,1152]{1,0:T(8,128)(2,1)}, bf16[64,1152]{1,0:T(8,128)(2,1)S(1)}, u32[]{:S(2)}, u32[]{:S(2)}) collective-permute-start(bf16[64,1152]{1,0:T(8,128)(2,1)} %refs_0_.3), channel_id=1, source_target_pairs={{0,1},{1,0},{2,3},{3,2},{4,5},{5,4},{6,7},{7,6},{128,129},{129,128... | collective-permute-start | bytes 442376 | tf_op jit(solution)/shard_map/gC/ppermute | solution.py:28
  0.7 11.2 %collective-permute-start = (bf16[64,1152]{1,0:T(8,128)(2,1)}, bf16[64,1152]{1,0:T(8,128)(2,1)S(1)}, u32[]{:S(2)}, u32[]{:S(2)}) collective-permute-start(bf16[64,1152]{1,0:T(8,128)(2,1)} %refs_0_.2), channel_id=1, source_target_pairs={{0,32},{1,9},{2,34},{3,11},{4,36},{5,13},{6,38},{7,15},{128,160},{... | collective-permute-start | bytes 442376 | tf_op jit(solution)/shard_map/gA1/ppermute | solution.py:28
  2.3 9.7 %collective-permute-start.1 = (bf16[64,1152]{1,0:T(8,128)(2,1)}, bf16[64,1152]{1,0:T(8,128)(2,1)S(1)}, u32[]{:S(2)}, u32[]{:S(2)}) collective-permute-start(bf16[64,1152]{1,0:T(8,128)(2,1)} %refs_0_.2), channel_id=1, source_target_pairs={{0,64},{1,17},{2,66},{3,19},{4,68},{5,21},{6,70},{7,23},{128,192},... | collective-permute-start | bytes 442376 | tf_op jit(solution)/shard_map/gA2/ppermute | solution.py:28
  5.0 6.9 %collective-permute-start.2 = (bf16[64,1152]{1,0:T(8,128)(2,1)}, bf16[64,1152]{1,0:T(8,128)(2,1)S(1)}, u32[]{:S(2)}, u32[]{:S(2)}) collective-permute-start(bf16[64,1152]{1,0:T(8,128)(2,1)} %refs_0_.2), channel_id=1, source_target_pairs={{0,96},{1,25},{2,98},{3,27},{4,100},{5,29},{6,102},{7,31},{128,224... | collective-permute-start | bytes 442376 | tf_op jit(solution)/shard_map/gA3/ppermute | solution.py:28
  6.5 10.9 %collective-permute-start.4 = (bf16[64,1152]{1,0:T(8,128)(2,1)}, bf16[64,1152]{1,0:T(8,128)(2,1)S(1)}, u32[]{:S(2)}, u32[]{:S(2)}) collective-permute-start(bf16[64,1152]{1,0:T(8,128)(2,1)} %refs_0_.3), channel_id=1, source_target_pairs={{0,4},{1,133},{2,6},{3,135},{4,128},{5,1},{6,130},{7,3},{128,132},... | collective-permute-start | bytes 442376 | tf_op jit(solution)/shard_map/gZ2/ppermute | solution.py:28
  11.0 1.0 %copy-start = (bf16[64,1152]{1,0:T(8,128)(2,1)S(1)}, bf16[64,1152]{1,0:T(8,128)(2,1)}, u32[]{:S(2)}) copy-start(bf16[64,1152]{1,0:T(8,128)(2,1)} %refs_0_.2) | copy-start | bytes 442372
  11.1 7.5 %collective-permute-start.5 = (bf16[64,1152]{1,0:T(8,128)(2,1)}, bf16[64,1152]{1,0:T(8,128)(2,1)S(1)}, u32[]{:S(2)}, u32[]{:S(2)}) collective-permute-start(bf16[64,1152]{1,0:T(8,128)(2,1)} %refs_0_.3), channel_id=1, source_target_pairs={{0,133},{1,4},{2,135},{3,6},{4,1},{5,128},{6,3},{7,130},{128,5},{1... | collective-permute-start | bytes 442376 | tf_op jit(solution)/shard_map/gX2/ppermute | solution.py:28
  12.0 6.6 %copy-start.1 = (bf16[64,1152]{1,0:T(8,128)(2,1)S(1)}, bf16[64,1152]{1,0:T(8,128)(2,1)}, u32[]{:S(2)}) copy-start(bf16[64,1152]{1,0:T(8,128)(2,1)} %refs_0_.3) | copy-start | bytes 442372
  12.2 23.8 %collective-permute-start.8 = (bf16[256,1152]{1,0:T(8,128)(2,1)S(1)}, bf16[256,1152]{1,0:T(8,128)(2,1)S(1)}, u32[]{:S(2)}, u32[]{:S(2)}) collective-permute-start(bf16[256,1152]{1,0:T(8,128)(2,1)S(1)} %shard_map.60.refs_0_), channel_id=1, source_target_pairs={{0,8},{1,33},{2,10},{3,35},{4,12},{5,37},{6,14},{7,39},{128,136},{... | collective-permute-start | bytes 1769480 | tf_op jit(solution)/shard_map/gB1/ppermute | solution.py:28
  15.3 20.8 %collective-permute-start.9 = (bf16[256,1152]{1,0:T(8,128)(2,1)S(1)}, bf16[256,1152]{1,0:T(8,128)(2,1)S(1)}, u32[]{:S(2)}, u32[]{:S(2)}) collective-permute-start(bf16[256,1152]{1,0:T(8,128)(2,1)S(1)} %shard_map.60.refs_0_), channel_id=1, source_target_pairs={{0,24},{1,97},{2,26},{3,99},{4,28},{5,101},{6,30},{7,103},{128,152... | collective-permute-start | bytes 1769480 | tf_op jit(solution)/shard_map/gB3/ppermute | solution.py:28
  15.3 20.8 %collective-permute-start.10 = (bf16[256,1152]{1,0:T(8,128)(2,1)S(1)}, bf16[256,1152]{1,0:T(8,128)(2,1)S(1)}, u32[]{:S(2)}, u32[]{:S(2)}) collective-permute-start(bf16[256,1152]{1,0:T(8,128)(2,1)S(1)} %shard_map.60.refs_0_), channel_id=1, source_target_pairs={{0,16},{1,65},{2,18},{3,67},{4,20},{5,69},{6,22},{7,71},{128,144},... | collective-permute-start | bytes 1769480 | tf_op jit(solution)/shard_map/gB2/ppermute | solution.py:28
  18.8 12.7 %collective-permute-start.6 = (bf16[256,1152]{1,0:T(8,128)(2,1)S(1)}, bf16[256,1152]{1,0:T(8,128)(2,1)S(1)}, u32[]{:S(2)}, u32[]{:S(2)}) collective-permute-start(bf16[256,1152]{1,0:T(8,128)(2,1)S(1)} %shard_map.61.refs_0_), channel_id=1, source_target_pairs={{0,2},{1,135},{2,4},{3,1},{4,6},{5,3},{6,128},{7,5},{128,130},{129... | collective-permute-start | bytes 1769480 | tf_op jit(solution)/shard_map/gZ13/ppermute | solution.py:28
  22.3 13.8 %collective-permute-start.7 = (bf16[64,1152]{1,0:T(8,128)(2,1)S(1)}, bf16[64,1152]{1,0:T(8,128)(2,1)S(1)}, u32[]{:S(2)}, u32[]{:S(2)}) collective-permute-start(bf16[64,1152]{1,0:T(8,128)(2,1)S(1)} %collective-permute-done.4.refs_2_), channel_id=1, source_target_pairs={{0,4},{1,133},{2,6},{3,135},{4,128},{5,1},{6,130},{7,3},{128,132},... | collective-permute-start | bytes 442376 | tf_op jit(solution)/shard_map/gZ4/ppermute | solution.py:28
  36.3 3.7 %collective-permute-start.11 = (bf16[512,1152]{1,0:T(8,128)(2,1)S(1)}, bf16[512,1152]{1,0:T(8,128)(2,1)S(1)}, u32[]{:S(2)}, u32[]{:S(2)}) collective-permute-start(bf16[512,1152]{1,0:T(8,128)(2,1)S(1)} %shard_map.66.refs_0_.refs_2_), channel_id=1, source_target_pairs={{0,1},{1,0},{2,3},{3,2},{4,5},{5,4},{6,7},{7,6},{128,129},{129,128... | collective-permute-start | bytes 3538952 | tf_op jit(solution)/shard_map/gS/ppermute | solution.py:28
  43.1 4.5 %collective-permute-start.12 = (bf16[512,1152]{1,0:T(8,128)(2,1)S(1)}, bf16[512,1152]{1,0:T(8,128)(2,1)S(1)}, u32[]{:S(2)}, u32[]{:S(2)}) collective-permute-start(bf16[512,1152]{1,0:T(8,128)(2,1)S(1)} %get-tuple-element.31.refs_4_), channel_id=1, source_target_pairs={{0,1},{1,0},{2,3},{3,2},{4,5},{5,4},{6,7},{7,6},{128,129},{129,128... | collective-permute-start | bytes 3538952 | tf_op jit(solution)/shard_map/rC/ppermute | solution.py:28
  44.5 10.9 %collective-permute-start.13 = (bf16[256,1152]{1,0:T(8,128)(2,1)S(1)}, bf16[256,1152]{1,0:T(8,128)(2,1)S(1)}, u32[]{:S(2)}, u32[]{:S(2)}) collective-permute-start(bf16[256,1152]{1,0:T(8,128)(2,1)S(1)} %shard_map.69.refs_4_), channel_id=1, source_target_pairs={{0,8},{1,33},{2,10},{3,35},{4,12},{5,37},{6,14},{7,39},{128,136},{... | collective-permute-start | bytes 1769480 | tf_op jit(solution)/shard_map/rB3/ppermute | solution.py:28
  45.7 17.5 %collective-permute-start.14 = (bf16[256,1152]{1,0:T(8,128)(2,1)S(1)}, bf16[256,1152]{1,0:T(8,128)(2,1)S(1)}, u32[]{:S(2)}, u32[]{:S(2)}) collective-permute-start(bf16[256,1152]{1,0:T(8,128)(2,1)S(1)} %shard_map.70.refs_2_), channel_id=1, source_target_pairs={{0,24},{1,97},{2,26},{3,99},{4,28},{5,101},{6,30},{7,103},{128,152... | collective-permute-start | bytes 1769480 | tf_op jit(solution)/shard_map/rB1/ppermute | solution.py:28
  47.8 15.5 %collective-permute-start.16 = (bf16[256,1152]{1,0:T(8,128)(2,1)S(1)}, bf16[256,1152]{1,0:T(8,128)(2,1)S(1)}, u32[]{:S(2)}, u32[]{:S(2)}) collective-permute-start(bf16[256,1152]{1,0:T(8,128)(2,1)S(1)} %get-tuple-element.32.refs_4_), channel_id=1, source_target_pairs={{0,134},{1,3},{2,0},{3,5},{4,2},{5,7},{6,4},{7,129},{128,6},{129,1... | collective-permute-start | bytes 1769480 | tf_op jit(solution)/shard_map/rZ13/ppermute | solution.py:28
  50.1 13.5 %collective-permute-start.15 = (bf16[256,1152]{1,0:T(8,128)(2,1)S(1)}, bf16[256,1152]{1,0:T(8,128)(2,1)S(1)}, u32[]{:S(2)}, u32[]{:S(2)}) collective-permute-start(bf16[256,1152]{1,0:T(8,128)(2,1)S(1)} %shard_map.72.refs_4_), channel_id=1, source_target_pairs={{0,16},{1,65},{2,18},{3,67},{4,20},{5,69},{6,22},{7,71},{128,144},... | collective-permute-start | bytes 1769480 | tf_op jit(solution)/shard_map/rB2/ppermute | solution.py:28
  51.4 12.0 %collective-permute-start.17 = (bf16[64,1152]{1,0:T(8,128)(2,1)S(1)}, bf16[64,1152]{1,0:T(8,128)(2,1)S(1)}, u32[]{:S(2)}, u32[]{:S(2)}) collective-permute-start(bf16[64,1152]{1,0:T(8,128)(2,1)S(1)} %get-tuple-element.34), channel_id=1, source_target_pairs={{0,132},{1,5},{2,134},{3,7},{4,0},{5,129},{6,2},{7,131},{128,4},{1... | collective-permute-start | bytes 442376 | tf_op jit(solution)/shard_map/rZ4/ppermute | solution.py:28
  63.5 9.0 %collective-permute-start.21 = (bf16[128,1152]{1,0:T(8,128)(2,1)S(1)}, bf16[128,1152]{1,0:T(8,128)(2,1)S(1)}, u32[]{:S(2)}, u32[]{:S(2)}) collective-permute-start(bf16[128,1152]{1,0:T(8,128)(2,1)S(1)} %shard_map.76.refs_0_), channel_id=1, source_target_pairs={{0,132},{1,5},{2,134},{3,7},{4,0},{5,129},{6,2},{7,131},{128,4},{1... | collective-permute-start | bytes 884744 | tf_op jit(solution)/shard_map/rZ2/ppermute | solution.py:28
  63.7 8.9 %collective-permute-start.18 = (bf16[64,1152]{1,0:T(8,128)(2,1)S(1)}, bf16[64,1152]{1,0:T(8,128)(2,1)S(1)}, u32[]{:S(2)}, u32[]{:S(2)}) collective-permute-start(bf16[64,1152]{1,0:T(8,128)(2,1)S(1)} %get-tuple-element.36), channel_id=1, source_target_pairs={{0,96},{1,25},{2,98},{3,27},{4,100},{5,29},{6,102},{7,31},{128,224... | collective-permute-start | bytes 442376 | tf_op jit(solution)/shard_map/rA1/ppermute | solution.py:28
  67.4 6.8 %collective-permute-start.19 = (bf16[64,1152]{1,0:T(8,128)(2,1)S(1)}, bf16[64,1152]{1,0:T(8,128)(2,1)S(1)}, u32[]{:S(2)}, u32[]{:S(2)}) collective-permute-start(bf16[64,1152]{1,0:T(8,128)(2,1)S(1)} %get-tuple-element.37), channel_id=1, source_target_pairs={{0,64},{1,17},{2,66},{3,19},{4,68},{5,21},{6,70},{7,23},{128,192},... | collective-permute-start | bytes 442376 | tf_op jit(solution)/shard_map/rA2/ppermute | solution.py:28
  67.8 7.9 %collective-permute-start.20 = (bf16[64,1152]{1,0:T(8,128)(2,1)S(1)}, bf16[64,1152]{1,0:T(8,128)(2,1)S(1)}, u32[]{:S(2)}, u32[]{:S(2)}) collective-permute-start(bf16[64,1152]{1,0:T(8,128)(2,1)S(1)} %get-tuple-element.38), channel_id=1, source_target_pairs={{0,32},{1,9},{2,34},{3,11},{4,36},{5,13},{6,38},{7,15},{128,160},{... | collective-permute-start | bytes 442376 | tf_op jit(solution)/shard_map/rA3/ppermute | solution.py:28
  72.5 3.1 %collective-permute-start.22 = (bf16[64,1152]{1,0:T(8,128)(2,1)S(1)}, bf16[64,1152]{1,0:T(8,128)(2,1)S(1)}, u32[]{:S(2)}, u32[]{:S(2)}) collective-permute-start(bf16[64,1152]{1,0:T(8,128)(2,1)S(1)} %get-tuple-element.43), channel_id=1, source_target_pairs={{0,1},{1,0},{2,3},{3,2},{4,5},{5,4},{6,7},{7,6},{128,129},{129,128... | collective-permute-start | bytes 442376 | tf_op jit(solution)/shard_map/rS/ppermute | solution.py:28

commit v15 on v14

--- a/solution.py
+++ b/solution.py
@@ -277,29 +277,29 @@
             [w_mine, w_theirs, mine, theirs], ties=ties, flops=flops // 2, limit=24,
         )[0]
 
-    grad3 = image_grads(2, BF16, [send])
+    grad2 = image_grads(3, BF16, [send])
+    back2 = shift(grad2, second(-2), "rB2")
+    grad3 = image_grads(2, BF16, [grad2])
     back3 = shift(grad3, second(-3), "rB3")
-    grad1 = image_grads(1, BF16, [grad3])
-    back1 = shift(grad1, second(-1), "rB1")
 
     total_own, part13, part2, part4 = call(
         total_kernel,
         [((own, dim), F32), ((4 * own, dim), BF16), ((2 * own, dim), F32), ((own, dim), BF16)],
-        [keep, shift(send, other, "rC")], ties=[grad1],
-    )
-    grad2 = image_grads(3, BF16, [part13])
-    back2 = shift(grad2, second(-2), "rB2")
-    grad0 = image_grads(0, F32, [grad2])
-    (partial,) = call(partial_kernel, [((each, dim), F32)], [grad0, back3, back1])
+        [keep, shift(send, other, "rC")], ties=[grad3],
+    )
+    grad1 = image_grads(1, BF16, [part13])
+    back1 = shift(grad1, second(-1), "rB1")
+    grad0 = image_grads(0, F32, [grad1])
+    (partial,) = call(partial_kernel, [((each, dim), F32)], [grad0, back2, back3])
     got13 = shift(part13, line(-1), "rZ13")
     got4 = shift(part4, line(-2), "rZ4")
-    (middle,) = call(middle_kernel, [((2 * own, dim), BF16)], [part2, got13, got4], [token(got13, partial)])
+    (middle,) = call(middle_kernel, [((2 * own, dim), BF16)], [part2, got13, got4], [partial])
     got2 = shift(middle, line(-2), "rZ2")
     txt_sum, txt_send = call(landed_kernel, [((own, dim), F32), ((own, dim), BF16)], [total_own, got13, got2])
     txt_last = shift(txt_send, other, "rS")
 
     img_sum, *parts = call(
-        sums_kernel, [((own, dim), F32)] + [((own, dim), BF16)] * 3, [partial, back2], ties=[token(middle)]
+        sums_kernel, [((own, dim), F32)] + [((own, dim), BF16)] * 3, [partial, back1], ties=[token(middle)]
     )
     last = [shift(p, first(-k), "rA%d" % k) for k, p in zip((1, 2, 3), parts)]
 

time: 76.9 us -> 76.8 us (level)
  starting transfers between devices: 34.8 us -> 37 us
  waiting for transfers between devices: 26.9 us -> 24.8 us
    ppermute x23, starting transfers between devices: 34.8 us -> 37 us  [shift(): return lax.ppermute(values, AXES, pairs)]
    ppermute x23, waiting for transfers between devices: 26.9 us -> 24.8 us  [shift(): return lax.ppermute(values, AXES, pairs)]
    pallas_call x22 -> x21, Pallas kernels: 12.9 us -> 12.8 us  [call(): pl.pallas_call(lambda *refs: kernel(*refs[:n_in], *refs[n_in + len(ties):...]
  transfers between devices with their start and end apart: 23 -> 23, of which waited for: 7 -> 9; matrix products, arithmetic and copies ran while one was open for 0% -> 0% of each run, Pallas kernels for 11% -> 11%
where the time goes in v15:
time: 76.8 us; the launch traced here: 76.7 us
  starting transfers between devices  37 us (48%)
  waiting for transfers between devices  24.8 us (32%)
  Pallas kernels  12.8 us (17%)
  between operations  2.11 us (3%)
    ppermute x23, starting transfers between devices, shift(): return lax.ppermute(values, AXES, pairs)  37 us
    ppermute x23, waiting for transfers between devices, shift(): return lax.ppermute(values, AXES, pairs)  24.8 us
    pallas_call x21, Pallas kernels, call(): pl.pallas_call(lambda *refs: kernel(*refs[:n_in], *refs[n_in + len(ties):...  12.8 us
  transfers between devices with their start and end apart: 23, of which 9 were waited for; matrix products, arithmetic and copies ran while one was open for 0% of the time, Pallas kernels for 11%

profile of v15, /device:TPU:24, one launch (start us, length us, event | category | flops | bytes accessed | tf_op | source)
XLA Modules:
  0.0 76.7 jit_solution(7598334380896900258)
XLA Ops:
  0.6 0.1 collective-permute-start.3
  0.7 1.6 %collective-permute-start = (bf16[64,1152]{1,0:T(8,128)(2,1)}, bf16[64,1152]{1,0:T(8,128)(2,1)S(1)}, u32[]{:S(2)}, u32[]{:S(2)}) collective-permute-start(bf16[64,1152]{1,0:T(8,128)(2,1)} %refs_0_.2), channel_id=1, source_target_pairs={{0,32},{1,9},{2,34},{3,11},{4,36},{5,13},{6,38},{7,15},{128,160},{... | collective-permute-start | bytes 442376 | tf_op jit(solution)/shard_map/gA1/ppermute | solution.py:28
  2.3 2.7 %collective-permute-start.1 = (bf16[64,1152]{1,0:T(8,128)(2,1)}, bf16[64,1152]{1,0:T(8,128)(2,1)S(1)}, u32[]{:S(2)}, u32[]{:S(2)}) collective-permute-start(bf16[64,1152]{1,0:T(8,128)(2,1)} %refs_0_.2), channel_id=1, source_target_pairs={{0,64},{1,17},{2,66},{3,19},{4,68},{5,21},{6,70},{7,23},{128,192},... | collective-permute-start | bytes 442376 | tf_op jit(solution)/shard_map/gA2/ppermute | solution.py:28
  5.0 1.4 %collective-permute-start.2 = (bf16[64,1152]{1,0:T(8,128)(2,1)}, bf16[64,1152]{1,0:T(8,128)(2,1)S(1)}, u32[]{:S(2)}, u32[]{:S(2)}) collective-permute-start(bf16[64,1152]{1,0:T(8,128)(2,1)} %refs_0_.2), channel_id=1, source_target_pairs={{0,96},{1,25},{2,98},{3,27},{4,100},{5,29},{6,102},{7,31},{128,224... | collective-permute-start | bytes 442376 | tf_op jit(solution)/shard_map/gA3/ppermute | solution.py:28
  6.5 3.3 %collective-permute-start.4 = (bf16[64,1152]{1,0:T(8,128)(2,1)}, bf16[64,1152]{1,0:T(8,128)(2,1)S(1)}, u32[]{:S(2)}, u32[]{:S(2)}) collective-permute-start(bf16[64,1152]{1,0:T(8,128)(2,1)} %refs_0_.3), channel_id=1, source_target_pairs={{0,4},{1,133},{2,6},{3,135},{4,128},{5,1},{6,130},{7,3},{128,132},... | collective-permute-start | bytes 442376 | tf_op jit(solution)/shard_map/gZ2/ppermute | solution.py:28
  11.0 0.0 collective-permute-done.3.refs_0_.refs_1_
  11.1 0.9 %collective-permute-start.5 = (bf16[64,1152]{1,0:T(8,128)(2,1)}, bf16[64,1152]{1,0:T(8,128)(2,1)S(1)}, u32[]{:S(2)}, u32[]{:S(2)}) collective-permute-start(bf16[64,1152]{1,0:T(8,128)(2,1)} %refs_0_.3), channel_id=1, source_target_pairs={{0,133},{1,4},{2,135},{3,6},{4,1},{5,128},{6,3},{7,130},{128,5},{1... | collective-permute-start | bytes 442376 | tf_op jit(solution)/shard_map/gX2/ppermute | solution.py:28
  12.0 0.0 collective-permute-done.refs_1_
  12.0 0.0 collective-permute-done.1.refs_2_
  12.0 0.0 collective-permute-done.2.refs_3_
  12.0 0.2 shard_map.60.refs_0_
  12.2 3.0 %collective-permute-start.8 = (bf16[256,1152]{1,0:T(8,128)(2,1)S(1)}, bf16[256,1152]{1,0:T(8,128)(2,1)S(1)}, u32[]{:S(2)}, u32[]{:S(2)}) collective-permute-start(bf16[256,1152]{1,0:T(8,128)(2,1)S(1)} %shard_map.60.refs_0_), channel_id=1, source_target_pairs={{0,8},{1,33},{2,10},{3,35},{4,12},{5,37},{6,14},{7,39},{128,136},{... | collective-permute-start | bytes 1769480 | tf_op jit(solution)/shard_map/gB1/ppermute | solution.py:28
  15.3 0.0 collective-permute-start.9
  15.3 2.1 %collective-permute-start.10 = (bf16[256,1152]{1,0:T(8,128)(2,1)S(1)}, bf16[256,1152]{1,0:T(8,128)(2,1)S(1)}, u32[]{:S(2)}, u32[]{:S(2)}) collective-permute-start(bf16[256,1152]{1,0:T(8,128)(2,1)S(1)} %shard_map.60.refs_0_), channel_id=1, source_target_pairs={{0,16},{1,65},{2,18},{3,67},{4,20},{5,69},{6,22},{7,71},{128,144},... | collective-permute-start | bytes 1769480 | tf_op jit(solution)/shard_map/gB2/ppermute | solution.py:28
  17.4 0.0 collective-permute-done.4.refs_2_
  17.4 1.1 %collective-permute-done.5.refs_3_ = bf16[64,1152]{1,0:T(8,128)(2,1)S(1)} collective-permute-done((bf16[64,1152]{1,0:T(8,128)(2,1)}, bf16[64,1152]{1,0:T(8,128)(2,1)S(1)}, u32[]{:S(2)}, u32[]{:S(2)}) %collective-permute-start.5) | collective-permute-done | bytes 147488 | tf_op jit(solution)/shard_map/gX2/ppermute | solution.py:28
  18.6 0.2 shard_map.61.refs_0_
  18.8 3.5 %collective-permute-start.6 = (bf16[256,1152]{1,0:T(8,128)(2,1)S(1)}, bf16[256,1152]{1,0:T(8,128)(2,1)S(1)}, u32[]{:S(2)}, u32[]{:S(2)}) collective-permute-start(bf16[256,1152]{1,0:T(8,128)(2,1)S(1)} %shard_map.61.refs_0_), channel_id=1, source_target_pairs={{0,2},{1,135},{2,4},{3,1},{4,6},{5,3},{6,128},{7,5},{128,130},{129... | collective-permute-start | bytes 1769480 | tf_op jit(solution)/shard_map/gZ13/ppermute | solution.py:28
  22.3 1.7 %collective-permute-start.7 = (bf16[64,1152]{1,0:T(8,128)(2,1)S(1)}, bf16[64,1152]{1,0:T(8,128)(2,1)S(1)}, u32[]{:S(2)}, u32[]{:S(2)}) collective-permute-start(bf16[64,1152]{1,0:T(8,128)(2,1)S(1)} %collective-permute-done.4.refs_2_), channel_id=1, source_target_pairs={{0,4},{1,133},{2,6},{3,135},{4,128},{5,1},{6,130},{7,3},{128,132},... | collective-permute-start | bytes 442376 | tf_op jit(solution)/shard_map/gZ4/ppermute | solution.py:28
  24.0 7.5 %collective-permute-done.6.refs_2_.refs_1_ = bf16[256,1152]{1,0:T(8,128)(2,1)S(1)} collective-permute-done((bf16[256,1152]{1,0:T(8,128)(2,1)S(1)}, bf16[256,1152]{1,0:T(8,128)(2,1)S(1)}, u32[]{:S(2)}, u32[]{:S(2)}) %collective-permute-start.6) | collective-permute-done | bytes 589856 | tf_op jit(solution)/shard_map/gZ13/ppermute | solution.py:28
  31.5 0.1 shard_map.62.refs_1_
  31.6 0.2 shard_map.63
  31.8 0.2 shard_map.64
  32.0 4.1 %collective-permute-done.7.refs_2_ = bf16[64,1152]{1,0:T(8,128)(2,1)S(1)} collective-permute-done((bf16[64,1152]{1,0:T(8,128)(2,1)S(1)}, bf16[64,1152]{1,0:T(8,128)(2,1)S(1)}, u32[]{:S(2)}, u32[]{:S(2)}) %collective-permute-start.7) | collective-permute-done | bytes 147488 | tf_op jit(solution)/shard_map/gZ4/ppermute | solution.py:28
  36.0 0.0 collective-permute-done.8.refs_5_.refs_3_
  36.0 0.0 collective-permute-done.9.refs_6_.refs_4_
  36.0 0.0 collective-permute-done.10.refs_7_.refs_5_
  36.0 0.3 shard_map.66.refs_0_.refs_2_
  36.3 0.3 collective-permute-start.11
  36.6 3.4 %shard_map.67 = (bf16[1024,512]{1,0:T(8,128)(2,1)S(1)}, bf16[1024,1152]{1,0:T(8,128)(2,1)S(1)}, bf16[512,1152]{1,0:T(8,128)(2,1)S(1)}) custom-call(bf16[512,1152]{1,0:T(8,128)(2,1)S(1)} %shard_map.66.refs_0_.refs_2_, f32[8,128]{1,0:T(8,128)S(1)} %shard_map.62.refs_1_, bf16[256,1152]{1,0:T(8,128)(2,1)S(1)} %get-tuple-element.26.refs_3_.refs_2_, ...), custom_call_target="tpu_custom_call" | custom-call | flops 2415919104 | bytes 1024 | tf_op jit(solution)/shard_map/pallas_call | solution.py:55
  40.0 0.0 collective-permute-done.11.refs_0_.refs_3_
  40.1 3.0 %shard_map.68 = (bf16[1024,512]{1,0:T(8,128)(2,1)S(1)}, bf16[512,1152]{1,0:T(8,128)(2,1)S(1)}) custom-call(bf16[512,1152]{1,0:T(8,128)(2,1)S(1)} %collective-permute-done.11.refs_0_.refs_3_, f32[8,128]{1,0:T(8,128)S(1)} %shard_map.62.refs_1_, bf16[1024,1152]{1,0:T(8,128)(2,1)S(1)} %get-tuple-element.28.refs_2_, ...), custom_call_target="tpu_custom_call" | custom-call | flops 2415919104 | bytes 1024 | tf_op jit(solution)/shard_map/pallas_call | solution.py:55
  43.1 0.6 collective-permute-start.12
  43.7 0.8 %shard_map.69.refs_4_ = bf16[256,1152]{1,0:T(8,128)(2,1)S(1)} custom-call(bf16[1024,512]{1,0:T(8,128)(2,1)S(1)} %get-tuple-element.27.refs_0_, bf16[1024,512]{1,0:T(8,128)(2,1)S(1)} %get-tuple-element.30.refs_1_, bf16[512,1152]{1,0:T(8,128)(2,1)S(1)} %shard_map.66.refs_0_.refs_2_, bf16[512,1152]{1,0:T(8,128)(2,1)S(1)} %collective-permute-done.11.refs_0_.refs_3_, ...), custom_call_target="tpu_custom_call" | custom-call | flops 603979776 | bytes 1024 | tf_op jit(solution)/shard_map/pallas_call | solution.py:55
  44.5 1.3 %collective-permute-start.13 = (bf16[256,1152]{1,0:T(8,128)(2,1)S(1)}, bf16[256,1152]{1,0:T(8,128)(2,1)S(1)}, u32[]{:S(2)}, u32[]{:S(2)}) collective-permute-start(bf16[256,1152]{1,0:T(8,128)(2,1)S(1)} %shard_map.69.refs_4_), channel_id=1, source_target_pairs={{0,16},{1,65},{2,18},{3,67},{4,20},{5,69},{6,22},{7,71},{128,144},... | collective-permute-start | bytes 1769480 | tf_op jit(solution)/shard_map/rB2/ppermute | solution.py:28
  45.9 0.8 %shard_map.70.refs_2_ = bf16[256,1152]{1,0:T(8,128)(2,1)S(1)} custom-call(bf16[1024,512]{1,0:T(8,128)(2,1)S(1)} %get-tuple-element.27.refs_0_, bf16[1024,512]{1,0:T(8,128)(2,1)S(1)} %get-tuple-element.30.refs_1_, bf16[512,1152]{1,0:T(8,128)(2,1)S(1)} %shard_map.66.refs_0_.refs_2_, bf16[512,1152]{1,0:T(8,128)(2,1)S(1)} %collective-permute-done.11.refs_0_.refs_3_, ...), custom_call_target="tpu_custom_call" | custom-call | flops 603979776 | bytes 1024 | tf_op jit(solution)/shard_map/pallas_call | solution.py:55
  46.7 2.3 %collective-permute-start.14 = (bf16[256,1152]{1,0:T(8,128)(2,1)S(1)}, bf16[256,1152]{1,0:T(8,128)(2,1)S(1)}, u32[]{:S(2)}, u32[]{:S(2)}) collective-permute-start(bf16[256,1152]{1,0:T(8,128)(2,1)S(1)} %shard_map.70.refs_2_), channel_id=1, source_target_pairs={{0,8},{1,33},{2,10},{3,35},{4,12},{5,37},{6,14},{7,39},{128,136},{... | collective-permute-start | bytes 1769480 | tf_op jit(solution)/shard_map/rB3/ppermute | solution.py:28
  49.0 0.0 collective-permute-done.12.refs_1_
  49.0 0.3 shard_map.71
  49.2 1.4 %collective-permute-start.16 = (bf16[256,1152]{1,0:T(8,128)(2,1)S(1)}, bf16[256,1152]{1,0:T(8,128)(2,1)S(1)}, u32[]{:S(2)}, u32[]{:S(2)}) collective-permute-start(bf16[256,1152]{1,0:T(8,128)(2,1)S(1)} %get-tuple-element.32.refs_4_), channel_id=1, source_target_pairs={{0,134},{1,3},{2,0},{3,5},{4,2},{5,7},{6,4},{7,129},{128,6},{129,1... | collective-permute-start | bytes 1769480 | tf_op jit(solution)/shard_map/rZ13/ppermute | solution.py:28
  50.6 3.1 %collective-permute-start.17 = (bf16[64,1152]{1,0:T(8,128)(2,1)S(1)}, bf16[64,1152]{1,0:T(8,128)(2,1)S(1)}, u32[]{:S(2)}, u32[]{:S(2)}) collective-permute-start(bf16[64,1152]{1,0:T(8,128)(2,1)S(1)} %get-tuple-element.34), channel_id=1, source_target_pairs={{0,132},{1,5},{2,134},{3,7},{4,0},{5,129},{6,2},{7,131},{128,4},{1... | collective-permute-start | bytes 442376 | tf_op jit(solution)/shard_map/rZ4/ppermute | solution.py:28
  53.8 0.8 %shard_map.72.refs_4_ = bf16[256,1152]{1,0:T(8,128)(2,1)S(1)} custom-call(bf16[1024,512]{1,0:T(8,128)(2,1)S(1)} %get-tuple-element.27.refs_0_, bf16[1024,512]{1,0:T(8,128)(2,1)S(1)} %get-tuple-element.30.refs_1_, bf16[512,1152]{1,0:T(8,128)(2,1)S(1)} %shard_map.66.refs_0_.refs_2_, bf16[512,1152]{1,0:T(8,128)(2,1)S(1)} %collective-permute-done.11.refs_0_.refs_3_, ...), custom_call_target="tpu_custom_call" | custom-call | flops 603979776 | bytes 1024 | tf_op jit(solution)/shard_map/pallas_call | solution.py:55
  54.6 0.3 collective-permute-start.15
  54.9 0.8 %shard_map.73.refs_0_ = f32[256,1152]{1,0:T(8,128)S(1)} custom-call(bf16[1024,512]{1,0:T(8,128)(2,1)S(1)} %get-tuple-element.27.refs_0_, bf16[1024,512]{1,0:T(8,128)(2,1)S(1)} %get-tuple-element.30.refs_1_, bf16[512,1152]{1,0:T(8,128)(2,1)S(1)} %shard_map.66.refs_0_.refs_2_, bf16[512,1152]{1,0:T(8,128)(2,1)S(1)} %collective-permute-done.11.refs_0_.refs_3_, ...), custom_call_target="tpu_custom_call" | custom-call | flops 603979776 | bytes 1024 | tf_op jit(solution)/shard_map/pallas_call | solution.py:55
  55.8 0.2 collective-permute-done.13.refs_1_
  56.0 3.9 %collective-permute-done.14.refs_2_ = bf16[256,1152]{1,0:T(8,128)(2,1)S(1)} collective-permute-done((bf16[256,1152]{1,0:T(8,128)(2,1)S(1)}, bf16[256,1152]{1,0:T(8,128)(2,1)S(1)}, u32[]{:S(2)}, u32[]{:S(2)}) %collective-permute-start.14) | collective-permute-done | bytes 589856 | tf_op jit(solution)/shard_map/rB3/ppermute | solution.py:28
  59.9 0.2 shard_map.74.refs_3_.refs_0_
  60.1 1.1 %collective-permute-done.17.refs_2_ = bf16[64,1152]{1,0:T(8,128)(2,1)S(1)} collective-permute-done((bf16[64,1152]{1,0:T(8,128)(2,1)S(1)}, bf16[64,1152]{1,0:T(8,128)(2,1)S(1)}, u32[]{:S(2)}, u32[]{:S(2)}) %collective-permute-start.17) | collective-permute-done | bytes 147488 | tf_op jit(solution)/shard_map/rZ4/ppermute | solution.py:28
  61.2 0.0 collective-permute-done.16.refs_1_
  61.2 0.1 shard_map.75.refs_0_
  61.3 3.5 %collective-permute-start.21 = (bf16[128,1152]{1,0:T(8,128)(2,1)S(1)}, bf16[128,1152]{1,0:T(8,128)(2,1)S(1)}, u32[]{:S(2)}, u32[]{:S(2)}) collective-permute-start(bf16[128,1152]{1,0:T(8,128)(2,1)S(1)} %shard_map.75.refs_0_), channel_id=1, source_target_pairs={{0,132},{1,5},{2,134},{3,7},{4,0},{5,129},{6,2},{7,131},{128,4},{1... | collective-permute-start | bytes 884744 | tf_op jit(solution)/shard_map/rZ2/ppermute | solution.py:28
  64.8 1.3 %collective-permute-done.15.refs_1_ = bf16[256,1152]{1,0:T(8,128)(2,1)S(1)} collective-permute-done((bf16[256,1152]{1,0:T(8,128)(2,1)S(1)}, bf16[256,1152]{1,0:T(8,128)(2,1)S(1)}, u32[]{:S(2)}, u32[]{:S(2)}) %collective-permute-start.15) | collective-permute-done | bytes 589856 | tf_op jit(solution)/shard_map/rB1/ppermute | solution.py:28
  66.0 0.1 shard_map.77
  66.1 0.1 collective-permute-start.18
  66.2 3.0 %collective-permute-start.19 = (bf16[64,1152]{1,0:T(8,128)(2,1)S(1)}, bf16[64,1152]{1,0:T(8,128)(2,1)S(1)}, u32[]{:S(2)}, u32[]{:S(2)}) collective-permute-start(bf16[64,1152]{1,0:T(8,128)(2,1)S(1)} %get-tuple-element.37), channel_id=1, source_target_pairs={{0,64},{1,17},{2,66},{3,19},{4,68},{5,21},{6,70},{7,23},{128,192},... | collective-permute-start | bytes 442376 | tf_op jit(solution)/shard_map/rA2/ppermute | solution.py:28
  69.3 0.0 collective-permute-start.20
  69.3 3.1 %collective-permute-done.21.refs_2_ = bf16[128,1152]{1,0:T(8,128)(2,1)S(1)} collective-permute-done((bf16[128,1152]{1,0:T(8,128)(2,1)S(1)}, bf16[128,1152]{1,0:T(8,128)(2,1)S(1)}, u32[]{:S(2)}, u32[]{:S(2)}) %collective-permute-start.21) | collective-permute-done | bytes 294944 | tf_op jit(solution)/shard_map/rZ2/ppermute | solution.py:28
  72.4 0.1 shard_map.78
  72.5 0.7 collective-permute-start.22
  73.2 0.0 collective-permute-done.18.refs_3_
  73.2 0.0 collective-permute-done.19.refs_4_
  73.2 2.5 %collective-permute-done.20.refs_5_ = bf16[64,1152]{1,0:T(8,128)(2,1)S(1)} collective-permute-done((bf16[64,1152]{1,0:T(8,128)(2,1)S(1)}, bf16[64,1152]{1,0:T(8,128)(2,1)S(1)}, u32[]{:S(2)}, u32[]{:S(2)}) %collective-permute-start.20) | collective-permute-done | bytes 147488 | tf_op jit(solution)/shard_map/rA3/ppermute | solution.py:28
  75.6 0.0 collective-permute-done.22.refs_9_
  75.6 1.1 %shard_map.79 = (f32[64,1152]{1,0:T(8,128)}, f32[64,1152]{1,0:T(8,128)}) custom-call(f32[64,1152]{1,0:T(8,128)S(1)} %get-tuple-element.23.refs_0_, f32[64,128]{1,0:T(8,128)S(1)} %get-tuple-element.24.refs_1_, f32[64,1152]{1,0:T(8,128)S(1)} %get-tuple-element.35.refs_2_, bf16[64,1152]{1,0:T(8,128)(2,1)S(1)} %collective-permute-done.18.refs_3_, ...), custom_call_target="tpu_custom_call" | custom-call | bytes 1024 | tf_op jit(solution)/shard_map/pallas_call | solution.py:55
  (7 shorter events, 0.0 us)
Async XLA Ops:
  0.6 10.4 %collective-permute-start.3 = (bf16[64,1152]{1,0:T(8,128)(2,1)}, bf16[64,1152]{1,0:T(8,128)(2,1)S(1)}, u32[]{:S(2)}, u32[]{:S(2)}) collective-permute-start(bf16[64,1152]{1,0:T(8,128)(2,1)} %refs_0_.3), channel_id=1, source_target_pairs={{0,1},{1,0},{2,3},{3,2},{4,5},{5,4},{6,7},{7,6},{128,129},{129,128... | collective-permute-start | bytes 442376 | tf_op jit(solution)/shard_map/gC/ppermute | solution.py:28
  0.7 11.2 %collective-permute-start = (bf16[64,1152]{1,0:T(8,128)(2,1)}, bf16[64,1152]{1,0:T(8,128)(2,1)S(1)}, u32[]{:S(2)}, u32[]{:S(2)}) collective-permute-start(bf16[64,1152]{1,0:T(8,128)(2,1)} %refs_0_.2), channel_id=1, source_target_pairs={{0,32},{1,9},{2,34},{3,11},{4,36},{5,13},{6,38},{7,15},{128,160},{... | collective-permute-start | bytes 442376 | tf_op jit(solution)/shard_map/gA1/ppermute | solution.py:28
  2.3 9.7 %collective-permute-start.1 = (bf16[64,1152]{1,0:T(8,128)(2,1)}, bf16[64,1152]{1,0:T(8,128)(2,1)S(1)}, u32[]{:S(2)}, u32[]{:S(2)}) collective-permute-start(bf16[64,1152]{1,0:T(8,128)(2,1)} %refs_0_.2), channel_id=1, source_target_pairs={{0,64},{1,17},{2,66},{3,19},{4,68},{5,21},{6,70},{7,23},{128,192},... | collective-permute-start | bytes 442376 | tf_op jit(solution)/shard_map/gA2/ppermute | solution.py:28
  5.0 6.9 %collective-permute-start.2 = (bf16[64,1152]{1,0:T(8,128)(2,1)}, bf16[64,1152]{1,0:T(8,128)(2,1)S(1)}, u32[]{:S(2)}, u32[]{:S(2)}) collective-permute-start(bf16[64,1152]{1,0:T(8,128)(2,1)} %refs_0_.2), channel_id=1, source_target_pairs={{0,96},{1,25},{2,98},{3,27},{4,100},{5,29},{6,102},{7,31},{128,224... | collective-permute-start | bytes 442376 | tf_op jit(solution)/shard_map/gA3/ppermute | solution.py:28
  6.5 10.9 %collective-permute-start.4 = (bf16[64,1152]{1,0:T(8,128)(2,1)}, bf16[64,1152]{1,0:T(8,128)(2,1)S(1)}, u32[]{:S(2)}, u32[]{:S(2)}) collective-permute-start(bf16[64,1152]{1,0:T(8,128)(2,1)} %refs_0_.3), channel_id=1, source_target_pairs={{0,4},{1,133},{2,6},{3,135},{4,128},{5,1},{6,130},{7,3},{128,132},... | collective-permute-start | bytes 442376 | tf_op jit(solution)/shard_map/gZ2/ppermute | solution.py:28
  11.0 1.0 %copy-start = (bf16[64,1152]{1,0:T(8,128)(2,1)S(1)}, bf16[64,1152]{1,0:T(8,128)(2,1)}, u32[]{:S(2)}) copy-start(bf16[64,1152]{1,0:T(8,128)(2,1)} %refs_0_.2) | copy-start | bytes 442372
  11.1 7.5 %collective-permute-start.5 = (bf16[64,1152]{1,0:T(8,128)(2,1)}, bf16[64,1152]{1,0:T(8,128)(2,1)S(1)}, u32[]{:S(2)}, u32[]{:S(2)}) collective-permute-start(bf16[64,1152]{1,0:T(8,128)(2,1)} %refs_0_.3), channel_id=1, source_target_pairs={{0,133},{1,4},{2,135},{3,6},{4,1},{5,128},{6,3},{7,130},{128,5},{1... | collective-permute-start | bytes 442376 | tf_op jit(solution)/shard_map/gX2/ppermute | solution.py:28
  12.0 6.6 %copy-start.1 = (bf16[64,1152]{1,0:T(8,128)(2,1)S(1)}, bf16[64,1152]{1,0:T(8,128)(2,1)}, u32[]{:S(2)}) copy-start(bf16[64,1152]{1,0:T(8,128)(2,1)} %refs_0_.3) | copy-start | bytes 442372
  12.2 23.8 %collective-permute-start.8 = (bf16[256,1152]{1,0:T(8,128)(2,1)S(1)}, bf16[256,1152]{1,0:T(8,128)(2,1)S(1)}, u32[]{:S(2)}, u32[]{:S(2)}) collective-permute-start(bf16[256,1152]{1,0:T(8,128)(2,1)S(1)} %shard_map.60.refs_0_), channel_id=1, source_target_pairs={{0,8},{1,33},{2,10},{3,35},{4,12},{5,37},{6,14},{7,39},{128,136},{... | collective-permute-start | bytes 1769480 | tf_op jit(solution)/shard_map/gB1/ppermute | solution.py:28
  15.3 20.8 %collective-permute-start.9 = (bf16[256,1152]{1,0:T(8,128)(2,1)S(1)}, bf16[256,1152]{1,0:T(8,128)(2,1)S(1)}, u32[]{:S(2)}, u32[]{:S(2)}) collective-permute-start(bf16[256,1152]{1,0:T(8,128)(2,1)S(1)} %shard_map.60.refs_0_), channel_id=1, source_target_pairs={{0,24},{1,97},{2,26},{3,99},{4,28},{5,101},{6,30},{7,103},{128,152... | collective-permute-start | bytes 1769480 | tf_op jit(solution)/shard_map/gB3/ppermute | solution.py:28
  15.3 20.8 %collective-permute-start.10 = (bf16[256,1152]{1,0:T(8,128)(2,1)S(1)}, bf16[256,1152]{1,0:T(8,128)(2,1)S(1)}, u32[]{:S(2)}, u32[]{:S(2)}) collective-permute-start(bf16[256,1152]{1,0:T(8,128)(2,1)S(1)} %shard_map.60.refs_0_), channel_id=1, source_target_pairs={{0,16},{1,65},{2,18},{3,67},{4,20},{5,69},{6,22},{7,71},{128,144},... | collective-permute-start | bytes 1769480 | tf_op jit(solution)/shard_map/gB2/ppermute | solution.py:28
  18.8 12.7 %collective-permute-start.6 = (bf16[256,1152]{1,0:T(8,128)(2,1)S(1)}, bf16[256,1152]{1,0:T(8,128)(2,1)S(1)}, u32[]{:S(2)}, u32[]{:S(2)}) collective-permute-start(bf16[256,1152]{1,0:T(8,128)(2,1)S(1)} %shard_map.61.refs_0_), channel_id=1, source_target_pairs={{0,2},{1,135},{2,4},{3,1},{4,6},{5,3},{6,128},{7,5},{128,130},{129... | collective-permute-start | bytes 1769480 | tf_op jit(solution)/shard_map/gZ13/ppermute | solution.py:28
  22.3 13.8 %collective-permute-start.7 = (bf16[64,1152]{1,0:T(8,128)(2,1)S(1)}, bf16[64,1152]{1,0:T(8,128)(2,1)S(1)}, u32[]{:S(2)}, u32[]{:S(2)}) collective-permute-start(bf16[64,1152]{1,0:T(8,128)(2,1)S(1)} %collective-permute-done.4.refs_2_), channel_id=1, source_target_pairs={{0,4},{1,133},{2,6},{3,135},{4,128},{5,1},{6,130},{7,3},{128,132},... | collective-permute-start | bytes 442376 | tf_op jit(solution)/shard_map/gZ4/ppermute | solution.py:28
  36.3 3.7 %collective-permute-start.11 = (bf16[512,1152]{1,0:T(8,128)(2,1)S(1)}, bf16[512,1152]{1,0:T(8,128)(2,1)S(1)}, u32[]{:S(2)}, u32[]{:S(2)}) collective-permute-start(bf16[512,1152]{1,0:T(8,128)(2,1)S(1)} %shard_map.66.refs_0_.refs_2_), channel_id=1, source_target_pairs={{0,1},{1,0},{2,3},{3,2},{4,5},{5,4},{6,7},{7,6},{128,129},{129,128... | collective-permute-start | bytes 3538952 | tf_op jit(solution)/shard_map/gS/ppermute | solution.py:28
  43.1 5.9 %collective-permute-start.12 = (bf16[512,1152]{1,0:T(8,128)(2,1)S(1)}, bf16[512,1152]{1,0:T(8,128)(2,1)S(1)}, u32[]{:S(2)}, u32[]{:S(2)}) collective-permute-start(bf16[512,1152]{1,0:T(8,128)(2,1)S(1)} %get-tuple-element.31.refs_4_), channel_id=1, source_target_pairs={{0,1},{1,0},{2,3},{3,2},{4,5},{5,4},{6,7},{7,6},{128,129},{129,128... | collective-permute-start | bytes 3538952 | tf_op jit(solution)/shard_map/rC/ppermute | solution.py:28
  44.5 11.5 %collective-permute-start.13 = (bf16[256,1152]{1,0:T(8,128)(2,1)S(1)}, bf16[256,1152]{1,0:T(8,128)(2,1)S(1)}, u32[]{:S(2)}, u32[]{:S(2)}) collective-permute-start(bf16[256,1152]{1,0:T(8,128)(2,1)S(1)} %shard_map.69.refs_4_), channel_id=1, source_target_pairs={{0,16},{1,65},{2,18},{3,67},{4,20},{5,69},{6,22},{7,71},{128,144},... | collective-permute-start | bytes 1769480 | tf_op jit(solution)/shard_map/rB2/ppermute | solution.py:28
  46.7 13.2 %collective-permute-start.14 = (bf16[256,1152]{1,0:T(8,128)(2,1)S(1)}, bf16[256,1152]{1,0:T(8,128)(2,1)S(1)}, u32[]{:S(2)}, u32[]{:S(2)}) collective-permute-start(bf16[256,1152]{1,0:T(8,128)(2,1)S(1)} %shard_map.70.refs_2_), channel_id=1, source_target_pairs={{0,8},{1,33},{2,10},{3,35},{4,12},{5,37},{6,14},{7,39},{128,136},{... | collective-permute-start | bytes 1769480 | tf_op jit(solution)/shard_map/rB3/ppermute | solution.py:28
  49.2 11.9 %collective-permute-start.16 = (bf16[256,1152]{1,0:T(8,128)(2,1)S(1)}, bf16[256,1152]{1,0:T(8,128)(2,1)S(1)}, u32[]{:S(2)}, u32[]{:S(2)}) collective-permute-start(bf16[256,1152]{1,0:T(8,128)(2,1)S(1)} %get-tuple-element.32.refs_4_), channel_id=1, source_target_pairs={{0,134},{1,3},{2,0},{3,5},{4,2},{5,7},{6,4},{7,129},{128,6},{129,1... | collective-permute-start | bytes 1769480 | tf_op jit(solution)/shard_map/rZ13/ppermute | solution.py:28
  50.6 10.5 %collective-permute-start.17 = (bf16[64,1152]{1,0:T(8,128)(2,1)S(1)}, bf16[64,1152]{1,0:T(8,128)(2,1)S(1)}, u32[]{:S(2)}, u32[]{:S(2)}) collective-permute-start(bf16[64,1152]{1,0:T(8,128)(2,1)S(1)} %get-tuple-element.34), channel_id=1, source_target_pairs={{0,132},{1,5},{2,134},{3,7},{4,0},{5,129},{6,2},{7,131},{128,4},{1... | collective-permute-start | bytes 442376 | tf_op jit(solution)/shard_map/rZ4/ppermute | solution.py:28
  54.6 11.4 %collective-permute-start.15 = (bf16[256,1152]{1,0:T(8,128)(2,1)S(1)}, bf16[256,1152]{1,0:T(8,128)(2,1)S(1)}, u32[]{:S(2)}, u32[]{:S(2)}) collective-permute-start(bf16[256,1152]{1,0:T(8,128)(2,1)S(1)} %shard_map.72.refs_4_), channel_id=1, source_target_pairs={{0,24},{1,97},{2,26},{3,99},{4,28},{5,101},{6,30},{7,103},{128,152... | collective-permute-start | bytes 1769480 | tf_op jit(solution)/shard_map/rB1/ppermute | solution.py:28
  61.3 11.1 %collective-permute-start.21 = (bf16[128,1152]{1,0:T(8,128)(2,1)S(1)}, bf16[128,1152]{1,0:T(8,128)(2,1)S(1)}, u32[]{:S(2)}, u32[]{:S(2)}) collective-permute-start(bf16[128,1152]{1,0:T(8,128)(2,1)S(1)} %shard_map.75.refs_0_), channel_id=1, source_target_pairs={{0,132},{1,5},{2,134},{3,7},{4,0},{5,129},{6,2},{7,131},{128,4},{1... | collective-permute-start | bytes 884744 | tf_op jit(solution)/shard_map/rZ2/ppermute | solution.py:28
  66.1 7.0 %collective-permute-start.18 = (bf16[64,1152]{1,0:T(8,128)(2,1)S(1)}, bf16[64,1152]{1,0:T(8,128)(2,1)S(1)}, u32[]{:S(2)}, u32[]{:S(2)}) collective-permute-start(bf16[64,1152]{1,0:T(8,128)(2,1)S(1)} %get-tuple-element.36), channel_id=1, source_target_pairs={{0,96},{1,25},{2,98},{3,27},{4,100},{5,29},{6,102},{7,31},{128,224... | collective-permute-start | bytes 442376 | tf_op jit(solution)/shard_map/rA1/ppermute | solution.py:28
  66.2 6.9 %collective-permute-start.19 = (bf16[64,1152]{1,0:T(8,128)(2,1)S(1)}, bf16[64,1152]{1,0:T(8,128)(2,1)S(1)}, u32[]{:S(2)}, u32[]{:S(2)}) collective-permute-start(bf16[64,1152]{1,0:T(8,128)(2,1)S(1)} %get-tuple-element.37), channel_id=1, source_target_pairs={{0,64},{1,17},{2,66},{3,19},{4,68},{5,21},{6,70},{7,23},{128,192},... | collective-permute-start | bytes 442376 | tf_op jit(solution)/shard_map/rA2/ppermute | solution.py:28
  69.3 6.4 %collective-permute-start.20 = (bf16[64,1152]{1,0:T(8,128)(2,1)S(1)}, bf16[64,1152]{1,0:T(8,128)(2,1)S(1)}, u32[]{:S(2)}, u32[]{:S(2)}) collective-permute-start(bf16[64,1152]{1,0:T(8,128)(2,1)S(1)} %get-tuple-element.38), channel_id=1, source_target_pairs={{0,32},{1,9},{2,34},{3,11},{4,36},{5,13},{6,38},{7,15},{128,160},{... | collective-permute-start | bytes 442376 | tf_op jit(solution)/shard_map/rA3/ppermute | solution.py:28
  72.5 3.2 %collective-permute-start.22 = (bf16[64,1152]{1,0:T(8,128)(2,1)S(1)}, bf16[64,1152]{1,0:T(8,128)(2,1)S(1)}, u32[]{:S(2)}, u32[]{:S(2)}) collective-permute-start(bf16[64,1152]{1,0:T(8,128)(2,1)S(1)} %get-tuple-element.43), channel_id=1, source_target_pairs={{0,1},{1,0},{2,3},{3,2},{4,5},{5,4},{6,7},{7,6},{128,129},{129,128... | collective-permute-start | bytes 442376 | tf_op jit(solution)/shard_map/rS/ppermute | solution.py:28

commit v16 on v15

--- a/solution.py
+++ b/solution.py
@@ -293,7 +293,7 @@
     (partial,) = call(partial_kernel, [((each, dim), F32)], [grad0, back2, back3])
     got13 = shift(part13, line(-1), "rZ13")
     got4 = shift(part4, line(-2), "rZ4")
-    (middle,) = call(middle_kernel, [((2 * own, dim), BF16)], [part2, got13, got4], [partial])
+    (middle,) = call(middle_kernel, [((2 * own, dim), BF16)], [part2, got13, got4], [token(got13, partial)])
     got2 = shift(middle, line(-2), "rZ2")
     txt_sum, txt_send = call(landed_kernel, [((own, dim), F32), ((own, dim), BF16)], [total_own, got13, got2])
     txt_last = shift(txt_send, other, "rS")

time: 76.8 us -> 76.8 us (level); the launches traced: 76.7 us -> 75.5 us
  waiting for transfers between devices: 24.8 us -> 23.6 us
    ppermute x23, waiting for transfers between devices: 24.8 us -> 23.6 us  [shift(): return lax.ppermute(values, AXES, pairs)]
    pallas_call x21 -> x22, Pallas kernels: 12.8 us -> 12.9 us  [call(): pl.pallas_call(lambda *refs: kernel(*refs[:n_in], *refs[n_in + len(ties):...]
where the time goes in v16:
time: 76.8 us; the launch traced here: 75.5 us
  starting transfers between devices  36.8 us (48%)
  waiting for transfers between devices  23.6 us (31%)
  Pallas kernels  12.9 us (17%)
  between operations  2.1 us (3%)
    ppermute x23, starting transfers between devices, shift(): return lax.ppermute(values, AXES, pairs)  36.8 us
    ppermute x23, waiting for transfers between devices, shift(): return lax.ppermute(values, AXES, pairs)  23.6 us
    pallas_call x22, Pallas kernels, call(): pl.pallas_call(lambda *refs: kernel(*refs[:n_in], *refs[n_in + len(ties):...  12.9 us
  transfers between devices with their start and end apart: 23, of which 9 were waited for; matrix products, arithmetic and copies ran while one was open for 0% of the time, Pallas kernels for 11%

profile of v16, /device:TPU:24, one launch (start us, length us, event | category | flops | bytes accessed | tf_op | source)
XLA Modules:
  0.0 75.5 jit_solution(13735152080402578180)
XLA Ops:
  0.6 0.1 collective-permute-start.3
  0.7 1.6 %collective-permute-start = (bf16[64,1152]{1,0:T(8,128)(2,1)}, bf16[64,1152]{1,0:T(8,128)(2,1)S(1)}, u32[]{:S(2)}, u32[]{:S(2)}) collective-permute-start(bf16[64,1152]{1,0:T(8,128)(2,1)} %refs_0_.2), channel_id=1, source_target_pairs={{0,32},{1,9},{2,34},{3,11},{4,36},{5,13},{6,38},{7,15},{128,160},{... | collective-permute-start | bytes 442376 | tf_op jit(solution)/shard_map/gA1/ppermute | solution.py:28
  2.3 2.7 %collective-permute-start.1 = (bf16[64,1152]{1,0:T(8,128)(2,1)}, bf16[64,1152]{1,0:T(8,128)(2,1)S(1)}, u32[]{:S(2)}, u32[]{:S(2)}) collective-permute-start(bf16[64,1152]{1,0:T(8,128)(2,1)} %refs_0_.2), channel_id=1, source_target_pairs={{0,64},{1,17},{2,66},{3,19},{4,68},{5,21},{6,70},{7,23},{128,192},... | collective-permute-start | bytes 442376 | tf_op jit(solution)/shard_map/gA2/ppermute | solution.py:28
  5.0 1.4 %collective-permute-start.2 = (bf16[64,1152]{1,0:T(8,128)(2,1)}, bf16[64,1152]{1,0:T(8,128)(2,1)S(1)}, u32[]{:S(2)}, u32[]{:S(2)}) collective-permute-start(bf16[64,1152]{1,0:T(8,128)(2,1)} %refs_0_.2), channel_id=1, source_target_pairs={{0,96},{1,25},{2,98},{3,27},{4,100},{5,29},{6,102},{7,31},{128,224... | collective-permute-start | bytes 442376 | tf_op jit(solution)/shard_map/gA3/ppermute | solution.py:28
  6.5 3.3 %collective-permute-start.4 = (bf16[64,1152]{1,0:T(8,128)(2,1)}, bf16[64,1152]{1,0:T(8,128)(2,1)S(1)}, u32[]{:S(2)}, u32[]{:S(2)}) collective-permute-start(bf16[64,1152]{1,0:T(8,128)(2,1)} %refs_0_.3), channel_id=1, source_target_pairs={{0,4},{1,133},{2,6},{3,135},{4,128},{5,1},{6,130},{7,3},{128,132},... | collective-permute-start | bytes 442376 | tf_op jit(solution)/shard_map/gZ2/ppermute | solution.py:28
  11.0 0.0 collective-permute-done.3.refs_0_.refs_1_
  11.1 0.9 %collective-permute-start.5 = (bf16[64,1152]{1,0:T(8,128)(2,1)}, bf16[64,1152]{1,0:T(8,128)(2,1)S(1)}, u32[]{:S(2)}, u32[]{:S(2)}) collective-permute-start(bf16[64,1152]{1,0:T(8,128)(2,1)} %refs_0_.3), channel_id=1, source_target_pairs={{0,133},{1,4},{2,135},{3,6},{4,1},{5,128},{6,3},{7,130},{128,5},{1... | collective-permute-start | bytes 442376 | tf_op jit(solution)/shard_map/gX2/ppermute | solution.py:28
  12.0 0.0 collective-permute-done.refs_1_
  12.0 0.0 collective-permute-done.1.refs_2_
  12.0 0.0 collective-permute-done.2.refs_3_
  12.0 0.2 shard_map.60.refs_0_
  12.2 3.0 %collective-permute-start.8 = (bf16[256,1152]{1,0:T(8,128)(2,1)S(1)}, bf16[256,1152]{1,0:T(8,128)(2,1)S(1)}, u32[]{:S(2)}, u32[]{:S(2)}) collective-permute-start(bf16[256,1152]{1,0:T(8,128)(2,1)S(1)} %shard_map.60.refs_0_), channel_id=1, source_target_pairs={{0,8},{1,33},{2,10},{3,35},{4,12},{5,37},{6,14},{7,39},{128,136},{... | collective-permute-start | bytes 1769480 | tf_op jit(solution)/shard_map/gB1/ppermute | solution.py:28
  15.3 0.0 collective-permute-start.9
  15.3 2.1 %collective-permute-start.10 = (bf16[256,1152]{1,0:T(8,128)(2,1)S(1)}, bf16[256,1152]{1,0:T(8,128)(2,1)S(1)}, u32[]{:S(2)}, u32[]{:S(2)}) collective-permute-start(bf16[256,1152]{1,0:T(8,128)(2,1)S(1)} %shard_map.60.refs_0_), channel_id=1, source_target_pairs={{0,16},{1,65},{2,18},{3,67},{4,20},{5,69},{6,22},{7,71},{128,144},... | collective-permute-start | bytes 1769480 | tf_op jit(solution)/shard_map/gB2/ppermute | solution.py:28
  17.4 0.0 collective-permute-done.4.refs_2_
  17.4 1.1 %collective-permute-done.5.refs_3_ = bf16[64,1152]{1,0:T(8,128)(2,1)S(1)} collective-permute-done((bf16[64,1152]{1,0:T(8,128)(2,1)}, bf16[64,1152]{1,0:T(8,128)(2,1)S(1)}, u32[]{:S(2)}, u32[]{:S(2)}) %collective-permute-start.5) | collective-permute-done | bytes 147488 | tf_op jit(solution)/shard_map/gX2/ppermute | solution.py:28
  18.6 0.2 shard_map.61.refs_0_
  18.8 3.5 %collective-permute-start.6 = (bf16[256,1152]{1,0:T(8,128)(2,1)S(1)}, bf16[256,1152]{1,0:T(8,128)(2,1)S(1)}, u32[]{:S(2)}, u32[]{:S(2)}) collective-permute-start(bf16[256,1152]{1,0:T(8,128)(2,1)S(1)} %shard_map.61.refs_0_), channel_id=1, source_target_pairs={{0,2},{1,135},{2,4},{3,1},{4,6},{5,3},{6,128},{7,5},{128,130},{129... | collective-permute-start | bytes 1769480 | tf_op jit(solution)/shard_map/gZ13/ppermute | solution.py:28
  22.3 1.7 %collective-permute-start.7 = (bf16[64,1152]{1,0:T(8,128)(2,1)S(1)}, bf16[64,1152]{1,0:T(8,128)(2,1)S(1)}, u32[]{:S(2)}, u32[]{:S(2)}) collective-permute-start(bf16[64,1152]{1,0:T(8,128)(2,1)S(1)} %collective-permute-done.4.refs_2_), channel_id=1, source_target_pairs={{0,4},{1,133},{2,6},{3,135},{4,128},{5,1},{6,130},{7,3},{128,132},... | collective-permute-start | bytes 442376 | tf_op jit(solution)/shard_map/gZ4/ppermute | solution.py:28
  24.0 7.5 %collective-permute-done.6.refs_2_.refs_1_ = bf16[256,1152]{1,0:T(8,128)(2,1)S(1)} collective-permute-done((bf16[256,1152]{1,0:T(8,128)(2,1)S(1)}, bf16[256,1152]{1,0:T(8,128)(2,1)S(1)}, u32[]{:S(2)}, u32[]{:S(2)}) %collective-permute-start.6) | collective-permute-done | bytes 589856 | tf_op jit(solution)/shard_map/gZ13/ppermute | solution.py:28
  31.5 0.1 shard_map.62.refs_1_
  31.6 0.2 shard_map.63
  31.8 0.2 shard_map.64
  32.0 4.1 %collective-permute-done.7.refs_2_ = bf16[64,1152]{1,0:T(8,128)(2,1)S(1)} collective-permute-done((bf16[64,1152]{1,0:T(8,128)(2,1)S(1)}, bf16[64,1152]{1,0:T(8,128)(2,1)S(1)}, u32[]{:S(2)}, u32[]{:S(2)}) %collective-permute-start.7) | collective-permute-done | bytes 147488 | tf_op jit(solution)/shard_map/gZ4/ppermute | solution.py:28
  36.0 0.0 collective-permute-done.8.refs_5_.refs_3_
  36.0 0.0 collective-permute-done.9.refs_6_.refs_4_
  36.0 0.0 collective-permute-done.10.refs_7_.refs_5_
  36.0 0.3 shard_map.66.refs_0_.refs_2_
  36.3 0.3 collective-permute-start.11
  36.6 3.4 %shard_map.67 = (bf16[1024,512]{1,0:T(8,128)(2,1)S(1)}, bf16[1024,1152]{1,0:T(8,128)(2,1)S(1)}, bf16[512,1152]{1,0:T(8,128)(2,1)S(1)}) custom-call(bf16[512,1152]{1,0:T(8,128)(2,1)S(1)} %shard_map.66.refs_0_.refs_2_, f32[8,128]{1,0:T(8,128)S(1)} %shard_map.62.refs_1_, bf16[256,1152]{1,0:T(8,128)(2,1)S(1)} %get-tuple-element.26.refs_3_.refs_2_, ...), custom_call_target="tpu_custom_call" | custom-call | flops 2415919104 | bytes 1024 | tf_op jit(solution)/shard_map/pallas_call | solution.py:55
  40.0 0.0 collective-permute-done.11.refs_0_.refs_3_
  40.1 3.0 %shard_map.68 = (bf16[1024,512]{1,0:T(8,128)(2,1)S(1)}, bf16[512,1152]{1,0:T(8,128)(2,1)S(1)}) custom-call(bf16[512,1152]{1,0:T(8,128)(2,1)S(1)} %collective-permute-done.11.refs_0_.refs_3_, f32[8,128]{1,0:T(8,128)S(1)} %shard_map.62.refs_1_, bf16[1024,1152]{1,0:T(8,128)(2,1)S(1)} %get-tuple-element.28.refs_2_, ...), custom_call_target="tpu_custom_call" | custom-call | flops 2415919104 | bytes 1024 | tf_op jit(solution)/shard_map/pallas_call | solution.py:55
  43.1 0.6 collective-permute-start.12
  43.7 0.8 %shard_map.69.refs_4_ = bf16[256,1152]{1,0:T(8,128)(2,1)S(1)} custom-call(bf16[1024,512]{1,0:T(8,128)(2,1)S(1)} %get-tuple-element.27.refs_0_, bf16[1024,512]{1,0:T(8,128)(2,1)S(1)} %get-tuple-element.30.refs_1_, bf16[512,1152]{1,0:T(8,128)(2,1)S(1)} %shard_map.66.refs_0_.refs_2_, bf16[512,1152]{1,0:T(8,128)(2,1)S(1)} %collective-permute-done.11.refs_0_.refs_3_, ...), custom_call_target="tpu_custom_call" | custom-call | flops 603979776 | bytes 1024 | tf_op jit(solution)/shard_map/pallas_call | solution.py:55
  44.5 1.3 %collective-permute-start.13 = (bf16[256,1152]{1,0:T(8,128)(2,1)S(1)}, bf16[256,1152]{1,0:T(8,128)(2,1)S(1)}, u32[]{:S(2)}, u32[]{:S(2)}) collective-permute-start(bf16[256,1152]{1,0:T(8,128)(2,1)S(1)} %shard_map.69.refs_4_), channel_id=1, source_target_pairs={{0,16},{1,65},{2,18},{3,67},{4,20},{5,69},{6,22},{7,71},{128,144},... | collective-permute-start | bytes 1769480 | tf_op jit(solution)/shard_map/rB2/ppermute | solution.py:28
  45.9 0.8 %shard_map.70.refs_2_ = bf16[256,1152]{1,0:T(8,128)(2,1)S(1)} custom-call(bf16[1024,512]{1,0:T(8,128)(2,1)S(1)} %get-tuple-element.27.refs_0_, bf16[1024,512]{1,0:T(8,128)(2,1)S(1)} %get-tuple-element.30.refs_1_, bf16[512,1152]{1,0:T(8,128)(2,1)S(1)} %shard_map.66.refs_0_.refs_2_, bf16[512,1152]{1,0:T(8,128)(2,1)S(1)} %collective-permute-done.11.refs_0_.refs_3_, ...), custom_call_target="tpu_custom_call" | custom-call | flops 603979776 | bytes 1024 | tf_op jit(solution)/shard_map/pallas_call | solution.py:55
  46.7 2.3 %collective-permute-start.14 = (bf16[256,1152]{1,0:T(8,128)(2,1)S(1)}, bf16[256,1152]{1,0:T(8,128)(2,1)S(1)}, u32[]{:S(2)}, u32[]{:S(2)}) collective-permute-start(bf16[256,1152]{1,0:T(8,128)(2,1)S(1)} %shard_map.70.refs_2_), channel_id=1, source_target_pairs={{0,8},{1,33},{2,10},{3,35},{4,12},{5,37},{6,14},{7,39},{128,136},{... | collective-permute-start | bytes 1769480 | tf_op jit(solution)/shard_map/rB3/ppermute | solution.py:28
  49.0 0.0 collective-permute-done.12.refs_1_
  49.0 0.3 shard_map.71
  49.2 1.4 %collective-permute-start.16 = (bf16[256,1152]{1,0:T(8,128)(2,1)S(1)}, bf16[256,1152]{1,0:T(8,128)(2,1)S(1)}, u32[]{:S(2)}, u32[]{:S(2)}) collective-permute-start(bf16[256,1152]{1,0:T(8,128)(2,1)S(1)} %get-tuple-element.32.refs_4_), channel_id=1, source_target_pairs={{0,134},{1,3},{2,0},{3,5},{4,2},{5,7},{6,4},{7,129},{128,6},{129,1... | collective-permute-start | bytes 1769480 | tf_op jit(solution)/shard_map/rZ13/ppermute | solution.py:28
  50.6 0.8 %shard_map.72.refs_4_ = bf16[256,1152]{1,0:T(8,128)(2,1)S(1)} custom-call(bf16[1024,512]{1,0:T(8,128)(2,1)S(1)} %get-tuple-element.27.refs_0_, bf16[1024,512]{1,0:T(8,128)(2,1)S(1)} %get-tuple-element.30.refs_1_, bf16[512,1152]{1,0:T(8,128)(2,1)S(1)} %shard_map.66.refs_0_.refs_2_, bf16[512,1152]{1,0:T(8,128)(2,1)S(1)} %collective-permute-done.11.refs_0_.refs_3_, ...), custom_call_target="tpu_custom_call" | custom-call | flops 603979776 | bytes 1024 | tf_op jit(solution)/shard_map/pallas_call | solution.py:55
  51.5 0.1 collective-permute-start.15
  51.6 3.4 %collective-permute-start.17 = (bf16[64,1152]{1,0:T(8,128)(2,1)S(1)}, bf16[64,1152]{1,0:T(8,128)(2,1)S(1)}, u32[]{:S(2)}, u32[]{:S(2)}) collective-permute-start(bf16[64,1152]{1,0:T(8,128)(2,1)S(1)} %get-tuple-element.34), channel_id=1, source_target_pairs={{0,132},{1,5},{2,134},{3,7},{4,0},{5,129},{6,2},{7,131},{128,4},{1... | collective-permute-start | bytes 442376 | tf_op jit(solution)/shard_map/rZ4/ppermute | solution.py:28
  55.0 0.8 %shard_map.73.refs_0_ = f32[256,1152]{1,0:T(8,128)S(1)} custom-call(bf16[1024,512]{1,0:T(8,128)(2,1)S(1)} %get-tuple-element.27.refs_0_, bf16[1024,512]{1,0:T(8,128)(2,1)S(1)} %get-tuple-element.30.refs_1_, bf16[512,1152]{1,0:T(8,128)(2,1)S(1)} %shard_map.66.refs_0_.refs_2_, bf16[512,1152]{1,0:T(8,128)(2,1)S(1)} %collective-permute-done.11.refs_0_.refs_3_, ...), custom_call_target="tpu_custom_call" | custom-call | flops 603979776 | bytes 1024 | tf_op jit(solution)/shard_map/pallas_call | solution.py:55
  55.8 0.2 collective-permute-done.13.refs_1_
  56.0 3.9 %collective-permute-done.14.refs_2_ = bf16[256,1152]{1,0:T(8,128)(2,1)S(1)} collective-permute-done((bf16[256,1152]{1,0:T(8,128)(2,1)S(1)}, bf16[256,1152]{1,0:T(8,128)(2,1)S(1)}, u32[]{:S(2)}, u32[]{:S(2)}) %collective-permute-start.14) | collective-permute-done | bytes 589856 | tf_op jit(solution)/shard_map/rB3/ppermute | solution.py:28
  59.9 0.2 shard_map.74.refs_1_.refs_0_
  60.1 0.1 collective-permute-done.16.refs_0_.refs_1_
  60.2 0.9 %collective-permute-done.17.refs_2_ = bf16[64,1152]{1,0:T(8,128)(2,1)S(1)} collective-permute-done((bf16[64,1152]{1,0:T(8,128)(2,1)S(1)}, bf16[64,1152]{1,0:T(8,128)(2,1)S(1)}, u32[]{:S(2)}, u32[]{:S(2)}) %collective-permute-start.17) | collective-permute-done | bytes 147488 | tf_op jit(solution)/shard_map/rZ4/ppermute | solution.py:28
  61.2 0.1 shard_map.76.refs_0_
  61.3 3.5 %collective-permute-start.21 = (bf16[128,1152]{1,0:T(8,128)(2,1)S(1)}, bf16[128,1152]{1,0:T(8,128)(2,1)S(1)}, u32[]{:S(2)}, u32[]{:S(2)}) collective-permute-start(bf16[128,1152]{1,0:T(8,128)(2,1)S(1)} %shard_map.76.refs_0_), channel_id=1, source_target_pairs={{0,132},{1,5},{2,134},{3,7},{4,0},{5,129},{6,2},{7,131},{128,4},{1... | collective-permute-start | bytes 884744 | tf_op jit(solution)/shard_map/rZ2/ppermute | solution.py:28
  64.8 0.0 collective-permute-done.15.refs_1_
  64.8 0.1 shard_map.78
  64.9 1.2 %collective-permute-start.18 = (bf16[64,1152]{1,0:T(8,128)(2,1)S(1)}, bf16[64,1152]{1,0:T(8,128)(2,1)S(1)}, u32[]{:S(2)}, u32[]{:S(2)}) collective-permute-start(bf16[64,1152]{1,0:T(8,128)(2,1)S(1)} %get-tuple-element.36), channel_id=1, source_target_pairs={{0,96},{1,25},{2,98},{3,27},{4,100},{5,29},{6,102},{7,31},{128,224... | collective-permute-start | bytes 442376 | tf_op jit(solution)/shard_map/rA1/ppermute | solution.py:28
  66.2 1.5 %collective-permute-start.19 = (bf16[64,1152]{1,0:T(8,128)(2,1)S(1)}, bf16[64,1152]{1,0:T(8,128)(2,1)S(1)}, u32[]{:S(2)}, u32[]{:S(2)}) collective-permute-start(bf16[64,1152]{1,0:T(8,128)(2,1)S(1)} %get-tuple-element.37), channel_id=1, source_target_pairs={{0,64},{1,17},{2,66},{3,19},{4,68},{5,21},{6,70},{7,23},{128,192},... | collective-permute-start | bytes 442376 | tf_op jit(solution)/shard_map/rA2/ppermute | solution.py:28
  67.6 0.3 collective-permute-start.20
  67.9 4.5 %collective-permute-done.21.refs_2_ = bf16[128,1152]{1,0:T(8,128)(2,1)S(1)} collective-permute-done((bf16[128,1152]{1,0:T(8,128)(2,1)S(1)}, bf16[128,1152]{1,0:T(8,128)(2,1)S(1)}, u32[]{:S(2)}, u32[]{:S(2)}) %collective-permute-start.21) | collective-permute-done | bytes 294944 | tf_op jit(solution)/shard_map/rZ2/ppermute | solution.py:28
  72.4 0.1 shard_map.79
  72.5 0.6 collective-permute-start.22
  73.1 0.0 collective-permute-done.18.refs_3_
  73.1 0.0 collective-permute-done.19.refs_4_
  73.1 1.3 %collective-permute-done.20.refs_5_ = bf16[64,1152]{1,0:T(8,128)(2,1)S(1)} collective-permute-done((bf16[64,1152]{1,0:T(8,128)(2,1)S(1)}, bf16[64,1152]{1,0:T(8,128)(2,1)S(1)}, u32[]{:S(2)}, u32[]{:S(2)}) %collective-permute-start.20) | collective-permute-done | bytes 147488 | tf_op jit(solution)/shard_map/rA3/ppermute | solution.py:28
  74.4 0.0 collective-permute-done.22.refs_9_
  74.4 1.1 %shard_map.80 = (f32[64,1152]{1,0:T(8,128)}, f32[64,1152]{1,0:T(8,128)}) custom-call(f32[64,1152]{1,0:T(8,128)S(1)} %get-tuple-element.23.refs_0_, f32[64,128]{1,0:T(8,128)S(1)} %get-tuple-element.24.refs_1_, f32[64,1152]{1,0:T(8,128)S(1)} %get-tuple-element.35.refs_2_, bf16[64,1152]{1,0:T(8,128)(2,1)S(1)} %collective-permute-done.18.refs_3_, ...), custom_call_target="tpu_custom_call" | custom-call | bytes 1024 | tf_op jit(solution)/shard_map/pallas_call | solution.py:55
  (8 shorter events, 0.0 us)
Async XLA Ops:
  0.6 10.4 %collective-permute-start.3 = (bf16[64,1152]{1,0:T(8,128)(2,1)}, bf16[64,1152]{1,0:T(8,128)(2,1)S(1)}, u32[]{:S(2)}, u32[]{:S(2)}) collective-permute-start(bf16[64,1152]{1,0:T(8,128)(2,1)} %refs_0_.3), channel_id=1, source_target_pairs={{0,1},{1,0},{2,3},{3,2},{4,5},{5,4},{6,7},{7,6},{128,129},{129,128... | collective-permute-start | bytes 442376 | tf_op jit(solution)/shard_map/gC/ppermute | solution.py:28
  0.7 11.2 %collective-permute-start = (bf16[64,1152]{1,0:T(8,128)(2,1)}, bf16[64,1152]{1,0:T(8,128)(2,1)S(1)}, u32[]{:S(2)}, u32[]{:S(2)}) collective-permute-start(bf16[64,1152]{1,0:T(8,128)(2,1)} %refs_0_.2), channel_id=1, source_target_pairs={{0,32},{1,9},{2,34},{3,11},{4,36},{5,13},{6,38},{7,15},{128,160},{... | collective-permute-start | bytes 442376 | tf_op jit(solution)/shard_map/gA1/ppermute | solution.py:28
  2.3 9.7 %collective-permute-start.1 = (bf16[64,1152]{1,0:T(8,128)(2,1)}, bf16[64,1152]{1,0:T(8,128)(2,1)S(1)}, u32[]{:S(2)}, u32[]{:S(2)}) collective-permute-start(bf16[64,1152]{1,0:T(8,128)(2,1)} %refs_0_.2), channel_id=1, source_target_pairs={{0,64},{1,17},{2,66},{3,19},{4,68},{5,21},{6,70},{7,23},{128,192},... | collective-permute-start | bytes 442376 | tf_op jit(solution)/shard_map/gA2/ppermute | solution.py:28
  5.0 6.9 %collective-permute-start.2 = (bf16[64,1152]{1,0:T(8,128)(2,1)}, bf16[64,1152]{1,0:T(8,128)(2,1)S(1)}, u32[]{:S(2)}, u32[]{:S(2)}) collective-permute-start(bf16[64,1152]{1,0:T(8,128)(2,1)} %refs_0_.2), channel_id=1, source_target_pairs={{0,96},{1,25},{2,98},{3,27},{4,100},{5,29},{6,102},{7,31},{128,224... | collective-permute-start | bytes 442376 | tf_op jit(solution)/shard_map/gA3/ppermute | solution.py:28
  6.5 10.9 %collective-permute-start.4 = (bf16[64,1152]{1,0:T(8,128)(2,1)}, bf16[64,1152]{1,0:T(8,128)(2,1)S(1)}, u32[]{:S(2)}, u32[]{:S(2)}) collective-permute-start(bf16[64,1152]{1,0:T(8,128)(2,1)} %refs_0_.3), channel_id=1, source_target_pairs={{0,4},{1,133},{2,6},{3,135},{4,128},{5,1},{6,130},{7,3},{128,132},... | collective-permute-start | bytes 442376 | tf_op jit(solution)/shard_map/gZ2/ppermute | solution.py:28
  11.0 1.0 %copy-start = (bf16[64,1152]{1,0:T(8,128)(2,1)S(1)}, bf16[64,1152]{1,0:T(8,128)(2,1)}, u32[]{:S(2)}) copy-start(bf16[64,1152]{1,0:T(8,128)(2,1)} %refs_0_.2) | copy-start | bytes 442372
  11.1 7.5 %collective-permute-start.5 = (bf16[64,1152]{1,0:T(8,128)(2,1)}, bf16[64,1152]{1,0:T(8,128)(2,1)S(1)}, u32[]{:S(2)}, u32[]{:S(2)}) collective-permute-start(bf16[64,1152]{1,0:T(8,128)(2,1)} %refs_0_.3), channel_id=1, source_target_pairs={{0,133},{1,4},{2,135},{3,6},{4,1},{5,128},{6,3},{7,130},{128,5},{1... | collective-permute-start | bytes 442376 | tf_op jit(solution)/shard_map/gX2/ppermute | solution.py:28
  12.0 6.6 %copy-start.1 = (bf16[64,1152]{1,0:T(8,128)(2,1)S(1)}, bf16[64,1152]{1,0:T(8,128)(2,1)}, u32[]{:S(2)}) copy-start(bf16[64,1152]{1,0:T(8,128)(2,1)} %refs_0_.3) | copy-start | bytes 442372
  12.2 23.8 %collective-permute-start.8 = (bf16[256,1152]{1,0:T(8,128)(2,1)S(1)}, bf16[256,1152]{1,0:T(8,128)(2,1)S(1)}, u32[]{:S(2)}, u32[]{:S(2)}) collective-permute-start(bf16[256,1152]{1,0:T(8,128)(2,1)S(1)} %shard_map.60.refs_0_), channel_id=1, source_target_pairs={{0,8},{1,33},{2,10},{3,35},{4,12},{5,37},{6,14},{7,39},{128,136},{... | collective-permute-start | bytes 1769480 | tf_op jit(solution)/shard_map/gB1/ppermute | solution.py:28
  15.3 20.8 %collective-permute-start.9 = (bf16[256,1152]{1,0:T(8,128)(2,1)S(1)}, bf16[256,1152]{1,0:T(8,128)(2,1)S(1)}, u32[]{:S(2)}, u32[]{:S(2)}) collective-permute-start(bf16[256,1152]{1,0:T(8,128)(2,1)S(1)} %shard_map.60.refs_0_), channel_id=1, source_target_pairs={{0,24},{1,97},{2,26},{3,99},{4,28},{5,101},{6,30},{7,103},{128,152... | collective-permute-start | bytes 1769480 | tf_op jit(solution)/shard_map/gB3/ppermute | solution.py:28
  15.3 20.8 %collective-permute-start.10 = (bf16[256,1152]{1,0:T(8,128)(2,1)S(1)}, bf16[256,1152]{1,0:T(8,128)(2,1)S(1)}, u32[]{:S(2)}, u32[]{:S(2)}) collective-permute-start(bf16[256,1152]{1,0:T(8,128)(2,1)S(1)} %shard_map.60.refs_0_), channel_id=1, source_target_pairs={{0,16},{1,65},{2,18},{3,67},{4,20},{5,69},{6,22},{7,71},{128,144},... | collective-permute-start | bytes 1769480 | tf_op jit(solution)/shard_map/gB2/ppermute | solution.py:28
  18.8 12.7 %collective-permute-start.6 = (bf16[256,1152]{1,0:T(8,128)(2,1)S(1)}, bf16[256,1152]{1,0:T(8,128)(2,1)S(1)}, u32[]{:S(2)}, u32[]{:S(2)}) collective-permute-start(bf16[256,1152]{1,0:T(8,128)(2,1)S(1)} %shard_map.61.refs_0_), channel_id=1, source_target_pairs={{0,2},{1,135},{2,4},{3,1},{4,6},{5,3},{6,128},{7,5},{128,130},{129... | collective-permute-start | bytes 1769480 | tf_op jit(solution)/shard_map/gZ13/ppermute | solution.py:28
  22.3 13.8 %collective-permute-start.7 = (bf16[64,1152]{1,0:T(8,128)(2,1)S(1)}, bf16[64,1152]{1,0:T(8,128)(2,1)S(1)}, u32[]{:S(2)}, u32[]{:S(2)}) collective-permute-start(bf16[64,1152]{1,0:T(8,128)(2,1)S(1)} %collective-permute-done.4.refs_2_), channel_id=1, source_target_pairs={{0,4},{1,133},{2,6},{3,135},{4,128},{5,1},{6,130},{7,3},{128,132},... | collective-permute-start | bytes 442376 | tf_op jit(solution)/shard_map/gZ4/ppermute | solution.py:28
  36.3 3.7 %collective-permute-start.11 = (bf16[512,1152]{1,0:T(8,128)(2,1)S(1)}, bf16[512,1152]{1,0:T(8,128)(2,1)S(1)}, u32[]{:S(2)}, u32[]{:S(2)}) collective-permute-start(bf16[512,1152]{1,0:T(8,128)(2,1)S(1)} %shard_map.66.refs_0_.refs_2_), channel_id=1, source_target_pairs={{0,1},{1,0},{2,3},{3,2},{4,5},{5,4},{6,7},{7,6},{128,129},{129,128... | collective-permute-start | bytes 3538952 | tf_op jit(solution)/shard_map/gS/ppermute | solution.py:28
  43.1 5.9 %collective-permute-start.12 = (bf16[512,1152]{1,0:T(8,128)(2,1)S(1)}, bf16[512,1152]{1,0:T(8,128)(2,1)S(1)}, u32[]{:S(2)}, u32[]{:S(2)}) collective-permute-start(bf16[512,1152]{1,0:T(8,128)(2,1)S(1)} %get-tuple-element.31.refs_4_), channel_id=1, source_target_pairs={{0,1},{1,0},{2,3},{3,2},{4,5},{5,4},{6,7},{7,6},{128,129},{129,128... | collective-permute-start | bytes 3538952 | tf_op jit(solution)/shard_map/rC/ppermute | solution.py:28
  44.5 11.5 %collective-permute-start.13 = (bf16[256,1152]{1,0:T(8,128)(2,1)S(1)}, bf16[256,1152]{1,0:T(8,128)(2,1)S(1)}, u32[]{:S(2)}, u32[]{:S(2)}) collective-permute-start(bf16[256,1152]{1,0:T(8,128)(2,1)S(1)} %shard_map.69.refs_4_), channel_id=1, source_target_pairs={{0,16},{1,65},{2,18},{3,67},{4,20},{5,69},{6,22},{7,71},{128,144},... | collective-permute-start | bytes 1769480 | tf_op jit(solution)/shard_map/rB2/ppermute | solution.py:28
  46.7 13.2 %collective-permute-start.14 = (bf16[256,1152]{1,0:T(8,128)(2,1)S(1)}, bf16[256,1152]{1,0:T(8,128)(2,1)S(1)}, u32[]{:S(2)}, u32[]{:S(2)}) collective-permute-start(bf16[256,1152]{1,0:T(8,128)(2,1)S(1)} %shard_map.70.refs_2_), channel_id=1, source_target_pairs={{0,8},{1,33},{2,10},{3,35},{4,12},{5,37},{6,14},{7,39},{128,136},{... | collective-permute-start | bytes 1769480 | tf_op jit(solution)/shard_map/rB3/ppermute | solution.py:28
  49.2 11.0 %collective-permute-start.16 = (bf16[256,1152]{1,0:T(8,128)(2,1)S(1)}, bf16[256,1152]{1,0:T(8,128)(2,1)S(1)}, u32[]{:S(2)}, u32[]{:S(2)}) collective-permute-start(bf16[256,1152]{1,0:T(8,128)(2,1)S(1)} %get-tuple-element.32.refs_4_), channel_id=1, source_target_pairs={{0,134},{1,3},{2,0},{3,5},{4,2},{5,7},{6,4},{7,129},{128,6},{129,1... | collective-permute-start | bytes 1769480 | tf_op jit(solution)/shard_map/rZ13/ppermute | solution.py:28
  51.5 13.3 %collective-permute-start.15 = (bf16[256,1152]{1,0:T(8,128)(2,1)S(1)}, bf16[256,1152]{1,0:T(8,128)(2,1)S(1)}, u32[]{:S(2)}, u32[]{:S(2)}) collective-permute-start(bf16[256,1152]{1,0:T(8,128)(2,1)S(1)} %shard_map.72.refs_4_), channel_id=1, source_target_pairs={{0,24},{1,97},{2,26},{3,99},{4,28},{5,101},{6,30},{7,103},{128,152... | collective-permute-start | bytes 1769480 | tf_op jit(solution)/shard_map/rB1/ppermute | solution.py:28
  51.6 9.6 %collective-permute-start.17 = (bf16[64,1152]{1,0:T(8,128)(2,1)S(1)}, bf16[64,1152]{1,0:T(8,128)(2,1)S(1)}, u32[]{:S(2)}, u32[]{:S(2)}) collective-permute-start(bf16[64,1152]{1,0:T(8,128)(2,1)S(1)} %get-tuple-element.34), channel_id=1, source_target_pairs={{0,132},{1,5},{2,134},{3,7},{4,0},{5,129},{6,2},{7,131},{128,4},{1... | collective-permute-start | bytes 442376 | tf_op jit(solution)/shard_map/rZ4/ppermute | solution.py:28
  61.3 11.1 %collective-permute-start.21 = (bf16[128,1152]{1,0:T(8,128)(2,1)S(1)}, bf16[128,1152]{1,0:T(8,128)(2,1)S(1)}, u32[]{:S(2)}, u32[]{:S(2)}) collective-permute-start(bf16[128,1152]{1,0:T(8,128)(2,1)S(1)} %shard_map.76.refs_0_), channel_id=1, source_target_pairs={{0,132},{1,5},{2,134},{3,7},{4,0},{5,129},{6,2},{7,131},{128,4},{1... | collective-permute-start | bytes 884744 | tf_op jit(solution)/shard_map/rZ2/ppermute | solution.py:28
  64.9 8.2 %collective-permute-start.18 = (bf16[64,1152]{1,0:T(8,128)(2,1)S(1)}, bf16[64,1152]{1,0:T(8,128)(2,1)S(1)}, u32[]{:S(2)}, u32[]{:S(2)}) collective-permute-start(bf16[64,1152]{1,0:T(8,128)(2,1)S(1)} %get-tuple-element.36), channel_id=1, source_target_pairs={{0,96},{1,25},{2,98},{3,27},{4,100},{5,29},{6,102},{7,31},{128,224... | collective-permute-start | bytes 442376 | tf_op jit(solution)/shard_map/rA1/ppermute | solution.py:28
  66.2 6.9 %collective-permute-start.19 = (bf16[64,1152]{1,0:T(8,128)(2,1)S(1)}, bf16[64,1152]{1,0:T(8,128)(2,1)S(1)}, u32[]{:S(2)}, u32[]{:S(2)}) collective-permute-start(bf16[64,1152]{1,0:T(8,128)(2,1)S(1)} %get-tuple-element.37), channel_id=1, source_target_pairs={{0,64},{1,17},{2,66},{3,19},{4,68},{5,21},{6,70},{7,23},{128,192},... | collective-permute-start | bytes 442376 | tf_op jit(solution)/shard_map/rA2/ppermute | solution.py:28
  67.6 6.7 %collective-permute-start.20 = (bf16[64,1152]{1,0:T(8,128)(2,1)S(1)}, bf16[64,1152]{1,0:T(8,128)(2,1)S(1)}, u32[]{:S(2)}, u32[]{:S(2)}) collective-permute-start(bf16[64,1152]{1,0:T(8,128)(2,1)S(1)} %get-tuple-element.38), channel_id=1, source_target_pairs={{0,32},{1,9},{2,34},{3,11},{4,36},{5,13},{6,38},{7,15},{128,160},{... | collective-permute-start | bytes 442376 | tf_op jit(solution)/shard_map/rA3/ppermute | solution.py:28
  72.5 1.9 %collective-permute-start.22 = (bf16[64,1152]{1,0:T(8,128)(2,1)S(1)}, bf16[64,1152]{1,0:T(8,128)(2,1)S(1)}, u32[]{:S(2)}, u32[]{:S(2)}) collective-permute-start(bf16[64,1152]{1,0:T(8,128)(2,1)S(1)} %get-tuple-element.43), channel_id=1, source_target_pairs={{0,1},{1,0},{2,3},{3,2},{4,5},{5,4},{6,7},{7,6},{128,129},{129,128... | collective-permute-start | bytes 442376 | tf_op jit(solution)/shard_map/rS/ppermute | solution.py:28
